TPU v7x, 32 devices: a whole 2x2x4 slice. The times are simulated.
32 devices in a mesh: groups: 2 (over x), gx: 4 (over z), gy: 4 (over y, core).
Axes of the slice: x: 2, y: 2, z: 4, core: 2. Of those that a mesh axis runs over, the one named last changes fastest.
Arguments:
- tokens: bfloat16 [16, 4, 2, 9216], P('groups', 'gx', None, 'gy'), parts along dimension 0, may hold values from -6 to 6
- gain: float32 [9216], P('gy'), may hold values from 0.1 to 1.9
- w_query: bfloat16 [9216, 6144], P('gy', 'gx'), may hold values from -0.15625 to 0.15625
- w_keyval: bfloat16 [9216, 512], P('gy', 'gx'), may hold values from -0.0625 to 0.0625
- w_gate: bfloat16 [9216, 36864], P('gy', 'gx'), may hold values from -0.0625 to 0.0625
- w_up: bfloat16 [9216, 36864], P('gy', 'gx'), may hold values from -0.0625 to 0.0625
- cache: bfloat16 [16, 4, 1024, 512], P(('groups', 'gy'), 'gx'), parts along dimension 0, may hold values from -40 to 40
- lengths: int32 [16, 4], P(('groups', 'gy'), 'gx'), parts along dimension 0, may hold values from 1 to 1024, as said below
Outputs:
- context: bfloat16 [16, 4, 2, 6144], P(('groups', 'gy'), 'gx'), parts along dimension 0
- hidden: bfloat16 [16, 4, 2, 36864], P(('groups', 'gy'), None, None, 'gx'), parts along dimension 0
There are 2 independent parts, one for each index of `groups`. A program takes and returns all parts, laid end to end along the dimension named above; an argument that names none is the same for every part. Nothing has to cross between parts.
Inputs may be any that keep to these rules, and one draw needn't show every extreme that they name: `lengths`: the largest of each draw is exactly 1024.
All inputs are finite; a program needn't handle non-finite values.
Results may differ from a plain program's by a relative error of at most 0.012.
The roundings to bfloat16 on the way count: a program that leaves them out, or rounds other values in their place, can miss the bound.
Values may be sent and summed in bfloat16 or wider, within the bound.
No kernel may reach another device: no remote copies, remote signals or barrier semaphores. Data moves between devices by JAX's collectives and lax.ppermute only.
A program may use at most 192 MiB of HBM per device.

v0:
```python
import jax
import jax.numpy as jnp
from jax import lax
from jax.sharding import PartitionSpec as P

D = 9216
HEADS = 24
HD = 256


EPSILON = 1e-05
MASKED = -1e30


def scale_rows(floats, sums, squares, gain):
    average = sums / D
    inverse_std = lax.rsqrt(squares / D - average * average + EPSILON)
    return ((floats - average[..., None]) * inverse_std[..., None] * gain).astype(jnp.bfloat16)


def attend(queries, new_pairs, cache, lengths):
    batch = queries.shape[0]
    steps = queries.shape[1]
    every_head = queries.reshape(batch, steps * HEADS, HD)
    stored_key_cache = cache[..., :HD]
    stored_value_cache = cache[..., HD:]
    appended_keys = new_pairs[..., :HD]
    appended_values = new_pairs[..., HD:]
    rescale_factor = HD ** (-0.5)
    cache_scores = (
        jnp.einsum("eaf,eif->eai", every_head, stored_key_cache, preferred_element_type=jnp.float32)
        * rescale_factor
    )
    positions = jnp.arange(cache.shape[1], dtype=jnp.int32)
    visible = positions[None, None, :] < lengths[:, None, None]
    cache_scores = jnp.where(visible, cache_scores, MASKED)
    new_token_scores = (
        jnp.einsum("izr,igr->izg", every_head, appended_keys, preferred_element_type=jnp.float32)
        * rescale_factor
    )
    owner_step = jnp.arange(steps * HEADS, dtype=jnp.int32) // HEADS
    causal = jnp.arange(steps, dtype=jnp.int32)[None, :] <= owner_step[:, None]
    new_token_scores = jnp.where(causal[None], new_token_scores, MASKED)
    highest = jnp.maximum(jnp.max(cache_scores, axis=-1), jnp.max(new_token_scores, axis=-1))
    exp_cached = jnp.exp(cache_scores - highest[..., None])
    exp_fresh = jnp.exp(new_token_scores - highest[..., None])
    totals = jnp.sum(exp_cached, axis=-1) + jnp.sum(exp_fresh, axis=-1)
    cache_part_weight = (exp_cached / totals[..., None]).astype(jnp.bfloat16)
    new_part_weight = (exp_fresh / totals[..., None]).astype(jnp.bfloat16)
    context = jnp.einsum(
        "wyi,wit->wyt", cache_part_weight, stored_value_cache, preferred_element_type=jnp.float32
    )
    context = context + jnp.einsum(
        "nga,nax->ngx", new_part_weight, appended_values, preferred_element_type=jnp.float32
    )
    return context.astype(jnp.bfloat16).reshape(batch, steps, HEADS * HD)


def on_device(tokens, gain, w_query, w_keyval, w_gate, w_up, cache, lengths):
    floats = tokens.astype(jnp.float32)
    sums, squares = lax.psum((jnp.sum(floats, axis=-1), jnp.sum(floats * floats, axis=-1)), "gy")
    normed = scale_rows(floats, sums, squares, gain)
    gathered = lax.all_gather(normed, "gx", axis=1, tiled=True)
    features = gathered.shape[-1]
    row_block = gathered.reshape(-1, features)
    matrices = (w_query, w_keyval, w_gate, w_up)
    joined = lax.psum_scatter(
        jnp.concatenate(
            [jnp.dot(row_block, matrix, preferred_element_type=jnp.float32) for matrix in matrices],
            axis=1,
        ),
        "gy",
        scatter_dimension=0,
        tiled=True,
    )
    query_cols = w_query.shape[1]
    pair_cols = w_keyval.shape[1]
    hidden_cols = w_gate.shape[1]
    local_seqs = cache.shape[0]
    mesh_x = lax.axis_size("gx")
    steps = tokens.shape[2]
    queries = (
        joined[:, :query_cols].astype(jnp.bfloat16).reshape(local_seqs, mesh_x, steps, query_cols)
    )
    pairs = (
        joined[:, query_cols : query_cols + pair_cols]
        .astype(jnp.bfloat16)
        .reshape(local_seqs, mesh_x, steps, pair_cols)
    )
    gate_start = query_cols + pair_cols
    gate_part = joined[:, gate_start : gate_start + hidden_cols]
    up_part = joined[:, gate_start + hidden_cols :]
    hidden = (
        (jax.nn.silu(gate_part) * up_part)
        .astype(jnp.bfloat16)
        .reshape(local_seqs, mesh_x, steps, hidden_cols)
    )
    queries, pairs = (
        lax.all_to_all(queries, "gx", split_axis=1, concat_axis=3, tiled=True),
        lax.all_to_all(pairs, "gx", split_axis=1, concat_axis=3, tiled=True),
    )
    context = attend(
        queries.reshape(local_seqs, steps, HEADS * HD),
        pairs.reshape(local_seqs, steps, 2 * HD),
        cache.reshape(local_seqs, cache.shape[2], cache.shape[3]),
        lengths.reshape(local_seqs),
    )
    return (context.reshape(local_seqs, 1, steps, HEADS * HD), hidden)


def solution(mesh):
    return jax.shard_map(
        on_device,
        mesh=mesh,
        in_specs=(
            P("groups", "gx", None, "gy"),
            P("gy"),
            P("gy", "gx"),
            P("gy", "gx"),
            P("gy", "gx"),
            P("gy", "gx"),
            P(("groups", "gy"), "gx", None, None),
            P(("groups", "gy"), "gx"),
        ),
        out_specs=(P(("groups", "gy"), "gx", None, None), P(("groups", "gy"), None, None, "gx")),
        check_vma=False,
    )
```

profile of v0, /device:TPU:0, one launch (start us, length us, event | category | flops | bytes accessed | tf_op | source)
XLA Modules:
  0.0 155.2 jit_solution(4279975210067418155)
XLA Ops:
  7.2 0.0 copy-start
  7.2 0.0 reduce-scatter.2.cloned.1.call-start
  7.2 1.1 convert_reduce_fusion
  8.4 0.1 copy.14
  8.4 0.1 copy.16
  8.5 8.3 %all-reduce = (f32[8,1,2]{0,2,1:T(2,128)S(1)}, f32[8,1,2]{0,2,1:T(2,128)S(1)}) all-reduce(f32[8,1,2]{0,2,1:T(2,128)S(1)} %bitcast.35, f32[8,1,2]{0,2,1:T(2,128)S(1)} %bitcast.34), channel_id=1, replica_groups=mesh['groups'=2,'gx'=4,'gy'=4] {'gy'}, use_global_device_ids=true, to_apply=%region_3.0 | all-reduce | flops 32 | bytes 256 | tf_op jit(solution)/shard_map/psum | solution.py:61
  16.9 0.1 copy.15
  17.0 0.1 copy.17
  17.0 1.1 fusion.12
  18.1 14.3 %all_gather.3 = bf16[8,4,2,2304]{3,2,1,0:T(2,128)(2,1)S(1)} all-gather(bf16[8,1,2,2304]{3,2,1,0:T(2,128)(2,1)S(1)} %fusion.12), channel_id=1, replica_groups=mesh['groups'=2,'gx'=4,'gy'=4] {'gx'}, dimensions={1}, use_global_device_ids=true | all-gather | bytes 368640 | tf_op jit(solution)/shard_map/all_gather | solution.py:63
  32.4 0.1 reshape.100
  32.5 16.9 %fusion.23 = f32[64,9216]{1,0:T(8,128)S(1)} fusion(bf16[64,2304]{1,0:T(8,128)(2,1)S(1)} %reshape.100, bf16[2304,9216]{1,0:T(8,128)(2,1)} %param.12), kind=kOutput, calls=%fused_computation.43 | convolution fusion | flops 2717908992 | bytes 45121536 | tf_op jit(solution)/shard_map/dot_general | solution.py:69
  49.5 16.9 %fusion.24 = f32[64,9216]{1,0:T(8,128)S(1)} fusion(bf16[64,2304]{1,0:T(8,128)(2,1)S(1)} %reshape.100, bf16[2304,9216]{1,0:T(8,128)(2,1)} %param.13), kind=kOutput, calls=%fused_computation.44 | convolution fusion | flops 2717908992 | bytes 45121536 | tf_op jit(solution)/shard_map/dot_general | solution.py:69
  66.4 4.3 %fusion.21 = f32[64,1536]{1,0:T(8,128)S(1)} fusion(bf16[64,2304]{1,0:T(8,128)(2,1)S(1)} %reshape.100, bf16[2304,1536]{1,0:T(8,128)(2,1)} %param.10), kind=kOutput, calls=%fused_computation.41 | convolution fusion | flops 452984832 | bytes 7766016 | tf_op jit(solution)/shard_map/dot_general | solution.py:69
  70.7 0.0 copy-done
  70.7 0.2 fusion.22
  70.9 2.6 %pad_maximum_fusion = f32[64,20096]{1,0:T(8,128)} fusion(f32[64,9216]{1,0:T(8,128)S(1)} %fusion.24, f32[64,9216]{1,0:T(8,128)S(1)} %fusion.23, f32[64,128]{1,0:T(8,128)S(1)} %fusion.22, f32[64,1536]{1,0:T(8,128)S(1)} %fusion.21), kind=kLoop, calls=%fused_computation | loop fusion | flops 3858432 | bytes 10289152 | tf_op jit(solution)/shard_map/concatenate | solution.py:68
  73.6 0.0 copy-start.1
  73.6 0.0 copy-start.2
  73.6 0.0 reduce-scatter.2.cloned.1.call-update
  73.6 0.6 copy-done.1
  74.2 0.1 iota_compare_fusion
  74.3 50.8 %reduce-scatter.2.cloned.1.call-done = f32[16,20096]{1,0:T(8,128)} async-done(((f32[64,20096]{1,0:T(8,128)}), f32[16,20096]{1,0:T(8,128)}) %reduce-scatter.2.cloned.1.call-update) | async-done | bytes 1286160 | tf_op jit(solution)/shard_map/reduce_scatter | solution.py:67
  125.1 1.4 convert.4
  126.5 0.6 copy.20
  127.1 4.6 %all-to-all-start.1 = ((bf16[2,4,2,128]{3,2,0,1:T(2,128)(2,1)}), bf16[2,4,2,128]{3,2,0,1:T(2,128)(2,1)S(1)}, u32[]{:S(2)}, u32[]{:S(2)}) async-start(bf16[2,4,2,128]{3,2,0,1:T(2,128)(2,1)} %copy.20), calls=%async_computation.2 | async-start | bytes 8192 | tf_op jit(solution)/shard_map/all_to_all | solution.py:100
  131.7 0.7 copy.18
  132.4 4.9 %all-to-all-done.1 = bf16[2,4,2,128]{3,2,0,1:T(2,128)(2,1)S(1)} async-done(((bf16[2,4,2,128]{3,2,0,1:T(2,128)(2,1)}), bf16[2,4,2,128]{3,2,0,1:T(2,128)(2,1)S(1)}, u32[]{:S(2)}, u32[]{:S(2)}) %all-to-all-start.1) | async-done | bytes 4128 | tf_op jit(solution)/shard_map/all_to_all | solution.py:100
  137.2 3.3 %all-to-all-start = ((bf16[2,4,2,1536]{3,2,0,1:T(2,128)(2,1)}), bf16[2,4,2,1536]{3,2,0,1:T(2,128)(2,1)S(1)}, u32[]{:S(2)}, u32[]{:S(2)}) async-start(bf16[2,4,2,1536]{3,2,0,1:T(2,128)(2,1)} %copy.18), calls=%async_computation.1 | async-start | bytes 98304 | tf_op jit(solution)/shard_map/all_to_all | solution.py:99
  140.5 1.4 fusion.6
  141.9 0.8 reshape.105
  142.8 3.4 %all-to-all-done = bf16[2,4,2,1536]{3,2,0,1:T(2,128)(2,1)S(1)} async-done(((bf16[2,4,2,1536]{3,2,0,1:T(2,128)(2,1)}), bf16[2,4,2,1536]{3,2,0,1:T(2,128)(2,1)S(1)}, u32[]{:S(2)}, u32[]{:S(2)}) %all-to-all-start) | async-done | bytes 49184 | tf_op jit(solution)/shard_map/all_to_all | solution.py:99
  146.2 0.1 fusion.20
  146.4 0.0 copy-done.2
  146.4 0.5 fusion.19
  146.9 0.2 fusion.7
  147.2 0.4 fusion.3
  147.5 0.2 fusion.1
  147.7 0.6 reshape_reshape.7
  (13 shorter events, 0.2 us)
Async XLA Ops:
  7.2 63.5 %copy-start = (bf16[2304,128]{1,0:T(8,128)(2,1)S(1)}, bf16[2304,128]{1,0:T(8,128)(2,1)}, u32[]{:S(2)}) copy-start(bf16[2304,128]{1,0:T(8,128)(2,1)} %param.11) | copy-start | bytes 1769476
  7.2 117.9 %reduce-scatter.2.cloned.1.call-start = ((), (), s32[]{:S(2)}) async-start(), calls=%async_computation.3 | async-start | bytes 6430720 | tf_op jit(solution)/shard_map/reduce_scatter | solution.py:67
  73.6 0.7 copy-start.1
  73.6 72.8 %copy-start.2 = (bf16[2,1,1024,512]{3,2,1,0:T(8,128)(2,1)S(1)}, bf16[2,1,1024,512]{3,2,1,0:T(8,128)(2,1)}, u32[]{:S(2)}) copy-start(bf16[2,1,1024,512]{3,2,1,0:T(8,128)(2,1)} %param.14) | copy-start | bytes 6291460
  127.1 10.2 %all-to-all-start.1 = ((bf16[2,4,2,128]{3,2,0,1:T(2,128)(2,1)}), bf16[2,4,2,128]{3,2,0,1:T(2,128)(2,1)S(1)}, u32[]{:S(2)}, u32[]{:S(2)}) async-start(bf16[2,4,2,128]{3,2,0,1:T(2,128)(2,1)} %copy.20), calls=%async_computation.2 | async-start | bytes 8192 | tf_op jit(solution)/shard_map/all_to_all | solution.py:100
  137.2 8.9 %all-to-all-start = ((bf16[2,4,2,1536]{3,2,0,1:T(2,128)(2,1)}), bf16[2,4,2,1536]{3,2,0,1:T(2,128)(2,1)S(1)}, u32[]{:S(2)}, u32[]{:S(2)}) async-start(bf16[2,4,2,1536]{3,2,0,1:T(2,128)(2,1)} %copy.18), calls=%async_computation.1 | async-start | bytes 98304 | tf_op jit(solution)/shard_map/all_to_all | solution.py:99
Sparse Core Ops, SparseCore 0:
  73.7 51.3 reduce-scatter.1
where the time goes:
time: 156 us; the launch traced here: 155 us
  waiting for transfers between devices  59.1 us (38%)
  matrix products  39.6 us (25%)
  blocking collectives  22.6 us (14%)
  between operations  14.2 us (9%)
  other arithmetic  7.95 us (5%)
  starting transfers between devices  7.9 us (5%)
  local copies, waits for them, and re-layouts  3.89 us (2%)
    reduce_scatter x1, waiting for transfers between devices, on_device(): lax.psum_scatter(jnp.concatenate([jnp.dot(row_block, matrix, preferred_el...  50.8 us
    dot_general x4, matrix products, on_device(): jnp.dot(row_block, matrix, preferred_element_type=jnp.float32)  38.4 us
    all_gather x1, blocking collectives, on_device(): gathered = lax.all_gather(normed, 'gx', axis=1, tiled=True)  14.3 us
    psum x1, blocking collectives, on_device(): lax.psum((jnp.sum(floats, axis=-1), jnp.sum(floats * floats, axis=-1)), '...  8.34 us
    all_to_all x1, waiting for transfers between devices, on_device(): lax.all_to_all(pairs, 'gx', split_axis=1, concat_axis=3, tiled=True)  4.87 us
    all_to_all x1, starting transfers between devices, on_device(): lax.all_to_all(pairs, 'gx', split_axis=1, concat_axis=3, tiled=True)  4.58 us
    all_to_all x1, waiting for transfers between devices, on_device(): lax.all_to_all(queries, 'gx', split_axis=1, concat_axis=3, tiled=True)  3.41 us
    all_to_all x1, starting transfers between devices, on_device(): lax.all_to_all(queries, 'gx', split_axis=1, concat_axis=3, tiled=True)  3.27 us
  transfers between devices with their start and end apart: 3, of which 3 were waited for; matrix products, arithmetic and copies ran while one was open for 2% of the time, Pallas kernels for 0%

commit v1 on v0

v1 whole, which is shorter than its diff:
```python
import functools

import jax
import jax.numpy as jnp
from jax import lax
from jax.experimental import pallas as pl
from jax.experimental.pallas import tpu as pltpu
from jax.sharding import PartitionSpec as P

D = 9216
HEADS = 24
HD = 256
EPSILON = 1e-05
MASKED = -1e30
MIB = 1024 * 1024
F32 = jnp.float32
BF16 = jnp.bfloat16


def whole(memory_space=pltpu.VMEM):
    return pl.BlockSpec(memory_space=memory_space)


def params(mib):
    return pltpu.CompilerParams(vmem_limit_bytes=mib * MIB)


def tile_of(cols, most):
    best = cols
    for tile in range(128, min(cols, most) + 1, 128):
        if cols % tile == 0:
            best = tile
    return best


def stats_kernel(tokens_ref, out_ref):
    floats = tokens_ref[...].astype(F32)
    sums = jnp.sum(floats, axis=-1, keepdims=True)
    squares = jnp.sum(floats * floats, axis=-1, keepdims=True)
    lane = lax.broadcasted_iota(jnp.int32, out_ref.shape, 1)
    out_ref[...] = jnp.where(lane < 64, sums, squares)


def partial_stats(tokens):
    return pl.pallas_call(
        stats_kernel,
        out_shape=jax.ShapeDtypeStruct((tokens.shape[0], 128), F32),
        in_specs=[whole()],
        out_specs=whole(),
    )(tokens)


def norm_kernel(count, source_ref, gain_ref, *refs):
    token_refs, stat_refs, out_ref = refs[:count], refs[count : 2 * count], refs[2 * count]
    gain = gain_ref[...]
    parts = []
    for token_ref, stat_ref in zip(token_refs, stat_refs):
        stats = stat_ref[...]
        average = stats[:, 0:1] / D
        inverse_std = lax.rsqrt(stats[:, 64:65] / D - average * average + EPSILON)
        floats = token_ref[...].astype(F32)
        parts.append(((floats - average) * inverse_std * gain).astype(BF16))
    normed = jnp.concatenate(parts, axis=0)
    rows = normed.shape[0]
    place = lax.broadcasted_iota(jnp.int32, (rows, rows), 1) == source_ref[...]
    out_ref[...] = jnp.dot(
        jnp.where(place, 1.0, 0.0).astype(BF16), normed, preferred_element_type=F32
    ).astype(BF16)


def normed_rows(source, gain, tokens, stats):
    rows = sum(t.shape[0] for t in tokens)
    features = gain.shape[0]
    return pl.pallas_call(
        functools.partial(norm_kernel, len(tokens)),
        out_shape=jax.ShapeDtypeStruct((rows, features), BF16),
        in_specs=[whole()] * (2 + 2 * len(tokens)),
        out_specs=whole(),
        compiler_params=params(16),
    )(source, gain.reshape(1, features), *tokens, *stats)


def small_kernel(x_ref, wq_ref, wkv_ref, send_ref, keep_ref):
    x = x_ref[...]
    half = x.shape[0] // 2
    cols = wq_ref.shape[1]
    q = jnp.dot(x, wq_ref[...], preferred_element_type=F32)
    send_ref[:, :cols] = q[:half]
    keep_ref[:, :cols] = q[half:]
    kv = jnp.dot(x, wkv_ref[...], preferred_element_type=F32)
    send_ref[:, cols:] = kv[:half]
    keep_ref[:, cols:] = kv[half:]


def query_sums(x, w_query, w_keyval):
    rows, features = x.shape
    cols = w_query.shape[1] + w_keyval.shape[1]
    out = jax.ShapeDtypeStruct((rows // 2, cols), F32)
    return pl.pallas_call(
        small_kernel,
        out_shape=(out, out),
        in_specs=[whole()] * 3,
        out_specs=(whole(), whole()),
        compiler_params=params(24),
        cost_estimate=pl.CostEstimate(
            flops=2 * rows * features * cols,
            bytes_accessed=2 * features * cols,
            transcendentals=0,
        ),
    )(x, w_query, w_keyval)


def wide_kernel(x_ref, wg_ref, wu_ref, send_ref, keep_ref):
    x = x_ref[...]
    half = x.shape[0] // 2
    for index, ref in enumerate((wg_ref, wu_ref)):
        part = jnp.dot(x, ref[...], preferred_element_type=F32)
        send_ref[index] = part[:half].astype(BF16)
        keep_ref[index] = part[half:]


def wide_sums(x, w_gate, w_up, start, cols):
    rows, features = x.shape
    tile = tile_of(cols, 384)
    first = start // tile
    weight = pl.BlockSpec((features, tile), lambda j: (0, first + j))
    out = pl.BlockSpec((2, rows // 2, tile), lambda j: (0, 0, j))
    return pl.pallas_call(
        wide_kernel,
        grid=(cols // tile,),
        out_shape=(
            jax.ShapeDtypeStruct((2, rows // 2, cols), BF16),
            jax.ShapeDtypeStruct((2, rows // 2, cols), F32),
        ),
        in_specs=[pl.BlockSpec((rows, features), lambda j: (0, 0)), weight, weight],
        out_specs=(out, out),
        compiler_params=params(32),
        cost_estimate=pl.CostEstimate(
            flops=4 * rows * features * cols,
            bytes_accessed=4 * features * cols,
            transcendentals=0,
        ),
    )(x, w_gate, w_up)


def query_rows_kernel(source_ref, *refs):
    out_ref = refs[-1]
    total = refs[0][...]
    for ref in refs[1:-1]:
        total = total + ref[...]
    rows = total.shape[0]
    place = lax.broadcasted_iota(jnp.int32, (rows, rows), 1) == source_ref[...]
    out_ref[...] = jnp.dot(
        jnp.where(place, 1.0, 0.0).astype(BF16), total.astype(BF16), preferred_element_type=F32
    ).astype(BF16)


def query_rows(source, terms):
    return pl.pallas_call(
        query_rows_kernel,
        out_shape=jax.ShapeDtypeStruct(terms[0].shape, BF16),
        in_specs=[whole()] * (1 + len(terms)),
        out_specs=whole(),
    )(source, *terms)


def attend_kernel(count, steps, query_cols, slot_ref, lengths_ref, cache_ref, *refs):
    part_refs, (out_ref, held, fresh) = refs[:count], refs[count:]
    for index, ref in enumerate(part_refs):
        held[slot_ref[index]] = ref[...].astype(F32)
    pair_cols = held.shape[2] - query_cols
    heads = query_cols // HD
    scale = HD ** (-0.5)
    batch, positions = cache_ref.shape[0], cache_ref.shape[1]
    fresh[...] = jnp.zeros_like(fresh)
    for b in range(batch):
        rows = pl.ds(b * steps, steps)
        for c in range(count):
            fresh[b, :steps, c * pair_cols : (c + 1) * pair_cols] = held[c, rows, query_cols:]
        queries = jnp.concatenate(
            [held[c, rows, h * HD : (h + 1) * HD] for c in range(count) for h in range(heads)],
            axis=0,
        ).astype(BF16)
        pairs = fresh[b].astype(BF16)
        dims = (((1,), (1,)), ((), ()))
        old = lax.dot_general(
            queries, cache_ref[b, :, :HD], dims, preferred_element_type=F32
        ) * scale
        position = lax.broadcasted_iota(jnp.int32, old.shape, 1)
        old = jnp.where(position < lengths_ref[b], old, MASKED)
        new = lax.dot_general(queries, pairs[:, :HD], dims, preferred_element_type=F32) * scale
        step = lax.broadcasted_iota(jnp.int32, new.shape, 0) % steps
        new = jnp.where(lax.broadcasted_iota(jnp.int32, new.shape, 1) <= step, new, MASKED)
        highest = jnp.maximum(
            jnp.max(old, axis=-1, keepdims=True), jnp.max(new, axis=-1, keepdims=True)
        )
        old = jnp.exp(old - highest)
        new = jnp.exp(new - highest)
        total = jnp.sum(old, axis=-1, keepdims=True) + jnp.sum(new, axis=-1, keepdims=True)
        context = jnp.dot(
            (old / total).astype(BF16), cache_ref[b, :, HD:], preferred_element_type=F32
        ) + jnp.dot((new / total).astype(BF16), pairs[:, HD:], preferred_element_type=F32)
        for h in range(HEADS):
            out_ref[rows, h * HD : (h + 1) * HD] = context[h * steps : (h + 1) * steps].astype(BF16)


def attend(slots, lengths, cache, parts, steps, query_cols):
    batch = cache.shape[0]
    count = len(parts)
    rows, cols = parts[0].shape
    return pl.pallas_call(
        functools.partial(attend_kernel, count, steps, query_cols),
        out_shape=jax.ShapeDtypeStruct((rows, HEADS * HD), BF16),
        in_specs=[whole(pltpu.SMEM), whole(pltpu.SMEM)] + [whole()] * (1 + count),
        out_specs=whole(),
        scratch_shapes=[
            pltpu.VMEM((count, rows, cols), F32),
            pltpu.VMEM((batch, 8, 2 * HD), F32),
        ],
        compiler_params=params(16),
        cost_estimate=pl.CostEstimate(
            flops=4 * batch * steps * HEADS * HD * cache.shape[1],
            bytes_accessed=2 * cache.size,
            transcendentals=batch * steps * HEADS * cache.shape[1],
        ),
    )(slots, lengths, cache, *parts)


def on_device(tokens, gain, w_query, w_keyval, w_gate, w_up, cache, lengths):
    size_x, size_y = lax.axis_size("gx"), lax.axis_size("gy")
    chips = size_y // 2
    me_x, me_y = lax.axis_index("gx"), lax.axis_index("gy")
    tall, _, steps, features = tokens.shape
    local = cache.shape[0]
    block = local * size_x * steps

    def shift_x(value, by):
        return lax.ppermute(value, "gx", [(i, (i + by) % size_x) for i in range(size_x)])

    def shift_y(value, by):
        return lax.ppermute(value, "gy", [(i, (i + by) % size_y) for i in range(size_y)])

    def swap(value):
        return lax.ppermute(value, "gy", [(i, i ^ 1) for i in range(size_y)])

    mine = tokens.reshape(tall * steps, features)
    gathered = [mine] + [shift_x(mine, by) for by in range(1, size_x)]
    stats = partial_stats(mine)
    stats = sum([shift_y(stats, by) for by in range(1, size_y)], stats)
    every_stat = [stats] + [shift_x(stats, by) for by in range(1, size_x)]

    row = jnp.arange(2 * chips * block, dtype=jnp.int32)
    core = jnp.where(row < chips * block, 1 - me_y % 2, me_y % 2)
    chip = (me_y // 2 + 1 + row // block % chips) % chips
    sequence = (chip * 2 + core) * local + row % block // (size_x * steps)
    column = row // steps % size_x
    source = (me_x - column) % size_x * (tall * steps) + sequence * steps + row % steps
    x = normed_rows(source[:, None], gain, gathered, every_stat)

    send, keep = query_sums(x, w_query, w_keyval)
    total = keep + swap(send)
    terms = [total[(chips - 1) * block :]] + [
        shift_y(total[(by - 1) * block : by * block], 2 * by) for by in range(1, chips)
    ]
    row = jnp.arange(block, dtype=jnp.int32)
    to = (me_x + row // (local * steps)) % size_x
    order = row // steps % local * (size_x * steps) + to * steps + row % steps
    ready = query_rows(order[:, None], terms)
    per = local * steps
    parts = [ready[:per]] + [
        shift_x(ready[by * per : (by + 1) * per], by) for by in range(1, size_x)
    ]
    slots = (me_x - jnp.arange(size_x, dtype=jnp.int32)) % size_x

    hidden_cols = w_gate.shape[1]
    chunks = 4
    cols = hidden_cols // chunks
    pieces = []
    for chunk in range(chunks):
        send, keep = wide_sums(x, w_gate, w_up, chunk * cols, cols)
        total = keep + swap(send).astype(F32)
        whole_sum = total[:, (chips - 1) * block :]
        for by in range(1, chips):
            part = total[:, (by - 1) * block : by * block].astype(BF16)
            whole_sum = whole_sum + shift_y(part, 2 * by).astype(F32)
        pieces.append((jax.nn.silu(whole_sum[0]) * whole_sum[1]).astype(BF16))
    hidden = jnp.concatenate(pieces, axis=1).reshape(local, size_x, steps, hidden_cols)

    context = attend(
        slots,
        lengths.reshape(local),
        cache.reshape(local, cache.shape[2], cache.shape[3]),
        parts,
        steps,
        w_query.shape[1],
    )
    return (context.reshape(local, 1, steps, HEADS * HD), hidden)


def solution(mesh):
    return jax.shard_map(
        on_device,
        mesh=mesh,
        in_specs=(
            P("groups", "gx", None, "gy"),
            P("gy"),
            P("gy", "gx"),
            P("gy", "gx"),
            P("gy", "gx"),
            P("gy", "gx"),
            P(("groups", "gy"), "gx", None, None),
            P(("groups", "gy"), "gx"),
        ),
        out_specs=(P(("groups", "gy"), "gx", None, None), P(("groups", "gy"), None, None, "gx")),
        check_vma=False,
    )
```

time: 156 us -> 93 us (0.60)
  waiting for transfers between devices: 59.1 us -> 8.7 us
  Pallas kernels: 0 us -> 46.4 us
  matrix products: 39.6 us -> 0 us
  blocking collectives: 22.6 us -> 0 us
  between operations: 14.2 us -> 1 us
  starting transfers between devices: 7.9 us -> 19.6 us
  local copies, waits for them, and re-layouts: 3.89 us -> 8.5 us
    reduce_scatter x1 -> x0, waiting for transfers between devices: 50.8 us -> none  [on_device(): lax.psum_scatter(jnp.concatenate([jnp.dot(row_block, matrix, preferred_el...]
    pallas_call x0 -> x9, Pallas kernels: none -> 46.4 us  [the longest x4 39.4 us: wide_sums(): pl.pallas_call(wide_kernel, grid=(cols // tile,), out_shape=(jax.ShapeDty...]
    dot_general x8 -> x0, matrix products: 39.6 us -> none  [the longest x4 38.4 us: on_device(): jnp.dot(row_block, matrix, preferred_element_type=jnp.float32)]
    ppermute x0 -> x22, starting transfers between devices: none -> 19.6 us  [the longest x9 11.4 us: shift_x(): lax.ppermute(value, 'gx', [(i, (i + by) % size_x) for i in range(size_x)])]
    all_gather x1 -> x0, blocking collectives: 14.3 us -> none  [on_device(): gathered = lax.all_gather(normed, 'gx', axis=1, tiled=True)]
    ppermute x0 -> x22, waiting for transfers between devices: none -> 8.7 us  [the longest x9 6.79 us: shift_x(): lax.ppermute(value, 'gx', [(i, (i + by) % size_x) for i in range(size_x)])]
    psum x1 -> x0, blocking collectives: 8.34 us -> none  [on_device(): lax.psum((jnp.sum(floats, axis=-1), jnp.sum(floats * floats, axis=-1)), '...]
    all_to_all x2 -> x0, waiting for transfers between devices: 8.28 us -> none  [the longest x1 4.87 us: on_device(): lax.all_to_all(pairs, 'gx', split_axis=1, concat_axis=3, tiled=True)]
  transfers between devices with their start and end apart: 3 -> 22, of which waited for: 3 -> 4; matrix products, arithmetic and copies ran while one was open for 2% -> 13% of each run, Pallas kernels for 0% -> 25%
where the time goes in v1:
time: 93 us; the launch traced here: 92.4 us
  Pallas kernels  46.4 us (50%)
  starting transfers between devices  19.6 us (21%)
  waiting for transfers between devices  8.7 us (9%)
  local copies, waits for them, and re-layouts  8.5 us (9%)
  other arithmetic  8.15 us (9%)
  between operations  1 us (1%)
    pallas_call x4, Pallas kernels, wide_sums(): pl.pallas_call(wide_kernel, grid=(cols // tile,), out_shape=(jax.ShapeDty...  39.4 us
    ppermute x9, starting transfers between devices, shift_x(): lax.ppermute(value, 'gx', [(i, (i + by) % size_x) for i in range(size_x)])  11.4 us
    ppermute x8, starting transfers between devices, shift_y(): lax.ppermute(value, 'gy', [(i, (i + by) % size_y) for i in range(size_y)])  6.99 us
    ppermute x9, waiting for transfers between devices, shift_x(): lax.ppermute(value, 'gx', [(i, (i + by) % size_x) for i in range(size_x)])  6.79 us
    add x4, other arithmetic, on_device(): whole_sum = whole_sum + shift_y(part, 2 * by).astype(F32)  3.12 us
    add x4, other arithmetic, on_device(): total = keep + swap(send).astype(F32)  1.99 us
    ppermute x8, waiting for transfers between devices, shift_y(): lax.ppermute(value, 'gy', [(i, (i + by) % size_y) for i in range(size_y)])  1.9 us
  transfers between devices with their start and end apart: 22, of which 4 were waited for; matrix products, arithmetic and copies ran while one was open for 13% of the time, Pallas kernels for 25%

profile of v1, /device:TPU:0, one launch (start us, length us, event | category | flops | bytes accessed | tf_op | source)
XLA Modules:
  0.0 92.4 jit_solution(9533298649100607189)
XLA Ops:
  0.6 1.5 %reshape.493.tokens_ref.refs_0_ = bf16[16,2304]{1,0:T(8,128)(2,1)} reshape(bf16[8,1,2,2304]{3,2,1,0:T(2,128)(2,1)} %param.8) | data formatting | bytes 147456 | tf_op jit(solution)/shard_map/reshape | solution.py:246
  2.2 1.6 %shard_map.95 = f32[16,128]{1,0:T(8,128)} custom-call(bf16[16,2304]{1,0:T(8,128)(2,1)} %reshape.493.tokens_ref.refs_0_), custom_call_target="tpu_custom_call" | custom-call | tf_op jit(solution)/shard_map/pallas_call | solution.py:45
  3.8 2.4 %collective-permute-start.5 = (f32[16,128]{1,0:T(8,128)}, f32[16,128]{1,0:T(8,128)S(1)}, u32[]{:S(2)}, u32[]{:S(2)}) collective-permute-start(f32[16,128]{1,0:T(8,128)} %shard_map.95), channel_id=1, source_target_pairs={{0,3},{1,0},{2,1},{3,2},{4,7},{5,4},{6,5},{7,6},{8,11},{9,8},{10,9... | collective-permute-start | bytes 24584 | tf_op jit(solution)/shard_map/ppermute | solution.py:241
  6.2 0.6 collective-permute-start.4
  6.7 0.2 collective-permute-start.3
  7.0 3.6 %collective-permute-start.2 = (bf16[16,2304]{1,0:T(8,128)(2,1)}, bf16[16,2304]{1,0:T(8,128)(2,1)S(1)}, u32[]{:S(2)}, u32[]{:S(2)}) collective-permute-start(bf16[16,2304]{1,0:T(8,128)(2,1)} %reshape.493.tokens_ref.refs_0_), channel_id=1, source_target_pairs={{0,12},{4,0},{8,4},{12,8},{1,13},{5,1},{9,5},{13,9},{2,14},{6,2},{... | collective-permute-start | bytes 221192 | tf_op jit(solution)/shard_map/ppermute | solution.py:238
  10.6 0.1 fusion.26.source_ref
  10.6 1.1 %collective-permute-start = (bf16[16,2304]{1,0:T(8,128)(2,1)}, bf16[16,2304]{1,0:T(8,128)(2,1)S(1)}, u32[]{:S(2)}, u32[]{:S(2)}) collective-permute-start(bf16[16,2304]{1,0:T(8,128)(2,1)} %reshape.493.tokens_ref.refs_0_), channel_id=1, source_target_pairs={{0,4},{4,8},{8,12},{12,0},{1,5},{5,9},{9,13},{13,1},{2,6},{6,10},{... | collective-permute-start | bytes 221192 | tf_op jit(solution)/shard_map/ppermute | solution.py:238
  11.7 0.7 add_add_fusion.refs_4_
  12.4 2.8 %collective-permute-start.8 = (f32[16,128]{1,0:T(8,128)S(1)}, f32[16,128]{1,0:T(8,128)S(1)}, u32[]{:S(2)}, u32[]{:S(2)}) collective-permute-start(f32[16,128]{1,0:T(8,128)S(1)} %add_add_fusion.refs_4_), channel_id=1, source_target_pairs={{0,12},{4,0},{8,4},{12,8},{1,13},{5,1},{9,5},{13,9},{2,14},{6,2},{... | collective-permute-start | bytes 24584 | tf_op jit(solution)/shard_map/ppermute | solution.py:238
  15.2 0.6 fusion.47.source_ref
  15.8 1.1 %collective-permute-start.7 = (f32[16,128]{1,0:T(8,128)S(1)}, f32[16,128]{1,0:T(8,128)S(1)}, u32[]{:S(2)}, u32[]{:S(2)}) collective-permute-start(f32[16,128]{1,0:T(8,128)S(1)} %add_add_fusion.refs_4_), channel_id=1, source_target_pairs={{0,8},{4,12},{8,0},{12,4},{1,9},{5,13},{9,1},{13,5},{2,10},{6,14},... | collective-permute-start | bytes 24584 | tf_op jit(solution)/shard_map/ppermute | solution.py:238
  17.0 2.3 %collective-permute-done.8.refs_7_ = f32[16,128]{1,0:T(8,128)S(1)} collective-permute-done((f32[16,128]{1,0:T(8,128)S(1)}, f32[16,128]{1,0:T(8,128)S(1)}, u32[]{:S(2)}, u32[]{:S(2)}) %collective-permute-start.8) | collective-permute-done | bytes 8224 | tf_op jit(solution)/shard_map/ppermute | solution.py:238
  19.3 0.7 collective-permute-start.6
  20.0 0.7 reshape.492.gain_ref
  20.7 4.0 %collective-permute-done.6.refs_5_ = f32[16,128]{1,0:T(8,128)S(1)} collective-permute-done((f32[16,128]{1,0:T(8,128)S(1)}, f32[16,128]{1,0:T(8,128)S(1)}, u32[]{:S(2)}, u32[]{:S(2)}) %collective-permute-start.6) | collective-permute-done | bytes 8224 | tf_op jit(solution)/shard_map/ppermute | solution.py:238
  24.7 0.9 copy-done.1
  25.6 0.4 shard_map.96.x_ref
  26.0 9.9 %shard_map.103 = (bf16[2,32,2304]{2,1,0:T(8,128)(2,1)S(1)}, f32[2,32,2304]{2,1,0:T(8,128)S(1)}) custom-call(bf16[64,2304]{1,0:T(8,128)(2,1)S(1)} %shard_map.96.x_ref, bf16[2304,9216]{1,0:T(8,128)(2,1)} %wg_ref.7, bf16[2304,9216]{1,0:T(8,128)(2,1)} %wu_ref.7), custom_call_target="tpu_custom_call" | custom-call | flops 1358954496 | bytes 21233664 | tf_op jit(solution)/shard_map/pallas_call | solution.py:128
  35.9 10.0 %shard_map.102 = (bf16[2,32,2304]{2,1,0:T(8,128)(2,1)S(1)}, f32[2,32,2304]{2,1,0:T(8,128)S(1)}) custom-call(bf16[64,2304]{1,0:T(8,128)(2,1)S(1)} %shard_map.96.x_ref, bf16[2304,9216]{1,0:T(8,128)(2,1)} %wg_ref.7, bf16[2304,9216]{1,0:T(8,128)(2,1)} %wu_ref.7), custom_call_target="tpu_custom_call" | custom-call | flops 1358954496 | bytes 21233664 | tf_op jit(solution)/shard_map/pallas_call | solution.py:128
  46.0 1.4 %shard_map.97 = (f32[32,1664]{1,0:T(8,128)S(1)}, f32[32,1664]{1,0:T(8,128)S(1)}) custom-call(bf16[64,2304]{1,0:T(8,128)(2,1)S(1)} %shard_map.96.x_ref, bf16[2304,1536]{1,0:T(8,128)(2,1)S(1)} %bitcast.4, bf16[2304,128]{1,0:T(8,128)(2,1)S(1)} %copy-done.2), custom_call_target="tpu_custom_call" | custom-call | flops 490733568 | bytes 7667712 | tf_op jit(solution)/shard_map/pallas_call | solution.py:99
  47.5 0.1 collective-permute-start.9
  47.5 0.5 collective-permute-start.20
  48.0 0.1 collective-permute-start.18
  48.1 9.7 %shard_map.101 = (bf16[2,32,2304]{2,1,0:T(8,128)(2,1)S(1)}, f32[2,32,2304]{2,1,0:T(8,128)S(1)}) custom-call(bf16[64,2304]{1,0:T(8,128)(2,1)S(1)} %shard_map.96.x_ref, bf16[2304,9216]{1,0:T(8,128)(2,1)} %wg_ref.7, bf16[2304,9216]{1,0:T(8,128)(2,1)} %wu_ref.7), custom_call_target="tpu_custom_call" | custom-call | flops 1358954496 | bytes 21233664 | tf_op jit(solution)/shard_map/pallas_call | solution.py:128
  57.9 0.5 collective-permute-start.16
  58.4 9.7 %shard_map.100 = (bf16[2,32,2304]{2,1,0:T(8,128)(2,1)S(1)}, f32[2,32,2304]{2,1,0:T(8,128)S(1)}) custom-call(bf16[64,2304]{1,0:T(8,128)(2,1)S(1)} %shard_map.96.x_ref, bf16[2304,9216]{1,0:T(8,128)(2,1)} %wg_ref.7, bf16[2304,9216]{1,0:T(8,128)(2,1)} %wu_ref.7), custom_call_target="tpu_custom_call" | custom-call | flops 1358954496 | bytes 21233664 | tf_op jit(solution)/shard_map/pallas_call | solution.py:128
  68.1 0.1 collective-permute-start.14
  68.3 0.7 fusion.59
  68.9 0.1 convert_add_fusion
  69.0 2.1 %collective-permute-start.21 = (bf16[2,16,2304]{2,1,0:T(8,128)(2,1)S(1)}, bf16[2,16,2304]{2,1,0:T(8,128)(2,1)}, u32[]{:S(2)}, u32[]{:S(2)}) collective-permute-start(bf16[2,16,2304]{2,1,0:T(8,128)(2,1)S(1)} %slice.122), channel_id=1, source_target_pairs={{0,2},{1,3},{2,0},{3,1},{4,6},{5,7},{6,4},{7,5},{8,10},{9,11},{10,... | collective-permute-start | bytes 442376 | tf_op jit(solution)/shard_map/ppermute | solution.py:241
  71.1 0.1 convert_add_fusion.1
  71.2 0.7 slice.123
  71.9 0.0 collective-permute-start.19
  72.0 0.9 convert_add_fusion.2
  72.8 1.9 %collective-permute-done.10.refs_1_ = f32[16,1664]{1,0:T(8,128)S(1)} collective-permute-done((f32[16,1664]{1,0:T(8,128)S(1)}, f32[16,1664]{1,0:T(8,128)S(1)}, u32[]{:S(2)}, u32[]{:S(2)}) %collective-permute-start.10) | collective-permute-done | bytes 106528 | tf_op jit(solution)/shard_map/ppermute | solution.py:241
  74.7 0.6 copy-done.6
  75.4 1.8 %shard_map.98 = bf16[16,1664]{1,0:T(8,128)(2,1)} custom-call(s32[16,1]{1,0:T(8,128)} %fusion.47.source_ref, f32[16,1664]{1,0:T(8,128)} %get-tuple-element.35.refs_0_, f32[16,1664]{1,0:T(8,128)} %copy-done.6), custom_call_target="tpu_custom_call" | custom-call | tf_op jit(solution)/shard_map/pallas_call | solution.py:159
  77.1 0.8 fusion.60
  78.0 0.1 collective-permute-start.13
  78.1 0.3 collective-permute-start.12
  78.4 1.7 %collective-permute-start.11 = (bf16[4,1664]{1,0:T(4,128)(2,1)S(1)}, bf16[4,1664]{1,0:T(4,128)(2,1)S(1)}, u32[]{:S(2)}, u32[]{:S(2)}) collective-permute-start(bf16[4,1664]{1,0:T(4,128)(2,1)S(1)} %get-tuple-element.38), channel_id=1, source_target_pairs={{0,4},{4,8},{8,12},{12,0},{1,5},{5,9},{9,13},{13,1},{2,6},{6,10},{... | collective-permute-start | bytes 39944 | tf_op jit(solution)/shard_map/ppermute | solution.py:238
  80.1 1.0 %convert_add_fusion.3 = f32[2,32,2304]{2,1,0:T(8,128)S(1)} fusion(f32[2,32,2304]{2,1,0:T(8,128)S(1)} %get-tuple-element.14, bf16[2,32,2304]{2,1,0:T(8,128)(2,1)} %collective-permute-done.14), kind=kLoop, calls=%fused_computation.3 | loop fusion | flops 294912 | bytes 1474560 | tf_op jit(solution)/shard_map/add | solution.py:281
  81.1 1.0 %slice.124 = bf16[2,16,2304]{2,1,0:T(8,128)(2,1)S(1)} slice(f32[2,32,2304]{2,1,0:T(8,128)} %convert_add_fusion.2), slice={[0:2], [0:16], [0:2304]} | slice | bytes 294912 | tf_op jit(solution)/shard_map/slice | solution.py:284
  82.1 0.2 collective-permute-start.17
  82.3 0.4 collective-permute-done.12.refs_2_
  82.7 1.5 %collective-permute-start.15 = (bf16[2,16,2304]{2,1,0:T(8,128)(2,1)S(1)}, bf16[2,16,2304]{2,1,0:T(8,128)(2,1)S(1)}, u32[]{:S(2)}, u32[]{:S(2)}) collective-permute-start(bf16[2,16,2304]{2,1,0:T(8,128)(2,1)S(1)} %slice.125), channel_id=1, source_target_pairs={{0,2},{1,3},{2,0},{3,1},{4,6},{5,7},{6,4},{7,5},{8,10},{9,11},{10,... | collective-permute-start | bytes 442376 | tf_op jit(solution)/shard_map/ppermute | solution.py:241
  84.2 0.0 collective-permute-done.11.refs_1_
  84.3 1.9 %shard_map.99 = bf16[4,6144]{1,0:T(4,128)(2,1)S(1)} custom-call(s32[4]{0:T(128)S(1)} %and_select_fusion.slot_ref, s32[2]{0:T(128)S(1)} %bitcast.6, bf16[2,1024,512]{2,1,0:T(8,128)(2,1)S(1)} %bitcast.5, bf16[4,1664]{1,0:T(4,128)(2,1)S(1)} %get-tuple-element.39.refs_0_, bf16[4,1664]{1,0:T(4,128)(2,1)S(1)} %collective-permute-done.11.refs_1_, ...), custom_call_target="tpu_custom_call" | custom-call | flops 100663296 | bytes 2097152 | tf_op jit(solution)/shard_map/pallas_call | solution.py:211
  86.1 0.7 reshape.494
  86.8 1.0 %slice_add_fusion = f32[2,16,2304]{2,1,0:T(8,128)S(1)} fusion(f32[2,32,2304]{2,1,0:T(8,128)} %copy-done.4, bf16[2,16,2304]{2,1,0:T(8,128)(2,1)} %collective-permute-done.21), kind=kLoop, calls=%fused_computation.5 | loop fusion | flops 147456 | bytes 737280 | tf_op jit(solution)/shard_map/add | solution.py:285
  87.8 1.0 %slice_add_fusion.1 = f32[2,16,2304]{2,1,0:T(8,128)S(1)} fusion(f32[2,32,2304]{2,1,0:T(8,128)} %copy-done.5, bf16[2,16,2304]{2,1,0:T(8,128)(2,1)} %collective-permute-done.19), kind=kLoop, calls=%fused_computation.7 | loop fusion | flops 147456 | bytes 737280 | tf_op jit(solution)/shard_map/add | solution.py:285
  88.9 1.0 %slice_add_fusion.2 = f32[2,16,2304]{2,1,0:T(8,128)S(1)} fusion(f32[2,32,2304]{2,1,0:T(8,128)} %convert_add_fusion.2, bf16[2,16,2304]{2,1,0:T(8,128)(2,1)} %collective-permute-done.17), kind=kLoop, calls=%fused_computation.9 | loop fusion | flops 147456 | bytes 737280 | tf_op jit(solution)/shard_map/add | solution.py:285
  90.0 0.1 squeeze.30
  90.1 0.1 squeeze.31
  90.2 0.1 squeeze.28
  90.3 0.1 squeeze.29
  90.3 0.1 squeeze.26
  90.4 0.1 squeeze.27
  90.6 0.1 squeeze.24
  90.7 0.1 squeeze.25
  90.8 0.3 fusion.4
  91.1 0.3 fusion.6
  91.4 1.0 %pad_maximum_fusion = bf16[2,4,2,9216]{3,2,1,0:T(2,128)(2,1)} fusion(bf16[2,4,2,2304]{3,2,1,0:T(2,128)(2,1)S(1)} %get-tuple-element.40, bf16[2,4,2,2304]{3,2,1,0:T(2,128)(2,1)S(1)} %get-tuple-element.41, bf16[2,4,2,2304]{3,2,1,0:T(2,128)(2,1)S(1)} %get-tuple-element.42, bf16[2,4,2,2304]{3,2,1,0:T(2,128)(2,1)S(1)} %get-tuple-element.43), kind=kLoop, calls=%fused_computation.12 | loop fusion | flops 1179648 | bytes 589824 | tf_op jit(solution)/shard_map/concatenate | solution.py:287
  (45 shorter events, 0.3 us)
Async XLA Ops:
  3.8 6.9 %collective-permute-start.5 = (f32[16,128]{1,0:T(8,128)}, f32[16,128]{1,0:T(8,128)S(1)}, u32[]{:S(2)}, u32[]{:S(2)}) collective-permute-start(f32[16,128]{1,0:T(8,128)} %shard_map.95), channel_id=1, source_target_pairs={{0,3},{1,0},{2,1},{3,2},{4,7},{5,4},{6,5},{7,6},{8,11},{9,8},{10,9... | collective-permute-start | bytes 24584 | tf_op jit(solution)/shard_map/ppermute | solution.py:241
  6.2 5.5 %collective-permute-start.4 = (f32[16,128]{1,0:T(8,128)}, f32[16,128]{1,0:T(8,128)S(1)}, u32[]{:S(2)}, u32[]{:S(2)}) collective-permute-start(f32[16,128]{1,0:T(8,128)} %shard_map.95), channel_id=1, source_target_pairs={{0,2},{1,3},{2,0},{3,1},{4,6},{5,7},{6,4},{7,5},{8,10},{9,11},{10,... | collective-permute-start | bytes 24584 | tf_op jit(solution)/shard_map/ppermute | solution.py:241
  6.7 5.0 %collective-permute-start.3 = (f32[16,128]{1,0:T(8,128)}, f32[16,128]{1,0:T(8,128)S(1)}, u32[]{:S(2)}, u32[]{:S(2)}) collective-permute-start(f32[16,128]{1,0:T(8,128)} %shard_map.95), channel_id=1, source_target_pairs={{0,1},{1,2},{2,3},{3,0},{4,5},{5,6},{6,7},{7,4},{8,9},{9,10},{10,1... | collective-permute-start | bytes 24584 | tf_op jit(solution)/shard_map/ppermute | solution.py:241
  7.0 17.7 %collective-permute-start.2 = (bf16[16,2304]{1,0:T(8,128)(2,1)}, bf16[16,2304]{1,0:T(8,128)(2,1)S(1)}, u32[]{:S(2)}, u32[]{:S(2)}) collective-permute-start(bf16[16,2304]{1,0:T(8,128)(2,1)} %reshape.493.tokens_ref.refs_0_), channel_id=1, source_target_pairs={{0,12},{4,0},{8,4},{12,8},{1,13},{5,1},{9,5},{13,9},{2,14},{6,2},{... | collective-permute-start | bytes 221192 | tf_op jit(solution)/shard_map/ppermute | solution.py:238
  10.6 14.1 %collective-permute-start.1 = (bf16[16,2304]{1,0:T(8,128)(2,1)}, bf16[16,2304]{1,0:T(8,128)(2,1)S(1)}, u32[]{:S(2)}, u32[]{:S(2)}) collective-permute-start(bf16[16,2304]{1,0:T(8,128)(2,1)} %reshape.493.tokens_ref.refs_0_), channel_id=1, source_target_pairs={{0,8},{4,12},{8,0},{12,4},{1,9},{5,13},{9,1},{13,5},{2,10},{6,14},... | collective-permute-start | bytes 221192 | tf_op jit(solution)/shard_map/ppermute | solution.py:238
  10.6 14.1 %collective-permute-start = (bf16[16,2304]{1,0:T(8,128)(2,1)}, bf16[16,2304]{1,0:T(8,128)(2,1)S(1)}, u32[]{:S(2)}, u32[]{:S(2)}) collective-permute-start(bf16[16,2304]{1,0:T(8,128)(2,1)} %reshape.493.tokens_ref.refs_0_), channel_id=1, source_target_pairs={{0,4},{4,8},{8,12},{12,0},{1,5},{5,9},{9,13},{13,1},{2,6},{6,10},{... | collective-permute-start | bytes 221192 | tf_op jit(solution)/shard_map/ppermute | solution.py:238
  12.4 6.8 %collective-permute-start.8 = (f32[16,128]{1,0:T(8,128)S(1)}, f32[16,128]{1,0:T(8,128)S(1)}, u32[]{:S(2)}, u32[]{:S(2)}) collective-permute-start(f32[16,128]{1,0:T(8,128)S(1)} %add_add_fusion.refs_4_), channel_id=1, source_target_pairs={{0,12},{4,0},{8,4},{12,8},{1,13},{5,1},{9,5},{13,9},{2,14},{6,2},{... | collective-permute-start | bytes 24584 | tf_op jit(solution)/shard_map/ppermute | solution.py:238
  15.8 4.8 %collective-permute-start.7 = (f32[16,128]{1,0:T(8,128)S(1)}, f32[16,128]{1,0:T(8,128)S(1)}, u32[]{:S(2)}, u32[]{:S(2)}) collective-permute-start(f32[16,128]{1,0:T(8,128)S(1)} %add_add_fusion.refs_4_), channel_id=1, source_target_pairs={{0,8},{4,12},{8,0},{12,4},{1,9},{5,13},{9,1},{13,5},{2,10},{6,14},... | collective-permute-start | bytes 24584 | tf_op jit(solution)/shard_map/ppermute | solution.py:238
  19.3 5.4 %collective-permute-start.6 = (f32[16,128]{1,0:T(8,128)S(1)}, f32[16,128]{1,0:T(8,128)S(1)}, u32[]{:S(2)}, u32[]{:S(2)}) collective-permute-start(f32[16,128]{1,0:T(8,128)S(1)} %add_add_fusion.refs_4_), channel_id=1, source_target_pairs={{0,4},{4,8},{8,12},{12,0},{1,5},{5,9},{9,13},{13,1},{2,6},{6,10},{... | collective-permute-start | bytes 24584 | tf_op jit(solution)/shard_map/ppermute | solution.py:238
  24.7 0.9 copy-start.1
  26.0 20.0 %slice-start = ((s8[7077888]{0:T(1024)(128)(4,1)}), s8[4194304]{0:T(1024)(128)(4,1)S(1)}, s32[]{:S(2)}) async-start(s8[7077888]{0:T(1024)(128)(4,1)} %bitcast.3), calls=%async_computation | async-start | bytes 8388608
  35.9 10.1 %slice-start.1 = ((s8[7077888]{0:T(1024)(128)(4,1)}), s8[2883584]{0:T(1024)(128)(4,1)S(1)}, s32[]{:S(2)}) async-start(s8[7077888]{0:T(1024)(128)(4,1)} %bitcast.3), calls=%async_computation.1 | async-start | bytes 5767168
  35.9 10.1 %copy-start.2 = (bf16[2304,128]{1,0:T(8,128)(2,1)S(1)}, bf16[2304,128]{1,0:T(8,128)(2,1)}, u32[]{:S(2)}) copy-start(bf16[2304,128]{1,0:T(8,128)(2,1)} %wkv_ref.1) | copy-start | bytes 1769476
  47.5 20.8 %collective-permute-start.9 = (f32[32,1664]{1,0:T(8,128)S(1)}, f32[32,1664]{1,0:T(8,128)S(1)}, u32[]{:S(2)}, u32[]{:S(2)}) collective-permute-start(f32[32,1664]{1,0:T(8,128)S(1)} %get-tuple-element.13), channel_id=1, source_target_pairs={{0,1},{1,0},{2,3},{3,2},{4,5},{5,4},{6,7},{7,6},{8,9},{9,8},{10,11... | collective-permute-start | bytes 638984 | tf_op jit(solution)/shard_map/ppermute | solution.py:244
  47.5 21.4 %collective-permute-start.20 = (bf16[2,32,2304]{2,1,0:T(8,128)(2,1)S(1)}, bf16[2,32,2304]{2,1,0:T(8,128)(2,1)S(1)}, u32[]{:S(2)}, u32[]{:S(2)}) collective-permute-start(bf16[2,32,2304]{2,1,0:T(8,128)(2,1)S(1)} %get-tuple-element.21), channel_id=1, source_target_pairs={{0,1},{1,0},{2,3},{3,2},{4,5},{5,4},{6,7},{7,6},{8,9},{9,8},{10,11... | collective-permute-start | bytes 884744 | tf_op jit(solution)/shard_map/ppermute | solution.py:244
  48.0 23.1 %collective-permute-start.18 = (bf16[2,32,2304]{2,1,0:T(8,128)(2,1)S(1)}, bf16[2,32,2304]{2,1,0:T(8,128)(2,1)S(1)}, u32[]{:S(2)}, u32[]{:S(2)}) collective-permute-start(bf16[2,32,2304]{2,1,0:T(8,128)(2,1)S(1)} %get-tuple-element.19), channel_id=1, source_target_pairs={{0,1},{1,0},{2,3},{3,2},{4,5},{5,4},{6,7},{7,6},{8,9},{9,8},{10,11... | collective-permute-start | bytes 884744 | tf_op jit(solution)/shard_map/ppermute | solution.py:244
  57.9 26.4 %copy-start = (bf16[2,1,1024,512]{3,2,1,0:T(8,128)(2,1)S(1)}, bf16[2,1,1024,512]{3,2,1,0:T(8,128)(2,1)}, u32[]{:S(2)}) copy-start(bf16[2,1,1024,512]{3,2,1,0:T(8,128)(2,1)} %param.14) | copy-start | bytes 6291460
  57.9 26.4 %copy-start.3 = (s32[2,1]{0,1:T(1,128)S(1)}, s32[2,1]{0,1:T(1,128)}, u32[]{:S(2)}) copy-start(s32[2,1]{0,1:T(1,128)} %param.15) | copy-start | bytes 28
  57.9 14.1 %collective-permute-start.16 = (bf16[2,32,2304]{2,1,0:T(8,128)(2,1)S(1)}, bf16[2,32,2304]{2,1,0:T(8,128)(2,1)S(1)}, u32[]{:S(2)}, u32[]{:S(2)}) collective-permute-start(bf16[2,32,2304]{2,1,0:T(8,128)(2,1)S(1)} %get-tuple-element.17), channel_id=1, source_target_pairs={{0,1},{1,0},{2,3},{3,2},{4,5},{5,4},{6,7},{7,6},{8,9},{9,8},{10,11... | collective-permute-start | bytes 884744 | tf_op jit(solution)/shard_map/ppermute | solution.py:244
  68.1 10.3 %collective-permute-start.14 = (bf16[2,32,2304]{2,1,0:T(8,128)(2,1)S(1)}, bf16[2,32,2304]{2,1,0:T(8,128)(2,1)}, u32[]{:S(2)}, u32[]{:S(2)}) collective-permute-start(bf16[2,32,2304]{2,1,0:T(8,128)(2,1)S(1)} %get-tuple-element.15), channel_id=1, source_target_pairs={{0,1},{1,0},{2,3},{3,2},{4,5},{5,4},{6,7},{7,6},{8,9},{9,8},{10,11... | collective-permute-start | bytes 884744 | tf_op jit(solution)/shard_map/ppermute | solution.py:244
  68.9 5.8 %collective-permute-start.10 = (f32[16,1664]{1,0:T(8,128)S(1)}, f32[16,1664]{1,0:T(8,128)S(1)}, u32[]{:S(2)}, u32[]{:S(2)}) collective-permute-start(f32[16,1664]{1,0:T(8,128)S(1)} %get-tuple-element.34), channel_id=1, source_target_pairs={{0,2},{1,3},{2,0},{3,1},{4,6},{5,7},{6,4},{7,5},{8,10},{9,11},{10,... | collective-permute-start | bytes 319496 | tf_op jit(solution)/shard_map/ppermute | solution.py:241
  69.0 3.8 %copy-start.4 = (f32[2,32,2304]{2,1,0:T(8,128)}, f32[2,32,2304]{2,1,0:T(8,128)S(1)}, u32[]{:S(2)}) copy-start(f32[2,32,2304]{2,1,0:T(8,128)S(1)} %convert_add_fusion) | copy-start | bytes 1769476
  69.0 17.7 %collective-permute-start.21 = (bf16[2,16,2304]{2,1,0:T(8,128)(2,1)S(1)}, bf16[2,16,2304]{2,1,0:T(8,128)(2,1)}, u32[]{:S(2)}, u32[]{:S(2)}) collective-permute-start(bf16[2,16,2304]{2,1,0:T(8,128)(2,1)S(1)} %slice.122), channel_id=1, source_target_pairs={{0,2},{1,3},{2,0},{3,1},{4,6},{5,7},{6,4},{7,5},{8,10},{9,11},{10,... | collective-permute-start | bytes 442376 | tf_op jit(solution)/shard_map/ppermute | solution.py:241
  71.2 3.5 %copy-start.5 = (f32[2,32,2304]{2,1,0:T(8,128)}, f32[2,32,2304]{2,1,0:T(8,128)S(1)}, u32[]{:S(2)}) copy-start(f32[2,32,2304]{2,1,0:T(8,128)S(1)} %convert_add_fusion.1) | copy-start | bytes 1769476
  71.9 15.9 %collective-permute-start.19 = (bf16[2,16,2304]{2,1,0:T(8,128)(2,1)}, bf16[2,16,2304]{2,1,0:T(8,128)(2,1)}, u32[]{:S(2)}, u32[]{:S(2)}) collective-permute-start(bf16[2,16,2304]{2,1,0:T(8,128)(2,1)} %slice.123), channel_id=1, source_target_pairs={{0,2},{1,3},{2,0},{3,1},{4,6},{5,7},{6,4},{7,5},{8,10},{9,11},{10,... | collective-permute-start | bytes 442376 | tf_op jit(solution)/shard_map/ppermute | solution.py:241
  74.7 0.6 copy-start.6
  78.0 4.1 %collective-permute-start.13 = (bf16[4,1664]{1,0:T(4,128)(2,1)S(1)}, bf16[4,1664]{1,0:T(4,128)(2,1)S(1)}, u32[]{:S(2)}, u32[]{:S(2)}) collective-permute-start(bf16[4,1664]{1,0:T(4,128)(2,1)S(1)} %get-tuple-element.36), channel_id=1, source_target_pairs={{0,12},{4,0},{8,4},{12,8},{1,13},{5,1},{9,5},{13,9},{2,14},{6,2},{... | collective-permute-start | bytes 39944 | tf_op jit(solution)/shard_map/ppermute | solution.py:238
  78.1 4.7 %collective-permute-start.12 = (bf16[4,1664]{1,0:T(4,128)(2,1)S(1)}, bf16[4,1664]{1,0:T(4,128)(2,1)S(1)}, u32[]{:S(2)}, u32[]{:S(2)}) collective-permute-start(bf16[4,1664]{1,0:T(4,128)(2,1)S(1)} %get-tuple-element.37), channel_id=1, source_target_pairs={{0,8},{4,12},{8,0},{12,4},{1,9},{5,13},{9,1},{13,5},{2,10},{6,14},... | collective-permute-start | bytes 39944 | tf_op jit(solution)/shard_map/ppermute | solution.py:238
  78.4 5.9 %collective-permute-start.11 = (bf16[4,1664]{1,0:T(4,128)(2,1)S(1)}, bf16[4,1664]{1,0:T(4,128)(2,1)S(1)}, u32[]{:S(2)}, u32[]{:S(2)}) collective-permute-start(bf16[4,1664]{1,0:T(4,128)(2,1)S(1)} %get-tuple-element.38), channel_id=1, source_target_pairs={{0,4},{4,8},{8,12},{12,0},{1,5},{5,9},{9,13},{13,1},{2,6},{6,10},{... | collective-permute-start | bytes 39944 | tf_op jit(solution)/shard_map/ppermute | solution.py:238
  82.1 6.8 %collective-permute-start.17 = (bf16[2,16,2304]{2,1,0:T(8,128)(2,1)S(1)}, bf16[2,16,2304]{2,1,0:T(8,128)(2,1)}, u32[]{:S(2)}, u32[]{:S(2)}) collective-permute-start(bf16[2,16,2304]{2,1,0:T(8,128)(2,1)S(1)} %slice.124), channel_id=1, source_target_pairs={{0,2},{1,3},{2,0},{3,1},{4,6},{5,7},{6,4},{7,5},{8,10},{9,11},{10,... | collective-permute-start | bytes 442376 | tf_op jit(solution)/shard_map/ppermute | solution.py:241
  82.7 7.8 %collective-permute-start.15 = (bf16[2,16,2304]{2,1,0:T(8,128)(2,1)S(1)}, bf16[2,16,2304]{2,1,0:T(8,128)(2,1)S(1)}, u32[]{:S(2)}, u32[]{:S(2)}) collective-permute-start(bf16[2,16,2304]{2,1,0:T(8,128)(2,1)S(1)} %slice.125), channel_id=1, source_target_pairs={{0,2},{1,3},{2,0},{3,1},{4,6},{5,7},{6,4},{7,5},{8,10},{9,11},{10,... | collective-permute-start | bytes 442376 | tf_op jit(solution)/shard_map/ppermute | solution.py:241

commit v2 on v1

v2 whole, which is shorter than its diff:
```python
import functools

import jax
import jax.numpy as jnp
from jax import lax
from jax.experimental import pallas as pl
from jax.experimental.pallas import tpu as pltpu
from jax.sharding import PartitionSpec as P

D = 9216
HEADS = 24
HD = 256
EPSILON = 1e-05
MASKED = -1e30
MIB = 1024 * 1024
TILE = 256
DEPTH = 4
F32 = jnp.float32
BF16 = jnp.bfloat16


def whole(memory_space=pltpu.VMEM):
    return pl.BlockSpec(memory_space=memory_space)


def params():
    return pltpu.CompilerParams(vmem_limit_bytes=11 * MIB)


def stats_kernel(*refs):
    out_ref = refs[-1]
    rows = refs[0].shape[0]
    for index, ref in enumerate(refs[:-2]):
        floats = ref[...].astype(F32)
        sums = jnp.sum(floats, axis=-1, keepdims=True)
        squares = jnp.sum(floats * floats, axis=-1, keepdims=True)
        lane = lax.broadcasted_iota(jnp.int32, (rows, 128), 1)
        out_ref[index * rows : (index + 1) * rows] = jnp.where(lane < 64, sums, squares)


def partial_stats(tokens, after):
    return pl.pallas_call(
        stats_kernel,
        out_shape=jax.ShapeDtypeStruct((len(tokens) * tokens[0].shape[0], 128), F32),
        in_specs=[whole()] * len(tokens) + [whole(pl.ANY)],
        out_specs=whole(),
        compiler_params=params(),
    )(*tokens, after)


def norm_kernel(count, source_ref, gain_ref, *refs):
    token_refs, stat_refs, out_ref = refs[:count], refs[count:-2], refs[-1]
    gain = gain_ref[...]
    stats = stat_refs[0][...]
    for ref in stat_refs[1:]:
        stats = stats + ref[...]
    parts = []
    for index, token_ref in enumerate(token_refs):
        rows = token_ref.shape[0]
        mine = stats[index * rows : (index + 1) * rows]
        average = mine[:, 0:1] / D
        inverse_std = lax.rsqrt(mine[:, 64:65] / D - average * average + EPSILON)
        floats = token_ref[...].astype(F32)
        parts.append(((floats - average) * inverse_std * gain).astype(BF16))
    normed = jnp.concatenate(parts, axis=0)
    rows = normed.shape[0]
    place = lax.broadcasted_iota(jnp.int32, (rows, rows), 1) == source_ref[...]
    out_ref[...] = jnp.dot(
        jnp.where(place, 1.0, 0.0).astype(BF16), normed, preferred_element_type=F32
    ).astype(BF16)


def normed_rows(source, gain, tokens, stats, after):
    rows = sum(t.shape[0] for t in tokens)
    features = gain.shape[0]
    return pl.pallas_call(
        functools.partial(norm_kernel, len(tokens)),
        out_shape=jax.ShapeDtypeStruct((rows, features), BF16),
        in_specs=[whole()] * (2 + len(tokens) + len(stats)) + [whole(pl.ANY)],
        out_specs=whole(),
        compiler_params=params(),
    )(source, gain.reshape(1, features), *tokens, *stats, after)


def in_hbm(arrays):
    return [pltpu.with_memory_space_constraint(a, pltpu.HBM) for a in arrays]


def tile_copies(w_refs, tile, place, sems):
    columns = pl.ds(pl.multiple_of(tile * TILE, TILE), TILE)
    return [
        pltpu.make_async_copy(ref.at[:, columns], place.at[index], sems.at[index])
        for index, ref in enumerate(w_refs)
    ]


def load_kernel(first, small, w_refs, out_refs, sems):
    copies = [
        pltpu.make_async_copy(w_refs[2 + index], out_refs[1 + index], sems.at[0, index])
        for index in range(small)
    ]
    for copy in copies:
        copy.start()
    tiles = out_refs[0].shape[0]
    for tile in range(tiles):
        for copy in tile_copies(w_refs[:2], first + tile, out_refs[0].at[tile], sems.at[1 + tile]):
            copy.start()
    for tile in range(tiles):
        for copy in tile_copies(w_refs[:2], first + tile, out_refs[0].at[tile], sems.at[1 + tile]):
            copy.wait()
    for copy in copies:
        copy.wait()


def load(weights, smalls, first, tiles, after=()):
    features = weights[0].shape[0]

    def kernel(*refs):
        w_refs = refs[: 2 + len(smalls)]
        out_refs = refs[2 + len(smalls) + len(after) : -1]
        load_kernel(first, len(smalls), w_refs, out_refs, refs[-1])

    return pl.pallas_call(
        kernel,
        out_shape=[pltpu.VMEM((tiles, 2, features, TILE), BF16)]
        + [pltpu.VMEM(small.shape, small.dtype) for small in smalls],
        in_specs=[whole(pltpu.HBM)] * (2 + len(smalls)) + [whole(pl.ANY)] * len(after),
        out_specs=[whole()] * (1 + len(smalls)),
        scratch_shapes=[pltpu.SemaphoreType.DMA((1 + tiles, 2))],
        compiler_params=params(),
        cost_estimate=pl.CostEstimate(
            flops=0,
            bytes_accessed=4 * features * TILE * tiles + 2 * sum(s.size for s in smalls),
            transcendentals=0,
        ),
    )(*in_hbm(weights), *in_hbm(smalls), *after)


def small_kernel(x_ref, wq_ref, wkv_ref, send_ref, keep_ref):
    x = x_ref[...]
    half = x.shape[0] // 2
    cols = wq_ref.shape[1]
    q = jnp.dot(x, wq_ref[...], preferred_element_type=F32)
    send_ref[:, :cols] = q[:half]
    keep_ref[:, :cols] = q[half:]
    kv = jnp.dot(x, wkv_ref[...], preferred_element_type=F32)
    send_ref[:, cols:] = kv[:half]
    keep_ref[:, cols:] = kv[half:]


def query_sums(x, w_query, w_keyval):
    rows, features = x.shape
    cols = w_query.shape[1] + w_keyval.shape[1]
    out = pltpu.VMEM((rows // 2, cols), F32)
    return pl.pallas_call(
        small_kernel,
        out_shape=(out, out),
        in_specs=[whole()] * 3,
        out_specs=(whole(), whole()),
        compiler_params=params(),
        cost_estimate=pl.CostEstimate(
            flops=2 * rows * features * cols,
            bytes_accessed=2 * features * cols,
            transcendentals=0,
        ),
    )(
        x,
        pltpu.with_memory_space_constraint(w_query, pltpu.VMEM),
        pltpu.with_memory_space_constraint(w_keyval, pltpu.VMEM),
    )


def wide_kernel(first, tiles, x_ref, w_refs, pre_refs, send_ref, keep_ref, next_ref, ring, ring_sems, next_sems):
    held = sum(ref.shape[0] for ref in pre_refs)
    streamed = tiles - held
    depth = ring.shape[0]
    following = 0 if next_ref is None else next_ref.shape[0]
    half = x_ref.shape[0] // 2

    def fetch(index):
        return tile_copies(w_refs, first + held + index, ring.at[lax.rem(index, depth)], ring_sems.at[lax.rem(index, depth)])

    def fetch_next(index):
        return tile_copies(w_refs, first + tiles + index, next_ref.at[index], next_sems.at[index])

    def start(copies):
        for copy in copies:
            copy.start()

    def multiply(tile, place):
        columns = pl.ds(pl.multiple_of(tile * TILE, TILE), TILE)
        for index in range(2):
            part = jnp.dot(x_ref[...], place[index], preferred_element_type=F32)
            send_ref[index, :, columns] = part[:half].astype(BF16)
            keep_ref[index, :, columns] = part[half:]

    early = min(depth, streamed)
    for index in range(early):
        start(fetch(index))
    early_next = min(following, max(DEPTH - early, 0)) if streamed else following
    for index in range(early_next):
        start(fetch_next(index))
    done = 0
    for ref in pre_refs:

        def from_held(index, carry, ref=ref, done=done):
            multiply(done + index, ref.at[index])
            return carry

        lax.fori_loop(0, ref.shape[0], from_held, 0)
        done += ref.shape[0]

    def from_ring(index, carry):
        for copy in fetch(index):
            copy.wait()
        multiply(held + index, ring.at[lax.rem(index, depth)])

        @pl.when(index + depth < streamed)
        def _():
            start(fetch(index + depth))

        if following > early_next:
            later = index + early_next + depth - streamed

            @pl.when((later >= early_next) & (later < following))
            def _():
                start(fetch_next(later))

        return carry

    lax.fori_loop(0, streamed, from_ring, 0)
    for index in range(following):
        for copy in fetch_next(index):
            copy.wait()


def wide_sums(x, weights, held, first, tiles, following, after=()):
    rows, features = x.shape
    cols = tiles * TILE
    streamed = tiles - sum(h.shape[0] for h in held)
    depth = min(DEPTH, max(streamed, 1))

    def kernel(x_ref, wg_ref, wu_ref, *refs):
        pre_refs = refs[: len(held)]
        refs = refs[len(held) + len(after) :]
        send_ref, keep_ref = refs[:2]
        next_ref = refs[2] if following else None
        ring, ring_sems, next_sems = refs[-3:]
        wide_kernel(
            first, tiles, x_ref, (wg_ref, wu_ref), pre_refs, send_ref, keep_ref, next_ref, ring, ring_sems, next_sems
        )

    out_shape = [
        pltpu.VMEM((2, rows // 2, cols), BF16),
        pltpu.VMEM((2, rows // 2, cols), F32),
    ]
    if following:
        out_shape.append(pltpu.VMEM((following, 2, features, TILE), BF16))
    return pl.pallas_call(
        kernel,
        out_shape=out_shape,
        in_specs=[whole(), whole(pltpu.HBM), whole(pltpu.HBM)]
        + [whole()] * len(held)
        + [whole(pl.ANY)] * len(after),
        out_specs=[whole()] * len(out_shape),
        scratch_shapes=[
            pltpu.VMEM((depth, 2, features, TILE), BF16),
            pltpu.SemaphoreType.DMA((depth, 2)),
            pltpu.SemaphoreType.DMA((max(following, 1), 2)),
        ],
        compiler_params=params(),
        cost_estimate=pl.CostEstimate(
            flops=4 * rows * features * cols,
            bytes_accessed=4 * features * TILE * (streamed + following),
            transcendentals=0,
        ),
    )(x, *in_hbm(weights), *[pltpu.with_memory_space_constraint(h, pltpu.VMEM) for h in held], *after)


def attend_kernel(count, steps, query_cols, slot_ref, lengths_ref, cache_ref, *refs):
    part_refs, (out_ref, held, fresh) = refs[:count], refs[count:]
    for index, ref in enumerate(part_refs):
        for b in range(ref.shape[0]):
            held[slot_ref[index], b, :steps] = ref[b].astype(F32)
    pair_cols = held.shape[3] - query_cols
    heads = query_cols // HD
    scale = HD ** (-0.5)
    batch, positions = cache_ref.shape[0], cache_ref.shape[1]
    fresh[...] = jnp.zeros_like(fresh)
    for b in range(batch):
        rows = pl.ds(b * steps, steps)
        for c in range(count):
            fresh[b, :steps, c * pair_cols : (c + 1) * pair_cols] = held[c, b, :steps, query_cols:]
        queries = jnp.concatenate(
            [held[c, b, :steps, h * HD : (h + 1) * HD] for c in range(count) for h in range(heads)],
            axis=0,
        ).astype(BF16)
        pairs = fresh[b].astype(BF16)
        dims = (((1,), (1,)), ((), ()))
        old = lax.dot_general(
            queries, cache_ref[b, :, :HD], dims, preferred_element_type=F32
        ) * scale
        position = lax.broadcasted_iota(jnp.int32, old.shape, 1)
        old = jnp.where(position < lengths_ref[b], old, MASKED)
        new = lax.dot_general(queries, pairs[:, :HD], dims, preferred_element_type=F32) * scale
        step = lax.broadcasted_iota(jnp.int32, new.shape, 0) % steps
        new = jnp.where(lax.broadcasted_iota(jnp.int32, new.shape, 1) <= step, new, MASKED)
        highest = jnp.maximum(
            jnp.max(old, axis=-1, keepdims=True), jnp.max(new, axis=-1, keepdims=True)
        )
        old = jnp.exp(old - highest)
        new = jnp.exp(new - highest)
        total = jnp.sum(old, axis=-1, keepdims=True) + jnp.sum(new, axis=-1, keepdims=True)
        context = jnp.dot(
            (old / total).astype(BF16), cache_ref[b, :, HD:], preferred_element_type=F32
        ) + jnp.dot((new / total).astype(BF16), pairs[:, HD:], preferred_element_type=F32)
        for h in range(HEADS):
            out_ref[rows, h * HD : (h + 1) * HD] = context[h * steps : (h + 1) * steps].astype(BF16)


def attend(slots, lengths, cache, parts, steps, query_cols):
    batch = cache.shape[0]
    count = len(parts)
    rows, cols = batch * steps, parts[0].shape[2]
    return pl.pallas_call(
        functools.partial(attend_kernel, count, steps, query_cols),
        out_shape=jax.ShapeDtypeStruct((rows, HEADS * HD), BF16),
        in_specs=[whole(pltpu.SMEM), whole(pltpu.SMEM)] + [whole()] * (1 + count),
        out_specs=whole(),
        scratch_shapes=[
            pltpu.VMEM((count, batch, 8, cols), F32),
            pltpu.VMEM((batch, 8, 2 * HD), F32),
        ],
        compiler_params=params(),
        cost_estimate=pl.CostEstimate(
            flops=4 * batch * steps * HEADS * HD * cache.shape[1],
            bytes_accessed=2 * cache.size,
            transcendentals=batch * steps * HEADS * cache.shape[1],
        ),
    )(slots, lengths, cache, *parts)


def on_device(tokens, gain, w_query, w_keyval, w_gate, w_up, cache, lengths):
    size_x, size_y = lax.axis_size("gx"), lax.axis_size("gy")
    chips = size_y // 2
    me_x, me_y = lax.axis_index("gx"), lax.axis_index("gy")
    tall, _, steps, features = tokens.shape
    local = cache.shape[0]
    block = local * size_x * steps

    def shift_x(value, by):
        return lax.ppermute(value, "gx", [(i, (i + by) % size_x) for i in range(size_x)])

    def shift_y(value, by):
        return lax.ppermute(value, "gy", [(i, (i + by) % size_y) for i in range(size_y)])

    def swap(value):
        return lax.ppermute(value, "gy", [(i, i ^ 1) for i in range(size_y)])

    weights = (w_gate, w_up)
    tiles = w_gate.shape[1] // TILE
    bounds = [tiles * share // 36 for share in (0, 8, 19, 32, 36)]
    before = [tiles * share // 36 for share in (4, 4)]
    ahead = [max(1, tiles * share // 36) for share in (4, 4, 3)] + [0]
    gathered = [tokens] + [shift_x(tokens, by) for by in range(1, size_x)]
    gathered = [t.reshape(tall * steps, features) for t in gathered]
    first_tiles, w_query, w_keyval = load(weights, (w_query, w_keyval), 0, before[0])
    stats = partial_stats(gathered, first_tiles)
    every_stat = [stats] + [shift_y(stats, by) for by in range(1, size_y)]
    (second_tiles,) = load(weights, (), before[0], before[1], after=(stats,))

    row = jnp.arange(2 * chips * block, dtype=jnp.int32)
    core = jnp.where(row < chips * block, 1 - me_y % 2, me_y % 2)
    chip = (me_y // 2 + 1 + row // block % chips) % chips
    sequence = (chip * 2 + core) * local + row % block // (size_x * steps)
    column = row // steps % size_x
    source = (me_x - column) % size_x * (tall * steps) + sequence * steps + row % steps
    x = normed_rows(source[:, None], gain, gathered, every_stat, second_tiles)

    def across_chips(total, kind):
        whole_sum = total[..., (chips - 1) * block :, :]
        for by in range(1, chips):
            part = total[..., (by - 1) * block : by * block, :].astype(kind)
            whole_sum = whole_sum + shift_y(part, 2 * by).astype(F32)
        return whole_sum

    def gated(whole_sum):
        return (jax.nn.silu(whole_sum[0]) * whole_sum[1]).astype(BF16)

    def chunk_sums(chunk, held, after):
        return wide_sums(
            x, weights, held, bounds[chunk], bounds[chunk + 1] - bounds[chunk], ahead[chunk], after
        )

    query_cols = w_query.shape[1]
    send_q, keep_q = query_sums(x, w_query, w_keyval)
    send, keep, held = chunk_sums(0, (first_tiles, second_tiles), (send_q,))
    total_q = keep_q + swap(send_q)

    send_1, keep_1, held = chunk_sums(1, (held,), (total_q, send))
    total_0 = keep + swap(send).astype(F32)
    ready = across_chips(total_q, F32).astype(BF16).reshape(local, size_x, steps, -1)
    turned = [
        lax.dynamic_slice_in_dim(ready, (me_x + by) % size_x, 1, 1)[:, 0] for by in range(size_x)
    ]

    send_2, keep_2, held = chunk_sums(2, (held,), (total_0, turned[0], send_1))
    total_1 = keep_1 + swap(send_1).astype(F32)
    parts = [turned[0]] + [shift_x(turned[by], by) for by in range(1, size_x)]
    sum_0 = across_chips(total_0, BF16)

    send_3, keep_3 = chunk_sums(3, (held,), (total_1, parts[-1], sum_0, send_2))
    total_2 = keep_2 + swap(send_2).astype(F32)
    sum_1 = across_chips(total_1, BF16)
    total_3 = keep_3 + swap(send_3).astype(F32)
    sum_2 = across_chips(total_2, BF16)
    sum_3 = across_chips(total_3, BF16)
    pieces = [gated(s) for s in (sum_0, sum_1, sum_2, sum_3)]
    hidden = jnp.concatenate(pieces, axis=1).reshape(local, size_x, steps, -1)
    slots = (me_x - jnp.arange(size_x, dtype=jnp.int32)) % size_x

    context = attend(
        slots,
        lengths.reshape(local),
        cache.reshape(local, cache.shape[2], cache.shape[3]),
        parts,
        steps,
        query_cols,
    )
    return (context.reshape(local, 1, steps, HEADS * HD), hidden)


def solution(mesh):
    return jax.shard_map(
        on_device,
        mesh=mesh,
        in_specs=(
            P("groups", "gx", None, "gy"),
            P("gy"),
            P("gy", "gx"),
            P("gy", "gx"),
            P("gy", "gx"),
            P("gy", "gx"),
            P(("groups", "gy"), "gx", None, None),
            P(("groups", "gy"), "gx"),
        ),
        out_specs=(P(("groups", "gy"), "gx", None, None), P(("groups", "gy"), None, None, "gx")),
        check_vma=False,
    )
```

time: 93 us -> 107 us (1.15)
  local copies, waits for them, and re-layouts: 8.5 us -> 30 us
  Pallas kernels: 46.4 us -> 40 us
  other arithmetic: 8.15 us -> 4.96 us
  waiting for transfers between devices: 8.7 us -> 11.8 us
  starting transfers between devices: 19.6 us -> 18.3 us
    unnamed x18 -> x28, local copies, waits for them, and re-layouts: 1.56 us -> 27.4 us
    ppermute x8, waiting for transfers between devices: 1.9 us -> 11.3 us  [shift_y(): lax.ppermute(value, 'gy', [(i, (i + by) % size_y) for i in range(size_y)])]
    ppermute x9 -> x6, waiting for transfers between devices: 6.79 us -> 0.02 us  [shift_x(): lax.ppermute(value, 'gx', [(i, (i + by) % size_x) for i in range(size_x)])]
    pallas_call x6 -> x7, Pallas kernels: 42.8 us -> 36.3 us  [the longest x4 26.2 us: wide_sums(): pl.pallas_call(kernel, out_shape=out_shape, in_specs=[whole(), whole(pltp...]
    add x11 -> x9, other arithmetic: 6.45 us -> 3.24 us  [the longest x1 1.08 us: on_device(): total_2 = keep_2 + swap(send_2).astype(F32)]
    slice x10 -> x9, local copies, waits for them, and re-layouts: 3.35 us -> 0.17 us  [the longest x4 0.09 us: gated(): return (jax.nn.silu(whole_sum[0]) * whole_sum[1]).astype(BF16)]
    ppermute x9 -> x6, starting transfers between devices: 11.4 us -> 9.39 us  [shift_x(): lax.ppermute(value, 'gx', [(i, (i + by) % size_x) for i in range(size_x)])]
  transfers between devices with their start and end apart: 22 -> 19, of which waited for: 4 -> 5; matrix products, arithmetic and copies ran while one was open for 13% -> 6% of each run, Pallas kernels for 25% -> 36%
where the time goes in v2:
time: 107 us; the launch traced here: 106 us
  Pallas kernels  40 us (37%)
  local copies, waits for them, and re-layouts  30 us (28%)
  starting transfers between devices  18.3 us (17%)
  waiting for transfers between devices  11.8 us (11%)
  other arithmetic  4.96 us (5%)
  between operations  1.24 us (1%)
    unnamed x28, local copies, waits for them, and re-layouts  27.4 us
    pallas_call x4, Pallas kernels, wide_sums(): pl.pallas_call(kernel, out_shape=out_shape, in_specs=[whole(), whole(pltp...  26.2 us
    ppermute x8, waiting for transfers between devices, shift_y(): lax.ppermute(value, 'gy', [(i, (i + by) % size_y) for i in range(size_y)])  11.3 us
    pallas_call x2, Pallas kernels, load(): pl.pallas_call(kernel, out_shape=[pltpu.VMEM((tiles, 2, features, TILE),...  9.99 us
    ppermute x6, starting transfers between devices, shift_x(): lax.ppermute(value, 'gx', [(i, (i + by) % size_x) for i in range(size_x)])  9.39 us
    ppermute x8, starting transfers between devices, shift_y(): lax.ppermute(value, 'gy', [(i, (i + by) % size_y) for i in range(size_y)])  7.71 us
  transfers between devices with their start and end apart: 19, of which 5 were waited for; matrix products, arithmetic and copies ran while one was open for 6% of the time, Pallas kernels for 36%

profile of v2, /device:TPU:0, one launch (start us, length us, event | category | flops | bytes accessed | tf_op | source)
XLA Modules:
  0.0 106.2 jit_solution(11635088649857287190)
XLA Ops:
  0.6 3.1 %collective-permute-start = (bf16[8,1,2,2304]{3,2,1,0:T(2,128)(2,1)}, bf16[8,1,2,2304]{3,2,1,0:T(2,128)(2,1)S(1)}, u32[]{:S(2)}, u32[]{:S(2)}) collective-permute-start(bf16[8,1,2,2304]{3,2,1,0:T(2,128)(2,1)} %param.8), channel_id=1, source_target_pairs={{0,4},{4,8},{8,12},{12,0},{1,5},{5,9},{9,13},{13,1},{2,6},{6,10},{... | collective-permute-start | bytes 221192 | tf_op jit(solution)/shard_map/ppermute | solution.py:352
  3.7 2.6 %collective-permute-start.1 = (bf16[8,1,2,2304]{3,2,1,0:T(2,128)(2,1)}, bf16[8,1,2,2304]{3,2,1,0:T(2,128)(2,1)S(1)}, u32[]{:S(2)}, u32[]{:S(2)}) collective-permute-start(bf16[8,1,2,2304]{3,2,1,0:T(2,128)(2,1)} %param.8), channel_id=1, source_target_pairs={{0,8},{4,12},{8,0},{12,4},{1,9},{5,13},{9,1},{13,5},{2,10},{6,14},... | collective-permute-start | bytes 221192 | tf_op jit(solution)/shard_map/ppermute | solution.py:352
  6.3 1.3 %collective-permute-start.2 = (bf16[8,1,2,2304]{3,2,1,0:T(2,128)(2,1)}, bf16[8,1,2,2304]{3,2,1,0:T(2,128)(2,1)S(1)}, u32[]{:S(2)}, u32[]{:S(2)}) collective-permute-start(bf16[8,1,2,2304]{3,2,1,0:T(2,128)(2,1)} %param.8), channel_id=1, source_target_pairs={{0,12},{4,0},{8,4},{12,8},{1,13},{5,1},{9,5},{13,9},{2,14},{6,2},{... | collective-permute-start | bytes 221192 | tf_op jit(solution)/shard_map/ppermute | solution.py:352
  7.6 0.9 reshape.351.refs_0_
  8.6 6.1 %shard_map.95 = (bf16[4,2,2304,256]{3,2,1,0:T(8,128)(2,1)S(1)}, bf16[2304,1536]{1,0:T(8,128)(2,1)S(1)}, bf16[2304,128]{1,0:T(8,128)(2,1)S(1)}) custom-call(bf16[2304,9216]{1,0:T(8,128)(2,1)} %wg_ref.7, bf16[2304,9216]{1,0:T(8,128)(2,1)} %wu_ref.7, bf16[2304,1536]{1,0:T(8,128)(2,1)} %refs_2_.1, bf16[2304,128]{1,0:T(8,128)(2,1)} %refs_3_.1), custom_call_target="tpu_custom_call" | custom-call | bytes 17104896 | tf_op jit(solution)/shard_map/pallas_call | solution.py:123
  14.7 3.6 %copy-done = bf16[4,2,2304,256]{3,2,1,0:T(8,128)(2,1)} copy-done((bf16[4,2,2304,256]{3,2,1,0:T(8,128)(2,1)}, bf16[4,2,2304,256]{3,2,1,0:T(8,128)(2,1)S(1)}, u32[]{:S(2)}) %copy-start) | copy-done | bytes 9437208
  18.3 2.8 %copy-done.6 = bf16[2304,1536]{1,0:T(8,128)(2,1)} copy-done((bf16[2304,1536]{1,0:T(8,128)(2,1)}, bf16[2304,1536]{1,0:T(8,128)(2,1)S(1)}, u32[]{:S(2)}) %copy-start.6) | copy-done | bytes 7077912
  21.2 0.0 collective-permute-done
  21.3 3.7 %copy-done.1 = bf16[4,2,2304,256]{3,2,1,0:T(8,128)(2,1)S(1)} copy-done((bf16[4,2,2304,256]{3,2,1,0:T(8,128)(2,1)S(1)}, bf16[4,2,2304,256]{3,2,1,0:T(8,128)(2,1)}, u32[]{:S(2)}) %copy-start.1) | copy-done | bytes 9437208
  25.0 0.1 shard_map.96.refs_2_.refs_4_
  25.1 0.1 collective-permute-start.3
  25.2 1.6 %collective-permute-start.4 = (f32[64,128]{1,0:T(8,128)S(1)}, f32[64,128]{1,0:T(8,128)S(1)}, u32[]{:S(2)}, u32[]{:S(2)}) collective-permute-start(f32[64,128]{1,0:T(8,128)S(1)} %shard_map.96.refs_2_.refs_4_), channel_id=1, source_target_pairs={{0,2},{1,3},{2,0},{3,1},{4,6},{5,7},{6,4},{7,5},{8,10},{9,11},{10,... | collective-permute-start | bytes 98312 | tf_op jit(solution)/shard_map/ppermute | solution.py:355
  26.8 1.4 %collective-permute-start.5 = (f32[64,128]{1,0:T(8,128)S(1)}, f32[64,128]{1,0:T(8,128)S(1)}, u32[]{:S(2)}, u32[]{:S(2)}) collective-permute-start(f32[64,128]{1,0:T(8,128)S(1)} %shard_map.96.refs_2_.refs_4_), channel_id=1, source_target_pairs={{0,3},{1,0},{2,1},{3,2},{4,7},{5,4},{6,5},{7,6},{8,11},{9,8},{10,9... | collective-permute-start | bytes 98312 | tf_op jit(solution)/shard_map/ppermute | solution.py:355
  28.2 0.1 fusion.27.source_ref
  28.3 3.9 %shard_map.97.refs_8_.refs_1_ = bf16[4,2,2304,256]{3,2,1,0:T(8,128)(2,1)S(1)} custom-call(bf16[2304,9216]{1,0:T(8,128)(2,1)} %wg_ref.7, bf16[2304,9216]{1,0:T(8,128)(2,1)} %wu_ref.7, f32[64,128]{1,0:T(8,128)S(1)} %shard_map.96.refs_2_.refs_4_), custom_call_target="tpu_custom_call" | custom-call | bytes 9437184 | tf_op jit(solution)/shard_map/pallas_call | solution.py:123
  32.3 0.0 slice-start.1
  32.3 0.0 collective-permute-done.3.refs_5_
  32.3 0.4 shard_map.98.x_ref
  32.7 3.2 %copy-done.7 = bf16[2304,1536]{1,0:T(8,128)(2,1)S(1)} copy-done((bf16[2304,1536]{1,0:T(8,128)(2,1)S(1)}, bf16[2304,1536]{1,0:T(8,128)(2,1)}, u32[]{:S(2)}) %copy-start.7) | copy-done | bytes 7077912
  35.9 1.4 %shard_map.99 = (f32[32,1664]{1,0:T(8,128)S(1)}, f32[32,1664]{1,0:T(8,128)S(1)}) custom-call(bf16[64,2304]{1,0:T(8,128)(2,1)S(1)} %shard_map.98.x_ref, bf16[2304,1536]{1,0:T(8,128)(2,1)S(1)} %copy-done.7, bf16[2304,128]{1,0:T(8,128)(2,1)S(1)} %get-tuple-element.20.wkv_ref), custom_call_target="tpu_custom_call" | custom-call | flops 490733568 | bytes 7667712 | tf_op jit(solution)/shard_map/pallas_call | solution.py:155
  37.4 0.1 collective-permute-start.6
  37.5 0.9 slice-done.2
  38.3 4.4 %shard_map.101 = (bf16[2,32,2048]{2,1,0:T(8,128)(2,1)S(1)}, f32[2,32,2048]{2,1,0:T(8,128)S(1)}, bf16[4,2,2304,256]{3,2,1,0:T(8,128)(2,1)S(1)}) custom-call(bf16[64,2304]{1,0:T(8,128)(2,1)S(1)} %shard_map.98.x_ref, bf16[2304,9216]{1,0:T(8,128)(2,1)} %wg_ref.7, bf16[2304,9216]{1,0:T(8,128)(2,1)} %wu_ref.7, bf16[4,2,2304,256]{3,2,1,0:T(8,128)(2,1)S(1)} %bitcast.16, ...), custom_call_target="tpu_custom_call" | custom-call | flops 1207959552 | bytes 9437184 | tf_op jit(solution)/shard_map/pallas_call | solution.py:259
  42.7 0.1 collective-permute-start.11
  42.9 9.1 %shard_map.102 = (bf16[2,32,2816]{2,1,0:T(8,128)(2,1)S(1)}, f32[2,32,2816]{2,1,0:T(8,128)S(1)}, bf16[4,2,2304,256]{3,2,1,0:T(8,128)(2,1)S(1)}) custom-call(bf16[64,2304]{1,0:T(8,128)(2,1)S(1)} %shard_map.98.x_ref, bf16[2304,9216]{1,0:T(8,128)(2,1)} %wg_ref.7, bf16[2304,9216]{1,0:T(8,128)(2,1)} %wu_ref.7, ...), custom_call_target="tpu_custom_call" | custom-call | flops 1660944384 | bytes 25952256 | tf_op jit(solution)/shard_map/pallas_call | solution.py:259
  52.0 3.6 %copy-done.2 = bf16[4,2,2304,256]{3,2,1,0:T(8,128)(2,1)} copy-done((bf16[4,2,2304,256]{3,2,1,0:T(8,128)(2,1)}, bf16[4,2,2304,256]{3,2,1,0:T(8,128)(2,1)S(1)}, u32[]{:S(2)}) %copy-start.2) | copy-done | bytes 9437208
  55.6 0.5 collective-permute-start.13
  56.1 0.5 collective-permute-start.7
  56.7 1.6 %collective-permute-start.12 = (bf16[2,16,2048]{2,1,0:T(8,128)(2,1)S(1)}, bf16[2,16,2048]{2,1,0:T(8,128)(2,1)}, u32[]{:S(2)}, u32[]{:S(2)}) collective-permute-start(bf16[2,16,2048]{2,1,0:T(8,128)(2,1)S(1)} %slice.107), channel_id=1, source_target_pairs={{0,2},{1,3},{2,0},{3,1},{4,6},{5,7},{6,4},{7,5},{8,10},{9,11},{10,... | collective-permute-start | bytes 393224 | tf_op jit(solution)/shard_map/ppermute | solution.py:355
  58.3 3.7 %collective-permute-done.7 = f32[16,1664]{1,0:T(8,128)S(1)} collective-permute-done((f32[16,1664]{1,0:T(8,128)S(1)}, f32[16,1664]{1,0:T(8,128)S(1)}, u32[]{:S(2)}, u32[]{:S(2)}) %collective-permute-start.7) | collective-permute-done | bytes 106528 | tf_op jit(solution)/shard_map/ppermute | solution.py:355
  62.0 0.1 dynamic-slice_bitcast_fusion
  62.1 0.5 collective-permute-start.10
  62.6 1.6 %collective-permute-start.8 = (bf16[2,2,1664]{2,1,0:T(2,128)(2,1)S(1)}, bf16[2,2,1664]{2,1,0:T(2,128)(2,1)S(1)}, u32[]{:S(2)}, u32[]{:S(2)}) collective-permute-start(bf16[2,2,1664]{2,1,0:T(2,128)(2,1)S(1)} %get-tuple-element.49), channel_id=1, source_target_pairs={{0,4},{4,8},{8,12},{12,0},{1,5},{5,9},{9,13},{13,1},{2,6},{6,10},{... | collective-permute-start | bytes 39944 | tf_op jit(solution)/shard_map/ppermute | solution.py:352
  64.2 0.3 collective-permute-start.9
  64.5 3.7 %copy-done.3 = bf16[4,2,2304,256]{3,2,1,0:T(8,128)(2,1)S(1)} copy-done((bf16[4,2,2304,256]{3,2,1,0:T(8,128)(2,1)S(1)}, bf16[4,2,2304,256]{3,2,1,0:T(8,128)(2,1)}, u32[]{:S(2)}) %copy-start.3) | copy-done | bytes 9437208
  68.2 10.5 %shard_map.103 = (bf16[2,32,3328]{2,1,0:T(8,128)(2,1)S(1)}, f32[2,32,3328]{2,1,0:T(8,128)S(1)}, bf16[3,2,2304,256]{3,2,1,0:T(8,128)(2,1)S(1)}) custom-call(bf16[64,2304]{1,0:T(8,128)(2,1)S(1)} %shard_map.98.x_ref, bf16[2304,9216]{1,0:T(8,128)(2,1)} %wg_ref.7, bf16[2304,9216]{1,0:T(8,128)(2,1)} %wu_ref.7, bf16[4,2,2304,256]{3,2,1,0:T(8,128)(2,1)S(1)} %copy-done.3, ...), custom_call_target="tpu_custom_call" | custom-call | flops 1962934272 | bytes 28311552 | tf_op jit(solution)/shard_map/pallas_call | solution.py:259
  78.6 2.8 %copy-done.4 = bf16[3,2,2304,256]{3,2,1,0:T(8,128)(2,1)} copy-done((bf16[3,2,2304,256]{3,2,1,0:T(8,128)(2,1)}, bf16[3,2,2304,256]{3,2,1,0:T(8,128)(2,1)S(1)}, u32[]{:S(2)}) %copy-start.4) | copy-done | bytes 7077912
  81.5 0.0 collective-permute-done.8.refs_1_
  81.5 1.8 %shard_map.100 = bf16[4,6144]{1,0:T(4,128)(2,1)S(1)} custom-call(s32[4]{0:T(128)S(1)} %and_select_fusion.slot_ref, s32[2]{0:T(128)S(1)} %bitcast.18, bf16[2,1024,512]{2,1,0:T(8,128)(2,1)S(1)} %bitcast.17, bf16[2,2,1664]{2,1,0:T(2,128)(2,1)S(1)} %get-tuple-element.47.refs_0_.refs_2_, bf16[2,2,1664]{2,1,0:T(2,128)(2,1)S(1)} %collective-permute-done.8.refs_1_, ...), custom_call_target="tpu_custom_call" | custom-call | flops 100663296 | bytes 2097152 | tf_op jit(solution)/shard_map/pallas_call | solution.py:325
  83.4 0.7 reshape.356
  84.0 0.9 slice_add_fusion.2.refs_3_
  85.0 0.1 squeeze.40
  85.1 0.1 squeeze.41
  85.2 1.0 convert_add_fusion.1.refs_1_
  86.2 3.0 %copy-done.5 = bf16[3,2,2304,256]{3,2,1,0:T(8,128)(2,1)S(1)} copy-done((bf16[3,2,2304,256]{3,2,1,0:T(8,128)(2,1)S(1)}, bf16[3,2,2304,256]{3,2,1,0:T(8,128)(2,1)}, u32[]{:S(2)}) %copy-start.5) | copy-done | bytes 7077912
  89.2 2.2 %shard_map.104 = (bf16[2,32,1024]{2,1,0:T(8,128)(2,1)S(1)}, f32[2,32,1024]{2,1,0:T(8,128)S(1)}) custom-call(bf16[64,2304]{1,0:T(8,128)(2,1)S(1)} %shard_map.98.x_ref, bf16[2304,9216]{1,0:T(8,128)(2,1)} %wg_ref.7, bf16[2304,9216]{1,0:T(8,128)(2,1)} %wu_ref.7, bf16[3,2,2304,256]{3,2,1,0:T(8,128)(2,1)S(1)} %copy-done.5, ...), custom_call_target="tpu_custom_call" | custom-call | flops 603979776 | bytes 2359296 | tf_op jit(solution)/shard_map/pallas_call | solution.py:259
  91.4 0.6 collective-permute-start.17
  92.0 0.1 fusion.5
  92.2 0.4 collective-permute-start.14
  92.6 0.4 collective-permute-done.17
  93.0 1.4 %collective-permute-start.18 = (bf16[2,16,1024]{2,1,0:T(8,128)(2,1)S(1)}, bf16[2,16,1024]{2,1,0:T(8,128)(2,1)S(1)}, u32[]{:S(2)}, u32[]{:S(2)}) collective-permute-start(bf16[2,16,1024]{2,1,0:T(8,128)(2,1)S(1)} %slice.108), channel_id=1, source_target_pairs={{0,2},{1,3},{2,0},{3,1},{4,6},{5,7},{6,4},{7,5},{8,10},{9,11},{10,... | collective-permute-start | bytes 196616 | tf_op jit(solution)/shard_map/ppermute | solution.py:355
  94.4 1.1 %convert_add_fusion = f32[2,32,3328]{2,1,0:T(8,128)S(1)} fusion(f32[2,32,3328]{2,1,0:T(8,128)S(1)} %get-tuple-element.29, bf16[2,32,3328]{2,1,0:T(8,128)(2,1)} %collective-permute-done.15), kind=kLoop, calls=%fused_computation | loop fusion | flops 425984 | bytes 2129920 | tf_op jit(solution)/shard_map/add | solution.py:413
  95.5 0.8 collective-permute-start.16
  96.3 3.3 %collective-permute-done.14 = bf16[2,16,2816]{2,1,0:T(8,128)(2,1)S(1)} collective-permute-done((bf16[2,16,2816]{2,1,0:T(8,128)(2,1)S(1)}, bf16[2,16,2816]{2,1,0:T(8,128)(2,1)S(1)}, u32[]{:S(2)}, u32[]{:S(2)}) %collective-permute-start.14) | collective-permute-done | bytes 180256 | tf_op jit(solution)/shard_map/ppermute | solution.py:355
  99.7 0.1 squeeze.42
  99.8 0.1 squeeze.43
  99.9 0.2 fusion.3
  100.1 0.9 collective-permute-done.18
  101.2 0.1 fusion.12
  101.3 3.4 %collective-permute-done.16 = bf16[2,16,3328]{2,1,0:T(8,128)(2,1)S(1)} collective-permute-done((bf16[2,16,3328]{2,1,0:T(8,128)(2,1)S(1)}, bf16[2,16,3328]{2,1,0:T(8,128)(2,1)S(1)}, u32[]{:S(2)}, u32[]{:S(2)}) %collective-permute-start.16) | collective-permute-done | bytes 213024 | tf_op jit(solution)/shard_map/ppermute | solution.py:355
  104.8 0.1 squeeze.44
  104.9 0.1 squeeze.45
  105.0 0.2 fusion.1
  105.3 1.0 pad_maximum_fusion
  (55 shorter events, 0.7 us)
Async XLA Ops:
  0.6 20.5 %collective-permute-start = (bf16[8,1,2,2304]{3,2,1,0:T(2,128)(2,1)}, bf16[8,1,2,2304]{3,2,1,0:T(2,128)(2,1)S(1)}, u32[]{:S(2)}, u32[]{:S(2)}) collective-permute-start(bf16[8,1,2,2304]{3,2,1,0:T(2,128)(2,1)} %param.8), channel_id=1, source_target_pairs={{0,4},{4,8},{8,12},{12,0},{1,5},{5,9},{9,13},{13,1},{2,6},{6,10},{... | collective-permute-start | bytes 221192 | tf_op jit(solution)/shard_map/ppermute | solution.py:352
  3.7 17.5 %collective-permute-start.1 = (bf16[8,1,2,2304]{3,2,1,0:T(2,128)(2,1)}, bf16[8,1,2,2304]{3,2,1,0:T(2,128)(2,1)S(1)}, u32[]{:S(2)}, u32[]{:S(2)}) collective-permute-start(bf16[8,1,2,2304]{3,2,1,0:T(2,128)(2,1)} %param.8), channel_id=1, source_target_pairs={{0,8},{4,12},{8,0},{12,4},{1,9},{5,13},{9,1},{13,5},{2,10},{6,14},... | collective-permute-start | bytes 221192 | tf_op jit(solution)/shard_map/ppermute | solution.py:352
  6.3 15.0 %collective-permute-start.2 = (bf16[8,1,2,2304]{3,2,1,0:T(2,128)(2,1)}, bf16[8,1,2,2304]{3,2,1,0:T(2,128)(2,1)S(1)}, u32[]{:S(2)}, u32[]{:S(2)}) collective-permute-start(bf16[8,1,2,2304]{3,2,1,0:T(2,128)(2,1)} %param.8), channel_id=1, source_target_pairs={{0,12},{4,0},{8,4},{12,8},{1,13},{5,1},{9,5},{13,9},{2,14},{6,2},{... | collective-permute-start | bytes 221192 | tf_op jit(solution)/shard_map/ppermute | solution.py:352
  14.7 3.6 %copy-start = (bf16[4,2,2304,256]{3,2,1,0:T(8,128)(2,1)}, bf16[4,2,2304,256]{3,2,1,0:T(8,128)(2,1)S(1)}, u32[]{:S(2)}) copy-start(bf16[4,2,2304,256]{3,2,1,0:T(8,128)(2,1)S(1)} %get-tuple-element.18.refs_4_.refs_0_) | copy-start | bytes 28311556
  18.3 2.8 %copy-start.6 = (bf16[2304,1536]{1,0:T(8,128)(2,1)}, bf16[2304,1536]{1,0:T(8,128)(2,1)S(1)}, u32[]{:S(2)}) copy-start(bf16[2304,1536]{1,0:T(8,128)(2,1)S(1)} %get-tuple-element.19.wq_ref) | copy-start | bytes 21233668
  21.2 7.1 %copy-start.10 = (f32[2304]{0:T(1024)S(1)}, f32[2304]{0:T(1024)}, u32[]{:S(2)}) copy-start(f32[2304]{0:T(1024)} %param.9) | copy-start | bytes 27652
  21.3 3.7 %copy-start.1 = (bf16[4,2,2304,256]{3,2,1,0:T(8,128)(2,1)S(1)}, bf16[4,2,2304,256]{3,2,1,0:T(8,128)(2,1)}, u32[]{:S(2)}) copy-start(bf16[4,2,2304,256]{3,2,1,0:T(8,128)(2,1)} %copy-done) | copy-start | bytes 28311556
  25.1 7.2 %collective-permute-start.3 = (f32[64,128]{1,0:T(8,128)S(1)}, f32[64,128]{1,0:T(8,128)S(1)}, u32[]{:S(2)}, u32[]{:S(2)}) collective-permute-start(f32[64,128]{1,0:T(8,128)S(1)} %shard_map.96.refs_2_.refs_4_), channel_id=1, source_target_pairs={{0,1},{1,2},{2,3},{3,0},{4,5},{5,6},{6,7},{7,4},{8,9},{9,10},{10,1... | collective-permute-start | bytes 98312 | tf_op jit(solution)/shard_map/ppermute | solution.py:355
  25.2 7.1 %collective-permute-start.4 = (f32[64,128]{1,0:T(8,128)S(1)}, f32[64,128]{1,0:T(8,128)S(1)}, u32[]{:S(2)}, u32[]{:S(2)}) collective-permute-start(f32[64,128]{1,0:T(8,128)S(1)} %shard_map.96.refs_2_.refs_4_), channel_id=1, source_target_pairs={{0,2},{1,3},{2,0},{3,1},{4,6},{5,7},{6,4},{7,5},{8,10},{9,11},{10,... | collective-permute-start | bytes 98312 | tf_op jit(solution)/shard_map/ppermute | solution.py:355
  26.8 5.5 %collective-permute-start.5 = (f32[64,128]{1,0:T(8,128)S(1)}, f32[64,128]{1,0:T(8,128)S(1)}, u32[]{:S(2)}, u32[]{:S(2)}) collective-permute-start(f32[64,128]{1,0:T(8,128)S(1)} %shard_map.96.refs_2_.refs_4_), channel_id=1, source_target_pairs={{0,3},{1,0},{2,1},{3,2},{4,7},{5,4},{6,5},{7,6},{8,11},{9,8},{10,9... | collective-permute-start | bytes 98312 | tf_op jit(solution)/shard_map/ppermute | solution.py:355
  32.3 5.2 %slice-start = ((s8[9437184]{0:T(1024)(128)(4,1)}), s8[1048576]{0:T(1024)(128)(4,1)S(1)}, s32[]{:S(2)}) async-start(s8[9437184]{0:T(1024)(128)(4,1)} %bitcast.15), calls=%async_computation | async-start | bytes 2097152
  32.3 5.2 %slice-start.1 = ((s8[9437184]{0:T(1024)(128)(4,1)}), s8[4194304]{0:T(1024)(128)(4,1)S(1)}, s32[]{:S(2)}) async-start(s8[9437184]{0:T(1024)(128)(4,1)} %bitcast.15), calls=%async_computation.1 | async-start | bytes 8388608
  32.7 3.2 %copy-start.7 = (bf16[2304,1536]{1,0:T(8,128)(2,1)S(1)}, bf16[2304,1536]{1,0:T(8,128)(2,1)}, u32[]{:S(2)}) copy-start(bf16[2304,1536]{1,0:T(8,128)(2,1)} %copy-done.6) | copy-start | bytes 21233668
  35.9 2.4 %slice-start.2 = ((s8[9437184]{0:T(1024)(128)(4,1)}), s8[4194304]{0:T(1024)(128)(4,1)S(1)}, s32[]{:S(2)}) async-start(s8[9437184]{0:T(1024)(128)(4,1)} %bitcast.15), calls=%async_computation.2 | async-start | bytes 8388608
  37.4 5.5 %collective-permute-start.6 = (f32[32,1664]{1,0:T(8,128)S(1)}, f32[32,1664]{1,0:T(8,128)S(1)}, u32[]{:S(2)}, u32[]{:S(2)}) collective-permute-start(f32[32,1664]{1,0:T(8,128)S(1)} %get-tuple-element.22.refs_2_), channel_id=1, source_target_pairs={{0,1},{1,0},{2,3},{3,2},{4,5},{5,4},{6,7},{7,6},{8,9},{9,8},{10,11... | collective-permute-start | bytes 638984 | tf_op jit(solution)/shard_map/ppermute | solution.py:358
  42.7 13.9 %collective-permute-start.11 = (bf16[2,32,2048]{2,1,0:T(8,128)(2,1)S(1)}, bf16[2,32,2048]{2,1,0:T(8,128)(2,1)S(1)}, u32[]{:S(2)}, u32[]{:S(2)}) collective-permute-start(bf16[2,32,2048]{2,1,0:T(8,128)(2,1)S(1)} %get-tuple-element.24.refs_2_), channel_id=1, source_target_pairs={{0,1},{1,0},{2,3},{3,2},{4,5},{5,4},{6,7},{7,6},{8,9},{9,8},{10,11... | collective-permute-start | bytes 786440 | tf_op jit(solution)/shard_map/ppermute | solution.py:358
  52.0 3.6 %copy-start.2 = (bf16[4,2,2304,256]{3,2,1,0:T(8,128)(2,1)}, bf16[4,2,2304,256]{3,2,1,0:T(8,128)(2,1)S(1)}, u32[]{:S(2)}) copy-start(bf16[4,2,2304,256]{3,2,1,0:T(8,128)(2,1)S(1)} %get-tuple-element.28.refs_0_) | copy-start | bytes 28311556
  55.6 29.5 %collective-permute-start.13 = (bf16[2,32,2816]{2,1,0:T(8,128)(2,1)S(1)}, bf16[2,32,2816]{2,1,0:T(8,128)(2,1)}, u32[]{:S(2)}, u32[]{:S(2)}) collective-permute-start(bf16[2,32,2816]{2,1,0:T(8,128)(2,1)S(1)} %get-tuple-element.27.refs_3_), channel_id=1, source_target_pairs={{0,1},{1,0},{2,3},{3,2},{4,5},{5,4},{6,7},{7,6},{8,9},{9,8},{10,11... | collective-permute-start | bytes 1081352 | tf_op jit(solution)/shard_map/ppermute | solution.py:358
  56.1 5.9 %collective-permute-start.7 = (f32[16,1664]{1,0:T(8,128)S(1)}, f32[16,1664]{1,0:T(8,128)S(1)}, u32[]{:S(2)}, u32[]{:S(2)}) collective-permute-start(f32[16,1664]{1,0:T(8,128)S(1)} %slice.77), channel_id=1, source_target_pairs={{0,2},{1,3},{2,0},{3,1},{4,6},{5,7},{6,4},{7,5},{8,10},{9,11},{10,... | collective-permute-start | bytes 319496 | tf_op jit(solution)/shard_map/ppermute | solution.py:355
  56.7 27.3 %collective-permute-start.12 = (bf16[2,16,2048]{2,1,0:T(8,128)(2,1)S(1)}, bf16[2,16,2048]{2,1,0:T(8,128)(2,1)}, u32[]{:S(2)}, u32[]{:S(2)}) collective-permute-start(bf16[2,16,2048]{2,1,0:T(8,128)(2,1)S(1)} %slice.107), channel_id=1, source_target_pairs={{0,2},{1,3},{2,0},{3,1},{4,6},{5,7},{6,4},{7,5},{8,10},{9,11},{10,... | collective-permute-start | bytes 393224 | tf_op jit(solution)/shard_map/ppermute | solution.py:355
  62.1 19.4 %collective-permute-start.10 = (bf16[2,2,1664]{2,1,0:T(2,128)(2,1)S(1)}, bf16[2,2,1664]{2,1,0:T(2,128)(2,1)S(1)}, u32[]{:S(2)}, u32[]{:S(2)}) collective-permute-start(bf16[2,2,1664]{2,1,0:T(2,128)(2,1)S(1)} %get-tuple-element.46), channel_id=1, source_target_pairs={{0,12},{4,0},{8,4},{12,8},{1,13},{5,1},{9,5},{13,9},{2,14},{6,2},{... | collective-permute-start | bytes 39944 | tf_op jit(solution)/shard_map/ppermute | solution.py:352
  62.6 18.9 %collective-permute-start.8 = (bf16[2,2,1664]{2,1,0:T(2,128)(2,1)S(1)}, bf16[2,2,1664]{2,1,0:T(2,128)(2,1)S(1)}, u32[]{:S(2)}, u32[]{:S(2)}) collective-permute-start(bf16[2,2,1664]{2,1,0:T(2,128)(2,1)S(1)} %get-tuple-element.49), channel_id=1, source_target_pairs={{0,4},{4,8},{8,12},{12,0},{1,5},{5,9},{9,13},{13,1},{2,6},{6,10},{... | collective-permute-start | bytes 39944 | tf_op jit(solution)/shard_map/ppermute | solution.py:352
  64.2 17.3 %collective-permute-start.9 = (bf16[2,2,1664]{2,1,0:T(2,128)(2,1)S(1)}, bf16[2,2,1664]{2,1,0:T(2,128)(2,1)S(1)}, u32[]{:S(2)}, u32[]{:S(2)}) collective-permute-start(bf16[2,2,1664]{2,1,0:T(2,128)(2,1)S(1)} %get-tuple-element.48), channel_id=1, source_target_pairs={{0,8},{4,12},{8,0},{12,4},{1,9},{5,13},{9,1},{13,5},{2,10},{6,14},... | collective-permute-start | bytes 39944 | tf_op jit(solution)/shard_map/ppermute | solution.py:352
  64.5 3.7 %copy-start.3 = (bf16[4,2,2304,256]{3,2,1,0:T(8,128)(2,1)S(1)}, bf16[4,2,2304,256]{3,2,1,0:T(8,128)(2,1)}, u32[]{:S(2)}) copy-start(bf16[4,2,2304,256]{3,2,1,0:T(8,128)(2,1)} %copy-done.2) | copy-start | bytes 28311556
  68.2 13.3 %copy-start.8 = (bf16[2,1,1024,512]{3,2,1,0:T(8,128)(2,1)S(1)}, bf16[2,1,1024,512]{3,2,1,0:T(8,128)(2,1)}, u32[]{:S(2)}) copy-start(bf16[2,1,1024,512]{3,2,1,0:T(8,128)(2,1)} %param.14) | copy-start | bytes 6291460
  68.2 13.3 %copy-start.9 = (s32[2,1]{0,1:T(1,128)S(1)}, s32[2,1]{0,1:T(1,128)}, u32[]{:S(2)}) copy-start(s32[2,1]{0,1:T(1,128)} %param.15) | copy-start | bytes 28
  78.6 2.8 %copy-start.4 = (bf16[3,2,2304,256]{3,2,1,0:T(8,128)(2,1)}, bf16[3,2,2304,256]{3,2,1,0:T(8,128)(2,1)S(1)}, u32[]{:S(2)}) copy-start(bf16[3,2,2304,256]{3,2,1,0:T(8,128)(2,1)S(1)} %get-tuple-element.31.refs_0_) | copy-start | bytes 21233668
  81.5 12.9 %collective-permute-start.15 = (bf16[2,32,3328]{2,1,0:T(8,128)(2,1)S(1)}, bf16[2,32,3328]{2,1,0:T(8,128)(2,1)}, u32[]{:S(2)}, u32[]{:S(2)}) collective-permute-start(bf16[2,32,3328]{2,1,0:T(8,128)(2,1)S(1)} %get-tuple-element.30.refs_4_), channel_id=1, source_target_pairs={{0,1},{1,0},{2,3},{3,2},{4,5},{5,4},{6,7},{7,6},{8,9},{9,8},{10,11... | collective-permute-start | bytes 1277960 | tf_op jit(solution)/shard_map/ppermute | solution.py:358
  86.2 3.0 %copy-start.5 = (bf16[3,2,2304,256]{3,2,1,0:T(8,128)(2,1)S(1)}, bf16[3,2,2304,256]{3,2,1,0:T(8,128)(2,1)}, u32[]{:S(2)}) copy-start(bf16[3,2,2304,256]{3,2,1,0:T(8,128)(2,1)} %copy-done.4) | copy-start | bytes 21233668
  91.4 1.5 %collective-permute-start.17 = (bf16[2,32,1024]{2,1,0:T(8,128)(2,1)S(1)}, bf16[2,32,1024]{2,1,0:T(8,128)(2,1)S(1)}, u32[]{:S(2)}, u32[]{:S(2)}) collective-permute-start(bf16[2,32,1024]{2,1,0:T(8,128)(2,1)S(1)} %get-tuple-element.33), channel_id=1, source_target_pairs={{0,1},{1,0},{2,3},{3,2},{4,5},{5,4},{6,7},{7,6},{8,9},{9,8},{10,11... | collective-permute-start | bytes 393224 | tf_op jit(solution)/shard_map/ppermute | solution.py:358
  92.2 7.5 %collective-permute-start.14 = (bf16[2,16,2816]{2,1,0:T(8,128)(2,1)S(1)}, bf16[2,16,2816]{2,1,0:T(8,128)(2,1)S(1)}, u32[]{:S(2)}, u32[]{:S(2)}) collective-permute-start(bf16[2,16,2816]{2,1,0:T(8,128)(2,1)S(1)} %slice.106), channel_id=1, source_target_pairs={{0,2},{1,3},{2,0},{3,1},{4,6},{5,7},{6,4},{7,5},{8,10},{9,11},{10,... | collective-permute-start | bytes 540680 | tf_op jit(solution)/shard_map/ppermute | solution.py:355
  93.0 8.0 %collective-permute-start.18 = (bf16[2,16,1024]{2,1,0:T(8,128)(2,1)S(1)}, bf16[2,16,1024]{2,1,0:T(8,128)(2,1)S(1)}, u32[]{:S(2)}, u32[]{:S(2)}) collective-permute-start(bf16[2,16,1024]{2,1,0:T(8,128)(2,1)S(1)} %slice.108), channel_id=1, source_target_pairs={{0,2},{1,3},{2,0},{3,1},{4,6},{5,7},{6,4},{7,5},{8,10},{9,11},{10,... | collective-permute-start | bytes 196616 | tf_op jit(solution)/shard_map/ppermute | solution.py:355
  95.5 9.2 %collective-permute-start.16 = (bf16[2,16,3328]{2,1,0:T(8,128)(2,1)S(1)}, bf16[2,16,3328]{2,1,0:T(8,128)(2,1)S(1)}, u32[]{:S(2)}, u32[]{:S(2)}) collective-permute-start(bf16[2,16,3328]{2,1,0:T(8,128)(2,1)S(1)} %slice.105), channel_id=1, source_target_pairs={{0,2},{1,3},{2,0},{3,1},{4,6},{5,7},{6,4},{7,5},{8,10},{9,11},{10,... | collective-permute-start | bytes 638984 | tf_op jit(solution)/shard_map/ppermute | solution.py:355

commit v3 on v2

--- a/solution.py
+++ b/solution.py
@@ -14,7 +14,7 @@
 MASKED = -1e30
 MIB = 1024 * 1024
 TILE = 256
-DEPTH = 4
+DEPTH = 3
 F32 = jnp.float32
 BF16 = jnp.bfloat16
 
@@ -24,45 +24,43 @@
 
 
 def params():
-    return pltpu.CompilerParams(vmem_limit_bytes=11 * MIB)
-
-
-def stats_kernel(*refs):
-    out_ref = refs[-1]
-    rows = refs[0].shape[0]
-    for index, ref in enumerate(refs[:-2]):
-        floats = ref[...].astype(F32)
-        sums = jnp.sum(floats, axis=-1, keepdims=True)
-        squares = jnp.sum(floats * floats, axis=-1, keepdims=True)
-        lane = lax.broadcasted_iota(jnp.int32, (rows, 128), 1)
-        out_ref[index * rows : (index + 1) * rows] = jnp.where(lane < 64, sums, squares)
+    return pltpu.CompilerParams(vmem_limit_bytes=9 * MIB)
+
+
+def stats_kernel(count, *refs):
+    token_refs, (rows_ref, out_ref) = refs[:count], refs[-2:]
+    tall, _, steps, features = token_refs[0].shape
+    for index, ref in enumerate(token_refs):
+        for t in range(tall):
+            first = (index * tall + t) * steps
+            rows_ref[first : first + steps] = ref[t, 0].astype(F32)
+    floats = rows_ref[...]
+    sums = jnp.sum(floats, axis=-1, keepdims=True)
+    squares = jnp.sum(floats * floats, axis=-1, keepdims=True)
+    lane = lax.broadcasted_iota(jnp.int32, out_ref.shape, 1)
+    out_ref[...] = jnp.where(lane < 64, sums, squares)
 
 
 def partial_stats(tokens, after):
-    return pl.pallas_call(
-        stats_kernel,
-        out_shape=jax.ShapeDtypeStruct((len(tokens) * tokens[0].shape[0], 128), F32),
+    tall, _, steps, features = tokens[0].shape
+    rows = len(tokens) * tall * steps
+    return pl.pallas_call(
+        functools.partial(stats_kernel, len(tokens)),
+        out_shape=(pltpu.VMEM((rows, features), F32), pltpu.VMEM((rows, 128), F32)),
         in_specs=[whole()] * len(tokens) + [whole(pl.ANY)],
-        out_specs=whole(),
+        out_specs=(whole(), whole()),
         compiler_params=params(),
     )(*tokens, after)
 
 
-def norm_kernel(count, source_ref, gain_ref, *refs):
-    token_refs, stat_refs, out_ref = refs[:count], refs[count:-2], refs[-1]
-    gain = gain_ref[...]
+def norm_kernel(source_ref, gain_ref, rows_ref, *refs):
+    stat_refs, out_ref = refs[:-2], refs[-1]
     stats = stat_refs[0][...]
     for ref in stat_refs[1:]:
         stats = stats + ref[...]
-    parts = []
-    for index, token_ref in enumerate(token_refs):
-        rows = token_ref.shape[0]
-        mine = stats[index * rows : (index + 1) * rows]
-        average = mine[:, 0:1] / D
-        inverse_std = lax.rsqrt(mine[:, 64:65] / D - average * average + EPSILON)
-        floats = token_ref[...].astype(F32)
-        parts.append(((floats - average) * inverse_std * gain).astype(BF16))
-    normed = jnp.concatenate(parts, axis=0)
+    average = stats[:, 0:1] / D
+    inverse_std = lax.rsqrt(stats[:, 64:65] / D - average * average + EPSILON)
+    normed = ((rows_ref[...] - average) * inverse_std * gain_ref[...]).astype(BF16)
     rows = normed.shape[0]
     place = lax.broadcasted_iota(jnp.int32, (rows, rows), 1) == source_ref[...]
     out_ref[...] = jnp.dot(
@@ -70,16 +68,87 @@
     ).astype(BF16)
 
 
-def normed_rows(source, gain, tokens, stats, after):
-    rows = sum(t.shape[0] for t in tokens)
-    features = gain.shape[0]
-    return pl.pallas_call(
-        functools.partial(norm_kernel, len(tokens)),
-        out_shape=jax.ShapeDtypeStruct((rows, features), BF16),
-        in_specs=[whole()] * (2 + len(tokens) + len(stats)) + [whole(pl.ANY)],
+def normed_rows(source, gain, rows, stats, after):
+    return pl.pallas_call(
+        norm_kernel,
+        out_shape=pltpu.VMEM(rows.shape, BF16),
+        in_specs=[whole()] * (3 + len(stats)) + [whole(pl.ANY)],
         out_specs=whole(),
         compiler_params=params(),
-    )(source, gain.reshape(1, features), *tokens, *stats, after)
+    )(source, gain, rows, *stats, after)
+
+
+def combine_kernel(keep_ref, sent_ref, *out_refs):
+    total = keep_ref[...] + sent_ref[...].astype(F32)
+    block = out_refs[0].shape[-2]
+    for index, ref in enumerate(out_refs):
+        ref[...] = total[..., index * block : (index + 1) * block, :].astype(ref.dtype)
+
+
+def combine(keep, sent, chips):
+    shape = keep.shape[:-2] + (keep.shape[-2] // chips, keep.shape[-1])
+    return pl.pallas_call(
+        combine_kernel,
+        out_shape=[pltpu.VMEM(shape, sent.dtype)] * (chips - 1) + [pltpu.VMEM(shape, F32)],
+        in_specs=[whole()] * 2,
+        out_specs=[whole()] * chips,
+        compiler_params=params(),
+    )(keep, sent)
+
+
+def query_rows_kernel(count, source_ref, *refs):
+    term_refs, out_refs = refs[:-count], refs[-count:]
+    total = term_refs[0][...]
+    for ref in term_refs[1:]:
+        total = total + ref[...]
+    rows = total.shape[0]
+    place = lax.broadcasted_iota(jnp.int32, (rows, rows), 1) == source_ref[...]
+    turned = jnp.dot(
+        jnp.where(place, 1.0, 0.0).astype(BF16), total.astype(BF16), preferred_element_type=F32
+    )
+    each = rows // count
+    for index, ref in enumerate(out_refs):
+        ref[...] = turned[index * each : (index + 1) * each].astype(BF16)
+
+
+def query_rows(source, terms, count):
+    rows, cols = terms[0].shape
+    return pl.pallas_call(
+        functools.partial(query_rows_kernel, count),
+        out_shape=[pltpu.VMEM((rows // count, cols), BF16)] * count,
+        in_specs=[whole()] * (1 + len(terms)),
+        out_specs=[whole()] * count,
+        compiler_params=params(),
+    )(source, *terms)
+
+
+def gated_kernel(counts, *refs):
+    out_ref = refs[-1]
+    local, wide, steps, _ = out_ref.shape
+    taken, first = 0, 0
+    for count in counts:
+        total = refs[taken][...]
+        for ref in refs[taken + 1 : taken + count]:
+            total = total + ref[...].astype(F32)
+        taken += count
+        gate, up = total[0], total[1]
+        hidden = gate / (1.0 + jnp.exp(-gate)) * up
+        cols = hidden.shape[1]
+        for row in range(local * wide):
+            piece = hidden[row * steps : (row + 1) * steps].astype(BF16)
+            out_ref[row // wide, row % wide, :, first : first + cols] = piece
+        first += cols
+
+
+def gated(chunks, shape):
+    terms = [term for chunk in chunks for term in chunk]
+    return pl.pallas_call(
+        functools.partial(gated_kernel, [len(chunk) for chunk in chunks]),
+        out_shape=jax.ShapeDtypeStruct(shape, BF16),
+        in_specs=[whole()] * len(terms),
+        out_specs=whole(),
+        compiler_params=params(),
+    )(*terms)
 
 
 def in_hbm(arrays):
@@ -170,15 +239,15 @@
     )
 
 
-def wide_kernel(first, tiles, x_ref, w_refs, pre_refs, send_ref, keep_ref, next_ref, ring, ring_sems, next_sems):
+def wide_kernel(first, tiles, x_ref, w_refs, pre_refs, out_refs, next_ref, ring, ring_sems, next_sems):
     held = sum(ref.shape[0] for ref in pre_refs)
     streamed = tiles - held
     depth = ring.shape[0]
     following = 0 if next_ref is None else next_ref.shape[0]
-    half = x_ref.shape[0] // 2
 
     def fetch(index):
-        return tile_copies(w_refs, first + held + index, ring.at[lax.rem(index, depth)], ring_sems.at[lax.rem(index, depth)])
+        slot = lax.rem(index, depth)
+        return tile_copies(w_refs, first + held + index, ring.at[slot], ring_sems.at[slot])
 
     def fetch_next(index):
         return tile_copies(w_refs, first + tiles + index, next_ref.at[index], next_sems.at[index])
@@ -191,8 +260,11 @@
         columns = pl.ds(pl.multiple_of(tile * TILE, TILE), TILE)
         for index in range(2):
             part = jnp.dot(x_ref[...], place[index], preferred_element_type=F32)
-            send_ref[index, :, columns] = part[:half].astype(BF16)
-            keep_ref[index, :, columns] = part[half:]
+            row = 0
+            for ref in out_refs:
+                rows = ref.shape[1]
+                ref[index, :, columns] = part[row : row + rows].astype(ref.dtype)
+                row += rows
 
     early = min(depth, streamed)
     for index in range(early):
@@ -234,26 +306,21 @@
             copy.wait()
 
 
-def wide_sums(x, weights, held, first, tiles, following, after=()):
+def wide_sums(x, weights, held, first, tiles, following, blocks, after=()):
     rows, features = x.shape
     cols = tiles * TILE
     streamed = tiles - sum(h.shape[0] for h in held)
     depth = min(DEPTH, max(streamed, 1))
+    outs = len(blocks)
 
     def kernel(x_ref, wg_ref, wu_ref, *refs):
         pre_refs = refs[: len(held)]
         refs = refs[len(held) + len(after) :]
-        send_ref, keep_ref = refs[:2]
-        next_ref = refs[2] if following else None
-        ring, ring_sems, next_sems = refs[-3:]
-        wide_kernel(
-            first, tiles, x_ref, (wg_ref, wu_ref), pre_refs, send_ref, keep_ref, next_ref, ring, ring_sems, next_sems
-        )
-
-    out_shape = [
-        pltpu.VMEM((2, rows // 2, cols), BF16),
-        pltpu.VMEM((2, rows // 2, cols), F32),
-    ]
+        next_ref = refs[outs] if following else None
+        wide_kernel(first, tiles, x_ref, (wg_ref, wu_ref), pre_refs, refs[:outs], next_ref, *refs[-3:])
+
+    out_shape = [pltpu.VMEM((2, block, cols), BF16) for block in blocks[:-1]]
+    out_shape.append(pltpu.VMEM((2, blocks[-1], cols), F32))
     if following:
         out_shape.append(pltpu.VMEM((following, 2, features, TILE), BF16))
     return pl.pallas_call(
@@ -278,11 +345,10 @@
 
 
 def attend_kernel(count, steps, query_cols, slot_ref, lengths_ref, cache_ref, *refs):
-    part_refs, (out_ref, held, fresh) = refs[:count], refs[count:]
+    part_refs, (out_ref, held, fresh) = refs[:count], refs[-3:]
     for index, ref in enumerate(part_refs):
-        for b in range(ref.shape[0]):
-            held[slot_ref[index], b, :steps] = ref[b].astype(F32)
-    pair_cols = held.shape[3] - query_cols
+        held[slot_ref[index]] = ref[...].astype(F32)
+    pair_cols = held.shape[2] - query_cols
     heads = query_cols // HD
     scale = HD ** (-0.5)
     batch, positions = cache_ref.shape[0], cache_ref.shape[1]
@@ -290,9 +356,9 @@
     for b in range(batch):
         rows = pl.ds(b * steps, steps)
         for c in range(count):
-            fresh[b, :steps, c * pair_cols : (c + 1) * pair_cols] = held[c, b, :steps, query_cols:]
+            fresh[b, :steps, c * pair_cols : (c + 1) * pair_cols] = held[c, rows, query_cols:]
         queries = jnp.concatenate(
-            [held[c, b, :steps, h * HD : (h + 1) * HD] for c in range(count) for h in range(heads)],
+            [held[c, rows, h * HD : (h + 1) * HD] for c in range(count) for h in range(heads)],
             axis=0,
         ).astype(BF16)
         pairs = fresh[b].astype(BF16)
@@ -315,20 +381,21 @@
             (old / total).astype(BF16), cache_ref[b, :, HD:], preferred_element_type=F32
         ) + jnp.dot((new / total).astype(BF16), pairs[:, HD:], preferred_element_type=F32)
         for h in range(HEADS):
-            out_ref[rows, h * HD : (h + 1) * HD] = context[h * steps : (h + 1) * steps].astype(BF16)
-
-
-def attend(slots, lengths, cache, parts, steps, query_cols):
+            piece = context[h * steps : (h + 1) * steps].astype(BF16)
+            out_ref[b, 0, :, h * HD : (h + 1) * HD] = piece
+
+
+def attend(slots, lengths, cache, parts, steps, query_cols, after):
     batch = cache.shape[0]
     count = len(parts)
-    rows, cols = batch * steps, parts[0].shape[2]
+    rows, cols = parts[0].shape
     return pl.pallas_call(
         functools.partial(attend_kernel, count, steps, query_cols),
-        out_shape=jax.ShapeDtypeStruct((rows, HEADS * HD), BF16),
-        in_specs=[whole(pltpu.SMEM), whole(pltpu.SMEM)] + [whole()] * (1 + count),
+        out_shape=jax.ShapeDtypeStruct((batch, 1, steps, HEADS * HD), BF16),
+        in_specs=[whole(pltpu.SMEM), whole(pltpu.SMEM)] + [whole()] * (1 + count) + [whole(pl.ANY)] * len(after),
         out_specs=whole(),
         scratch_shapes=[
-            pltpu.VMEM((count, batch, 8, cols), F32),
+            pltpu.VMEM((count, rows, cols), F32),
             pltpu.VMEM((batch, 8, 2 * HD), F32),
         ],
         compiler_params=params(),
@@ -337,7 +404,7 @@
             bytes_accessed=2 * cache.size,
             transcendentals=batch * steps * HEADS * cache.shape[1],
         ),
-    )(slots, lengths, cache, *parts)
+    )(slots, lengths, cache, *parts, *after)
 
 
 def on_device(tokens, gain, w_query, w_keyval, w_gate, w_up, cache, lengths):
@@ -357,17 +424,11 @@
     def swap(value):
         return lax.ppermute(value, "gy", [(i, i ^ 1) for i in range(size_y)])
 
-    weights = (w_gate, w_up)
-    tiles = w_gate.shape[1] // TILE
-    bounds = [tiles * share // 36 for share in (0, 8, 19, 32, 36)]
-    before = [tiles * share // 36 for share in (4, 4)]
-    ahead = [max(1, tiles * share // 36) for share in (4, 4, 3)] + [0]
-    gathered = [tokens] + [shift_x(tokens, by) for by in range(1, size_x)]
-    gathered = [t.reshape(tall * steps, features) for t in gathered]
-    first_tiles, w_query, w_keyval = load(weights, (w_query, w_keyval), 0, before[0])
-    stats = partial_stats(gathered, first_tiles)
-    every_stat = [stats] + [shift_y(stats, by) for by in range(1, size_y)]
-    (second_tiles,) = load(weights, (), before[0], before[1], after=(stats,))
+    def across_core(value):
+        pairs = []
+        for i in range(size_y):
+            pairs.append((i, (i // 2 + 1) % chips * 2 + (1 - i % 2)))
+        return lax.ppermute(value, "gy", pairs)
 
     row = jnp.arange(2 * chips * block, dtype=jnp.int32)
     core = jnp.where(row < chips * block, 1 - me_y % 2, me_y % 2)
@@ -375,59 +436,60 @@
     sequence = (chip * 2 + core) * local + row % block // (size_x * steps)
     column = row // steps % size_x
     source = (me_x - column) % size_x * (tall * steps) + sequence * steps + row % steps
-    x = normed_rows(source[:, None], gain, gathered, every_stat, second_tiles)
-
-    def across_chips(total, kind):
-        whole_sum = total[..., (chips - 1) * block :, :]
-        for by in range(1, chips):
-            part = total[..., (by - 1) * block : by * block, :].astype(kind)
-            whole_sum = whole_sum + shift_y(part, 2 * by).astype(F32)
-        return whole_sum
-
-    def gated(whole_sum):
-        return (jax.nn.silu(whole_sum[0]) * whole_sum[1]).astype(BF16)
-
-    def chunk_sums(chunk, held, after):
-        return wide_sums(
-            x, weights, held, bounds[chunk], bounds[chunk + 1] - bounds[chunk], ahead[chunk], after
-        )
+    source = source[:, None]
+    row = jnp.arange(block, dtype=jnp.int32)
+    to = (me_x + row // (local * steps)) % size_x
+    order = row // steps % local * (size_x * steps) + to * steps + row % steps
+    order = order[:, None]
+    slots = (me_x - jnp.arange(size_x, dtype=jnp.int32)) % size_x
+    lengths = lengths.reshape(local)
+    gain = gain.reshape(1, features)
+
+    weights = (w_gate, w_up)
+    tiles = w_gate.shape[1] // TILE
+    before = [tiles * share // 36 for share in (5, 5)]
+    bounds = [0, sum(before)] + [tiles * share // 36 for share in (20, 28, 36)]
+    ahead = [max(1, tiles * share // 36) for share in (3, 3, 3)] + [0]
+    gathered = [tokens] + [shift_x(tokens, by) for by in range(1, size_x)]
+    (first_tiles,) = load(weights, (), 0, before[0], after=(source, order, slots, lengths, gain))
+    rows, stats = partial_stats(gathered, first_tiles)
+    every_stat = [stats] + [shift_y(stats, by) for by in range(1, size_y)]
+    (second_tiles,) = load(weights, (), before[0], before[1], after=(stats,))
+    x = normed_rows(source, gain, rows, every_stat, second_tiles)
+
+    halves = (chips * block, chips * block)
+    direct = chips == 2
+
+    def chunk_sums(chunk, held, after, blocks=halves):
+        count = bounds[chunk + 1] - bounds[chunk]
+        return wide_sums(x, weights, held, bounds[chunk], count, ahead[chunk], blocks, after)
+
+    def across_chips(parts):
+        return [parts[-1]] + [shift_y(part, 2 * by) for by, part in enumerate(parts[:-1], 1)]
 
     query_cols = w_query.shape[1]
     send_q, keep_q = query_sums(x, w_query, w_keyval)
-    send, keep, held = chunk_sums(0, (first_tiles, second_tiles), (send_q,))
-    total_q = keep_q + swap(send_q)
-
-    send_1, keep_1, held = chunk_sums(1, (held,), (total_q, send))
-    total_0 = keep + swap(send).astype(F32)
-    ready = across_chips(total_q, F32).astype(BF16).reshape(local, size_x, steps, -1)
-    turned = [
-        lax.dynamic_slice_in_dim(ready, (me_x + by) % size_x, 1, 1)[:, 0] for by in range(size_x)
-    ]
-
-    send_2, keep_2, held = chunk_sums(2, (held,), (total_0, turned[0], send_1))
-    total_1 = keep_1 + swap(send_1).astype(F32)
-    parts = [turned[0]] + [shift_x(turned[by], by) for by in range(1, size_x)]
-    sum_0 = across_chips(total_0, BF16)
-
-    send_3, keep_3 = chunk_sums(3, (held,), (total_1, parts[-1], sum_0, send_2))
-    total_2 = keep_2 + swap(send_2).astype(F32)
-    sum_1 = across_chips(total_1, BF16)
-    total_3 = keep_3 + swap(send_3).astype(F32)
-    sum_2 = across_chips(total_2, BF16)
-    sum_3 = across_chips(total_3, BF16)
-    pieces = [gated(s) for s in (sum_0, sum_1, sum_2, sum_3)]
-    hidden = jnp.concatenate(pieces, axis=1).reshape(local, size_x, steps, -1)
-    slots = (me_x - jnp.arange(size_x, dtype=jnp.int32)) % size_x
-
-    context = attend(
-        slots,
-        lengths.reshape(local),
-        cache.reshape(local, cache.shape[2], cache.shape[3]),
-        parts,
-        steps,
-        query_cols,
-    )
-    return (context.reshape(local, 1, steps, HEADS * HD), hidden)
+    send_0, keep_0, held = chunk_sums(0, (first_tiles, second_tiles), (send_q,))
+    parts_q = combine(keep_q, swap(send_q), chips)
+
+    send_1, keep_1, held = chunk_sums(1, (held,), (parts_q[0], send_0))
+    parts_0 = combine(keep_0, swap(send_0), chips)
+    turned = query_rows(order, across_chips(parts_q), size_x)
+
+    send_2, keep_2, held = chunk_sums(2, (held,), (parts_0[0], turned[0], send_1))
+    parts_1 = combine(keep_1, swap(send_1), chips)
+    new = [turned[0]] + [shift_x(turned[by], by) for by in range(1, size_x)]
+
+    last = chunk_sums(3, (held,), (parts_1[0], send_2), (block,) * 4 if direct else halves)
+    parts_2 = combine(keep_2, swap(send_2), chips)
+    cache = cache.reshape(local, cache.shape[2], cache.shape[3])
+    context = attend(slots, lengths, cache, new, steps, query_cols, (parts_2[0], last[0]))
+    if direct:
+        terms_3 = [last[3], across_core(last[0]), swap(last[1]), shift_y(last[2], 2)]
+    else:
+        terms_3 = across_chips(combine(last[1], swap(last[0]), chips))
+    chunks = [across_chips(parts) for parts in (parts_0, parts_1, parts_2)] + [terms_3]
+    return (context, gated(chunks, (local, size_x, steps, w_gate.shape[1])))
 
 
 def solution(mesh):

time: 107 us -> 74.6 us (0.70)
  local copies, waits for them, and re-layouts: 30 us -> 4.21 us
  waiting for transfers between devices: 11.8 us -> 5.3 us
  other arithmetic: 4.96 us -> 0.09 us
  starting transfers between devices: 18.3 us -> 21.5 us
  Pallas kernels: 40 us -> 42.3 us
    unnamed x28 -> x14, local copies, waits for them, and re-layouts: 27.4 us -> 3.49 us
    ppermute x8, waiting for transfers between devices: 11.3 us -> 5.27 us  [shift_y(): lax.ppermute(value, 'gy', [(i, (i + by) % size_y) for i in range(size_y)])]
    add x9 -> x1, other arithmetic: 3.24 us -> 0.02 us  [on_device(): order = row // steps % local * (size_x * steps) + to * steps + row % steps]
    ppermute x5, starting transfers between devices: 1.19 us -> 2.8 us  [swap(): return lax.ppermute(value, 'gy', [(i, i ^ 1) for i in range(size_y)])]
    pallas_call x2 -> x8, Pallas kernels: 0.52 us -> 2.11 us  [the longest x1 1.02 us: gated(): pl.pallas_call(functools.partial(gated_kernel, [len(chunk) for chunk in c...]
    ppermute x6, starting transfers between devices: 9.39 us -> 10.8 us  [shift_x(): lax.ppermute(value, 'gx', [(i, (i + by) % size_x) for i in range(size_x)])]
  transfers between devices with their start and end apart: 19 -> 20, of which waited for: 5 -> 2; matrix products, arithmetic and copies ran while one was open for 6% -> 1% of each run, Pallas kernels for 36% -> 53%
where the time goes in v3:
time: 74.6 us; the launch traced here: 74.3 us
  Pallas kernels  42.3 us (57%)
  starting transfers between devices  21.5 us (29%)
  waiting for transfers between devices  5.3 us (7%)
  local copies, waits for them, and re-layouts  4.21 us (6%)
  between operations  0.92 us (1%)
    pallas_call x4, Pallas kernels, wide_sums(): pl.pallas_call(kernel, out_shape=out_shape, in_specs=[whole(), whole(pltp...  27 us
    ppermute x6, starting transfers between devices, shift_x(): lax.ppermute(value, 'gx', [(i, (i + by) % size_x) for i in range(size_x)])  10.8 us
    pallas_call x2, Pallas kernels, load(): pl.pallas_call(kernel, out_shape=[pltpu.VMEM((tiles, 2, features, TILE),...  9.3 us
    ppermute x8, starting transfers between devices, shift_y(): lax.ppermute(value, 'gy', [(i, (i + by) % size_y) for i in range(size_y)])  7.72 us
    ppermute x8, waiting for transfers between devices, shift_y(): lax.ppermute(value, 'gy', [(i, (i + by) % size_y) for i in range(size_y)])  5.27 us
    unnamed x14, local copies, waits for them, and re-layouts  3.49 us
    ppermute x5, starting transfers between devices, swap(): return lax.ppermute(value, 'gy', [(i, i ^ 1) for i in range(size_y)])  2.8 us
    pallas_call x1, Pallas kernels, attend(): pl.pallas_call(functools.partial(attend_kernel, count, steps, query_cols)...  2.47 us
  transfers between devices with their start and end apart: 20, of which 2 were waited for; matrix products, arithmetic and copies ran while one was open for 1% of the time, Pallas kernels for 53%

profile of v3, /device:TPU:0, one launch (start us, length us, event | category | flops | bytes accessed | tf_op | source)
XLA Modules:
  0.0 74.3 jit_solution(8908665215478801140)
XLA Ops:
  0.6 3.1 %collective-permute-start = (bf16[8,1,2,2304]{3,2,1,0:T(2,128)(2,1)}, bf16[8,1,2,2304]{3,2,1,0:T(2,128)(2,1)S(1)}, u32[]{:S(2)}, u32[]{:S(2)}) collective-permute-start(bf16[8,1,2,2304]{3,2,1,0:T(2,128)(2,1)} %refs_0_.4), channel_id=1, source_target_pairs={{0,4},{4,8},{8,12},{12,0},{1,5},{5,9},{9,13},{13,1},{2,6},{6,10},{... | collective-permute-start | bytes 221192 | tf_op jit(solution)/shard_map/ppermute | solution.py:419
  3.7 2.6 %collective-permute-start.1 = (bf16[8,1,2,2304]{3,2,1,0:T(2,128)(2,1)}, bf16[8,1,2,2304]{3,2,1,0:T(2,128)(2,1)S(1)}, u32[]{:S(2)}, u32[]{:S(2)}) collective-permute-start(bf16[8,1,2,2304]{3,2,1,0:T(2,128)(2,1)} %refs_0_.4), channel_id=1, source_target_pairs={{0,8},{4,12},{8,0},{12,4},{1,9},{5,13},{9,1},{13,5},{2,10},{6,14},... | collective-permute-start | bytes 221192 | tf_op jit(solution)/shard_map/ppermute | solution.py:419
  6.3 1.3 %collective-permute-start.2 = (bf16[8,1,2,2304]{3,2,1,0:T(2,128)(2,1)}, bf16[8,1,2,2304]{3,2,1,0:T(2,128)(2,1)S(1)}, u32[]{:S(2)}, u32[]{:S(2)}) collective-permute-start(bf16[8,1,2,2304]{3,2,1,0:T(2,128)(2,1)} %refs_0_.4), channel_id=1, source_target_pairs={{0,12},{4,0},{8,4},{12,8},{1,13},{5,1},{9,5},{13,9},{2,14},{6,2},{... | collective-permute-start | bytes 221192 | tf_op jit(solution)/shard_map/ppermute | solution.py:419
  7.7 0.7 reshape.473.refs_6_.gain_ref
  8.4 0.1 fusion.18.refs_2_.source_ref
  8.5 0.0 copy-start.3
  8.5 0.6 copy-done.3
  9.1 4.7 %shard_map.95.refs_4_.refs_0_ = bf16[5,2,2304,256]{3,2,1,0:T(8,128)(2,1)S(1)} custom-call(bf16[2304,9216]{1,0:T(8,128)(2,1)} %wg_ref.7, bf16[2304,9216]{1,0:T(8,128)(2,1)} %wu_ref.7, s32[64,1]{1,0:T(8,128)S(1)} %fusion.18.refs_2_.source_ref, s32[16,1]{1,0:T(8,128)S(1)} %fusion.39.refs_3_.source_ref, s32[4]{0:T(128)S(1)} %and_select_fusion.refs_4_.slot_ref, ...), custom_call_target="tpu_custom_call" | custom-call | bytes 11796480 | tf_op jit(solution)/shard_map/pallas_call | solution.py:192
  13.8 0.0 collective-permute-done.refs_1_
  13.8 0.0 collective-permute-done.1.refs_2_
  13.8 0.0 collective-permute-done.2.refs_3_
  13.9 0.3 shard_map.96
  14.2 0.1 collective-permute-start.3
  14.2 1.6 %collective-permute-start.4 = (f32[64,128]{1,0:T(8,128)S(1)}, f32[64,128]{1,0:T(8,128)S(1)}, u32[]{:S(2)}, u32[]{:S(2)}) collective-permute-start(f32[64,128]{1,0:T(8,128)S(1)} %get-tuple-element.32.refs_2_.refs_0_), channel_id=1, source_target_pairs={{0,2},{1,3},{2,0},{3,1},{4,6},{5,7},{6,4},{7,5},{8,10},{9,11},{10,... | collective-permute-start | bytes 98312 | tf_op jit(solution)/shard_map/ppermute | solution.py:422
  15.8 1.4 %collective-permute-start.5 = (f32[64,128]{1,0:T(8,128)S(1)}, f32[64,128]{1,0:T(8,128)S(1)}, u32[]{:S(2)}, u32[]{:S(2)}) collective-permute-start(f32[64,128]{1,0:T(8,128)S(1)} %get-tuple-element.32.refs_2_.refs_0_), channel_id=1, source_target_pairs={{0,3},{1,0},{2,1},{3,2},{4,7},{5,4},{6,5},{7,6},{8,11},{9,8},{10,9... | collective-permute-start | bytes 98312 | tf_op jit(solution)/shard_map/ppermute | solution.py:422
  17.2 4.6 %shard_map.97.refs_4_.refs_1_ = bf16[5,2,2304,256]{3,2,1,0:T(8,128)(2,1)S(1)} custom-call(bf16[2304,9216]{1,0:T(8,128)(2,1)} %wg_ref.7, bf16[2304,9216]{1,0:T(8,128)(2,1)} %wu_ref.7, f32[64,128]{1,0:T(8,128)S(1)} %get-tuple-element.32.refs_2_.refs_0_), custom_call_target="tpu_custom_call" | custom-call | bytes 11796480 | tf_op jit(solution)/shard_map/pallas_call | solution.py:192
  21.8 0.0 slice-start
  21.9 0.0 copy-start.1
  21.9 0.0 collective-permute-done.3.refs_1_
  21.9 0.0 collective-permute-done.4.refs_2_
  21.9 0.0 collective-permute-done.5.refs_3_
  21.9 0.0 slice-start.1
  21.9 0.4 shard_map.98.x_ref
  22.3 1.7 %slice-done = s8[4194304]{0:T(1024)(128)(4,1)S(1)} async-done(((s8[7077888]{0:T(1024)(128)(4,1)}), s8[4194304]{0:T(1024)(128)(4,1)S(1)}, s32[]{:S(2)}) %slice-start) | async-done | bytes 4194328
  24.0 0.1 copy-done.1
  24.2 1.0 %slice-done.1 = s8[2883584]{0:T(1024)(128)(4,1)S(1)} async-done(((s8[7077888]{0:T(1024)(128)(4,1)}), s8[2883584]{0:T(1024)(128)(4,1)S(1)}, s32[]{:S(2)}) %slice-start.1) | async-done | bytes 2883608
  25.1 1.4 %shard_map.99 = (f32[32,1664]{1,0:T(8,128)S(1)}, f32[32,1664]{1,0:T(8,128)S(1)}) custom-call(bf16[64,2304]{1,0:T(8,128)(2,1)S(1)} %shard_map.98.x_ref, bf16[2304,1536]{1,0:T(8,128)(2,1)S(1)} %bitcast.3, bf16[2304,128]{1,0:T(8,128)(2,1)S(1)} %copy-done.1), custom_call_target="tpu_custom_call" | custom-call | flops 490733568 | bytes 7667712 | tf_op jit(solution)/shard_map/pallas_call | solution.py:224
  26.6 0.1 collective-permute-start.6
  26.7 5.5 %shard_map.102 = (bf16[2,32,2560]{2,1,0:T(8,128)(2,1)S(1)}, f32[2,32,2560]{2,1,0:T(8,128)S(1)}, bf16[3,2,2304,256]{3,2,1,0:T(8,128)(2,1)S(1)}) custom-call(bf16[64,2304]{1,0:T(8,128)(2,1)S(1)} %shard_map.98.x_ref, bf16[2304,9216]{1,0:T(8,128)(2,1)} %wg_ref.7, bf16[2304,9216]{1,0:T(8,128)(2,1)} %wu_ref.7, ...), custom_call_target="tpu_custom_call" | custom-call | flops 1509949440 | bytes 7077888 | tf_op jit(solution)/shard_map/pallas_call | solution.py:326
  32.1 0.6 collective-permute-start.11
  32.7 0.0 collective-permute-done.6.sent_ref
  32.7 0.6 collective-permute-start.7
  33.3 8.6 %shard_map.103 = (bf16[2,32,2560]{2,1,0:T(8,128)(2,1)S(1)}, f32[2,32,2560]{2,1,0:T(8,128)S(1)}, bf16[3,2,2304,256]{3,2,1,0:T(8,128)(2,1)S(1)}) custom-call(bf16[64,2304]{1,0:T(8,128)(2,1)S(1)} %shard_map.98.x_ref, bf16[2304,9216]{1,0:T(8,128)(2,1)} %wg_ref.7, bf16[2304,9216]{1,0:T(8,128)(2,1)} %wu_ref.7, ...), custom_call_target="tpu_custom_call" | custom-call | flops 1509949440 | bytes 23592960 | tf_op jit(solution)/shard_map/pallas_call | solution.py:326
  41.9 0.1 collective-permute-start.13
  42.0 0.0 collective-permute-done.7.refs_1_
  42.0 0.2 shard_map.101
  42.2 0.0 collective-permute-done.11.sent_ref
  42.2 0.1 shard_map.104
  42.2 7.1 %shard_map.105 = (bf16[2,32,2048]{2,1,0:T(8,128)(2,1)S(1)}, f32[2,32,2048]{2,1,0:T(8,128)S(1)}, bf16[3,2,2304,256]{3,2,1,0:T(8,128)(2,1)S(1)}) custom-call(bf16[64,2304]{1,0:T(8,128)(2,1)S(1)} %shard_map.98.x_ref, bf16[2304,9216]{1,0:T(8,128)(2,1)} %wg_ref.7, bf16[2304,9216]{1,0:T(8,128)(2,1)} %wu_ref.7, ...), custom_call_target="tpu_custom_call" | custom-call | flops 1207959552 | bytes 18874368 | tf_op jit(solution)/shard_map/pallas_call | solution.py:326
  49.3 0.6 collective-permute-start.12
  49.9 1.5 %collective-permute-start.14 = (bf16[2,16,2560]{2,1,0:T(8,128)(2,1)S(1)}, bf16[2,16,2560]{2,1,0:T(8,128)(2,1)S(1)}, u32[]{:S(2)}, u32[]{:S(2)}) collective-permute-start(bf16[2,16,2560]{2,1,0:T(8,128)(2,1)S(1)} %get-tuple-element.45.refs_1_), channel_id=1, source_target_pairs={{0,2},{1,3},{2,0},{3,1},{4,6},{5,7},{6,4},{7,5},{8,10},{9,11},{10,... | collective-permute-start | bytes 491528 | tf_op jit(solution)/shard_map/ppermute | solution.py:422
  51.4 0.7 collective-permute-start.8
  52.1 0.9 %collective-permute-start.9 = (bf16[4,1664]{1,0:T(4,128)(2,1)S(1)}, bf16[4,1664]{1,0:T(4,128)(2,1)S(1)}, u32[]{:S(2)}, u32[]{:S(2)}) collective-permute-start(bf16[4,1664]{1,0:T(4,128)(2,1)S(1)} %get-tuple-element.39), channel_id=1, source_target_pairs={{0,8},{4,12},{8,0},{12,4},{1,9},{5,13},{9,1},{13,5},{2,10},{6,14},... | collective-permute-start | bytes 39944 | tf_op jit(solution)/shard_map/ppermute | solution.py:419
  53.0 0.0 collective-permute-done.13.sent_ref
  53.0 2.2 %collective-permute-start.10 = (bf16[4,1664]{1,0:T(4,128)(2,1)S(1)}, bf16[4,1664]{1,0:T(4,128)(2,1)S(1)}, u32[]{:S(2)}, u32[]{:S(2)}) collective-permute-start(bf16[4,1664]{1,0:T(4,128)(2,1)S(1)} %get-tuple-element.40), channel_id=1, source_target_pairs={{0,12},{4,0},{8,4},{12,8},{1,13},{5,1},{9,5},{13,9},{2,14},{6,2},{... | collective-permute-start | bytes 39944 | tf_op jit(solution)/shard_map/ppermute | solution.py:419
  55.2 0.1 shard_map.107
  55.3 0.0 collective-permute-done.12.sent_ref
  55.3 0.6 collective-permute-start.15
  55.9 5.9 %shard_map.108 = (bf16[2,16,2048]{2,1,0:T(8,128)(2,1)S(1)}, bf16[2,16,2048]{2,1,0:T(8,128)(2,1)S(1)}, bf16[2,16,2048]{2,1,0:T(8,128)(2,1)S(1)}, f32[2,16,2048]{2,1,0:T(8,128)S(1)}) custom-call(bf16[64,2304]{1,0:T(8,128)(2,1)S(1)} %shard_map.98.x_ref, bf16[2304,9216]{1,0:T(8,128)(2,1)} %wg_ref.7, bf16[2304,9216]{1,0:T(8,128)(2,1)} %wu_ref.7, ...), custom_call_target="tpu_custom_call" | custom-call | flops 1207959552 | bytes 11796480 | tf_op jit(solution)/shard_map/pallas_call | solution.py:326
  61.8 0.0 collective-permute-done.8.refs_1_
  61.8 0.1 collective-permute-start.17
  62.0 0.0 collective-permute-done.9.refs_2_
  62.0 1.6 %collective-permute-start.18 = (bf16[2,16,2048]{2,1,0:T(8,128)(2,1)S(1)}, bf16[2,16,2048]{2,1,0:T(8,128)(2,1)S(1)}, u32[]{:S(2)}, u32[]{:S(2)}) collective-permute-start(bf16[2,16,2048]{2,1,0:T(8,128)(2,1)S(1)} %get-tuple-element.58), channel_id=1, source_target_pairs={{0,1},{1,0},{2,3},{3,2},{4,5},{5,4},{6,7},{7,6},{8,9},{9,8},{10,11... | collective-permute-start | bytes 393224 | tf_op jit(solution)/shard_map/ppermute | solution.py:425
  63.5 0.0 collective-permute-done.10.refs_3_
  63.5 0.5 collective-permute-start.19
  64.0 0.0 collective-permute-done.14.refs_1_
  64.0 1.5 %collective-permute-start.16 = (bf16[2,16,2048]{2,1,0:T(8,128)(2,1)S(1)}, bf16[2,16,2048]{2,1,0:T(8,128)(2,1)S(1)}, u32[]{:S(2)}, u32[]{:S(2)}) collective-permute-start(bf16[2,16,2048]{2,1,0:T(8,128)(2,1)S(1)} %get-tuple-element.49.refs_4_), channel_id=1, source_target_pairs={{0,2},{1,3},{2,0},{3,1},{4,6},{5,7},{6,4},{7,5},{8,10},{9,11},{10,... | collective-permute-start | bytes 393224 | tf_op jit(solution)/shard_map/ppermute | solution.py:422
  65.6 2.5 %shard_map.109 = bf16[2,1,2,6144]{3,2,1,0:T(2,128)(2,1)} custom-call(s32[4]{0:T(128)S(1)} %and_select_fusion.refs_4_.slot_ref, s32[2]{0:T(128)S(1)} %bitcast.6, bf16[2,1024,512]{2,1,0:T(8,128)(2,1)S(1)} %bitcast.4, bf16[4,1664]{1,0:T(4,128)(2,1)S(1)} %get-tuple-element.37.refs_2_.refs_0_, bf16[4,1664]{1,0:T(4,128)(2,1)S(1)} %collective-permute-done.8.refs_1_, ...), custom_call_target="tpu_custom_call" | custom-call | flops 100663296 | bytes 2097152 | tf_op jit(solution)/shard_map/pallas_call | solution.py:392
  68.0 0.0 collective-permute-done.17.refs_7_
  68.0 0.0 collective-permute-done.18.refs_8_
  68.0 2.5 %collective-permute-done.19.refs_9_ = bf16[2,16,2048]{2,1,0:T(8,128)(2,1)S(1)} collective-permute-done((bf16[2,16,2048]{2,1,0:T(8,128)(2,1)S(1)}, bf16[2,16,2048]{2,1,0:T(8,128)(2,1)S(1)}, u32[]{:S(2)}, u32[]{:S(2)}) %collective-permute-start.19) | collective-permute-done | bytes 131104 | tf_op jit(solution)/shard_map/ppermute | solution.py:422
  70.6 0.0 collective-permute-done.15.refs_3_
  70.6 2.7 %collective-permute-done.16.refs_5_ = bf16[2,16,2048]{2,1,0:T(8,128)(2,1)S(1)} collective-permute-done((bf16[2,16,2048]{2,1,0:T(8,128)(2,1)S(1)}, bf16[2,16,2048]{2,1,0:T(8,128)(2,1)S(1)}, u32[]{:S(2)}, u32[]{:S(2)}) %collective-permute-start.16) | collective-permute-done | bytes 131104 | tf_op jit(solution)/shard_map/ppermute | solution.py:422
  73.3 1.0 %shard_map.110 = bf16[2,4,2,9216]{3,2,1,0:T(2,128)(2,1)} custom-call(f32[2,16,2560]{2,1,0:T(8,128)S(1)} %get-tuple-element.54.refs_0_, bf16[2,16,2560]{2,1,0:T(8,128)(2,1)S(1)} %collective-permute-done.14.refs_1_, f32[2,16,2560]{2,1,0:T(8,128)S(1)} %get-tuple-element.55.refs_2_, bf16[2,16,2560]{2,1,0:T(8,128)(2,1)S(1)} %collective-permute-done.15.refs_3_, ...), custom_call_target="tpu_custom_call" | custom-call | tf_op jit(solution)/shard_map/pallas_call | solution.py:145
  (11 shorter events, 0.1 us)
Async XLA Ops:
  0.6 13.2 %collective-permute-start = (bf16[8,1,2,2304]{3,2,1,0:T(2,128)(2,1)}, bf16[8,1,2,2304]{3,2,1,0:T(2,128)(2,1)S(1)}, u32[]{:S(2)}, u32[]{:S(2)}) collective-permute-start(bf16[8,1,2,2304]{3,2,1,0:T(2,128)(2,1)} %refs_0_.4), channel_id=1, source_target_pairs={{0,4},{4,8},{8,12},{12,0},{1,5},{5,9},{9,13},{13,1},{2,6},{6,10},{... | collective-permute-start | bytes 221192 | tf_op jit(solution)/shard_map/ppermute | solution.py:419
  3.7 10.1 %collective-permute-start.1 = (bf16[8,1,2,2304]{3,2,1,0:T(2,128)(2,1)}, bf16[8,1,2,2304]{3,2,1,0:T(2,128)(2,1)S(1)}, u32[]{:S(2)}, u32[]{:S(2)}) collective-permute-start(bf16[8,1,2,2304]{3,2,1,0:T(2,128)(2,1)} %refs_0_.4), channel_id=1, source_target_pairs={{0,8},{4,12},{8,0},{12,4},{1,9},{5,13},{9,1},{13,5},{2,10},{6,14},... | collective-permute-start | bytes 221192 | tf_op jit(solution)/shard_map/ppermute | solution.py:419
  6.3 7.5 %collective-permute-start.2 = (bf16[8,1,2,2304]{3,2,1,0:T(2,128)(2,1)}, bf16[8,1,2,2304]{3,2,1,0:T(2,128)(2,1)S(1)}, u32[]{:S(2)}, u32[]{:S(2)}) collective-permute-start(bf16[8,1,2,2304]{3,2,1,0:T(2,128)(2,1)} %refs_0_.4), channel_id=1, source_target_pairs={{0,12},{4,0},{8,4},{12,8},{1,13},{5,1},{9,5},{13,9},{2,14},{6,2},{... | collective-permute-start | bytes 221192 | tf_op jit(solution)/shard_map/ppermute | solution.py:419
  8.5 0.7 copy-start.3
  9.1 4.7 %copy-start.2 = (bf16[8,1,2,2304]{3,2,1,0:T(2,128)(2,1)S(1)}, bf16[8,1,2,2304]{3,2,1,0:T(2,128)(2,1)}, u32[]{:S(2)}) copy-start(bf16[8,1,2,2304]{3,2,1,0:T(2,128)(2,1)} %refs_0_.4) | copy-start | bytes 221188
  14.2 7.7 %collective-permute-start.3 = (f32[64,128]{1,0:T(8,128)S(1)}, f32[64,128]{1,0:T(8,128)S(1)}, u32[]{:S(2)}, u32[]{:S(2)}) collective-permute-start(f32[64,128]{1,0:T(8,128)S(1)} %get-tuple-element.32.refs_2_.refs_0_), channel_id=1, source_target_pairs={{0,1},{1,2},{2,3},{3,0},{4,5},{5,6},{6,7},{7,4},{8,9},{9,10},{10,1... | collective-permute-start | bytes 98312 | tf_op jit(solution)/shard_map/ppermute | solution.py:422
  14.2 7.7 %collective-permute-start.4 = (f32[64,128]{1,0:T(8,128)S(1)}, f32[64,128]{1,0:T(8,128)S(1)}, u32[]{:S(2)}, u32[]{:S(2)}) collective-permute-start(f32[64,128]{1,0:T(8,128)S(1)} %get-tuple-element.32.refs_2_.refs_0_), channel_id=1, source_target_pairs={{0,2},{1,3},{2,0},{3,1},{4,6},{5,7},{6,4},{7,5},{8,10},{9,11},{10,... | collective-permute-start | bytes 98312 | tf_op jit(solution)/shard_map/ppermute | solution.py:422
  15.8 6.1 %collective-permute-start.5 = (f32[64,128]{1,0:T(8,128)S(1)}, f32[64,128]{1,0:T(8,128)S(1)}, u32[]{:S(2)}, u32[]{:S(2)}) collective-permute-start(f32[64,128]{1,0:T(8,128)S(1)} %get-tuple-element.32.refs_2_.refs_0_), channel_id=1, source_target_pairs={{0,3},{1,0},{2,1},{3,2},{4,7},{5,4},{6,5},{7,6},{8,11},{9,8},{10,9... | collective-permute-start | bytes 98312 | tf_op jit(solution)/shard_map/ppermute | solution.py:422
  21.8 2.2 %slice-start = ((s8[7077888]{0:T(1024)(128)(4,1)}), s8[4194304]{0:T(1024)(128)(4,1)S(1)}, s32[]{:S(2)}) async-start(s8[7077888]{0:T(1024)(128)(4,1)} %bitcast.2), calls=%async_computation | async-start | bytes 8388608
  21.9 2.3 %copy-start.1 = (bf16[2304,128]{1,0:T(8,128)(2,1)S(1)}, bf16[2304,128]{1,0:T(8,128)(2,1)}, u32[]{:S(2)}) copy-start(bf16[2304,128]{1,0:T(8,128)(2,1)} %wkv_ref.1) | copy-start | bytes 1769476
  21.9 3.2 %slice-start.1 = ((s8[7077888]{0:T(1024)(128)(4,1)}), s8[2883584]{0:T(1024)(128)(4,1)S(1)}, s32[]{:S(2)}) async-start(s8[7077888]{0:T(1024)(128)(4,1)} %bitcast.2), calls=%async_computation.1 | async-start | bytes 5767168
  26.6 6.1 %collective-permute-start.6 = (f32[32,1664]{1,0:T(8,128)S(1)}, f32[32,1664]{1,0:T(8,128)S(1)}, u32[]{:S(2)}, u32[]{:S(2)}) collective-permute-start(f32[32,1664]{1,0:T(8,128)S(1)} %get-tuple-element.34.refs_2_), channel_id=1, source_target_pairs={{0,1},{1,0},{2,3},{3,2},{4,5},{5,4},{6,7},{7,6},{8,9},{9,8},{10,11... | collective-permute-start | bytes 638984 | tf_op jit(solution)/shard_map/ppermute | solution.py:425
  32.1 10.0 %collective-permute-start.11 = (bf16[2,32,2560]{2,1,0:T(8,128)(2,1)S(1)}, bf16[2,32,2560]{2,1,0:T(8,128)(2,1)S(1)}, u32[]{:S(2)}, u32[]{:S(2)}) collective-permute-start(bf16[2,32,2560]{2,1,0:T(8,128)(2,1)S(1)} %get-tuple-element.42.refs_2_), channel_id=1, source_target_pairs={{0,1},{1,0},{2,3},{3,2},{4,5},{5,4},{6,7},{7,6},{8,9},{9,8},{10,11... | collective-permute-start | bytes 983048 | tf_op jit(solution)/shard_map/ppermute | solution.py:425
  32.7 9.2 %collective-permute-start.7 = (f32[16,1664]{1,0:T(8,128)S(1)}, f32[16,1664]{1,0:T(8,128)S(1)}, u32[]{:S(2)}, u32[]{:S(2)}) collective-permute-start(f32[16,1664]{1,0:T(8,128)S(1)} %get-tuple-element.36.refs_1_), channel_id=1, source_target_pairs={{0,2},{1,3},{2,0},{3,1},{4,6},{5,7},{6,4},{7,5},{8,10},{9,11},{10,... | collective-permute-start | bytes 319496 | tf_op jit(solution)/shard_map/ppermute | solution.py:422
  41.9 11.1 %collective-permute-start.13 = (bf16[2,32,2560]{2,1,0:T(8,128)(2,1)S(1)}, bf16[2,32,2560]{2,1,0:T(8,128)(2,1)S(1)}, u32[]{:S(2)}, u32[]{:S(2)}) collective-permute-start(bf16[2,32,2560]{2,1,0:T(8,128)(2,1)S(1)} %get-tuple-element.46.refs_3_), channel_id=1, source_target_pairs={{0,1},{1,0},{2,3},{3,2},{4,5},{5,4},{6,7},{7,6},{8,9},{9,8},{10,11... | collective-permute-start | bytes 983048 | tf_op jit(solution)/shard_map/ppermute | solution.py:425
  49.3 6.0 %collective-permute-start.12 = (bf16[2,32,2048]{2,1,0:T(8,128)(2,1)S(1)}, bf16[2,32,2048]{2,1,0:T(8,128)(2,1)S(1)}, u32[]{:S(2)}, u32[]{:S(2)}) collective-permute-start(bf16[2,32,2048]{2,1,0:T(8,128)(2,1)S(1)} %get-tuple-element.48.refs_2_), channel_id=1, source_target_pairs={{0,1},{1,0},{2,3},{3,2},{4,5},{5,4},{6,7},{7,6},{8,9},{9,8},{10,11... | collective-permute-start | bytes 786440 | tf_op jit(solution)/shard_map/ppermute | solution.py:425
  49.9 14.2 %collective-permute-start.14 = (bf16[2,16,2560]{2,1,0:T(8,128)(2,1)S(1)}, bf16[2,16,2560]{2,1,0:T(8,128)(2,1)S(1)}, u32[]{:S(2)}, u32[]{:S(2)}) collective-permute-start(bf16[2,16,2560]{2,1,0:T(8,128)(2,1)S(1)} %get-tuple-element.45.refs_1_), channel_id=1, source_target_pairs={{0,2},{1,3},{2,0},{3,1},{4,6},{5,7},{6,4},{7,5},{8,10},{9,11},{10,... | collective-permute-start | bytes 491528 | tf_op jit(solution)/shard_map/ppermute | solution.py:422
  51.4 10.4 %collective-permute-start.8 = (bf16[4,1664]{1,0:T(4,128)(2,1)S(1)}, bf16[4,1664]{1,0:T(4,128)(2,1)S(1)}, u32[]{:S(2)}, u32[]{:S(2)}) collective-permute-start(bf16[4,1664]{1,0:T(4,128)(2,1)S(1)} %get-tuple-element.38), channel_id=1, source_target_pairs={{0,4},{4,8},{8,12},{12,0},{1,5},{5,9},{9,13},{13,1},{2,6},{6,10},{... | collective-permute-start | bytes 39944 | tf_op jit(solution)/shard_map/ppermute | solution.py:419
  52.1 9.9 %collective-permute-start.9 = (bf16[4,1664]{1,0:T(4,128)(2,1)S(1)}, bf16[4,1664]{1,0:T(4,128)(2,1)S(1)}, u32[]{:S(2)}, u32[]{:S(2)}) collective-permute-start(bf16[4,1664]{1,0:T(4,128)(2,1)S(1)} %get-tuple-element.39), channel_id=1, source_target_pairs={{0,8},{4,12},{8,0},{12,4},{1,9},{5,13},{9,1},{13,5},{2,10},{6,14},... | collective-permute-start | bytes 39944 | tf_op jit(solution)/shard_map/ppermute | solution.py:419
  53.0 10.6 %collective-permute-start.10 = (bf16[4,1664]{1,0:T(4,128)(2,1)S(1)}, bf16[4,1664]{1,0:T(4,128)(2,1)S(1)}, u32[]{:S(2)}, u32[]{:S(2)}) collective-permute-start(bf16[4,1664]{1,0:T(4,128)(2,1)S(1)} %get-tuple-element.40), channel_id=1, source_target_pairs={{0,12},{4,0},{8,4},{12,8},{1,13},{5,1},{9,5},{13,9},{2,14},{6,2},{... | collective-permute-start | bytes 39944 | tf_op jit(solution)/shard_map/ppermute | solution.py:419
  55.3 15.3 %collective-permute-start.15 = (bf16[2,16,2560]{2,1,0:T(8,128)(2,1)S(1)}, bf16[2,16,2560]{2,1,0:T(8,128)(2,1)S(1)}, u32[]{:S(2)}, u32[]{:S(2)}) collective-permute-start(bf16[2,16,2560]{2,1,0:T(8,128)(2,1)S(1)} %get-tuple-element.52.refs_1_), channel_id=1, source_target_pairs={{0,2},{1,3},{2,0},{3,1},{4,6},{5,7},{6,4},{7,5},{8,10},{9,11},{10,... | collective-permute-start | bytes 491528 | tf_op jit(solution)/shard_map/ppermute | solution.py:422
  55.9 9.7 %copy-start = (bf16[2,1,1024,512]{3,2,1,0:T(8,128)(2,1)S(1)}, bf16[2,1,1024,512]{3,2,1,0:T(8,128)(2,1)}, u32[]{:S(2)}) copy-start(bf16[2,1,1024,512]{3,2,1,0:T(8,128)(2,1)} %param.14) | copy-start | bytes 6291460
  55.9 9.7 %copy-start.4 = (s32[2,1]{0,1:T(1,128)S(1)}, s32[2,1]{0,1:T(1,128)}, u32[]{:S(2)}) copy-start(s32[2,1]{0,1:T(1,128)} %param.15) | copy-start | bytes 28
  61.8 6.2 %collective-permute-start.17 = (bf16[2,16,2048]{2,1,0:T(8,128)(2,1)S(1)}, bf16[2,16,2048]{2,1,0:T(8,128)(2,1)S(1)}, u32[]{:S(2)}, u32[]{:S(2)}) collective-permute-start(bf16[2,16,2048]{2,1,0:T(8,128)(2,1)S(1)} %get-tuple-element.53.refs_5_), channel_id=1, source_target_pairs={{0,3},{1,2},{2,1},{3,0},{4,7},{5,6},{6,5},{7,4},{8,11},{9,10},{10,... | collective-permute-start | bytes 393224 | tf_op jit(solution)/shard_map/ppermute | solution.py:431
  62.0 6.1 %collective-permute-start.18 = (bf16[2,16,2048]{2,1,0:T(8,128)(2,1)S(1)}, bf16[2,16,2048]{2,1,0:T(8,128)(2,1)S(1)}, u32[]{:S(2)}, u32[]{:S(2)}) collective-permute-start(bf16[2,16,2048]{2,1,0:T(8,128)(2,1)S(1)} %get-tuple-element.58), channel_id=1, source_target_pairs={{0,1},{1,0},{2,3},{3,2},{4,5},{5,4},{6,7},{7,6},{8,9},{9,8},{10,11... | collective-permute-start | bytes 393224 | tf_op jit(solution)/shard_map/ppermute | solution.py:425
  63.5 7.0 %collective-permute-start.19 = (bf16[2,16,2048]{2,1,0:T(8,128)(2,1)S(1)}, bf16[2,16,2048]{2,1,0:T(8,128)(2,1)S(1)}, u32[]{:S(2)}, u32[]{:S(2)}) collective-permute-start(bf16[2,16,2048]{2,1,0:T(8,128)(2,1)S(1)} %get-tuple-element.59), channel_id=1, source_target_pairs={{0,2},{1,3},{2,0},{3,1},{4,6},{5,7},{6,4},{7,5},{8,10},{9,11},{10,... | collective-permute-start | bytes 393224 | tf_op jit(solution)/shard_map/ppermute | solution.py:422
  64.0 9.3 %collective-permute-start.16 = (bf16[2,16,2048]{2,1,0:T(8,128)(2,1)S(1)}, bf16[2,16,2048]{2,1,0:T(8,128)(2,1)S(1)}, u32[]{:S(2)}, u32[]{:S(2)}) collective-permute-start(bf16[2,16,2048]{2,1,0:T(8,128)(2,1)S(1)} %get-tuple-element.49.refs_4_), channel_id=1, source_target_pairs={{0,2},{1,3},{2,0},{3,1},{4,6},{5,7},{6,4},{7,5},{8,10},{9,11},{10,... | collective-permute-start | bytes 393224 | tf_op jit(solution)/shard_map/ppermute | solution.py:422

commit v4 on v3

v4 whole, which is shorter than its diff:
```python
import functools

import jax
import jax.numpy as jnp
from jax import lax
from jax.experimental import pallas as pl
from jax.experimental.pallas import tpu as pltpu
from jax.sharding import PartitionSpec as P

D = 9216
HEADS = 24
HD = 256
EPSILON = 1e-05
MASKED = -1e30
MIB = 1024 * 1024
TILE = 256
DEPTH = 3
F32 = jnp.float32
BF16 = jnp.bfloat16


def whole(memory_space=pltpu.VMEM):
    return pl.BlockSpec(memory_space=memory_space)


def cost_of(*arrays):
    size = sum(a.size for a in arrays)
    return pl.CostEstimate(flops=size, bytes_accessed=size // 16, transcendentals=0)


def params():
    return pltpu.CompilerParams(vmem_limit_bytes=9 * MIB)


def stats_kernel(count, *refs):
    token_refs, (rows_ref, out_ref) = refs[:count], refs[-2:]
    tall, _, steps, features = token_refs[0].shape
    for index, ref in enumerate(token_refs):
        for t in range(tall):
            first = (index * tall + t) * steps
            rows_ref[first : first + steps] = ref[t, 0].astype(F32)
    floats = rows_ref[...]
    sums = jnp.sum(floats, axis=-1, keepdims=True)
    squares = jnp.sum(floats * floats, axis=-1, keepdims=True)
    lane = lax.broadcasted_iota(jnp.int32, out_ref.shape, 1)
    out_ref[...] = jnp.where(lane < 64, sums, squares)


def partial_stats(tokens, after):
    tall, _, steps, features = tokens[0].shape
    rows = len(tokens) * tall * steps
    return pl.pallas_call(
        functools.partial(stats_kernel, len(tokens)),
        out_shape=(pltpu.VMEM((rows, features), F32), pltpu.VMEM((rows, 128), F32)),
        in_specs=[whole()] * len(tokens) + [whole(pl.ANY)],
        out_specs=(whole(), whole()),
        compiler_params=params(),
        cost_estimate=cost_of(*tokens),
    )(*tokens, after)


def norm_kernel(source_ref, gain_ref, rows_ref, *refs):
    stat_refs, out_ref = refs[:-2], refs[-1]
    stats = stat_refs[0][...]
    for ref in stat_refs[1:]:
        stats = stats + ref[...]
    average = stats[:, 0:1] / D
    inverse_std = lax.rsqrt(stats[:, 64:65] / D - average * average + EPSILON)
    normed = ((rows_ref[...] - average) * inverse_std * gain_ref[...][None, :]).astype(BF16)
    rows = normed.shape[0]
    place = lax.broadcasted_iota(jnp.int32, (rows, rows), 1) == source_ref[...]
    out_ref[...] = jnp.dot(
        jnp.where(place, 1.0, 0.0).astype(BF16), normed, preferred_element_type=F32
    ).astype(BF16)


def normed_rows(source, gain, rows, stats, after):
    return pl.pallas_call(
        norm_kernel,
        out_shape=pltpu.VMEM(rows.shape, BF16),
        in_specs=[whole()] * (3 + len(stats)) + [whole(pl.ANY)],
        out_specs=whole(),
        compiler_params=params(),
        cost_estimate=cost_of(rows),
    )(source, gain, rows, *stats, after)


def combine_kernel(chips, small, *refs):
    sent_ref, keep_ref = refs[:2]
    out_refs = refs[3 if small else 2 :]
    cols = keep_ref.shape[2]
    block = keep_ref.shape[1] // chips
    for index in range(chips):
        rows = slice(index * block, (index + 1) * block)
        total = keep_ref[:, rows] + sent_ref[:, rows, :cols].astype(F32)
        out_refs[index][:, :, :cols] = total.astype(out_refs[index].dtype)
        if small:
            sent = sent_ref[0, rows, cols:].astype(F32) + sent_ref[1, rows, cols:].astype(F32)
            total = refs[2][rows] + sent
            if index == chips - 1:
                out_refs[chips][...] = total
            else:
                store_split(out_refs[index], slice(cols, cols + small), total)


def combine(chips, sent, keep, keep_q=None):
    small = 0 if keep_q is None else keep_q.shape[1]
    block = keep.shape[1] // chips
    out_shape = [pltpu.VMEM((2, block, sent.shape[2]), BF16)] * (chips - 1)
    out_shape.append(pltpu.VMEM((2, block, keep.shape[2]), F32))
    if small:
        out_shape.append(pltpu.VMEM((block, small), F32))
    args = (sent, keep, keep_q) if small else (sent, keep)
    return pl.pallas_call(
        functools.partial(combine_kernel, chips, small),
        out_shape=out_shape,
        in_specs=[whole()] * len(args),
        out_specs=[whole()] * len(out_shape),
        compiler_params=params(),
        cost_estimate=cost_of(*args),
    )(*args)


def query_rows_kernel(count, source_ref, *refs):
    term_refs, out_refs = refs[:-count], refs[-count:]
    total = term_refs[0][...]
    rows, cols = total.shape
    for ref in term_refs[1:]:
        first = ref.shape[2] - cols
        total = total + (ref[0, :, first:].astype(F32) + ref[1, :, first:].astype(F32))
    place = lax.broadcasted_iota(jnp.int32, (rows, rows), 1) == source_ref[...]
    turned = jnp.dot(
        jnp.where(place, 1.0, 0.0).astype(BF16), total.astype(BF16), preferred_element_type=F32
    )
    each = rows // count
    for index, ref in enumerate(out_refs):
        ref[...] = turned[index * each : (index + 1) * each].astype(BF16)


def query_rows(source, terms, count):
    rows, cols = terms[0].shape
    return pl.pallas_call(
        functools.partial(query_rows_kernel, count),
        out_shape=[pltpu.VMEM((rows // count, cols), BF16)] * count,
        in_specs=[whole()] * (1 + len(terms)),
        out_specs=[whole()] * count,
        compiler_params=params(),
        cost_estimate=cost_of(*terms),
    )(source, *terms)


def gated_kernel(counts, ready, *refs):
    out_ref = refs[-1]
    local, wide, steps, _ = out_ref.shape
    taken, first = ready, 0
    for ref in refs[:ready]:
        out_ref[:, :, :, : ref.shape[3]] = ref[...]
        first = ref.shape[3]
    for count in counts:
        total = refs[taken][...]
        cols = total.shape[2]
        for ref in refs[taken + 1 : taken + count]:
            total = total + ref[:, :, :cols].astype(F32)
        taken += count
        gate, up = total[0], total[1]
        hidden = gate / (1.0 + jnp.exp(-gate)) * up
        for row in range(local * wide):
            piece = hidden[row * steps : (row + 1) * steps].astype(BF16)
            out_ref[row // wide, row % wide, :, first : first + cols] = piece
        first += cols


def gated(chunks, out_shape, ready=(), after=()):
    terms = [term for chunk in chunks for term in chunk]
    return pl.pallas_call(
        functools.partial(gated_kernel, [len(chunk) for chunk in chunks], len(ready)),
        out_shape=out_shape,
        in_specs=[whole()] * (len(ready) + len(terms)) + [whole(pl.ANY)] * len(after),
        out_specs=whole(),
        compiler_params=params(),
        cost_estimate=cost_of(*ready, *terms),
    )(*ready, *terms, *after)


def in_hbm(arrays):
    return [pltpu.with_memory_space_constraint(a, pltpu.HBM) for a in arrays]


def in_vmem(arrays):
    return [pltpu.with_memory_space_constraint(a, pltpu.VMEM) for a in arrays]


def tile_copies(w_refs, tile, place, sems):
    columns = pl.ds(pl.multiple_of(tile * TILE, TILE), TILE)
    return [
        pltpu.make_async_copy(
            ref.at[:, columns], place.at[:, index * TILE : (index + 1) * TILE], sems.at[index]
        )
        for index, ref in enumerate(w_refs)
    ]


def load_kernel(first, tiles, wg_ref, wu_ref, *refs):
    out_ref, sems = refs[-2:]

    def copies(tile):
        return tile_copies((wg_ref, wu_ref), first + tile, out_ref.at[tile], sems.at[tile])

    for tile in range(tiles):
        for copy in copies(tile):
            copy.start()
    for tile in range(tiles):
        for copy in copies(tile):
            copy.wait()


def load(weights, first, tiles, after):
    features = weights[0].shape[0]
    return pl.pallas_call(
        functools.partial(load_kernel, first, tiles),
        out_shape=pltpu.VMEM((tiles, features, 2 * TILE), BF16),
        in_specs=[whole(pltpu.HBM)] * 2 + [whole(pl.ANY)] * len(after),
        out_specs=whole(),
        scratch_shapes=[pltpu.SemaphoreType.DMA((tiles, 2))],
        compiler_params=params(),
        cost_estimate=pl.CostEstimate(
            flops=0, bytes_accessed=4 * features * TILE * tiles, transcendentals=0
        ),
    )(*in_hbm(weights), *after)


def store_split(ref, columns, value):
    high = value.astype(BF16)
    ref[0, :, columns] = high
    ref[1, :, columns] = (value - high.astype(F32)).astype(BF16)


def multiply(x_ref, place, tile, send_ref, keep_ref):
    part = jnp.dot(x_ref[...], place[...], preferred_element_type=F32)
    half = part.shape[0] // 2
    columns = pl.ds(pl.multiple_of(tile * TILE, TILE), TILE)
    for index in range(2):
        ref_columns = slice(index * TILE, (index + 1) * TILE)
        send_ref[index, :, columns] = part[:half, ref_columns].astype(BF16)
        keep_ref[index, :, columns] = part[half:, ref_columns]


def first_kernel(held, x_ref, wg_ref, wu_ref, wq_ref, wkv_ref, *refs):
    pre_refs = refs[:held]
    send_ref, keep_ref, keep_q_ref, next_ref, q_ref, kv_ref, small_sems, next_sems = refs[held:]
    tiles = sum(ref.shape[0] for ref in pre_refs)
    half = x_ref.shape[0] // 2
    smalls = [
        pltpu.make_async_copy(wq_ref, q_ref, small_sems.at[0]),
        pltpu.make_async_copy(wkv_ref, kv_ref, small_sems.at[1]),
    ]
    for copy in smalls:
        copy.start()

    def fetch_next(index):
        return tile_copies((wg_ref, wu_ref), tiles + index, next_ref.at[index], next_sems.at[index])

    for index in range(next_ref.shape[0]):
        for copy in fetch_next(index):
            copy.start()
    done = 0
    for ref in pre_refs:

        def from_held(index, carry, ref=ref, done=done):
            multiply(x_ref, ref.at[index], done + index, send_ref, keep_ref)
            return carry

        lax.fori_loop(0, ref.shape[0], from_held, 0)
        done += ref.shape[0]
    taken = 0
    for copy, ref in zip(smalls, (q_ref, kv_ref)):
        copy.wait()
        cols = ref.shape[1]
        part = jnp.dot(x_ref[...], ref[...], preferred_element_type=F32)
        store_split(send_ref, slice(tiles * TILE + taken, tiles * TILE + taken + cols), part[:half])
        keep_q_ref[:, taken : taken + cols] = part[half:]
        taken += cols
    for index in range(next_ref.shape[0]):
        for copy in fetch_next(index):
            copy.wait()


def first_sums(x, weights, w_query, w_keyval, held, following):
    rows, features = x.shape
    tiles = sum(h.shape[0] for h in held)
    cols, small = tiles * TILE, w_query.shape[1] + w_keyval.shape[1]
    return pl.pallas_call(
        functools.partial(first_kernel, len(held)),
        out_shape=[
            pltpu.VMEM((2, rows // 2, cols + small), BF16),
            pltpu.VMEM((2, rows // 2, cols), F32),
            pltpu.VMEM((rows // 2, small), F32),
            pltpu.VMEM((following, features, 2 * TILE), BF16),
        ],
        in_specs=[whole()] + [whole(pltpu.HBM)] * 4 + [whole()] * len(held),
        out_specs=[whole()] * 4,
        scratch_shapes=[
            pltpu.VMEM(w_query.shape, BF16),
            pltpu.VMEM(w_keyval.shape, BF16),
            pltpu.SemaphoreType.DMA((2,)),
            pltpu.SemaphoreType.DMA((following, 2)),
        ],
        compiler_params=params(),
        cost_estimate=pl.CostEstimate(
            flops=2 * rows * features * (2 * cols + small),
            bytes_accessed=4 * features * cols,
            transcendentals=0,
        ),
    )(x, *in_hbm((*weights, w_query, w_keyval)), *in_vmem(held))


def wide_kernel(first, tiles, following, after, x_ref, wg_ref, wu_ref, pre_ref, *refs):
    send_ref, keep_ref = refs[after : after + 2]
    next_ref = refs[after + 2] if following else None
    ring, ring_sems, next_sems = refs[-3:]
    held, depth = pre_ref.shape[0], ring.shape[0]
    streamed = tiles - held

    def fetch(index):
        slot = lax.rem(index, depth)
        return tile_copies((wg_ref, wu_ref), first + held + index, ring.at[slot], ring_sems.at[slot])

    def fetch_next(index):
        return tile_copies((wg_ref, wu_ref), first + tiles + index, next_ref.at[index], next_sems.at[index])

    def start(copies):
        for copy in copies:
            copy.start()

    early = min(depth, streamed)
    for index in range(early):
        start(fetch(index))
    early_next = min(following, depth - early)
    for index in range(early_next):
        start(fetch_next(index))

    def from_held(index, carry):
        multiply(x_ref, pre_ref.at[index], index, send_ref, keep_ref)
        return carry

    lax.fori_loop(0, held, from_held, 0)

    def from_ring(index, carry):
        for copy in fetch(index):
            copy.wait()
        multiply(x_ref, ring.at[lax.rem(index, depth)], held + index, send_ref, keep_ref)

        @pl.when(index + depth < streamed)
        def _():
            start(fetch(index + depth))

        if following > early_next:
            later = index + early_next + depth - streamed

            @pl.when((later >= early_next) & (later < following))
            def _():
                start(fetch_next(later))

        return carry

    lax.fori_loop(0, streamed, from_ring, 0)
    for index in range(following):
        for copy in fetch_next(index):
            copy.wait()


def wide_sums(x, weights, held, first, tiles, following, after):
    rows, features = x.shape
    cols = tiles * TILE
    streamed = tiles - held.shape[0]
    depth = min(DEPTH, max(streamed, 1))
    out_shape = [
        pltpu.VMEM((2, rows // 2, cols), BF16),
        pltpu.VMEM((2, rows // 2, cols), F32),
    ]
    if following:
        out_shape.append(pltpu.VMEM((following, features, 2 * TILE), BF16))
    return pl.pallas_call(
        functools.partial(wide_kernel, first, tiles, following, len(after)),
        out_shape=out_shape,
        in_specs=[whole(), whole(pltpu.HBM), whole(pltpu.HBM), whole()]
        + [whole(pl.ANY)] * len(after),
        out_specs=[whole()] * len(out_shape),
        scratch_shapes=[
            pltpu.VMEM((depth, features, 2 * TILE), BF16),
            pltpu.SemaphoreType.DMA((depth, 2)),
            pltpu.SemaphoreType.DMA((max(following, 1), 2)),
        ],
        compiler_params=params(),
        cost_estimate=pl.CostEstimate(
            flops=4 * rows * features * cols,
            bytes_accessed=4 * features * TILE * (streamed + following),
            transcendentals=0,
        ),
    )(x, *in_hbm(weights), *in_vmem((held,)), *after)


def attend_kernel(count, steps, query_cols, slot_ref, lengths_ref, cache_ref, *refs):
    part_refs, (out_ref, held, fresh) = refs[:count], refs[-3:]
    for index, ref in enumerate(part_refs):
        held[slot_ref[index]] = ref[...].astype(F32)
    pair_cols = held.shape[2] - query_cols
    heads = query_cols // HD
    scale = HD ** (-0.5)
    batch, positions = cache_ref.shape[0], cache_ref.shape[1]
    fresh[...] = jnp.zeros_like(fresh)
    for b in range(batch):
        rows = pl.ds(b * steps, steps)
        for c in range(count):
            fresh[b, :steps, c * pair_cols : (c + 1) * pair_cols] = held[c, rows, query_cols:]
        queries = jnp.concatenate(
            [held[c, rows, h * HD : (h + 1) * HD] for c in range(count) for h in range(heads)],
            axis=0,
        ).astype(BF16)
        pairs = fresh[b].astype(BF16)
        dims = (((1,), (1,)), ((), ()))
        old = lax.dot_general(
            queries, cache_ref[b, :, :HD], dims, preferred_element_type=F32
        ) * scale
        position = lax.broadcasted_iota(jnp.int32, old.shape, 1)
        old = jnp.where(position < lengths_ref[b, 0], old, MASKED)
        new = lax.dot_general(queries, pairs[:, :HD], dims, preferred_element_type=F32) * scale
        step = lax.broadcasted_iota(jnp.int32, new.shape, 0) % steps
        new = jnp.where(lax.broadcasted_iota(jnp.int32, new.shape, 1) <= step, new, MASKED)
        highest = jnp.maximum(
            jnp.max(old, axis=-1, keepdims=True), jnp.max(new, axis=-1, keepdims=True)
        )
        old = jnp.exp(old - highest)
        new = jnp.exp(new - highest)
        total = jnp.sum(old, axis=-1, keepdims=True) + jnp.sum(new, axis=-1, keepdims=True)
        context = jnp.dot(
            (old / total).astype(BF16), cache_ref[b, :, HD:], preferred_element_type=F32
        ) + jnp.dot((new / total).astype(BF16), pairs[:, HD:], preferred_element_type=F32)
        for h in range(HEADS):
            piece = context[h * steps : (h + 1) * steps].astype(BF16)
            out_ref[b, 0, :, h * HD : (h + 1) * HD] = piece


def attend(slots, lengths, cache, parts, steps, query_cols, after):
    batch = cache.shape[0]
    count = len(parts)
    rows, cols = parts[0].shape
    return pl.pallas_call(
        functools.partial(attend_kernel, count, steps, query_cols),
        out_shape=jax.ShapeDtypeStruct((batch, 1, steps, HEADS * HD), BF16),
        in_specs=[whole(pltpu.SMEM), whole(pltpu.SMEM)] + [whole()] * (1 + count) + [whole(pl.ANY)] * len(after),
        out_specs=whole(),
        scratch_shapes=[
            pltpu.VMEM((count, rows, cols), F32),
            pltpu.VMEM((batch, 8, 2 * HD), F32),
        ],
        compiler_params=params(),
        cost_estimate=pl.CostEstimate(
            flops=4 * batch * steps * HEADS * HD * cache.shape[1],
            bytes_accessed=2 * cache.size,
            transcendentals=batch * steps * HEADS * cache.shape[1],
        ),
    )(slots, lengths, cache, *parts, *after)


def on_device(tokens, gain, w_query, w_keyval, w_gate, w_up, cache, lengths):
    size_x, size_y = lax.axis_size("gx"), lax.axis_size("gy")
    chips = size_y // 2
    me_x, me_y = lax.axis_index("gx"), lax.axis_index("gy")
    tall, _, steps, features = tokens.shape
    local = cache.shape[0]
    block = local * size_x * steps

    def shift_x(value, by):
        return lax.ppermute(value, "gx", [(i, (i + by) % size_x) for i in range(size_x)])

    def shift_y(value, by):
        return lax.ppermute(value, "gy", [(i, (i + by) % size_y) for i in range(size_y)])

    def swap(value):
        return lax.ppermute(value, "gy", [(i, i ^ 1) for i in range(size_y)])

    row = jnp.arange(2 * chips * block, dtype=jnp.int32)
    core = jnp.where(row < chips * block, 1 - me_y % 2, me_y % 2)
    chip = (me_y // 2 + 1 + row // block % chips) % chips
    sequence = (chip * 2 + core) * local + row % block // (size_x * steps)
    column = row // steps % size_x
    source = (me_x - column) % size_x * (tall * steps) + sequence * steps + row % steps
    source = source[:, None]
    row = jnp.arange(block, dtype=jnp.int32)
    to = (me_x + row // (local * steps)) % size_x
    order = row // steps % local * (size_x * steps) + to * steps + row % steps
    order = order[:, None]
    slots = (me_x - jnp.arange(size_x, dtype=jnp.int32)) % size_x

    weights = (w_gate, w_up)
    tiles = w_gate.shape[1] // TILE
    before = [tiles * share // 36 for share in (4, 5)]
    bounds = [0, sum(before)] + [tiles * share // 36 for share in (23, 31, 36)]
    ahead = [max(1, tiles * share // 36) for share in (5, 3, 3)] + [0]
    gathered = [tokens] + [shift_x(tokens, by) for by in range(1, size_x)]
    first_tiles = load(weights, 0, before[0], (source, order, slots))
    rows, stats = partial_stats(gathered, first_tiles)
    every_stat = [stats] + [shift_y(stats, by) for by in range(1, size_y)]
    second_tiles = load(weights, before[0], before[1], (stats,))
    x = normed_rows(source, gain, rows, every_stat, second_tiles)

    def chunk_sums(chunk, held, after):
        count = bounds[chunk + 1] - bounds[chunk]
        return wide_sums(x, weights, held, bounds[chunk], count, ahead[chunk], after)

    def to_chips(parts):
        return [shift_y(part, 2 * by) for by, part in enumerate(parts[: chips - 1], 1)]

    send_0, keep_0, keep_q, held = first_sums(
        x, weights, w_query, w_keyval, (first_tiles, second_tiles), ahead[0]
    )
    send_1, keep_1, held = chunk_sums(1, held, (send_0,))
    parts_0 = combine(chips, swap(send_0), keep_0, keep_q)
    from_0 = to_chips(parts_0)

    send_2, keep_2, held = chunk_sums(2, held, (parts_0[0], send_1))
    parts_1 = combine(chips, swap(send_1), keep_1)
    from_1 = to_chips(parts_1)
    turned = query_rows(order, [parts_0[-1]] + from_0, size_x)
    new = [turned[0]] + [shift_x(turned[by], by) for by in range(1, size_x)]

    send_3, keep_3 = chunk_sums(3, held, (parts_1[0], turned[0], send_2))
    parts_2 = combine(chips, swap(send_2), keep_2)
    from_2 = to_chips(parts_2)
    context = attend(
        slots,
        lengths,
        cache.reshape(local, cache.shape[2], cache.shape[3]),
        new,
        steps,
        w_query.shape[1],
        (parts_2[0], send_3, from_1[0]),
    )
    parts_3 = combine(chips, swap(send_3), keep_3)
    from_3 = to_chips(parts_3)
    half_done = gated(
        [[parts_0[chips - 1]] + from_0, [parts_1[-1]] + from_1],
        pltpu.VMEM((local, size_x, steps, bounds[2] * TILE), BF16),
        (),
        (parts_3[0],),
    )
    hidden = gated(
        [[parts_2[-1]] + from_2, [parts_3[-1]] + from_3],
        jax.ShapeDtypeStruct((local, size_x, steps, w_gate.shape[1]), BF16),
        (half_done,),
    )
    return (context, hidden)


def solution(mesh):
    return jax.shard_map(
        on_device,
        mesh=mesh,
        in_specs=(
            P("groups", "gx", None, "gy"),
            P("gy"),
            P("gy", "gx"),
            P("gy", "gx"),
            P("gy", "gx"),
            P("gy", "gx"),
            P(("groups", "gy"), "gx", None, None),
            P(("groups", "gy"), "gx"),
        ),
        out_specs=(P(("groups", "gy"), "gx", None, None), P(("groups", "gy"), None, None, "gx")),
        check_vma=False,
    )
```

time: 74.6 us -> 72.8 us (0.976)
  Pallas kernels: 42.3 us -> 45 us
  starting transfers between devices: 21.5 us -> 18.9 us
  local copies, waits for them, and re-layouts: 4.21 us -> 3.28 us
  waiting for transfers between devices: 5.3 us -> 4.44 us
    ppermute x8 -> x7, waiting for transfers between devices: 5.27 us -> 0.02 us  [shift_y(): lax.ppermute(value, 'gy', [(i, (i + by) % size_y) for i in range(size_y)])]
    ppermute x6, waiting for transfers between devices: 0.02 us -> 4.41 us  [shift_x(): lax.ppermute(value, 'gx', [(i, (i + by) % size_x) for i in range(size_x)])]
    ppermute x5 -> x4, starting transfers between devices: 2.8 us -> 0.96 us  [swap(): return lax.ppermute(value, 'gy', [(i, i ^ 1) for i in range(size_y)])]
    pallas_call x1 -> x2, Pallas kernels: 1.02 us -> 1.96 us  [gated(): pl.pallas_call(functools.partial(gated_kernel, [len(chunk) for chunk in c...]
    pallas_call x11 -> x10, Pallas kernels: 37.9 us -> 38.8 us  [the longest x3 21.1 us: wide_sums(): pl.pallas_call(functools.partial(wide_kernel, first, tiles, following, le...]
    ppermute x8 -> x7, starting transfers between devices: 7.72 us -> 7.21 us  [shift_y(): lax.ppermute(value, 'gy', [(i, (i + by) % size_y) for i in range(size_y)])]
    unnamed x14 -> x15, local copies, waits for them, and re-layouts: 3.49 us -> 3.28 us
  transfers between devices with their start and end apart: 20 -> 17, of which waited for: 2 -> 2; matrix products, arithmetic and copies ran while one was open for 1% -> 1% of each run, Pallas kernels for 53% -> 48%
where the time goes in v4:
time: 72.8 us; the launch traced here: 72.5 us
  Pallas kernels  45 us (62%)
  starting transfers between devices  18.9 us (26%)
  waiting for transfers between devices  4.44 us (6%)
  local copies, waits for them, and re-layouts  3.28 us (5%)
  between operations  0.86 us (1%)
    pallas_call x3, Pallas kernels, wide_sums(): pl.pallas_call(functools.partial(wide_kernel, first, tiles, following, le...  21.1 us
    ppermute x6, starting transfers between devices, shift_x(): lax.ppermute(value, 'gx', [(i, (i + by) % size_x) for i in range(size_x)])  10.7 us
    pallas_call x2, Pallas kernels, load(): pl.pallas_call(functools.partial(load_kernel, first, tiles), out_shape=pl...  8.57 us
    pallas_call x1, Pallas kernels, first_sums(): pl.pallas_call(functools.partial(first_kernel, len(held)), out_shape=[plt...  7.68 us
    ppermute x7, starting transfers between devices, shift_y(): lax.ppermute(value, 'gy', [(i, (i + by) % size_y) for i in range(size_y)])  7.21 us
    ppermute x6, waiting for transfers between devices, shift_x(): lax.ppermute(value, 'gx', [(i, (i + by) % size_x) for i in range(size_x)])  4.41 us
    unnamed x15, local copies, waits for them, and re-layouts  3.28 us
    pallas_call x1, Pallas kernels, attend(): pl.pallas_call(functools.partial(attend_kernel, count, steps, query_cols)...  2.66 us
  transfers between devices with their start and end apart: 17, of which 2 were waited for; matrix products, arithmetic and copies ran while one was open for 1% of the time, Pallas kernels for 48%

profile of v4, /device:TPU:0, one launch (start us, length us, event | category | flops | bytes accessed | tf_op | source)
XLA Modules:
  0.0 72.5 jit_solution(16485755477552892505)
XLA Ops:
  0.6 3.1 %collective-permute-start = (bf16[8,1,2,2304]{3,2,1,0:T(2,128)(2,1)}, bf16[8,1,2,2304]{3,2,1,0:T(2,128)(2,1)S(1)}, u32[]{:S(2)}, u32[]{:S(2)}) collective-permute-start(bf16[8,1,2,2304]{3,2,1,0:T(2,128)(2,1)} %refs_0_.1), channel_id=1, source_target_pairs={{0,4},{4,8},{8,12},{12,0},{1,5},{5,9},{9,13},{13,1},{2,6},{6,10},{... | collective-permute-start | bytes 221192 | tf_op jit(solution)/shard_map/ppermute | solution.py:475
  3.7 2.6 %collective-permute-start.1 = (bf16[8,1,2,2304]{3,2,1,0:T(2,128)(2,1)}, bf16[8,1,2,2304]{3,2,1,0:T(2,128)(2,1)S(1)}, u32[]{:S(2)}, u32[]{:S(2)}) collective-permute-start(bf16[8,1,2,2304]{3,2,1,0:T(2,128)(2,1)} %refs_0_.1), channel_id=1, source_target_pairs={{0,8},{4,12},{8,0},{12,4},{1,9},{5,13},{9,1},{13,5},{2,10},{6,14},... | collective-permute-start | bytes 221192 | tf_op jit(solution)/shard_map/ppermute | solution.py:475
  6.3 1.3 %collective-permute-start.2 = (bf16[8,1,2,2304]{3,2,1,0:T(2,128)(2,1)}, bf16[8,1,2,2304]{3,2,1,0:T(2,128)(2,1)S(1)}, u32[]{:S(2)}, u32[]{:S(2)}) collective-permute-start(bf16[8,1,2,2304]{3,2,1,0:T(2,128)(2,1)} %refs_0_.1), channel_id=1, source_target_pairs={{0,12},{4,0},{8,4},{12,8},{1,13},{5,1},{9,5},{13,9},{2,14},{6,2},{... | collective-permute-start | bytes 221192 | tf_op jit(solution)/shard_map/ppermute | solution.py:475
  7.7 0.1 fusion.18.refs_0_.source_ref
  7.8 0.0 copy-start.5
  7.8 3.9 %shard_map.95.refs_4_.refs_0_ = bf16[4,2304,512]{2,1,0:T(8,128)(2,1)S(1)} custom-call(bf16[2304,9216]{1,0:T(8,128)(2,1)} %wg_ref.11, bf16[2304,9216]{1,0:T(8,128)(2,1)} %wu_ref.11, s32[64,1]{1,0:T(8,128)S(1)} %fusion.18.refs_0_.source_ref, s32[16,1]{1,0:T(8,128)S(1)} %fusion.39.refs_1_.source_ref, s32[4]{0:T(128)S(1)} %and_select_fusion.refs_2_.slot_ref), custom_call_target="tpu_custom_call" | custom-call | bytes 9437184 | tf_op jit(solution)/shard_map/pallas_call | solution.py:219
  11.7 0.0 collective-permute-done.refs_1_
  11.7 0.0 collective-permute-done.1.refs_2_
  11.7 0.0 collective-permute-done.2.refs_3_
  11.7 0.0 copy-done.5
  11.7 0.3 shard_map.96
  12.0 0.0 copy-start.6
  12.1 0.1 collective-permute-start.3
  12.1 1.6 %collective-permute-start.4 = (f32[64,128]{1,0:T(8,128)S(1)}, f32[64,128]{1,0:T(8,128)S(1)}, u32[]{:S(2)}, u32[]{:S(2)}) collective-permute-start(f32[64,128]{1,0:T(8,128)S(1)} %get-tuple-element.30.refs_0_), channel_id=1, source_target_pairs={{0,2},{1,3},{2,0},{3,1},{4,6},{5,7},{6,4},{7,5},{8,10},{9,11},{10,... | collective-permute-start | bytes 98312 | tf_op jit(solution)/shard_map/ppermute | solution.py:478
  13.7 1.4 %collective-permute-start.5 = (f32[64,128]{1,0:T(8,128)S(1)}, f32[64,128]{1,0:T(8,128)S(1)}, u32[]{:S(2)}, u32[]{:S(2)}) collective-permute-start(f32[64,128]{1,0:T(8,128)S(1)} %get-tuple-element.30.refs_0_), channel_id=1, source_target_pairs={{0,3},{1,0},{2,1},{3,2},{4,7},{5,4},{6,5},{7,6},{8,11},{9,8},{10,9... | collective-permute-start | bytes 98312 | tf_op jit(solution)/shard_map/ppermute | solution.py:478
  15.1 4.6 %shard_map.97.refs_4_.refs_1_ = bf16[5,2304,512]{2,1,0:T(8,128)(2,1)S(1)} custom-call(bf16[2304,9216]{1,0:T(8,128)(2,1)} %wg_ref.11, bf16[2304,9216]{1,0:T(8,128)(2,1)} %wu_ref.11, f32[64,128]{1,0:T(8,128)S(1)} %get-tuple-element.30.refs_0_), custom_call_target="tpu_custom_call" | custom-call | bytes 11796480 | tf_op jit(solution)/shard_map/pallas_call | solution.py:219
  19.7 0.0 collective-permute-done.3.refs_1_
  19.8 0.0 collective-permute-done.4.refs_2_
  19.8 0.0 collective-permute-done.5.refs_3_
  19.8 0.0 copy-done.6
  19.8 0.4 shard_map.98.x_ref
  20.2 7.7 %shard_map.99 = (bf16[2,32,3968]{2,1,0:T(8,128)(2,1)S(1)}, f32[2,32,2304]{2,1,0:T(8,128)S(1)}, f32[32,1664]{1,0:T(8,128)S(1)}, bf16[5,2304,512]{2,1,0:T(8,128)(2,1)S(1)}) custom-call(bf16[64,2304]{1,0:T(8,128)(2,1)S(1)} %shard_map.98.x_ref, bf16[2304,9216]{1,0:T(8,128)(2,1)} %wg_ref.11, bf16[2304,9216]{1,0:T(8,128)(2,1)} %wu_ref.11, ...), custom_call_target="tpu_custom_call" | custom-call | flops 1849688064 | bytes 21233664 | tf_op jit(solution)/shard_map/pallas_call | solution.py:292
  27.9 0.1 collective-permute-start.6
  28.0 10.9 %shard_map.102 = (bf16[2,32,3584]{2,1,0:T(8,128)(2,1)S(1)}, f32[2,32,3584]{2,1,0:T(8,128)S(1)}, bf16[3,2304,512]{2,1,0:T(8,128)(2,1)S(1)}) custom-call(bf16[64,2304]{1,0:T(8,128)(2,1)S(1)} %shard_map.98.x_ref, bf16[2304,9216]{1,0:T(8,128)(2,1)} %wg_ref.11, bf16[2304,9216]{1,0:T(8,128)(2,1)} %wu_ref.11, bf16[5,2304,512]{2,1,0:T(8,128)(2,1)S(1)} %get-tuple-element.40.pre_ref, ...), custom_call_target="tpu_custom_call" | custom-call | flops 2113929216 | bytes 28311552 | tf_op jit(solution)/shard_map/pallas_call | solution.py:383
  38.8 0.6 collective-permute-start.12
  39.4 0.0 collective-permute-done.6.refs_0_
  39.4 0.1 shard_map.100
  39.5 0.6 collective-permute-start.7
  40.0 7.1 %shard_map.103 = (bf16[2,32,2048]{2,1,0:T(8,128)(2,1)S(1)}, f32[2,32,2048]{2,1,0:T(8,128)S(1)}, bf16[3,2304,512]{2,1,0:T(8,128)(2,1)S(1)}) custom-call(bf16[64,2304]{1,0:T(8,128)(2,1)S(1)} %shard_map.98.x_ref, bf16[2304,9216]{1,0:T(8,128)(2,1)} %wg_ref.11, bf16[2304,9216]{1,0:T(8,128)(2,1)} %wu_ref.11, bf16[3,2304,512]{2,1,0:T(8,128)(2,1)S(1)} %get-tuple-element.41.pre_ref, ...), custom_call_target="tpu_custom_call" | custom-call | flops 1207959552 | bytes 18874368 | tf_op jit(solution)/shard_map/pallas_call | solution.py:383
  47.1 0.1 collective-permute-start.11
  47.2 0.0 collective-permute-done.12.refs_0_
  47.2 0.1 shard_map.105
  47.3 1.6 %collective-permute-start.13 = (bf16[2,16,3584]{2,1,0:T(8,128)(2,1)S(1)}, bf16[2,16,3584]{2,1,0:T(8,128)(2,1)S(1)}, u32[]{:S(2)}, u32[]{:S(2)}) collective-permute-start(bf16[2,16,3584]{2,1,0:T(8,128)(2,1)S(1)} %get-tuple-element.48.refs_0_), channel_id=1, source_target_pairs={{0,2},{1,3},{2,0},{3,1},{4,6},{5,7},{6,4},{7,5},{8,10},{9,11},{10,... | collective-permute-start | bytes 688136 | tf_op jit(solution)/shard_map/ppermute | solution.py:478
  48.9 0.0 collective-permute-done.7.refs_1_
  48.9 0.8 %shard_map.101 = (bf16[4,1664]{1,0:T(4,128)(2,1)S(1)}, bf16[4,1664]{1,0:T(4,128)(2,1)}, bf16[4,1664]{1,0:T(4,128)(2,1)}, bf16[4,1664]{1,0:T(4,128)(2,1)}) custom-call(s32[16,1]{1,0:T(8,128)S(1)} %fusion.39.refs_1_.source_ref, f32[16,1664]{1,0:T(8,128)S(1)} %get-tuple-element.34.refs_0_, bf16[2,16,3968]{2,1,0:T(8,128)(2,1)S(1)} %collective-permute-done.7.refs_1_), custom_call_target="tpu_custom_call" | custom-call | flops 153600 | bytes 9600 | tf_op jit(solution)/shard_map/pallas_call | solution.py:142
  49.7 0.0 copy-start
  49.7 3.1 %shard_map.106 = (bf16[2,32,1280]{2,1,0:T(8,128)(2,1)S(1)}, f32[2,32,1280]{2,1,0:T(8,128)S(1)}) custom-call(bf16[64,2304]{1,0:T(8,128)(2,1)S(1)} %shard_map.98.x_ref, bf16[2304,9216]{1,0:T(8,128)(2,1)} %wg_ref.11, bf16[2304,9216]{1,0:T(8,128)(2,1)} %wu_ref.11, bf16[3,2304,512]{2,1,0:T(8,128)(2,1)S(1)} %get-tuple-element.46.pre_ref, ...), custom_call_target="tpu_custom_call" | custom-call | flops 754974720 | bytes 4718592 | tf_op jit(solution)/shard_map/pallas_call | solution.py:383
  52.9 0.3 collective-permute-start.14
  53.1 0.0 collective-permute-done.11.refs_0_
  53.1 0.7 shard_map.104
  53.8 0.0 copy-start.1
  53.8 0.5 collective-permute-start.15
  54.3 0.0 collective-permute-done.14.refs_0_
  54.3 0.7 shard_map.108
  55.0 0.7 copy-done.3
  55.6 1.5 %collective-permute-start.16 = (bf16[2,16,1280]{2,1,0:T(8,128)(2,1)}, bf16[2,16,1280]{2,1,0:T(8,128)(2,1)}, u32[]{:S(2)}, u32[]{:S(2)}) collective-permute-start(bf16[2,16,1280]{2,1,0:T(8,128)(2,1)} %get-tuple-element.53.refs_4_), channel_id=1, source_target_pairs={{0,2},{1,3},{2,0},{3,1},{4,6},{5,7},{6,4},{7,5},{8,10},{9,11},{10,... | collective-permute-start | bytes 245768 | tf_op jit(solution)/shard_map/ppermute | solution.py:478
  57.2 3.1 %collective-permute-start.10 = (bf16[4,1664]{1,0:T(4,128)(2,1)}, bf16[4,1664]{1,0:T(4,128)(2,1)S(1)}, u32[]{:S(2)}, u32[]{:S(2)}) collective-permute-start(bf16[4,1664]{1,0:T(4,128)(2,1)} %get-tuple-element.39), channel_id=1, source_target_pairs={{0,12},{4,0},{8,4},{12,8},{1,13},{5,1},{9,5},{13,9},{2,14},{6,2},{... | collective-permute-start | bytes 39944 | tf_op jit(solution)/shard_map/ppermute | solution.py:475
  60.3 0.0 collective-permute-start.8
  60.3 0.0 collective-permute-done.13.refs_6_.refs_3_
  60.3 0.0 copy-done.1
  60.3 0.6 collective-permute-start.9
  60.9 0.7 %copy.10.lengths_ref = s32[2,1]{1,0:T(2,128)S(1)} copy(s32[2,1]{0,1:T(1,128)} %param.15) | data formatting | bytes 16 | tf_op args[7]
  61.6 0.3 collective-permute-done.10.refs_3_
  61.9 4.1 %collective-permute-done.8.refs_1_ = bf16[4,1664]{1,0:T(4,128)(2,1)S(1)} collective-permute-done((bf16[4,1664]{1,0:T(4,128)(2,1)}, bf16[4,1664]{1,0:T(4,128)(2,1)S(1)}, u32[]{:S(2)}, u32[]{:S(2)}) %collective-permute-start.8) | collective-permute-done | bytes 13344 | tf_op jit(solution)/shard_map/ppermute | solution.py:475
  66.0 0.0 collective-permute-done.9.refs_2_
  66.0 0.0 copy-done
  66.0 2.7 %shard_map.107 = bf16[2,1,2,6144]{3,2,1,0:T(2,128)(2,1)} custom-call(s32[4]{0:T(128)S(1)} %and_select_fusion.refs_2_.slot_ref, s32[2,1]{1,0:T(2,128)S(1)} %copy.10.lengths_ref, bf16[2,1024,512]{2,1,0:T(8,128)(2,1)S(1)} %bitcast.1, bf16[4,1664]{1,0:T(4,128)(2,1)S(1)} %get-tuple-element.36.refs_1_.refs_0_, bf16[4,1664]{1,0:T(4,128)(2,1)S(1)} %collective-permute-done.8.refs_1_, ...), custom_call_target="tpu_custom_call" | custom-call | flops 100663296 | bytes 2097152 | tf_op jit(solution)/shard_map/pallas_call | solution.py:448
  68.7 0.2 shard_map.109.refs_0_
  68.9 0.0 collective-permute-done.15.refs_2_
  68.9 0.0 collective-permute-done.16.refs_4_
  68.9 0.0 copy-start.2
  68.9 0.9 %copy-done.2 = f32[2,16,2048]{2,1,0:T(8,128)S(1)} copy-done((f32[2,16,2048]{2,1,0:T(8,128)S(1)}, f32[2,16,2048]{2,1,0:T(8,128)}, u32[]{:S(2)}) %copy-start.2) | copy-done | bytes 262168
  69.8 0.9 %copy-done.4 = f32[2,16,1280]{2,1,0:T(8,128)S(1)} copy-done((f32[2,16,1280]{2,1,0:T(8,128)S(1)}, f32[2,16,1280]{2,1,0:T(8,128)}, u32[]{:S(2)}) %copy-start.4) | copy-done | bytes 163864
  70.8 1.8 %shard_map.110 = bf16[2,4,2,9216]{3,2,1,0:T(2,128)(2,1)} custom-call(bf16[2,4,2,5888]{3,2,1,0:T(2,128)(2,1)S(1)} %shard_map.109.refs_0_, f32[2,16,2048]{2,1,0:T(8,128)S(1)} %copy-done.2, bf16[2,16,2048]{2,1,0:T(8,128)(2,1)} %collective-permute-done.15.refs_2_, f32[2,16,1280]{2,1,0:T(8,128)S(1)} %copy-done.4, bf16[2,16,1280]{2,1,0:T(8,128)(2,1)} %collective-permute-done.16.refs_4_), custom_call_target="tpu_custom_call" | custom-call | flops 307200 | bytes 19200 | tf_op jit(solution)/shard_map/pallas_call | solution.py:175
  (4 shorter events, 0.0 us)
Async XLA Ops:
  0.6 11.1 %collective-permute-start = (bf16[8,1,2,2304]{3,2,1,0:T(2,128)(2,1)}, bf16[8,1,2,2304]{3,2,1,0:T(2,128)(2,1)S(1)}, u32[]{:S(2)}, u32[]{:S(2)}) collective-permute-start(bf16[8,1,2,2304]{3,2,1,0:T(2,128)(2,1)} %refs_0_.1), channel_id=1, source_target_pairs={{0,4},{4,8},{8,12},{12,0},{1,5},{5,9},{9,13},{13,1},{2,6},{6,10},{... | collective-permute-start | bytes 221192 | tf_op jit(solution)/shard_map/ppermute | solution.py:475
  3.7 8.0 %collective-permute-start.1 = (bf16[8,1,2,2304]{3,2,1,0:T(2,128)(2,1)}, bf16[8,1,2,2304]{3,2,1,0:T(2,128)(2,1)S(1)}, u32[]{:S(2)}, u32[]{:S(2)}) collective-permute-start(bf16[8,1,2,2304]{3,2,1,0:T(2,128)(2,1)} %refs_0_.1), channel_id=1, source_target_pairs={{0,8},{4,12},{8,0},{12,4},{1,9},{5,13},{9,1},{13,5},{2,10},{6,14},... | collective-permute-start | bytes 221192 | tf_op jit(solution)/shard_map/ppermute | solution.py:475
  6.3 5.4 %collective-permute-start.2 = (bf16[8,1,2,2304]{3,2,1,0:T(2,128)(2,1)}, bf16[8,1,2,2304]{3,2,1,0:T(2,128)(2,1)S(1)}, u32[]{:S(2)}, u32[]{:S(2)}) collective-permute-start(bf16[8,1,2,2304]{3,2,1,0:T(2,128)(2,1)} %refs_0_.1), channel_id=1, source_target_pairs={{0,12},{4,0},{8,4},{12,8},{1,13},{5,1},{9,5},{13,9},{2,14},{6,2},{... | collective-permute-start | bytes 221192 | tf_op jit(solution)/shard_map/ppermute | solution.py:475
  7.8 4.0 %copy-start.5 = (bf16[8,1,2,2304]{3,2,1,0:T(2,128)(2,1)S(1)}, bf16[8,1,2,2304]{3,2,1,0:T(2,128)(2,1)}, u32[]{:S(2)}) copy-start(bf16[8,1,2,2304]{3,2,1,0:T(2,128)(2,1)} %refs_0_.1) | copy-start | bytes 221188
  12.0 7.7 %copy-start.6 = (f32[2304]{0:T(1024)S(1)}, f32[2304]{0:T(1024)}, u32[]{:S(2)}) copy-start(f32[2304]{0:T(1024)} %gain_ref.1) | copy-start | bytes 27652
  12.1 7.7 %collective-permute-start.3 = (f32[64,128]{1,0:T(8,128)S(1)}, f32[64,128]{1,0:T(8,128)S(1)}, u32[]{:S(2)}, u32[]{:S(2)}) collective-permute-start(f32[64,128]{1,0:T(8,128)S(1)} %get-tuple-element.30.refs_0_), channel_id=1, source_target_pairs={{0,1},{1,2},{2,3},{3,0},{4,5},{5,6},{6,7},{7,4},{8,9},{9,10},{10,1... | collective-permute-start | bytes 98312 | tf_op jit(solution)/shard_map/ppermute | solution.py:478
  12.1 7.6 %collective-permute-start.4 = (f32[64,128]{1,0:T(8,128)S(1)}, f32[64,128]{1,0:T(8,128)S(1)}, u32[]{:S(2)}, u32[]{:S(2)}) collective-permute-start(f32[64,128]{1,0:T(8,128)S(1)} %get-tuple-element.30.refs_0_), channel_id=1, source_target_pairs={{0,2},{1,3},{2,0},{3,1},{4,6},{5,7},{6,4},{7,5},{8,10},{9,11},{10,... | collective-permute-start | bytes 98312 | tf_op jit(solution)/shard_map/ppermute | solution.py:478
  13.7 6.1 %collective-permute-start.5 = (f32[64,128]{1,0:T(8,128)S(1)}, f32[64,128]{1,0:T(8,128)S(1)}, u32[]{:S(2)}, u32[]{:S(2)}) collective-permute-start(f32[64,128]{1,0:T(8,128)S(1)} %get-tuple-element.30.refs_0_), channel_id=1, source_target_pairs={{0,3},{1,0},{2,1},{3,2},{4,7},{5,4},{6,5},{7,6},{8,11},{9,8},{10,9... | collective-permute-start | bytes 98312 | tf_op jit(solution)/shard_map/ppermute | solution.py:478
  27.9 11.5 %collective-permute-start.6 = (bf16[2,32,3968]{2,1,0:T(8,128)(2,1)S(1)}, bf16[2,32,3968]{2,1,0:T(8,128)(2,1)S(1)}, u32[]{:S(2)}, u32[]{:S(2)}) collective-permute-start(bf16[2,32,3968]{2,1,0:T(8,128)(2,1)S(1)} %get-tuple-element.31.refs_0_), channel_id=1, source_target_pairs={{0,1},{1,0},{2,3},{3,2},{4,5},{5,4},{6,7},{7,6},{8,9},{9,8},{10,11... | collective-permute-start | bytes 1523720 | tf_op jit(solution)/shard_map/ppermute | solution.py:481
  38.8 8.4 %collective-permute-start.12 = (bf16[2,32,3584]{2,1,0:T(8,128)(2,1)S(1)}, bf16[2,32,3584]{2,1,0:T(8,128)(2,1)S(1)}, u32[]{:S(2)}, u32[]{:S(2)}) collective-permute-start(bf16[2,32,3584]{2,1,0:T(8,128)(2,1)S(1)} %get-tuple-element.42.refs_1_), channel_id=1, source_target_pairs={{0,1},{1,0},{2,3},{3,2},{4,5},{5,4},{6,7},{7,6},{8,9},{9,8},{10,11... | collective-permute-start | bytes 1376264 | tf_op jit(solution)/shard_map/ppermute | solution.py:481
  39.5 9.4 %collective-permute-start.7 = (bf16[2,16,3968]{2,1,0:T(8,128)(2,1)S(1)}, bf16[2,16,3968]{2,1,0:T(8,128)(2,1)S(1)}, u32[]{:S(2)}, u32[]{:S(2)}) collective-permute-start(bf16[2,16,3968]{2,1,0:T(8,128)(2,1)S(1)} %get-tuple-element.35.refs_0_), channel_id=1, source_target_pairs={{0,2},{1,3},{2,0},{3,1},{4,6},{5,7},{6,4},{7,5},{8,10},{9,11},{10,... | collective-permute-start | bytes 761864 | tf_op jit(solution)/shard_map/ppermute | solution.py:478
  47.1 6.0 %collective-permute-start.11 = (bf16[2,32,2048]{2,1,0:T(8,128)(2,1)S(1)}, bf16[2,32,2048]{2,1,0:T(8,128)(2,1)S(1)}, u32[]{:S(2)}, u32[]{:S(2)}) collective-permute-start(bf16[2,32,2048]{2,1,0:T(8,128)(2,1)S(1)} %get-tuple-element.43.refs_2_), channel_id=1, source_target_pairs={{0,1},{1,0},{2,3},{3,2},{4,5},{5,4},{6,7},{7,6},{8,9},{9,8},{10,11... | collective-permute-start | bytes 786440 | tf_op jit(solution)/shard_map/ppermute | solution.py:481
  47.3 13.0 %collective-permute-start.13 = (bf16[2,16,3584]{2,1,0:T(8,128)(2,1)S(1)}, bf16[2,16,3584]{2,1,0:T(8,128)(2,1)S(1)}, u32[]{:S(2)}, u32[]{:S(2)}) collective-permute-start(bf16[2,16,3584]{2,1,0:T(8,128)(2,1)S(1)} %get-tuple-element.48.refs_0_), channel_id=1, source_target_pairs={{0,2},{1,3},{2,0},{3,1},{4,6},{5,7},{6,4},{7,5},{8,10},{9,11},{10,... | collective-permute-start | bytes 688136 | tf_op jit(solution)/shard_map/ppermute | solution.py:478
  49.7 16.3 %copy-start = (bf16[2,1,1024,512]{3,2,1,0:T(8,128)(2,1)S(1)}, bf16[2,1,1024,512]{3,2,1,0:T(8,128)(2,1)}, u32[]{:S(2)}) copy-start(bf16[2,1,1024,512]{3,2,1,0:T(8,128)(2,1)} %param.14) | copy-start | bytes 6291460
  52.9 1.5 %collective-permute-start.14 = (bf16[2,32,1280]{2,1,0:T(8,128)(2,1)S(1)}, bf16[2,32,1280]{2,1,0:T(8,128)(2,1)S(1)}, u32[]{:S(2)}, u32[]{:S(2)}) collective-permute-start(bf16[2,32,1280]{2,1,0:T(8,128)(2,1)S(1)} %get-tuple-element.49.refs_5_), channel_id=1, source_target_pairs={{0,1},{1,0},{2,3},{3,2},{4,5},{5,4},{6,7},{7,6},{8,9},{9,8},{10,11... | collective-permute-start | bytes 491528 | tf_op jit(solution)/shard_map/ppermute | solution.py:481
  53.8 6.5 %copy-start.1 = (f32[2,16,2048]{2,1,0:T(8,128)}, f32[2,16,2048]{2,1,0:T(8,128)S(1)}, u32[]{:S(2)}) copy-start(f32[2,16,2048]{2,1,0:T(8,128)S(1)} %get-tuple-element.54.refs_1_) | copy-start | bytes 786436
  53.8 15.0 %collective-permute-start.15 = (bf16[2,16,2048]{2,1,0:T(8,128)(2,1)}, bf16[2,16,2048]{2,1,0:T(8,128)(2,1)}, u32[]{:S(2)}, u32[]{:S(2)}) collective-permute-start(bf16[2,16,2048]{2,1,0:T(8,128)(2,1)} %get-tuple-element.45.refs_4_), channel_id=1, source_target_pairs={{0,2},{1,3},{2,0},{3,1},{4,6},{5,7},{6,4},{7,5},{8,10},{9,11},{10,... | collective-permute-start | bytes 393224 | tf_op jit(solution)/shard_map/ppermute | solution.py:478
  55.0 0.7 copy-start.3
  55.6 13.2 %collective-permute-start.16 = (bf16[2,16,1280]{2,1,0:T(8,128)(2,1)}, bf16[2,16,1280]{2,1,0:T(8,128)(2,1)}, u32[]{:S(2)}, u32[]{:S(2)}) collective-permute-start(bf16[2,16,1280]{2,1,0:T(8,128)(2,1)} %get-tuple-element.53.refs_4_), channel_id=1, source_target_pairs={{0,2},{1,3},{2,0},{3,1},{4,6},{5,7},{6,4},{7,5},{8,10},{9,11},{10,... | collective-permute-start | bytes 245768 | tf_op jit(solution)/shard_map/ppermute | solution.py:478
  57.2 4.8 %collective-permute-start.10 = (bf16[4,1664]{1,0:T(4,128)(2,1)}, bf16[4,1664]{1,0:T(4,128)(2,1)S(1)}, u32[]{:S(2)}, u32[]{:S(2)}) collective-permute-start(bf16[4,1664]{1,0:T(4,128)(2,1)} %get-tuple-element.39), channel_id=1, source_target_pairs={{0,12},{4,0},{8,4},{12,8},{1,13},{5,1},{9,5},{13,9},{2,14},{6,2},{... | collective-permute-start | bytes 39944 | tf_op jit(solution)/shard_map/ppermute | solution.py:475
  60.3 5.7 %collective-permute-start.8 = (bf16[4,1664]{1,0:T(4,128)(2,1)}, bf16[4,1664]{1,0:T(4,128)(2,1)S(1)}, u32[]{:S(2)}, u32[]{:S(2)}) collective-permute-start(bf16[4,1664]{1,0:T(4,128)(2,1)} %get-tuple-element.37), channel_id=1, source_target_pairs={{0,4},{4,8},{8,12},{12,0},{1,5},{5,9},{9,13},{13,1},{2,6},{6,10},{... | collective-permute-start | bytes 39944 | tf_op jit(solution)/shard_map/ppermute | solution.py:475
  60.3 5.7 %collective-permute-start.9 = (bf16[4,1664]{1,0:T(4,128)(2,1)}, bf16[4,1664]{1,0:T(4,128)(2,1)}, u32[]{:S(2)}, u32[]{:S(2)}) collective-permute-start(bf16[4,1664]{1,0:T(4,128)(2,1)} %get-tuple-element.38), channel_id=1, source_target_pairs={{0,8},{4,12},{8,0},{12,4},{1,9},{5,13},{9,1},{13,5},{2,10},{6,14},... | collective-permute-start | bytes 39944 | tf_op jit(solution)/shard_map/ppermute | solution.py:475
  68.9 1.0 %copy-start.2 = (f32[2,16,2048]{2,1,0:T(8,128)S(1)}, f32[2,16,2048]{2,1,0:T(8,128)}, u32[]{:S(2)}) copy-start(f32[2,16,2048]{2,1,0:T(8,128)} %copy-done.1) | copy-start | bytes 786436
  69.8 0.9 %copy-start.4 = (f32[2,16,1280]{2,1,0:T(8,128)S(1)}, f32[2,16,1280]{2,1,0:T(8,128)}, u32[]{:S(2)}) copy-start(f32[2,16,1280]{2,1,0:T(8,128)} %copy-done.3) | copy-start | bytes 491524

commit v5 on v4

--- a/solution.py
+++ b/solution.py
@@ -14,7 +14,8 @@
 MASKED = -1e30
 MIB = 1024 * 1024
 TILE = 256
-DEPTH = 3
+DEPTH = 6
+WIDE = 15
 F32 = jnp.float32
 BF16 = jnp.bfloat16
 
@@ -28,8 +29,8 @@
     return pl.CostEstimate(flops=size, bytes_accessed=size // 16, transcendentals=0)
 
 
-def params():
-    return pltpu.CompilerParams(vmem_limit_bytes=9 * MIB)
+def params(mib=9):
+    return pltpu.CompilerParams(vmem_limit_bytes=mib * MIB)
 
 
 def stats_kernel(count, *refs):
@@ -85,9 +86,9 @@
     )(source, gain, rows, *stats, after)
 
 
-def combine_kernel(chips, small, *refs):
+def combine_kernel(chips, small, skip, *refs):
     sent_ref, keep_ref = refs[:2]
-    out_refs = refs[3 if small else 2 :]
+    out_refs = refs[skip:]
     cols = keep_ref.shape[2]
     block = keep_ref.shape[1] // chips
     for index in range(chips):
@@ -103,7 +104,7 @@
                 store_split(out_refs[index], slice(cols, cols + small), total)
 
 
-def combine(chips, sent, keep, keep_q=None):
+def combine(chips, sent, keep, keep_q=None, carry=None, after=()):
     small = 0 if keep_q is None else keep_q.shape[1]
     block = keep.shape[1] // chips
     out_shape = [pltpu.VMEM((2, block, sent.shape[2]), BF16)] * (chips - 1)
@@ -111,14 +112,24 @@
     if small:
         out_shape.append(pltpu.VMEM((block, small), F32))
     args = (sent, keep, keep_q) if small else (sent, keep)
-    return pl.pallas_call(
-        functools.partial(combine_kernel, chips, small),
+    extra = [*after] if carry is None else [*after, *in_vmem((carry,))]
+    out_specs = [whole()] * len(out_shape)
+    aliases = {}
+    if carry is not None:
+        aliases = {len(args) + len(after): len(out_shape)}
+        out_shape.append(pltpu.VMEM(carry.shape, carry.dtype))
+        out_specs.append(whole())
+    return pl.pallas_call(
+        functools.partial(combine_kernel, chips, small, len(args) + len(extra)),
         out_shape=out_shape,
-        in_specs=[whole()] * len(args),
-        out_specs=[whole()] * len(out_shape),
+        in_specs=[whole()] * len(args)
+        + [whole(pl.ANY)] * len(after)
+        + [whole()] * (len(extra) - len(after)),
+        out_specs=out_specs,
+        input_output_aliases=aliases,
         compiler_params=params(),
         cost_estimate=cost_of(*args),
-    )(*args)
+    )(*args, *extra)
 
 
 def query_rows_kernel(count, source_ref, *refs):
@@ -265,12 +276,8 @@
             copy.start()
     done = 0
     for ref in pre_refs:
-
-        def from_held(index, carry, ref=ref, done=done):
+        for index in range(ref.shape[0]):
             multiply(x_ref, ref.at[index], done + index, send_ref, keep_ref)
-            return carry
-
-        lax.fori_loop(0, ref.shape[0], from_held, 0)
         done += ref.shape[0]
     taken = 0
     for copy, ref in zip(smalls, (q_ref, kv_ref)):
@@ -335,15 +342,12 @@
     early = min(depth, streamed)
     for index in range(early):
         start(fetch(index))
-    early_next = min(following, depth - early)
+    early_next = min(following, DEPTH - early)
     for index in range(early_next):
         start(fetch_next(index))
 
-    def from_held(index, carry):
+    for index in range(held):
         multiply(x_ref, pre_ref.at[index], index, send_ref, keep_ref)
-        return carry
-
-    lax.fori_loop(0, held, from_held, 0)
 
     def from_ring(index, carry):
         for copy in fetch(index):
@@ -391,7 +395,7 @@
             pltpu.SemaphoreType.DMA((depth, 2)),
             pltpu.SemaphoreType.DMA((max(following, 1), 2)),
         ],
-        compiler_params=params(),
+        compiler_params=params(WIDE),
         cost_estimate=pl.CostEstimate(
             flops=4 * rows * features * cols,
             bytes_accessed=4 * features * TILE * (streamed + following),
@@ -423,7 +427,7 @@
             queries, cache_ref[b, :, :HD], dims, preferred_element_type=F32
         ) * scale
         position = lax.broadcasted_iota(jnp.int32, old.shape, 1)
-        old = jnp.where(position < lengths_ref[b, 0], old, MASKED)
+        old = jnp.where(position < lengths_ref[b], old, MASKED)
         new = lax.dot_general(queries, pairs[:, :HD], dims, preferred_element_type=F32) * scale
         step = lax.broadcasted_iota(jnp.int32, new.shape, 0) % steps
         new = jnp.where(lax.broadcasted_iota(jnp.int32, new.shape, 1) <= step, new, MASKED)
@@ -496,8 +500,8 @@
     weights = (w_gate, w_up)
     tiles = w_gate.shape[1] // TILE
     before = [tiles * share // 36 for share in (4, 5)]
-    bounds = [0, sum(before)] + [tiles * share // 36 for share in (23, 31, 36)]
-    ahead = [max(1, tiles * share // 36) for share in (5, 3, 3)] + [0]
+    bounds = [0, sum(before)] + [tiles * share // 36 for share in (21, 30, 36)]
+    ahead = [max(1, tiles * share // 36) for share in (5, 4, 4)] + [0]
     gathered = [tokens] + [shift_x(tokens, by) for by in range(1, size_x)]
     first_tiles = load(weights, 0, before[0], (source, order, slots))
     rows, stats = partial_stats(gathered, first_tiles)
@@ -526,16 +530,16 @@
     new = [turned[0]] + [shift_x(turned[by], by) for by in range(1, size_x)]
 
     send_3, keep_3 = chunk_sums(3, held, (parts_1[0], turned[0], send_2))
-    parts_2 = combine(chips, swap(send_2), keep_2)
+    *parts_2, send_3 = combine(chips, swap(send_2), keep_2, None, send_3, (*new[1:], from_1[0]))
     from_2 = to_chips(parts_2)
     context = attend(
         slots,
-        lengths,
+        lengths.reshape(local),
         cache.reshape(local, cache.shape[2], cache.shape[3]),
         new,
         steps,
         w_query.shape[1],
-        (parts_2[0], send_3, from_1[0]),
+        (parts_2[0], send_3),
     )
     parts_3 = combine(chips, swap(send_3), keep_3)
     from_3 = to_chips(parts_3)

time: 72.8 us -> 72 us (0.989)
  local copies, waits for them, and re-layouts: 3.28 us -> 0.02 us
  Pallas kernels: 45 us -> 46.6 us
  starting transfers between devices: 18.9 us -> 20.1 us
    ppermute x6, waiting for transfers between devices: 4.41 us -> 0.02 us  [shift_x(): lax.ppermute(value, 'gx', [(i, (i + by) % size_x) for i in range(size_x)])]
    pallas_call x1, Pallas kernels: 7.68 us -> 11.3 us  [first_sums(): pl.pallas_call(functools.partial(first_kernel, len(held)), out_shape=[plt...]
    ppermute x7, waiting for transfers between devices: 0.02 us -> 3.48 us  [shift_y(): lax.ppermute(value, 'gy', [(i, (i + by) % size_y) for i in range(size_y)])]
    unnamed x15 -> x8, local copies, waits for them, and re-layouts: 3.28 us -> 0.02 us
    ppermute x6, starting transfers between devices: 10.7 us -> 13.6 us  [shift_x(): lax.ppermute(value, 'gx', [(i, (i + by) % size_x) for i in range(size_x)])]
    ppermute x7, starting transfers between devices: 7.21 us -> 5.52 us  [shift_y(): lax.ppermute(value, 'gy', [(i, (i + by) % size_y) for i in range(size_y)])]
    pallas_call x4, Pallas kernels: 1.53 us -> 0.25 us  [combine(): pl.pallas_call(functools.partial(combine_kernel, chips, small, len(args)...]
    pallas_call x3, Pallas kernels: 21.1 us -> 22.1 us  [wide_sums(): pl.pallas_call(functools.partial(wide_kernel, first, tiles, following, le...]
  transfers between devices with their start and end apart: 17 -> 17, of which waited for: 2 -> 3; matrix products, arithmetic and copies ran while one was open for 1% -> 0% of each run, Pallas kernels for 48% -> 47%
where the time goes in v5:
time: 72 us; the launch traced here: 71.8 us
  Pallas kernels  46.6 us (65%)
  starting transfers between devices  20.1 us (28%)
  waiting for transfers between devices  4.16 us (6%)
  between operations  0.88 us (1%)
    pallas_call x3, Pallas kernels, wide_sums(): pl.pallas_call(functools.partial(wide_kernel, first, tiles, following, le...  22.1 us
    ppermute x6, starting transfers between devices, shift_x(): lax.ppermute(value, 'gx', [(i, (i + by) % size_x) for i in range(size_x)])  13.6 us
    pallas_call x1, Pallas kernels, first_sums(): pl.pallas_call(functools.partial(first_kernel, len(held)), out_shape=[plt...  11.3 us
    pallas_call x2, Pallas kernels, load(): pl.pallas_call(functools.partial(load_kernel, first, tiles), out_shape=pl...  8.57 us
    ppermute x7, starting transfers between devices, shift_y(): lax.ppermute(value, 'gy', [(i, (i + by) % size_y) for i in range(size_y)])  5.52 us
    ppermute x7, waiting for transfers between devices, shift_y(): lax.ppermute(value, 'gy', [(i, (i + by) % size_y) for i in range(size_y)])  3.48 us
    pallas_call x1, Pallas kernels, attend(): pl.pallas_call(functools.partial(attend_kernel, count, steps, query_cols)...  2.47 us
  transfers between devices with their start and end apart: 17, of which 3 were waited for; matrix products, arithmetic and copies ran while one was open for 0% of the time, Pallas kernels for 47%

profile of v5, /device:TPU:0, one launch (start us, length us, event | category | flops | bytes accessed | tf_op | source)
XLA Modules:
  0.0 71.8 jit_solution(5642038360484592878)
XLA Ops:
  0.6 4.1 %collective-permute-start.1 = (bf16[8,1,2,2304]{3,2,1,0:T(2,128)(2,1)}, bf16[8,1,2,2304]{3,2,1,0:T(2,128)(2,1)S(1)}, u32[]{:S(2)}, u32[]{:S(2)}) collective-permute-start(bf16[8,1,2,2304]{3,2,1,0:T(2,128)(2,1)} %refs_0_.1), channel_id=1, source_target_pairs={{0,8},{4,12},{8,0},{12,4},{1,9},{5,13},{9,1},{13,5},{2,10},{6,14},... | collective-permute-start | bytes 221192 | tf_op jit(solution)/shard_map/ppermute | solution.py:479
  4.7 1.6 %collective-permute-start = (bf16[8,1,2,2304]{3,2,1,0:T(2,128)(2,1)}, bf16[8,1,2,2304]{3,2,1,0:T(2,128)(2,1)S(1)}, u32[]{:S(2)}, u32[]{:S(2)}) collective-permute-start(bf16[8,1,2,2304]{3,2,1,0:T(2,128)(2,1)} %refs_0_.1), channel_id=1, source_target_pairs={{0,4},{4,8},{8,12},{12,0},{1,5},{5,9},{9,13},{13,1},{2,6},{6,10},{... | collective-permute-start | bytes 221192 | tf_op jit(solution)/shard_map/ppermute | solution.py:479
  6.3 2.2 %collective-permute-start.2 = (bf16[8,1,2,2304]{3,2,1,0:T(2,128)(2,1)}, bf16[8,1,2,2304]{3,2,1,0:T(2,128)(2,1)S(1)}, u32[]{:S(2)}, u32[]{:S(2)}) collective-permute-start(bf16[8,1,2,2304]{3,2,1,0:T(2,128)(2,1)} %refs_0_.1), channel_id=1, source_target_pairs={{0,12},{4,0},{8,4},{12,8},{1,13},{5,1},{9,5},{13,9},{2,14},{6,2},{... | collective-permute-start | bytes 221192 | tf_op jit(solution)/shard_map/ppermute | solution.py:479
  8.6 0.1 fusion.18.refs_0_.source_ref
  8.7 0.0 copy-start.1
  8.7 3.9 %shard_map.95.refs_4_.refs_0_ = bf16[4,2304,512]{2,1,0:T(8,128)(2,1)S(1)} custom-call(bf16[2304,9216]{1,0:T(8,128)(2,1)} %wg_ref.11, bf16[2304,9216]{1,0:T(8,128)(2,1)} %wu_ref.11, s32[64,1]{1,0:T(8,128)S(1)} %fusion.18.refs_0_.source_ref, s32[16,1]{1,0:T(8,128)S(1)} %fusion.39.refs_1_.source_ref, s32[4]{0:T(128)S(1)} %and_select_fusion.refs_2_.slot_ref), custom_call_target="tpu_custom_call" | custom-call | bytes 9437184 | tf_op jit(solution)/shard_map/pallas_call | solution.py:230
  12.6 0.0 collective-permute-done.1.refs_2_
  12.6 0.0 collective-permute-done.refs_1_
  12.6 0.0 collective-permute-done.2.refs_3_
  12.6 0.0 copy-done.1
  12.7 0.3 shard_map.96
  13.0 0.0 copy-start.2
  13.0 0.2 collective-permute-start.5
  13.1 1.5 %collective-permute-start.4 = (f32[64,128]{1,0:T(8,128)S(1)}, f32[64,128]{1,0:T(8,128)S(1)}, u32[]{:S(2)}, u32[]{:S(2)}) collective-permute-start(f32[64,128]{1,0:T(8,128)S(1)} %get-tuple-element.31.refs_0_), channel_id=1, source_target_pairs={{0,2},{1,3},{2,0},{3,1},{4,6},{5,7},{6,4},{7,5},{8,10},{9,11},{10,... | collective-permute-start | bytes 98312 | tf_op jit(solution)/shard_map/ppermute | solution.py:482
  14.6 0.2 collective-permute-start.3
  14.8 4.6 %shard_map.97.refs_4_.refs_1_ = bf16[5,2304,512]{2,1,0:T(8,128)(2,1)S(1)} custom-call(bf16[2304,9216]{1,0:T(8,128)(2,1)} %wg_ref.11, bf16[2304,9216]{1,0:T(8,128)(2,1)} %wu_ref.11, f32[64,128]{1,0:T(8,128)S(1)} %get-tuple-element.31.refs_0_), custom_call_target="tpu_custom_call" | custom-call | bytes 11796480 | tf_op jit(solution)/shard_map/pallas_call | solution.py:230
  19.4 0.0 collective-permute-done.5.refs_3_
  19.4 0.0 collective-permute-done.4.refs_2_
  19.5 0.0 collective-permute-done.3.refs_1_
  19.5 0.0 copy-done.2
  19.5 0.4 shard_map.98.x_ref
  19.9 11.3 %shard_map.99 = (bf16[2,32,3968]{2,1,0:T(8,128)(2,1)S(1)}, f32[2,32,2304]{2,1,0:T(8,128)S(1)}, f32[32,1664]{1,0:T(8,128)S(1)}, bf16[5,2304,512]{2,1,0:T(8,128)(2,1)S(1)}) custom-call(bf16[64,2304]{1,0:T(8,128)(2,1)S(1)} %shard_map.98.x_ref, bf16[2304,9216]{1,0:T(8,128)(2,1)} %wg_ref.11, bf16[2304,9216]{1,0:T(8,128)(2,1)} %wu_ref.11, ...), custom_call_target="tpu_custom_call" | custom-call | flops 1849688064 | bytes 21233664 | tf_op jit(solution)/shard_map/pallas_call | solution.py:299
  31.1 0.6 collective-permute-start.6
  31.7 10.4 %shard_map.102 = (bf16[2,32,3072]{2,1,0:T(8,128)(2,1)S(1)}, f32[2,32,3072]{2,1,0:T(8,128)S(1)}, bf16[4,2304,512]{2,1,0:T(8,128)(2,1)S(1)}) custom-call(bf16[64,2304]{1,0:T(8,128)(2,1)S(1)} %shard_map.98.x_ref, bf16[2304,9216]{1,0:T(8,128)(2,1)} %wg_ref.11, bf16[2304,9216]{1,0:T(8,128)(2,1)} %wu_ref.11, bf16[5,2304,512]{2,1,0:T(8,128)(2,1)S(1)} %get-tuple-element.41.pre_ref, ...), custom_call_target="tpu_custom_call" | custom-call | flops 1811939328 | bytes 25952256 | tf_op jit(solution)/shard_map/pallas_call | solution.py:387
  42.1 0.1 collective-permute-start.12
  42.2 0.0 collective-permute-done.6.refs_0_
  42.2 0.1 shard_map.100
  42.3 1.5 %collective-permute-start.7 = (bf16[2,16,3968]{2,1,0:T(8,128)(2,1)S(1)}, bf16[2,16,3968]{2,1,0:T(8,128)(2,1)S(1)}, u32[]{:S(2)}, u32[]{:S(2)}) collective-permute-start(bf16[2,16,3968]{2,1,0:T(8,128)(2,1)S(1)} %get-tuple-element.36.refs_0_), channel_id=1, source_target_pairs={{0,2},{1,3},{2,0},{3,1},{4,6},{5,7},{6,4},{7,5},{8,10},{9,11},{10,... | collective-permute-start | bytes 761864 | tf_op jit(solution)/shard_map/ppermute | solution.py:482
  43.8 8.6 %shard_map.103 = (bf16[2,32,2304]{2,1,0:T(8,128)(2,1)S(1)}, f32[2,32,2304]{2,1,0:T(8,128)S(1)}, bf16[4,2304,512]{2,1,0:T(8,128)(2,1)S(1)}) custom-call(bf16[64,2304]{1,0:T(8,128)(2,1)S(1)} %shard_map.98.x_ref, bf16[2304,9216]{1,0:T(8,128)(2,1)} %wg_ref.11, bf16[2304,9216]{1,0:T(8,128)(2,1)} %wu_ref.11, bf16[4,2304,512]{2,1,0:T(8,128)(2,1)S(1)} %get-tuple-element.42.pre_ref, ...), custom_call_target="tpu_custom_call" | custom-call | flops 1358954496 | bytes 21233664 | tf_op jit(solution)/shard_map/pallas_call | solution.py:387
  52.4 0.3 collective-permute-start.11
  52.7 0.0 collective-permute-done.12.refs_0_
  52.7 0.1 shard_map.104
  52.8 0.6 collective-permute-start.13
  53.4 0.0 collective-permute-done.7.refs_1_
  53.4 0.2 shard_map.101
  53.6 0.8 %collective-permute-start.8 = (bf16[4,1664]{1,0:T(4,128)(2,1)S(1)}, bf16[4,1664]{1,0:T(4,128)(2,1)S(1)}, u32[]{:S(2)}, u32[]{:S(2)}) collective-permute-start(bf16[4,1664]{1,0:T(4,128)(2,1)S(1)} %get-tuple-element.38), channel_id=1, source_target_pairs={{0,4},{4,8},{8,12},{12,0},{1,5},{5,9},{9,13},{13,1},{2,6},{6,10},{... | collective-permute-start | bytes 39944 | tf_op jit(solution)/shard_map/ppermute | solution.py:479
  54.4 2.1 %collective-permute-start.9 = (bf16[4,1664]{1,0:T(4,128)(2,1)S(1)}, bf16[4,1664]{1,0:T(4,128)(2,1)S(1)}, u32[]{:S(2)}, u32[]{:S(2)}) collective-permute-start(bf16[4,1664]{1,0:T(4,128)(2,1)S(1)} %get-tuple-element.39), channel_id=1, source_target_pairs={{0,8},{4,12},{8,0},{12,4},{1,9},{5,13},{9,1},{13,5},{2,10},{6,14},... | collective-permute-start | bytes 39944 | tf_op jit(solution)/shard_map/ppermute | solution.py:479
  56.5 2.7 %collective-permute-start.10 = (bf16[4,1664]{1,0:T(4,128)(2,1)S(1)}, bf16[4,1664]{1,0:T(4,128)(2,1)S(1)}, u32[]{:S(2)}, u32[]{:S(2)}) collective-permute-start(bf16[4,1664]{1,0:T(4,128)(2,1)S(1)} %get-tuple-element.40), channel_id=1, source_target_pairs={{0,12},{4,0},{8,4},{12,8},{1,13},{5,1},{9,5},{13,9},{2,14},{6,2},{... | collective-permute-start | bytes 39944 | tf_op jit(solution)/shard_map/ppermute | solution.py:479
  59.3 0.0 copy-start
  59.3 0.0 copy-start.3
  59.3 3.2 %shard_map.105 = (bf16[2,32,1536]{2,1,0:T(8,128)(2,1)S(1)}, f32[2,32,1536]{2,1,0:T(8,128)S(1)}) custom-call(bf16[64,2304]{1,0:T(8,128)(2,1)S(1)} %shard_map.98.x_ref, bf16[2304,9216]{1,0:T(8,128)(2,1)} %wg_ref.11, bf16[2304,9216]{1,0:T(8,128)(2,1)} %wu_ref.11, bf16[4,2304,512]{2,1,0:T(8,128)(2,1)S(1)} %get-tuple-element.48.pre_ref, ...), custom_call_target="tpu_custom_call" | custom-call | flops 905969664 | bytes 4718592 | tf_op jit(solution)/shard_map/pallas_call | solution.py:387
  62.4 0.0 collective-permute-done.13.refs_5_.refs_3_
  62.4 0.0 collective-permute-done.8.refs_2_.refs_1_
  62.4 0.0 collective-permute-done.9.refs_3_.refs_2_
  62.5 0.0 collective-permute-done.10.refs_4_.refs_3_
  62.5 0.0 collective-permute-done.11.refs_0_
  62.5 0.1 shard_map.106
  62.5 0.1 collective-permute-start.14
  62.6 0.8 %collective-permute-start.15 = (bf16[2,16,2304]{2,1,0:T(8,128)(2,1)S(1)}, bf16[2,16,2304]{2,1,0:T(8,128)(2,1)S(1)}, u32[]{:S(2)}, u32[]{:S(2)}) collective-permute-start(bf16[2,16,2304]{2,1,0:T(8,128)(2,1)S(1)} %get-tuple-element.50.refs_4_), channel_id=1, source_target_pairs={{0,2},{1,3},{2,0},{3,1},{4,6},{5,7},{6,4},{7,5},{8,10},{9,11},{10,... | collective-permute-start | bytes 442376 | tf_op jit(solution)/shard_map/ppermute | solution.py:482
  63.4 0.7 collective-permute-done.14.refs_0_
  64.1 0.8 %collective-permute-start.16 = (bf16[2,16,1536]{2,1,0:T(8,128)(2,1)S(1)}, bf16[2,16,1536]{2,1,0:T(8,128)(2,1)S(1)}, u32[]{:S(2)}, u32[]{:S(2)}) collective-permute-start(bf16[2,16,1536]{2,1,0:T(8,128)(2,1)S(1)} %get-tuple-element.55.refs_4_), channel_id=1, source_target_pairs={{0,2},{1,3},{2,0},{3,1},{4,6},{5,7},{6,4},{7,5},{8,10},{9,11},{10,... | collective-permute-start | bytes 294920 | tf_op jit(solution)/shard_map/ppermute | solution.py:482
  64.9 0.0 copy-done
  64.9 0.0 copy-done.3
  64.9 2.5 %shard_map.107 = bf16[2,1,2,6144]{3,2,1,0:T(2,128)(2,1)} custom-call(s32[4]{0:T(128)S(1)} %and_select_fusion.refs_2_.slot_ref, s32[2]{0:T(128)S(1)} %bitcast.3, bf16[2,1024,512]{2,1,0:T(8,128)(2,1)S(1)} %bitcast.2, bf16[4,1664]{1,0:T(4,128)(2,1)S(1)} %get-tuple-element.37.refs_1_.refs_0_, bf16[4,1664]{1,0:T(4,128)(2,1)S(1)} %collective-permute-done.8.refs_2_.refs_1_, ...), custom_call_target="tpu_custom_call" | custom-call | flops 100663296 | bytes 2097152 | tf_op jit(solution)/shard_map/pallas_call | solution.py:452
  67.4 0.2 shard_map.109.refs_0_
  67.5 1.8 %collective-permute-done.15.refs_2_ = bf16[2,16,2304]{2,1,0:T(8,128)(2,1)S(1)} collective-permute-done((bf16[2,16,2304]{2,1,0:T(8,128)(2,1)S(1)}, bf16[2,16,2304]{2,1,0:T(8,128)(2,1)S(1)}, u32[]{:S(2)}, u32[]{:S(2)}) %collective-permute-start.15) | collective-permute-done | bytes 147488 | tf_op jit(solution)/shard_map/ppermute | solution.py:482
  69.3 1.7 %collective-permute-done.16.refs_4_ = bf16[2,16,1536]{2,1,0:T(8,128)(2,1)S(1)} collective-permute-done((bf16[2,16,1536]{2,1,0:T(8,128)(2,1)S(1)}, bf16[2,16,1536]{2,1,0:T(8,128)(2,1)S(1)}, u32[]{:S(2)}, u32[]{:S(2)}) %collective-permute-start.16) | collective-permute-done | bytes 98336 | tf_op jit(solution)/shard_map/ppermute | solution.py:482
  71.0 0.8 %shard_map.110 = bf16[2,4,2,9216]{3,2,1,0:T(2,128)(2,1)} custom-call(bf16[2,4,2,5376]{3,2,1,0:T(2,128)(2,1)S(1)} %shard_map.109.refs_0_, f32[2,16,2304]{2,1,0:T(8,128)S(1)} %get-tuple-element.56.refs_1_, bf16[2,16,2304]{2,1,0:T(8,128)(2,1)S(1)} %collective-permute-done.15.refs_2_, f32[2,16,1536]{2,1,0:T(8,128)S(1)} %get-tuple-element.57.refs_3_, ...), custom_call_target="tpu_custom_call" | custom-call | flops 331776 | bytes 20736 | tf_op jit(solution)/shard_map/pallas_call | solution.py:186
  (3 shorter events, 0.1 us)
Async XLA Ops:
  0.6 12.0 %collective-permute-start.1 = (bf16[8,1,2,2304]{3,2,1,0:T(2,128)(2,1)}, bf16[8,1,2,2304]{3,2,1,0:T(2,128)(2,1)S(1)}, u32[]{:S(2)}, u32[]{:S(2)}) collective-permute-start(bf16[8,1,2,2304]{3,2,1,0:T(2,128)(2,1)} %refs_0_.1), channel_id=1, source_target_pairs={{0,8},{4,12},{8,0},{12,4},{1,9},{5,13},{9,1},{13,5},{2,10},{6,14},... | collective-permute-start | bytes 221192 | tf_op jit(solution)/shard_map/ppermute | solution.py:479
  4.7 7.9 %collective-permute-start = (bf16[8,1,2,2304]{3,2,1,0:T(2,128)(2,1)}, bf16[8,1,2,2304]{3,2,1,0:T(2,128)(2,1)S(1)}, u32[]{:S(2)}, u32[]{:S(2)}) collective-permute-start(bf16[8,1,2,2304]{3,2,1,0:T(2,128)(2,1)} %refs_0_.1), channel_id=1, source_target_pairs={{0,4},{4,8},{8,12},{12,0},{1,5},{5,9},{9,13},{13,1},{2,6},{6,10},{... | collective-permute-start | bytes 221192 | tf_op jit(solution)/shard_map/ppermute | solution.py:479
  6.3 6.3 %collective-permute-start.2 = (bf16[8,1,2,2304]{3,2,1,0:T(2,128)(2,1)}, bf16[8,1,2,2304]{3,2,1,0:T(2,128)(2,1)S(1)}, u32[]{:S(2)}, u32[]{:S(2)}) collective-permute-start(bf16[8,1,2,2304]{3,2,1,0:T(2,128)(2,1)} %refs_0_.1), channel_id=1, source_target_pairs={{0,12},{4,0},{8,4},{12,8},{1,13},{5,1},{9,5},{13,9},{2,14},{6,2},{... | collective-permute-start | bytes 221192 | tf_op jit(solution)/shard_map/ppermute | solution.py:479
  8.7 4.0 %copy-start.1 = (bf16[8,1,2,2304]{3,2,1,0:T(2,128)(2,1)S(1)}, bf16[8,1,2,2304]{3,2,1,0:T(2,128)(2,1)}, u32[]{:S(2)}) copy-start(bf16[8,1,2,2304]{3,2,1,0:T(2,128)(2,1)} %refs_0_.1) | copy-start | bytes 221188
  13.0 6.5 %copy-start.2 = (f32[2304]{0:T(1024)S(1)}, f32[2304]{0:T(1024)}, u32[]{:S(2)}) copy-start(f32[2304]{0:T(1024)} %gain_ref.1) | copy-start | bytes 27652
  13.0 6.5 %collective-permute-start.5 = (f32[64,128]{1,0:T(8,128)S(1)}, f32[64,128]{1,0:T(8,128)S(1)}, u32[]{:S(2)}, u32[]{:S(2)}) collective-permute-start(f32[64,128]{1,0:T(8,128)S(1)} %get-tuple-element.31.refs_0_), channel_id=1, source_target_pairs={{0,3},{1,0},{2,1},{3,2},{4,7},{5,4},{6,5},{7,6},{8,11},{9,8},{10,9... | collective-permute-start | bytes 98312 | tf_op jit(solution)/shard_map/ppermute | solution.py:482
  13.1 6.3 %collective-permute-start.4 = (f32[64,128]{1,0:T(8,128)S(1)}, f32[64,128]{1,0:T(8,128)S(1)}, u32[]{:S(2)}, u32[]{:S(2)}) collective-permute-start(f32[64,128]{1,0:T(8,128)S(1)} %get-tuple-element.31.refs_0_), channel_id=1, source_target_pairs={{0,2},{1,3},{2,0},{3,1},{4,6},{5,7},{6,4},{7,5},{8,10},{9,11},{10,... | collective-permute-start | bytes 98312 | tf_op jit(solution)/shard_map/ppermute | solution.py:482
  14.6 4.8 %collective-permute-start.3 = (f32[64,128]{1,0:T(8,128)S(1)}, f32[64,128]{1,0:T(8,128)S(1)}, u32[]{:S(2)}, u32[]{:S(2)}) collective-permute-start(f32[64,128]{1,0:T(8,128)S(1)} %get-tuple-element.31.refs_0_), channel_id=1, source_target_pairs={{0,1},{1,2},{2,3},{3,0},{4,5},{5,6},{6,7},{7,4},{8,9},{9,10},{10,1... | collective-permute-start | bytes 98312 | tf_op jit(solution)/shard_map/ppermute | solution.py:482
  31.1 11.1 %collective-permute-start.6 = (bf16[2,32,3968]{2,1,0:T(8,128)(2,1)S(1)}, bf16[2,32,3968]{2,1,0:T(8,128)(2,1)S(1)}, u32[]{:S(2)}, u32[]{:S(2)}) collective-permute-start(bf16[2,32,3968]{2,1,0:T(8,128)(2,1)S(1)} %get-tuple-element.32.refs_0_), channel_id=1, source_target_pairs={{0,1},{1,0},{2,3},{3,2},{4,5},{5,4},{6,7},{7,6},{8,9},{9,8},{10,11... | collective-permute-start | bytes 1523720 | tf_op jit(solution)/shard_map/ppermute | solution.py:485
  42.1 10.5 %collective-permute-start.12 = (bf16[2,32,3072]{2,1,0:T(8,128)(2,1)S(1)}, bf16[2,32,3072]{2,1,0:T(8,128)(2,1)S(1)}, u32[]{:S(2)}, u32[]{:S(2)}) collective-permute-start(bf16[2,32,3072]{2,1,0:T(8,128)(2,1)S(1)} %get-tuple-element.43.refs_1_), channel_id=1, source_target_pairs={{0,1},{1,0},{2,3},{3,2},{4,5},{5,4},{6,7},{7,6},{8,9},{9,8},{10,11... | collective-permute-start | bytes 1179656 | tf_op jit(solution)/shard_map/ppermute | solution.py:485
  42.3 11.1 %collective-permute-start.7 = (bf16[2,16,3968]{2,1,0:T(8,128)(2,1)S(1)}, bf16[2,16,3968]{2,1,0:T(8,128)(2,1)S(1)}, u32[]{:S(2)}, u32[]{:S(2)}) collective-permute-start(bf16[2,16,3968]{2,1,0:T(8,128)(2,1)S(1)} %get-tuple-element.36.refs_0_), channel_id=1, source_target_pairs={{0,2},{1,3},{2,0},{3,1},{4,6},{5,7},{6,4},{7,5},{8,10},{9,11},{10,... | collective-permute-start | bytes 761864 | tf_op jit(solution)/shard_map/ppermute | solution.py:482
  52.4 10.1 %collective-permute-start.11 = (bf16[2,32,2304]{2,1,0:T(8,128)(2,1)S(1)}, bf16[2,32,2304]{2,1,0:T(8,128)(2,1)S(1)}, u32[]{:S(2)}, u32[]{:S(2)}) collective-permute-start(bf16[2,32,2304]{2,1,0:T(8,128)(2,1)S(1)} %get-tuple-element.44.refs_2_), channel_id=1, source_target_pairs={{0,1},{1,0},{2,3},{3,2},{4,5},{5,4},{6,7},{7,6},{8,9},{9,8},{10,11... | collective-permute-start | bytes 884744 | tf_op jit(solution)/shard_map/ppermute | solution.py:485
  52.8 9.7 %collective-permute-start.13 = (bf16[2,16,3072]{2,1,0:T(8,128)(2,1)S(1)}, bf16[2,16,3072]{2,1,0:T(8,128)(2,1)S(1)}, u32[]{:S(2)}, u32[]{:S(2)}) collective-permute-start(bf16[2,16,3072]{2,1,0:T(8,128)(2,1)S(1)} %get-tuple-element.47.refs_0_), channel_id=1, source_target_pairs={{0,2},{1,3},{2,0},{3,1},{4,6},{5,7},{6,4},{7,5},{8,10},{9,11},{10,... | collective-permute-start | bytes 589832 | tf_op jit(solution)/shard_map/ppermute | solution.py:482
  53.6 8.8 %collective-permute-start.8 = (bf16[4,1664]{1,0:T(4,128)(2,1)S(1)}, bf16[4,1664]{1,0:T(4,128)(2,1)S(1)}, u32[]{:S(2)}, u32[]{:S(2)}) collective-permute-start(bf16[4,1664]{1,0:T(4,128)(2,1)S(1)} %get-tuple-element.38), channel_id=1, source_target_pairs={{0,4},{4,8},{8,12},{12,0},{1,5},{5,9},{9,13},{13,1},{2,6},{6,10},{... | collective-permute-start | bytes 39944 | tf_op jit(solution)/shard_map/ppermute | solution.py:479
  54.4 8.0 %collective-permute-start.9 = (bf16[4,1664]{1,0:T(4,128)(2,1)S(1)}, bf16[4,1664]{1,0:T(4,128)(2,1)S(1)}, u32[]{:S(2)}, u32[]{:S(2)}) collective-permute-start(bf16[4,1664]{1,0:T(4,128)(2,1)S(1)} %get-tuple-element.39), channel_id=1, source_target_pairs={{0,8},{4,12},{8,0},{12,4},{1,9},{5,13},{9,1},{13,5},{2,10},{6,14},... | collective-permute-start | bytes 39944 | tf_op jit(solution)/shard_map/ppermute | solution.py:479
  56.5 5.9 %collective-permute-start.10 = (bf16[4,1664]{1,0:T(4,128)(2,1)S(1)}, bf16[4,1664]{1,0:T(4,128)(2,1)S(1)}, u32[]{:S(2)}, u32[]{:S(2)}) collective-permute-start(bf16[4,1664]{1,0:T(4,128)(2,1)S(1)} %get-tuple-element.40), channel_id=1, source_target_pairs={{0,12},{4,0},{8,4},{12,8},{1,13},{5,1},{9,5},{13,9},{2,14},{6,2},{... | collective-permute-start | bytes 39944 | tf_op jit(solution)/shard_map/ppermute | solution.py:479
  59.3 5.6 %copy-start = (bf16[2,1,1024,512]{3,2,1,0:T(8,128)(2,1)S(1)}, bf16[2,1,1024,512]{3,2,1,0:T(8,128)(2,1)}, u32[]{:S(2)}) copy-start(bf16[2,1,1024,512]{3,2,1,0:T(8,128)(2,1)} %param.14) | copy-start | bytes 6291460
  59.3 5.6 %copy-start.3 = (s32[2,1]{0,1:T(1,128)S(1)}, s32[2,1]{0,1:T(1,128)}, u32[]{:S(2)}) copy-start(s32[2,1]{0,1:T(1,128)} %param.15) | copy-start | bytes 28
  62.5 1.5 %collective-permute-start.14 = (bf16[2,32,1536]{2,1,0:T(8,128)(2,1)S(1)}, bf16[2,32,1536]{2,1,0:T(8,128)(2,1)S(1)}, u32[]{:S(2)}, u32[]{:S(2)}) collective-permute-start(bf16[2,32,1536]{2,1,0:T(8,128)(2,1)S(1)} %get-tuple-element.51.refs_5_), channel_id=1, source_target_pairs={{0,1},{1,0},{2,3},{3,2},{4,5},{5,4},{6,7},{7,6},{8,9},{9,8},{10,11... | collective-permute-start | bytes 589832 | tf_op jit(solution)/shard_map/ppermute | solution.py:485
  62.6 6.7 %collective-permute-start.15 = (bf16[2,16,2304]{2,1,0:T(8,128)(2,1)S(1)}, bf16[2,16,2304]{2,1,0:T(8,128)(2,1)S(1)}, u32[]{:S(2)}, u32[]{:S(2)}) collective-permute-start(bf16[2,16,2304]{2,1,0:T(8,128)(2,1)S(1)} %get-tuple-element.50.refs_4_), channel_id=1, source_target_pairs={{0,2},{1,3},{2,0},{3,1},{4,6},{5,7},{6,4},{7,5},{8,10},{9,11},{10,... | collective-permute-start | bytes 442376 | tf_op jit(solution)/shard_map/ppermute | solution.py:482
  64.1 6.9 %collective-permute-start.16 = (bf16[2,16,1536]{2,1,0:T(8,128)(2,1)S(1)}, bf16[2,16,1536]{2,1,0:T(8,128)(2,1)S(1)}, u32[]{:S(2)}, u32[]{:S(2)}) collective-permute-start(bf16[2,16,1536]{2,1,0:T(8,128)(2,1)S(1)} %get-tuple-element.55.refs_4_), channel_id=1, source_target_pairs={{0,2},{1,3},{2,0},{3,1},{4,6},{5,7},{6,4},{7,5},{8,10},{9,11},{10,... | collective-permute-start | bytes 294920 | tf_op jit(solution)/shard_map/ppermute | solution.py:482

commit v6 on v5

--- a/solution.py
+++ b/solution.py
@@ -14,8 +14,7 @@
 MASKED = -1e30
 MIB = 1024 * 1024
 TILE = 256
-DEPTH = 6
-WIDE = 15
+SLOTS = 10
 F32 = jnp.float32
 BF16 = jnp.bfloat16
 
@@ -29,8 +28,8 @@
     return pl.CostEstimate(flops=size, bytes_accessed=size // 16, transcendentals=0)
 
 
-def params(mib=9):
-    return pltpu.CompilerParams(vmem_limit_bytes=mib * MIB)
+def params():
+    return pltpu.CompilerParams(vmem_limit_bytes=9 * MIB)
 
 
 def stats_kernel(count, *refs):
@@ -145,14 +144,14 @@
     )
     each = rows // count
     for index, ref in enumerate(out_refs):
-        ref[...] = turned[index * each : (index + 1) * each].astype(BF16)
+        ref[0] = turned[index * each : (index + 1) * each].astype(BF16)
 
 
 def query_rows(source, terms, count):
     rows, cols = terms[0].shape
     return pl.pallas_call(
         functools.partial(query_rows_kernel, count),
-        out_shape=[pltpu.VMEM((rows // count, cols), BF16)] * count,
+        out_shape=[pltpu.VMEM((1, rows // count, cols), BF16)] * count,
         in_specs=[whole()] * (1 + len(terms)),
         out_specs=[whole()] * count,
         compiler_params=params(),
@@ -201,43 +200,59 @@
     return [pltpu.with_memory_space_constraint(a, pltpu.VMEM) for a in arrays]
 
 
-def tile_copies(w_refs, tile, place, sems):
+def tile_copies(w_refs, tile, ring, sems):
     columns = pl.ds(pl.multiple_of(tile * TILE, TILE), TILE)
+    slot = lax.rem(tile, SLOTS)
     return [
         pltpu.make_async_copy(
-            ref.at[:, columns], place.at[:, index * TILE : (index + 1) * TILE], sems.at[index]
+            ref.at[:, columns], ring.at[slot, :, index * TILE : (index + 1) * TILE], sems.at[slot, index]
         )
         for index, ref in enumerate(w_refs)
     ]
 
 
-def load_kernel(first, tiles, wg_ref, wu_ref, *refs):
-    out_ref, sems = refs[-2:]
-
-    def copies(tile):
-        return tile_copies((wg_ref, wu_ref), first + tile, out_ref.at[tile], sems.at[tile])
-
-    for tile in range(tiles):
-        for copy in copies(tile):
+def each_tile(first, last, action):
+    def body(tile, carry):
+        action(tile)
+        return carry
+
+    lax.fori_loop(first, last, body, 0)
+
+
+def ring_shape(features):
+    return pltpu.VMEM((SLOTS, features, 2 * TILE), BF16)
+
+
+def load_kernel(first, last, wg_ref, wu_ref, *refs):
+    ring, sems = refs[-2:]
+
+    def start(tile):
+        for copy in tile_copies((wg_ref, wu_ref), tile, ring, sems):
             copy.start()
-    for tile in range(tiles):
-        for copy in copies(tile):
+
+    def wait(tile):
+        for copy in tile_copies((wg_ref, wu_ref), tile, ring, sems):
             copy.wait()
 
-
-def load(weights, first, tiles, after):
+    each_tile(first, last, start)
+    each_tile(first, last, wait)
+
+
+def load(weights, first, last, ring, after):
     features = weights[0].shape[0]
-    return pl.pallas_call(
-        functools.partial(load_kernel, first, tiles),
-        out_shape=pltpu.VMEM((tiles, features, 2 * TILE), BF16),
-        in_specs=[whole(pltpu.HBM)] * 2 + [whole(pl.ANY)] * len(after),
+    rings = [] if ring is None else in_vmem((ring,))
+    return pl.pallas_call(
+        functools.partial(load_kernel, first, last),
+        out_shape=ring_shape(features),
+        in_specs=[whole(pltpu.HBM)] * 2 + [whole()] * len(rings) + [whole(pl.ANY)] * len(after),
         out_specs=whole(),
-        scratch_shapes=[pltpu.SemaphoreType.DMA((tiles, 2))],
+        scratch_shapes=[pltpu.SemaphoreType.DMA((SLOTS, 2))],
+        input_output_aliases={2: 0} if rings else {},
         compiler_params=params(),
         cost_estimate=pl.CostEstimate(
-            flops=0, bytes_accessed=4 * features * TILE * tiles, transcendentals=0
+            flops=0, bytes_accessed=4 * features * TILE * (last - first), transcendentals=0
         ),
-    )(*in_hbm(weights), *after)
+    )(*in_hbm(weights), *rings, *after)
 
 
 def store_split(ref, columns, value):
@@ -246,20 +261,46 @@
     ref[1, :, columns] = (value - high.astype(F32)).astype(BF16)
 
 
-def multiply(x_ref, place, tile, send_ref, keep_ref):
-    part = jnp.dot(x_ref[...], place[...], preferred_element_type=F32)
-    half = part.shape[0] // 2
-    columns = pl.ds(pl.multiple_of(tile * TILE, TILE), TILE)
-    for index in range(2):
-        ref_columns = slice(index * TILE, (index + 1) * TILE)
-        send_ref[index, :, columns] = part[:half, ref_columns].astype(BF16)
-        keep_ref[index, :, columns] = part[half:, ref_columns]
-
-
-def first_kernel(held, x_ref, wg_ref, wu_ref, wq_ref, wkv_ref, *refs):
-    pre_refs = refs[:held]
-    send_ref, keep_ref, keep_q_ref, next_ref, q_ref, kv_ref, small_sems, next_sems = refs[held:]
-    tiles = sum(ref.shape[0] for ref in pre_refs)
+def multiply_tiles(first, tiles, held, following, x_ref, w_refs, ring, sems, send_ref, keep_ref):
+    loads = tiles + following - held
+    early = min(6, SLOTS - held, loads)
+
+    def start(index):
+        for copy in tile_copies(w_refs, first + held + index, ring, sems):
+            copy.start()
+
+    def wait(index):
+        for copy in tile_copies(w_refs, first + held + index, ring, sems):
+            copy.wait()
+
+    def multiply(index):
+        if held < tiles:
+
+            @pl.when(index >= held)
+            def _():
+                wait(index - held)
+
+        place = ring.at[lax.rem(first + index, SLOTS)]
+        part = jnp.dot(x_ref[...], place[...], preferred_element_type=F32)
+        half = part.shape[0] // 2
+        columns = pl.ds(pl.multiple_of(index * TILE, TILE), TILE)
+        for which in range(2):
+            lanes = slice(which * TILE, (which + 1) * TILE)
+            send_ref[which, :, columns] = part[:half, lanes].astype(BF16)
+            keep_ref[which, :, columns] = part[half:, lanes]
+        if early < loads:
+
+            @pl.when(index + early < loads)
+            def _():
+                start(index + early)
+
+    each_tile(0, early, start)
+    each_tile(0, tiles, multiply)
+    return lambda: each_tile(tiles - held, loads, wait)
+
+
+def first_kernel(tiles, following, x_ref, wg_ref, wu_ref, wq_ref, wkv_ref, _, *refs):
+    send_ref, keep_ref, keep_q_ref, ring, q_ref, kv_ref, small_sems, sems = refs
     half = x_ref.shape[0] // 2
     smalls = [
         pltpu.make_async_copy(wq_ref, q_ref, small_sems.at[0]),
@@ -267,147 +308,115 @@
     ]
     for copy in smalls:
         copy.start()
-
-    def fetch_next(index):
-        return tile_copies((wg_ref, wu_ref), tiles + index, next_ref.at[index], next_sems.at[index])
-
-    for index in range(next_ref.shape[0]):
-        for copy in fetch_next(index):
-            copy.start()
-    done = 0
-    for ref in pre_refs:
-        for index in range(ref.shape[0]):
-            multiply(x_ref, ref.at[index], done + index, send_ref, keep_ref)
-        done += ref.shape[0]
-    taken = 0
-    for copy, ref in zip(smalls, (q_ref, kv_ref)):
+    finish = multiply_tiles(0, tiles, tiles, following, x_ref, (wg_ref, wu_ref), ring, sems, send_ref, keep_ref)
+    for copy in smalls:
         copy.wait()
-        cols = ref.shape[1]
-        part = jnp.dot(x_ref[...], ref[...], preferred_element_type=F32)
-        store_split(send_ref, slice(tiles * TILE + taken, tiles * TILE + taken + cols), part[:half])
-        keep_q_ref[:, taken : taken + cols] = part[half:]
-        taken += cols
-    for index in range(next_ref.shape[0]):
-        for copy in fetch_next(index):
-            copy.wait()
-
-
-def first_sums(x, weights, w_query, w_keyval, held, following):
+    q_cols, kv_cols, base = q_ref.shape[1], kv_ref.shape[1], tiles * TILE
+    piece = q_cols // 3
+
+    def queries(index):
+        columns = pl.ds(pl.multiple_of(index * piece, piece), piece)
+        part = jnp.dot(x_ref[...], q_ref[:, columns], preferred_element_type=F32)
+        sent = pl.ds(pl.multiple_of(base + index * piece, TILE), piece)
+        store_split(send_ref, sent, part[:half])
+        keep_q_ref[:, columns] = part[half:]
+
+    each_tile(0, 3, queries)
+    part = jnp.dot(x_ref[...], kv_ref[...], preferred_element_type=F32)
+    store_split(send_ref, slice(base + q_cols, base + q_cols + kv_cols), part[:half])
+    keep_q_ref[:, q_cols:] = part[half:]
+    finish()
+
+
+def first_sums(x, weights, w_query, w_keyval, ring, tiles, following):
     rows, features = x.shape
-    tiles = sum(h.shape[0] for h in held)
     cols, small = tiles * TILE, w_query.shape[1] + w_keyval.shape[1]
     return pl.pallas_call(
-        functools.partial(first_kernel, len(held)),
+        functools.partial(first_kernel, tiles, following),
         out_shape=[
             pltpu.VMEM((2, rows // 2, cols + small), BF16),
             pltpu.VMEM((2, rows // 2, cols), F32),
             pltpu.VMEM((rows // 2, small), F32),
-            pltpu.VMEM((following, features, 2 * TILE), BF16),
+            ring_shape(features),
         ],
-        in_specs=[whole()] + [whole(pltpu.HBM)] * 4 + [whole()] * len(held),
+        in_specs=[whole()] + [whole(pltpu.HBM)] * 4 + [whole()],
         out_specs=[whole()] * 4,
         scratch_shapes=[
             pltpu.VMEM(w_query.shape, BF16),
             pltpu.VMEM(w_keyval.shape, BF16),
             pltpu.SemaphoreType.DMA((2,)),
-            pltpu.SemaphoreType.DMA((following, 2)),
+            pltpu.SemaphoreType.DMA((SLOTS, 2)),
         ],
+        input_output_aliases={5: 3},
         compiler_params=params(),
         cost_estimate=pl.CostEstimate(
             flops=2 * rows * features * (2 * cols + small),
             bytes_accessed=4 * features * cols,
             transcendentals=0,
         ),
-    )(x, *in_hbm((*weights, w_query, w_keyval)), *in_vmem(held))
-
-
-def wide_kernel(first, tiles, following, after, x_ref, wg_ref, wu_ref, pre_ref, *refs):
-    send_ref, keep_ref = refs[after : after + 2]
-    next_ref = refs[after + 2] if following else None
-    ring, ring_sems, next_sems = refs[-3:]
-    held, depth = pre_ref.shape[0], ring.shape[0]
-    streamed = tiles - held
-
-    def fetch(index):
-        slot = lax.rem(index, depth)
-        return tile_copies((wg_ref, wu_ref), first + held + index, ring.at[slot], ring_sems.at[slot])
-
-    def fetch_next(index):
-        return tile_copies((wg_ref, wu_ref), first + tiles + index, next_ref.at[index], next_sems.at[index])
-
-    def start(copies):
-        for copy in copies:
-            copy.start()
-
-    early = min(depth, streamed)
-    for index in range(early):
-        start(fetch(index))
-    early_next = min(following, DEPTH - early)
-    for index in range(early_next):
-        start(fetch_next(index))
-
-    for index in range(held):
-        multiply(x_ref, pre_ref.at[index], index, send_ref, keep_ref)
-
-    def from_ring(index, carry):
-        for copy in fetch(index):
-            copy.wait()
-        multiply(x_ref, ring.at[lax.rem(index, depth)], held + index, send_ref, keep_ref)
-
-        @pl.when(index + depth < streamed)
-        def _():
-            start(fetch(index + depth))
-
-        if following > early_next:
-            later = index + early_next + depth - streamed
-
-            @pl.when((later >= early_next) & (later < following))
-            def _():
-                start(fetch_next(later))
-
-        return carry
-
-    lax.fori_loop(0, streamed, from_ring, 0)
-    for index in range(following):
-        for copy in fetch_next(index):
-            copy.wait()
-
-
-def wide_sums(x, weights, held, first, tiles, following, after):
+    )(x, *in_hbm((*weights, w_query, w_keyval)), *in_vmem((ring,)))
+
+
+def wide_kernel(first, tiles, held, following, x_ref, wg_ref, wu_ref, _, *refs):
+    send_ref, keep_ref, ring, sems = refs[-4:]
+    multiply_tiles(
+        first, tiles, held, following, x_ref, (wg_ref, wu_ref), ring, sems, send_ref, keep_ref
+    )()
+
+
+def wide_sums(x, weights, ring, first, tiles, held, following, after):
     rows, features = x.shape
     cols = tiles * TILE
-    streamed = tiles - held.shape[0]
-    depth = min(DEPTH, max(streamed, 1))
-    out_shape = [
-        pltpu.VMEM((2, rows // 2, cols), BF16),
-        pltpu.VMEM((2, rows // 2, cols), F32),
-    ]
-    if following:
-        out_shape.append(pltpu.VMEM((following, features, 2 * TILE), BF16))
-    return pl.pallas_call(
-        functools.partial(wide_kernel, first, tiles, following, len(after)),
-        out_shape=out_shape,
+    return pl.pallas_call(
+        functools.partial(wide_kernel, first, tiles, held, following),
+        out_shape=[
+            pltpu.VMEM((2, rows // 2, cols), BF16),
+            pltpu.VMEM((2, rows // 2, cols), F32),
+            ring_shape(features),
+        ],
         in_specs=[whole(), whole(pltpu.HBM), whole(pltpu.HBM), whole()]
         + [whole(pl.ANY)] * len(after),
-        out_specs=[whole()] * len(out_shape),
-        scratch_shapes=[
-            pltpu.VMEM((depth, features, 2 * TILE), BF16),
-            pltpu.SemaphoreType.DMA((depth, 2)),
-            pltpu.SemaphoreType.DMA((max(following, 1), 2)),
-        ],
-        compiler_params=params(WIDE),
+        out_specs=[whole()] * 3,
+        scratch_shapes=[pltpu.SemaphoreType.DMA((SLOTS, 2))],
+        input_output_aliases={3: 2},
+        compiler_params=params(),
         cost_estimate=pl.CostEstimate(
             flops=4 * rows * features * cols,
-            bytes_accessed=4 * features * TILE * (streamed + following),
+            bytes_accessed=4 * features * TILE * (tiles + following - held),
             transcendentals=0,
         ),
-    )(x, *in_hbm(weights), *in_vmem((held,)), *after)
+    )(x, *in_hbm(weights), *in_vmem((ring,)), *after)
+
+
+def merge_kernel(kept_ref, came_ref, keep_ref, send_ref):
+    half = keep_ref.shape[1]
+    count = kept_ref.shape[0]
+    for index in range(2 * count):
+        both = (kept_ref[index] if index < count else came_ref[index - count]).astype(F32)
+        keep_ref[index] = both[:half].astype(BF16)
+        send_ref[index] = both[half:].astype(BF16)
+
+
+def merge(kept, came):
+    count, rows, cols = kept.shape
+    out = pltpu.VMEM((2 * count, rows // 2, cols), BF16)
+    return pl.pallas_call(
+        merge_kernel,
+        out_shape=(out, out),
+        in_specs=[whole()] * 2,
+        out_specs=(whole(), whole()),
+        compiler_params=params(),
+        cost_estimate=cost_of(kept, came),
+    )(kept, came)
 
 
 def attend_kernel(count, steps, query_cols, slot_ref, lengths_ref, cache_ref, *refs):
     part_refs, (out_ref, held, fresh) = refs[:count], refs[-3:]
+    each = part_refs[0].shape[0]
     for index, ref in enumerate(part_refs):
-        held[slot_ref[index]] = ref[...].astype(F32)
+        for source in range(each):
+            held[slot_ref[index * each + source]] = ref[source].astype(F32)
+    count = count * each
     pair_cols = held.shape[2] - query_cols
     heads = query_cols // HD
     scale = HD ** (-0.5)
@@ -448,14 +457,14 @@
 def attend(slots, lengths, cache, parts, steps, query_cols, after):
     batch = cache.shape[0]
     count = len(parts)
-    rows, cols = parts[0].shape
+    sources, rows, cols = parts[0].shape
     return pl.pallas_call(
         functools.partial(attend_kernel, count, steps, query_cols),
         out_shape=jax.ShapeDtypeStruct((batch, 1, steps, HEADS * HD), BF16),
         in_specs=[whole(pltpu.SMEM), whole(pltpu.SMEM)] + [whole()] * (1 + count) + [whole(pl.ANY)] * len(after),
         out_specs=whole(),
         scratch_shapes=[
-            pltpu.VMEM((count, rows, cols), F32),
+            pltpu.VMEM((count * sources, rows, cols), F32),
             pltpu.VMEM((batch, 8, 2 * HD), F32),
         ],
         compiler_params=params(),
@@ -480,6 +489,9 @@
 
     def shift_y(value, by):
         return lax.ppermute(value, "gy", [(i, (i + by) % size_y) for i in range(size_y)])
+
+    def swap_x(value, bit):
+        return lax.ppermute(value, "gx", [(i, i ^ bit) for i in range(size_x)])
 
     def swap(value):
         return lax.ppermute(value, "gy", [(i, i ^ 1) for i in range(size_y)])
@@ -492,61 +504,68 @@
     source = (me_x - column) % size_x * (tall * steps) + sequence * steps + row % steps
     source = source[:, None]
     row = jnp.arange(block, dtype=jnp.int32)
-    to = (me_x + row // (local * steps)) % size_x
+    to = me_x ^ (row // (local * steps))
     order = row // steps % local * (size_x * steps) + to * steps + row % steps
     order = order[:, None]
-    slots = (me_x - jnp.arange(size_x, dtype=jnp.int32)) % size_x
+    bits, offsets = [], [0]
+    while len(offsets) < size_x:
+        bits.append(size_x // (2 * len(offsets)))
+        offsets = offsets + [offset ^ bits[-1] for offset in offsets]
+    slots = jnp.array(offsets, jnp.int32) ^ me_x
 
     weights = (w_gate, w_up)
     tiles = w_gate.shape[1] // TILE
-    before = [tiles * share // 36 for share in (4, 5)]
-    bounds = [0, sum(before)] + [tiles * share // 36 for share in (21, 30, 36)]
-    ahead = [max(1, tiles * share // 36) for share in (5, 4, 4)] + [0]
+    before = [tiles * share // 36 for share in (4, 9)]
+    bounds = [0, before[1]] + [tiles * share // 36 for share in (20, 29, 36)]
+    ahead = [before[1]] + [max(1, tiles * share // 36) for share in (5, 4, 4)] + [0]
     gathered = [tokens] + [shift_x(tokens, by) for by in range(1, size_x)]
-    first_tiles = load(weights, 0, before[0], (source, order, slots))
-    rows, stats = partial_stats(gathered, first_tiles)
+    ring = load(weights, 0, before[0], None, (source, order, slots))
+    rows, stats = partial_stats(gathered, ring)
     every_stat = [stats] + [shift_y(stats, by) for by in range(1, size_y)]
-    second_tiles = load(weights, before[0], before[1], (stats,))
-    x = normed_rows(source, gain, rows, every_stat, second_tiles)
-
-    def chunk_sums(chunk, held, after):
-        count = bounds[chunk + 1] - bounds[chunk]
-        return wide_sums(x, weights, held, bounds[chunk], count, ahead[chunk], after)
+    ring = load(weights, before[0], before[1], ring, (stats,))
+    x = normed_rows(source, gain, rows, every_stat, ring)
+
+    def chunk_sums(chunk, ring, after):
+        first, count = bounds[chunk], bounds[chunk + 1] - bounds[chunk]
+        return wide_sums(x, weights, ring, first, count, ahead[chunk], ahead[chunk + 1], after)
 
     def to_chips(parts):
         return [shift_y(part, 2 * by) for by, part in enumerate(parts[: chips - 1], 1)]
 
-    send_0, keep_0, keep_q, held = first_sums(
-        x, weights, w_query, w_keyval, (first_tiles, second_tiles), ahead[0]
+    send_0, keep_0, keep_q, ring = first_sums(
+        x, weights, w_query, w_keyval, ring, bounds[1], ahead[1]
     )
-    send_1, keep_1, held = chunk_sums(1, held, (send_0,))
+    send_1, keep_1, ring = chunk_sums(1, ring, (send_0,))
     parts_0 = combine(chips, swap(send_0), keep_0, keep_q)
     from_0 = to_chips(parts_0)
 
-    send_2, keep_2, held = chunk_sums(2, held, (parts_0[0], send_1))
+    send_2, keep_2, ring = chunk_sums(2, ring, (parts_0[0], send_1))
     parts_1 = combine(chips, swap(send_1), keep_1)
     from_1 = to_chips(parts_1)
-    turned = query_rows(order, [parts_0[-1]] + from_0, size_x)
-    new = [turned[0]] + [shift_x(turned[by], by) for by in range(1, size_x)]
-
-    send_3, keep_3 = chunk_sums(3, held, (parts_1[0], turned[0], send_2))
-    *parts_2, send_3 = combine(chips, swap(send_2), keep_2, None, send_3, (*new[1:], from_1[0]))
+    kept, leaving = query_rows(order, [parts_0[-1]] + from_0, 2)
+    came = swap_x(leaving, bits[0])
+
+    send_3, keep_3, _ = chunk_sums(3, ring, (parts_1[0], kept, send_2))
+    *parts_2, send_3 = combine(chips, swap(send_2), keep_2, None, send_3, (came, from_1[0]))
     from_2 = to_chips(parts_2)
-    context = attend(
-        slots,
-        lengths.reshape(local),
-        cache.reshape(local, cache.shape[2], cache.shape[3]),
-        new,
-        steps,
-        w_query.shape[1],
-        (parts_2[0], send_3),
-    )
+    for bit in bits[1:]:
+        kept, leaving = merge(kept, came)
+        came = swap_x(leaving, bit)
     parts_3 = combine(chips, swap(send_3), keep_3)
     from_3 = to_chips(parts_3)
     half_done = gated(
         [[parts_0[chips - 1]] + from_0, [parts_1[-1]] + from_1],
         pltpu.VMEM((local, size_x, steps, bounds[2] * TILE), BF16),
         (),
+        (parts_3[0],),
+    )
+    context = attend(
+        slots,
+        lengths.reshape(local),
+        cache.reshape(local, cache.shape[2], cache.shape[3]),
+        (kept, came),
+        steps,
+        w_query.shape[1],
         (parts_3[0],),
     )
     hidden = gated(

time: 72 us -> 63.5 us (0.88)
  Pallas kernels: 46.6 us -> 40.6 us
  starting transfers between devices: 20.1 us -> 17.9 us
  waiting for transfers between devices: 4.16 us -> 3.18 us
    ppermute x6 -> x3, starting transfers between devices: 13.6 us -> 7.01 us  [shift_x(): lax.ppermute(value, 'gx', [(i, (i + by) % size_x) for i in range(size_x)])]
    pallas_call x6 -> x7, Pallas kernels: 41.9 us -> 36 us  [the longest x3 20.2 us: wide_sums(): pl.pallas_call(functools.partial(wide_kernel, first, tiles, held, followi...]
    ppermute x7, waiting for transfers between devices: 3.48 us -> 0.48 us  [shift_y(): lax.ppermute(value, 'gy', [(i, (i + by) % size_y) for i in range(size_y)])]
    ppermute x7, starting transfers between devices: 5.52 us -> 8.24 us  [shift_y(): lax.ppermute(value, 'gy', [(i, (i + by) % size_y) for i in range(size_y)])]
    ppermute x0 -> x2, waiting for transfers between devices: none -> 2.68 us  [swap_x(): return lax.ppermute(value, 'gx', [(i, i ^ bit) for i in range(size_x)])]
    ppermute x0 -> x2, starting transfers between devices: none -> 1.84 us  [swap_x(): return lax.ppermute(value, 'gx', [(i, i ^ bit) for i in range(size_x)])]
  transfers between devices with their start and end apart: 17 -> 16, of which waited for: 3 -> 2; matrix products, arithmetic and copies ran while one was open for 0% -> 1% of each run, Pallas kernels for 47% -> 51%
where the time goes in v6:
time: 63.5 us; the launch traced here: 63.3 us
  Pallas kernels  40.6 us (64%)
  starting transfers between devices  17.9 us (28%)
  waiting for transfers between devices  3.18 us (5%)
  between operations  0.86 us (1%)
  other arithmetic  0.74 us (1%)
    pallas_call x3, Pallas kernels, wide_sums(): pl.pallas_call(functools.partial(wide_kernel, first, tiles, held, followi...  20.2 us
    pallas_call x2, Pallas kernels, load(): pl.pallas_call(functools.partial(load_kernel, first, last), out_shape=rin...  8.77 us
    ppermute x7, starting transfers between devices, shift_y(): lax.ppermute(value, 'gy', [(i, (i + by) % size_y) for i in range(size_y)])  8.24 us
    pallas_call x1, Pallas kernels, first_sums(): pl.pallas_call(functools.partial(first_kernel, tiles, following), out_sha...  7.05 us
    ppermute x3, starting transfers between devices, shift_x(): lax.ppermute(value, 'gx', [(i, (i + by) % size_x) for i in range(size_x)])  7.01 us
    ppermute x2, waiting for transfers between devices, swap_x(): return lax.ppermute(value, 'gx', [(i, i ^ bit) for i in range(size_x)])  2.68 us
    pallas_call x1, Pallas kernels, attend(): pl.pallas_call(functools.partial(attend_kernel, count, steps, query_cols)...  2.48 us
    ppermute x2, starting transfers between devices, swap_x(): return lax.ppermute(value, 'gx', [(i, i ^ bit) for i in range(size_x)])  1.84 us
  transfers between devices with their start and end apart: 16, of which 2 were waited for; matrix products, arithmetic and copies ran while one was open for 1% of the time, Pallas kernels for 51%

profile of v6, /device:TPU:0, one launch (start us, length us, event | category | flops | bytes accessed | tf_op | source)
XLA Modules:
  0.0 63.3 jit_solution(17806357687944020453)
XLA Ops:
  0.6 3.1 %collective-permute-start = (bf16[8,1,2,2304]{3,2,1,0:T(2,128)(2,1)}, bf16[8,1,2,2304]{3,2,1,0:T(2,128)(2,1)S(1)}, u32[]{:S(2)}, u32[]{:S(2)}) collective-permute-start(bf16[8,1,2,2304]{3,2,1,0:T(2,128)(2,1)} %refs_0_.1), channel_id=1, source_target_pairs={{0,4},{4,8},{8,12},{12,0},{1,5},{5,9},{9,13},{13,1},{2,6},{6,10},{... | collective-permute-start | bytes 221192 | tf_op jit(solution)/shard_map/ppermute | solution.py:488
  3.7 2.6 %collective-permute-start.1 = (bf16[8,1,2,2304]{3,2,1,0:T(2,128)(2,1)}, bf16[8,1,2,2304]{3,2,1,0:T(2,128)(2,1)S(1)}, u32[]{:S(2)}, u32[]{:S(2)}) collective-permute-start(bf16[8,1,2,2304]{3,2,1,0:T(2,128)(2,1)} %refs_0_.1), channel_id=1, source_target_pairs={{0,8},{4,12},{8,0},{12,4},{1,9},{5,13},{9,1},{13,5},{2,10},{6,14},... | collective-permute-start | bytes 221192 | tf_op jit(solution)/shard_map/ppermute | solution.py:488
  6.3 1.3 %collective-permute-start.2 = (bf16[8,1,2,2304]{3,2,1,0:T(2,128)(2,1)}, bf16[8,1,2,2304]{3,2,1,0:T(2,128)(2,1)S(1)}, u32[]{:S(2)}, u32[]{:S(2)}) collective-permute-start(bf16[8,1,2,2304]{3,2,1,0:T(2,128)(2,1)} %refs_0_.1), channel_id=1, source_target_pairs={{0,12},{4,0},{8,4},{12,8},{1,13},{5,1},{9,5},{13,9},{2,14},{6,2},{... | collective-permute-start | bytes 221192 | tf_op jit(solution)/shard_map/ppermute | solution.py:488
  7.6 0.7 %broadcast_xor_fusion.refs_2_.slot_ref = s32[4]{0:T(128)S(1)} fusion(s32[4]{0:T(128)} %constant.156.clone, s32[]{:T(128)S(6)} %axis_index.23), kind=kLoop, calls=%fused_computation.80 | loop fusion | flops 4 | bytes 36 | tf_op jit(solution)/shard_map/xor | solution.py:514
  8.3 0.0 copy-start.3
  8.3 0.1 fusion.18.refs_0_.source_ref
  8.4 0.0 copy-start.1
  8.4 4.0 %shard_map.104.refs_4_.refs_0_ = bf16[10,2304,512]{2,1,0:T(8,128)(2,1)S(1)} custom-call(bf16[2304,9216]{1,0:T(8,128)(2,1)} %wg_ref.11, bf16[2304,9216]{1,0:T(8,128)(2,1)} %wu_ref.11, s32[64,1]{1,0:T(8,128)S(1)} %fusion.18.refs_0_.source_ref, s32[16,1]{1,0:T(8,128)S(1)} %fusion.39.refs_1_.source_ref, s32[4]{0:T(128)S(1)} %broadcast_xor_fusion.refs_2_.slot_ref), custom_call_target="tpu_custom_call" | custom-call | bytes 9437184 | tf_op jit(solution)/shard_map/pallas_call | solution.py:244
  12.5 0.0 copy-done.3
  12.5 0.0 collective-permute-done.refs_1_
  12.5 0.0 collective-permute-done.1.refs_2_
  12.5 0.0 collective-permute-done.2.refs_3_
  12.5 0.0 copy-done.1
  12.5 0.3 shard_map.105
  12.8 0.0 copy-start.2
  12.8 0.1 collective-permute-start.3
  12.9 1.6 %collective-permute-start.4 = (f32[64,128]{1,0:T(8,128)S(1)}, f32[64,128]{1,0:T(8,128)S(1)}, u32[]{:S(2)}, u32[]{:S(2)}) collective-permute-start(f32[64,128]{1,0:T(8,128)S(1)} %get-tuple-element.31.refs_1_.refs_0_), channel_id=1, source_target_pairs={{0,2},{1,3},{2,0},{3,1},{4,6},{5,7},{6,4},{7,5},{8,10},{9,11},{10,... | collective-permute-start | bytes 98312 | tf_op jit(solution)/shard_map/ppermute | solution.py:491
  14.5 1.4 %collective-permute-start.5 = (f32[64,128]{1,0:T(8,128)S(1)}, f32[64,128]{1,0:T(8,128)S(1)}, u32[]{:S(2)}, u32[]{:S(2)}) collective-permute-start(f32[64,128]{1,0:T(8,128)S(1)} %get-tuple-element.31.refs_1_.refs_0_), channel_id=1, source_target_pairs={{0,3},{1,0},{2,1},{3,2},{4,7},{5,4},{6,5},{7,6},{8,11},{9,8},{10,9... | collective-permute-start | bytes 98312 | tf_op jit(solution)/shard_map/ppermute | solution.py:491
  15.9 4.7 %shard_map.106.refs_4_._ = bf16[10,2304,512]{2,1,0:T(8,128)(2,1)S(1)} custom-call(bf16[2304,9216]{1,0:T(8,128)(2,1)} %wg_ref.11, bf16[2304,9216]{1,0:T(8,128)(2,1)} %wu_ref.11, bf16[10,2304,512]{2,1,0:T(8,128)(2,1)S(1)} %shard_map.104.refs_4_.refs_0_, f32[64,128]{1,0:T(8,128)S(1)} %get-tuple-element.31.refs_1_.refs_0_), custom_call_target="tpu_custom_call", output_to_operand_aliasing={{}: (2, {})} | custom-call | bytes 11796480 | tf_op jit(solution)/shard_map/pallas_call | solution.py:244
  20.6 0.0 collective-permute-done.3.refs_1_
  20.6 0.0 collective-permute-done.4.refs_2_
  20.6 0.0 collective-permute-done.5.refs_3_
  20.6 0.0 copy-done.2
  20.6 0.4 shard_map.107.x_ref
  21.0 7.1 %shard_map.108 = (bf16[2,32,3968]{2,1,0:T(8,128)(2,1)S(1)}, f32[2,32,2304]{2,1,0:T(8,128)S(1)}, f32[32,1664]{1,0:T(8,128)S(1)}, bf16[10,2304,512]{2,1,0:T(8,128)(2,1)S(1)}) custom-call(bf16[64,2304]{1,0:T(8,128)(2,1)S(1)} %shard_map.107.x_ref, bf16[2304,9216]{1,0:T(8,128)(2,1)} %wg_ref.11, ...), custom_call_target="tpu_custom_call", output_to_operand_aliasing={{3}: (5, {})} | custom-call | flops 1849688064 | bytes 21233664 | tf_op jit(solution)/shard_map/pallas_call | solution.py:334
  28.1 0.1 collective-permute-start.6
  28.2 8.5 %shard_map.112 = (bf16[2,32,2816]{2,1,0:T(8,128)(2,1)S(1)}, f32[2,32,2816]{2,1,0:T(8,128)S(1)}, bf16[10,2304,512]{2,1,0:T(8,128)(2,1)S(1)}) custom-call(bf16[64,2304]{1,0:T(8,128)(2,1)S(1)} %shard_map.107.x_ref, bf16[2304,9216]{1,0:T(8,128)(2,1)} %wg_ref.11, bf16[2304,9216]{1,0:T(8,128)(2,1)} %wu_ref.11, ...), custom_call_target="tpu_custom_call", output_to_operand_aliasing={{2}: (3, {})} | custom-call | flops 1660944384 | bytes 23592960 | tf_op jit(solution)/shard_map/pallas_call | solution.py:370
  36.6 0.5 collective-permute-start.11
  37.2 0.0 collective-permute-done.6.refs_0_
  37.2 0.1 shard_map.109
  37.3 0.6 collective-permute-start.7
  37.9 7.7 %shard_map.113 = (bf16[2,32,2304]{2,1,0:T(8,128)(2,1)S(1)}, f32[2,32,2304]{2,1,0:T(8,128)S(1)}, bf16[10,2304,512]{2,1,0:T(8,128)(2,1)S(1)}) custom-call(bf16[64,2304]{1,0:T(8,128)(2,1)S(1)} %shard_map.107.x_ref, bf16[2304,9216]{1,0:T(8,128)(2,1)} %wg_ref.11, bf16[2304,9216]{1,0:T(8,128)(2,1)} %wu_ref.11, ...), custom_call_target="tpu_custom_call", output_to_operand_aliasing={{2}: (3, {})} | custom-call | flops 1358954496 | bytes 21233664 | tf_op jit(solution)/shard_map/pallas_call | solution.py:370
  45.6 0.1 collective-permute-start.10
  45.7 0.0 collective-permute-done.11.refs_0_
  45.7 0.1 shard_map.114
  45.8 1.6 %collective-permute-start.12 = (bf16[2,16,2816]{2,1,0:T(8,128)(2,1)S(1)}, bf16[2,16,2816]{2,1,0:T(8,128)(2,1)S(1)}, u32[]{:S(2)}, u32[]{:S(2)}) collective-permute-start(bf16[2,16,2816]{2,1,0:T(8,128)(2,1)S(1)} %get-tuple-element.47.refs_0_), channel_id=1, source_target_pairs={{0,2},{1,3},{2,0},{3,1},{4,6},{5,7},{6,4},{7,5},{8,10},{9,11},{10,... | collective-permute-start | bytes 540680 | tf_op jit(solution)/shard_map/ppermute | solution.py:491
  47.4 0.0 collective-permute-done.7.refs_1_
  47.4 0.2 shard_map.110
  47.6 0.8 %collective-permute-start.8 = (bf16[1,8,1664]{2,1,0:T(8,128)(2,1)S(1)}, bf16[1,8,1664]{2,1,0:T(8,128)(2,1)S(1)}, u32[]{:S(2)}, u32[]{:S(2)}) collective-permute-start(bf16[1,8,1664]{2,1,0:T(8,128)(2,1)S(1)} %get-tuple-element.38), channel_id=1, source_target_pairs={{0,8},{4,12},{8,0},{12,4},{1,9},{5,13},{9,1},{13,5},{2,10},{6,14},... | collective-permute-start | bytes 79880 | tf_op jit(solution)/shard_map/ppermute | solution.py:494
  48.3 0.0 copy-start
  48.3 0.0 copy-start.4
  48.3 0.0 copy-start.5
  48.3 4.0 %shard_map.115 = (bf16[2,32,1792]{2,1,0:T(8,128)(2,1)S(1)}, f32[2,32,1792]{2,1,0:T(8,128)S(1)}, bf16[10,2304,512]{2,1,0:T(8,128)(2,1)S(1)}) custom-call(bf16[64,2304]{1,0:T(8,128)(2,1)S(1)} %shard_map.107.x_ref, bf16[2304,9216]{1,0:T(8,128)(2,1)} %wg_ref.11, bf16[2304,9216]{1,0:T(8,128)(2,1)} %wu_ref.11, ...), custom_call_target="tpu_custom_call", output_to_operand_aliasing={{2}: (3, {})} | custom-call | flops 1056964608 | bytes 7077888 | tf_op jit(solution)/shard_map/pallas_call | solution.py:370
  52.3 0.5 collective-permute-done.12.refs_3_
  52.8 0.0 collective-permute-done.8.came_ref.refs_2_
  52.8 0.0 collective-permute-done.10.refs_0_
  52.9 0.1 collective-permute-start.13
  52.9 1.6 %collective-permute-start.14 = (bf16[2,16,2304]{2,1,0:T(8,128)(2,1)S(1)}, bf16[2,16,2304]{2,1,0:T(8,128)(2,1)S(1)}, u32[]{:S(2)}, u32[]{:S(2)}) collective-permute-start(bf16[2,16,2304]{2,1,0:T(8,128)(2,1)S(1)} %get-tuple-element.56), channel_id=1, source_target_pairs={{0,2},{1,3},{2,0},{3,1},{4,6},{5,7},{6,4},{7,5},{8,10},{9,11},{10,... | collective-permute-start | bytes 442376 | tf_op jit(solution)/shard_map/ppermute | solution.py:491
  54.5 0.0 collective-permute-done.13.refs_0_
  54.6 1.5 %collective-permute-start.15 = (bf16[2,16,1792]{2,1,0:T(8,128)(2,1)S(1)}, bf16[2,16,1792]{2,1,0:T(8,128)(2,1)S(1)}, u32[]{:S(2)}, u32[]{:S(2)}) collective-permute-start(bf16[2,16,1792]{2,1,0:T(8,128)(2,1)S(1)} %get-tuple-element.52.refs_2_.refs_4_), channel_id=1, source_target_pairs={{0,2},{1,3},{2,0},{3,1},{4,6},{5,7},{6,4},{7,5},{8,10},{9,11},{10,... | collective-permute-start | bytes 344072 | tf_op jit(solution)/shard_map/ppermute | solution.py:491
  56.1 1.1 %collective-permute-start.9 = (bf16[2,4,1664]{2,1,0:T(4,128)(2,1)S(1)}, bf16[2,4,1664]{2,1,0:T(4,128)(2,1)S(1)}, u32[]{:S(2)}, u32[]{:S(2)}) collective-permute-start(bf16[2,4,1664]{2,1,0:T(4,128)(2,1)S(1)} %get-tuple-element.40), channel_id=1, source_target_pairs={{0,4},{4,0},{8,12},{12,8},{1,5},{5,1},{9,13},{13,9},{2,6},{6,2},{1... | collective-permute-start | bytes 79880 | tf_op jit(solution)/shard_map/ppermute | solution.py:494
  57.1 0.2 shard_map.119.refs_0_
  57.3 2.7 %collective-permute-done.9.refs_1_ = bf16[2,4,1664]{2,1,0:T(4,128)(2,1)S(1)} collective-permute-done((bf16[2,4,1664]{2,1,0:T(4,128)(2,1)S(1)}, bf16[2,4,1664]{2,1,0:T(4,128)(2,1)S(1)}, u32[]{:S(2)}, u32[]{:S(2)}) %collective-permute-start.9) | collective-permute-done | bytes 26656 | tf_op jit(solution)/shard_map/ppermute | solution.py:494
  60.0 0.0 copy-done
  60.0 0.0 copy-done.4
  60.0 0.0 copy-done.5
  60.0 2.5 %shard_map.118 = bf16[2,1,2,6144]{3,2,1,0:T(2,128)(2,1)} custom-call(s32[4]{0:T(128)S(1)} %copy-done.4, s32[2]{0:T(128)S(1)} %bitcast.3, bf16[2,1024,512]{2,1,0:T(8,128)(2,1)S(1)} %bitcast.2, bf16[2,4,1664]{2,1,0:T(4,128)(2,1)S(1)} %get-tuple-element.39.refs_0_, bf16[2,4,1664]{2,1,0:T(4,128)(2,1)S(1)} %collective-permute-done.9.refs_1_, ...), custom_call_target="tpu_custom_call" | custom-call | flops 100663296 | bytes 2097152 | tf_op jit(solution)/shard_map/pallas_call | solution.py:461
  62.5 0.0 collective-permute-done.14.refs_2_
  62.5 0.0 collective-permute-done.15.refs_4_
  62.5 0.9 %shard_map.120 = bf16[2,4,2,9216]{3,2,1,0:T(2,128)(2,1)} custom-call(bf16[2,4,2,5120]{3,2,1,0:T(2,128)(2,1)S(1)} %shard_map.119.refs_0_, f32[2,16,2304]{2,1,0:T(8,128)S(1)} %get-tuple-element.55.refs_1_, bf16[2,16,2304]{2,1,0:T(8,128)(2,1)S(1)} %collective-permute-done.14.refs_2_, f32[2,16,1792]{2,1,0:T(8,128)S(1)} %get-tuple-element.57.refs_3_, ...), custom_call_target="tpu_custom_call" | custom-call | flops 344064 | bytes 21504 | tf_op jit(solution)/shard_map/pallas_call | solution.py:185
  (4 shorter events, 0.1 us)
Async XLA Ops:
  0.6 11.8 %collective-permute-start = (bf16[8,1,2,2304]{3,2,1,0:T(2,128)(2,1)}, bf16[8,1,2,2304]{3,2,1,0:T(2,128)(2,1)S(1)}, u32[]{:S(2)}, u32[]{:S(2)}) collective-permute-start(bf16[8,1,2,2304]{3,2,1,0:T(2,128)(2,1)} %refs_0_.1), channel_id=1, source_target_pairs={{0,4},{4,8},{8,12},{12,0},{1,5},{5,9},{9,13},{13,1},{2,6},{6,10},{... | collective-permute-start | bytes 221192 | tf_op jit(solution)/shard_map/ppermute | solution.py:488
  3.7 8.8 %collective-permute-start.1 = (bf16[8,1,2,2304]{3,2,1,0:T(2,128)(2,1)}, bf16[8,1,2,2304]{3,2,1,0:T(2,128)(2,1)S(1)}, u32[]{:S(2)}, u32[]{:S(2)}) collective-permute-start(bf16[8,1,2,2304]{3,2,1,0:T(2,128)(2,1)} %refs_0_.1), channel_id=1, source_target_pairs={{0,8},{4,12},{8,0},{12,4},{1,9},{5,13},{9,1},{13,5},{2,10},{6,14},... | collective-permute-start | bytes 221192 | tf_op jit(solution)/shard_map/ppermute | solution.py:488
  6.3 6.2 %collective-permute-start.2 = (bf16[8,1,2,2304]{3,2,1,0:T(2,128)(2,1)}, bf16[8,1,2,2304]{3,2,1,0:T(2,128)(2,1)S(1)}, u32[]{:S(2)}, u32[]{:S(2)}) collective-permute-start(bf16[8,1,2,2304]{3,2,1,0:T(2,128)(2,1)} %refs_0_.1), channel_id=1, source_target_pairs={{0,12},{4,0},{8,4},{12,8},{1,13},{5,1},{9,5},{13,9},{2,14},{6,2},{... | collective-permute-start | bytes 221192 | tf_op jit(solution)/shard_map/ppermute | solution.py:488
  8.3 4.2 %copy-start.3 = (s32[4]{0:T(128)}, s32[4]{0:T(128)S(1)}, u32[]{:S(2)}) copy-start(s32[4]{0:T(128)S(1)} %broadcast_xor_fusion.refs_2_.slot_ref) | copy-start | bytes 52
  8.4 4.1 %copy-start.1 = (bf16[8,1,2,2304]{3,2,1,0:T(2,128)(2,1)S(1)}, bf16[8,1,2,2304]{3,2,1,0:T(2,128)(2,1)}, u32[]{:S(2)}) copy-start(bf16[8,1,2,2304]{3,2,1,0:T(2,128)(2,1)} %refs_0_.1) | copy-start | bytes 221188
  12.8 7.8 %copy-start.2 = (f32[2304]{0:T(1024)S(1)}, f32[2304]{0:T(1024)}, u32[]{:S(2)}) copy-start(f32[2304]{0:T(1024)} %gain_ref.1) | copy-start | bytes 27652
  12.8 7.8 %collective-permute-start.3 = (f32[64,128]{1,0:T(8,128)S(1)}, f32[64,128]{1,0:T(8,128)S(1)}, u32[]{:S(2)}, u32[]{:S(2)}) collective-permute-start(f32[64,128]{1,0:T(8,128)S(1)} %get-tuple-element.31.refs_1_.refs_0_), channel_id=1, source_target_pairs={{0,1},{1,2},{2,3},{3,0},{4,5},{5,6},{6,7},{7,4},{8,9},{9,10},{10,1... | collective-permute-start | bytes 98312 | tf_op jit(solution)/shard_map/ppermute | solution.py:491
  12.9 7.7 %collective-permute-start.4 = (f32[64,128]{1,0:T(8,128)S(1)}, f32[64,128]{1,0:T(8,128)S(1)}, u32[]{:S(2)}, u32[]{:S(2)}) collective-permute-start(f32[64,128]{1,0:T(8,128)S(1)} %get-tuple-element.31.refs_1_.refs_0_), channel_id=1, source_target_pairs={{0,2},{1,3},{2,0},{3,1},{4,6},{5,7},{6,4},{7,5},{8,10},{9,11},{10,... | collective-permute-start | bytes 98312 | tf_op jit(solution)/shard_map/ppermute | solution.py:491
  14.5 6.1 %collective-permute-start.5 = (f32[64,128]{1,0:T(8,128)S(1)}, f32[64,128]{1,0:T(8,128)S(1)}, u32[]{:S(2)}, u32[]{:S(2)}) collective-permute-start(f32[64,128]{1,0:T(8,128)S(1)} %get-tuple-element.31.refs_1_.refs_0_), channel_id=1, source_target_pairs={{0,3},{1,0},{2,1},{3,2},{4,7},{5,4},{6,5},{7,6},{8,11},{9,8},{10,9... | collective-permute-start | bytes 98312 | tf_op jit(solution)/shard_map/ppermute | solution.py:491
  28.1 9.1 %collective-permute-start.6 = (bf16[2,32,3968]{2,1,0:T(8,128)(2,1)S(1)}, bf16[2,32,3968]{2,1,0:T(8,128)(2,1)S(1)}, u32[]{:S(2)}, u32[]{:S(2)}) collective-permute-start(bf16[2,32,3968]{2,1,0:T(8,128)(2,1)S(1)} %get-tuple-element.32.refs_0_), channel_id=1, source_target_pairs={{0,1},{1,0},{2,3},{3,2},{4,5},{5,4},{6,7},{7,6},{8,9},{9,8},{10,11... | collective-permute-start | bytes 1523720 | tf_op jit(solution)/shard_map/ppermute | solution.py:497
  36.6 9.0 %collective-permute-start.11 = (bf16[2,32,2816]{2,1,0:T(8,128)(2,1)S(1)}, bf16[2,32,2816]{2,1,0:T(8,128)(2,1)S(1)}, u32[]{:S(2)}, u32[]{:S(2)}) collective-permute-start(bf16[2,32,2816]{2,1,0:T(8,128)(2,1)S(1)} %get-tuple-element.43.refs_1_), channel_id=1, source_target_pairs={{0,1},{1,0},{2,3},{3,2},{4,5},{5,4},{6,7},{7,6},{8,9},{9,8},{10,11... | collective-permute-start | bytes 1081352 | tf_op jit(solution)/shard_map/ppermute | solution.py:497
  37.3 10.1 %collective-permute-start.7 = (bf16[2,16,3968]{2,1,0:T(8,128)(2,1)S(1)}, bf16[2,16,3968]{2,1,0:T(8,128)(2,1)S(1)}, u32[]{:S(2)}, u32[]{:S(2)}) collective-permute-start(bf16[2,16,3968]{2,1,0:T(8,128)(2,1)S(1)} %get-tuple-element.36.refs_0_), channel_id=1, source_target_pairs={{0,2},{1,3},{2,0},{3,1},{4,6},{5,7},{6,4},{7,5},{8,10},{9,11},{10,... | collective-permute-start | bytes 761864 | tf_op jit(solution)/shard_map/ppermute | solution.py:491
  45.6 7.2 %collective-permute-start.10 = (bf16[2,32,2304]{2,1,0:T(8,128)(2,1)S(1)}, bf16[2,32,2304]{2,1,0:T(8,128)(2,1)S(1)}, u32[]{:S(2)}, u32[]{:S(2)}) collective-permute-start(bf16[2,32,2304]{2,1,0:T(8,128)(2,1)S(1)} %get-tuple-element.44.refs_2_), channel_id=1, source_target_pairs={{0,1},{1,0},{2,3},{3,2},{4,5},{5,4},{6,7},{7,6},{8,9},{9,8},{10,11... | collective-permute-start | bytes 884744 | tf_op jit(solution)/shard_map/ppermute | solution.py:497
  45.8 7.0 %collective-permute-start.12 = (bf16[2,16,2816]{2,1,0:T(8,128)(2,1)S(1)}, bf16[2,16,2816]{2,1,0:T(8,128)(2,1)S(1)}, u32[]{:S(2)}, u32[]{:S(2)}) collective-permute-start(bf16[2,16,2816]{2,1,0:T(8,128)(2,1)S(1)} %get-tuple-element.47.refs_0_), channel_id=1, source_target_pairs={{0,2},{1,3},{2,0},{3,1},{4,6},{5,7},{6,4},{7,5},{8,10},{9,11},{10,... | collective-permute-start | bytes 540680 | tf_op jit(solution)/shard_map/ppermute | solution.py:491
  47.6 5.2 %collective-permute-start.8 = (bf16[1,8,1664]{2,1,0:T(8,128)(2,1)S(1)}, bf16[1,8,1664]{2,1,0:T(8,128)(2,1)S(1)}, u32[]{:S(2)}, u32[]{:S(2)}) collective-permute-start(bf16[1,8,1664]{2,1,0:T(8,128)(2,1)S(1)} %get-tuple-element.38), channel_id=1, source_target_pairs={{0,8},{4,12},{8,0},{12,4},{1,9},{5,13},{9,1},{13,5},{2,10},{6,14},... | collective-permute-start | bytes 79880 | tf_op jit(solution)/shard_map/ppermute | solution.py:494
  48.3 11.6 %copy-start = (bf16[2,1,1024,512]{3,2,1,0:T(8,128)(2,1)S(1)}, bf16[2,1,1024,512]{3,2,1,0:T(8,128)(2,1)}, u32[]{:S(2)}) copy-start(bf16[2,1,1024,512]{3,2,1,0:T(8,128)(2,1)} %param.15) | copy-start | bytes 6291460
  48.3 11.6 %copy-start.4 = (s32[4]{0:T(128)S(1)}, s32[4]{0:T(128)}, u32[]{:S(2)}) copy-start(s32[4]{0:T(128)} %copy-done.3) | copy-start | bytes 52
  48.3 11.6 %copy-start.5 = (s32[2,1]{0,1:T(1,128)S(1)}, s32[2,1]{0,1:T(1,128)}, u32[]{:S(2)}) copy-start(s32[2,1]{0,1:T(1,128)} %param.16) | copy-start | bytes 28
  52.9 1.7 %collective-permute-start.13 = (bf16[2,32,1792]{2,1,0:T(8,128)(2,1)S(1)}, bf16[2,32,1792]{2,1,0:T(8,128)(2,1)S(1)}, u32[]{:S(2)}, u32[]{:S(2)}) collective-permute-start(bf16[2,32,1792]{2,1,0:T(8,128)(2,1)S(1)} %get-tuple-element.50), channel_id=1, source_target_pairs={{0,1},{1,0},{2,3},{3,2},{4,5},{5,4},{6,7},{7,6},{8,9},{9,8},{10,11... | collective-permute-start | bytes 688136 | tf_op jit(solution)/shard_map/ppermute | solution.py:497
  52.9 9.5 %collective-permute-start.14 = (bf16[2,16,2304]{2,1,0:T(8,128)(2,1)S(1)}, bf16[2,16,2304]{2,1,0:T(8,128)(2,1)S(1)}, u32[]{:S(2)}, u32[]{:S(2)}) collective-permute-start(bf16[2,16,2304]{2,1,0:T(8,128)(2,1)S(1)} %get-tuple-element.56), channel_id=1, source_target_pairs={{0,2},{1,3},{2,0},{3,1},{4,6},{5,7},{6,4},{7,5},{8,10},{9,11},{10,... | collective-permute-start | bytes 442376 | tf_op jit(solution)/shard_map/ppermute | solution.py:491
  54.6 7.9 %collective-permute-start.15 = (bf16[2,16,1792]{2,1,0:T(8,128)(2,1)S(1)}, bf16[2,16,1792]{2,1,0:T(8,128)(2,1)S(1)}, u32[]{:S(2)}, u32[]{:S(2)}) collective-permute-start(bf16[2,16,1792]{2,1,0:T(8,128)(2,1)S(1)} %get-tuple-element.52.refs_2_.refs_4_), channel_id=1, source_target_pairs={{0,2},{1,3},{2,0},{3,1},{4,6},{5,7},{6,4},{7,5},{8,10},{9,11},{10,... | collective-permute-start | bytes 344072 | tf_op jit(solution)/shard_map/ppermute | solution.py:491
  56.1 3.9 %collective-permute-start.9 = (bf16[2,4,1664]{2,1,0:T(4,128)(2,1)S(1)}, bf16[2,4,1664]{2,1,0:T(4,128)(2,1)S(1)}, u32[]{:S(2)}, u32[]{:S(2)}) collective-permute-start(bf16[2,4,1664]{2,1,0:T(4,128)(2,1)S(1)} %get-tuple-element.40), channel_id=1, source_target_pairs={{0,4},{4,0},{8,12},{12,8},{1,5},{5,1},{9,13},{13,9},{2,6},{6,2},{1... | collective-permute-start | bytes 79880 | tf_op jit(solution)/shard_map/ppermute | solution.py:494

commit v7 on v6

--- a/solution.py
+++ b/solution.py
@@ -484,24 +484,21 @@
     local = cache.shape[0]
     block = local * size_x * steps
 
-    def shift_x(value, by):
-        return lax.ppermute(value, "gx", [(i, (i + by) % size_x) for i in range(size_x)])
-
     def shift_y(value, by):
         return lax.ppermute(value, "gy", [(i, (i + by) % size_y) for i in range(size_y)])
 
-    def swap_x(value, bit):
-        return lax.ppermute(value, "gx", [(i, i ^ bit) for i in range(size_x)])
-
-    def swap(value):
-        return lax.ppermute(value, "gy", [(i, i ^ 1) for i in range(size_y)])
+    def swap_x(value, bits):
+        return lax.ppermute(value, "gx", [(i, i ^ bits) for i in range(size_x)])
+
+    def swap(value, bits=1):
+        return lax.ppermute(value, "gy", [(i, i ^ bits) for i in range(size_y)])
 
     row = jnp.arange(2 * chips * block, dtype=jnp.int32)
     core = jnp.where(row < chips * block, 1 - me_y % 2, me_y % 2)
     chip = (me_y // 2 + 1 + row // block % chips) % chips
     sequence = (chip * 2 + core) * local + row % block // (size_x * steps)
     column = row // steps % size_x
-    source = (me_x - column) % size_x * (tall * steps) + sequence * steps + row % steps
+    source = (me_x ^ column) * (tall * steps) + sequence * steps + row % steps
     source = source[:, None]
     row = jnp.arange(block, dtype=jnp.int32)
     to = me_x ^ (row // (local * steps))
@@ -511,17 +508,18 @@
     while len(offsets) < size_x:
         bits.append(size_x // (2 * len(offsets)))
         offsets = offsets + [offset ^ bits[-1] for offset in offsets]
-    slots = jnp.array(offsets, jnp.int32) ^ me_x
+    number = jnp.arange(size_x, dtype=jnp.int32)
+    slots = me_x ^ sum((number >> place & 1) * bit for place, bit in enumerate(bits))
 
     weights = (w_gate, w_up)
     tiles = w_gate.shape[1] // TILE
     before = [tiles * share // 36 for share in (4, 9)]
     bounds = [0, before[1]] + [tiles * share // 36 for share in (20, 29, 36)]
     ahead = [before[1]] + [max(1, tiles * share // 36) for share in (5, 4, 4)] + [0]
-    gathered = [tokens] + [shift_x(tokens, by) for by in range(1, size_x)]
+    gathered = [tokens] + [swap_x(tokens, bits) for bits in range(1, size_x)]
     ring = load(weights, 0, before[0], None, (source, order, slots))
     rows, stats = partial_stats(gathered, ring)
-    every_stat = [stats] + [shift_y(stats, by) for by in range(1, size_y)]
+    every_stat = [stats] + [swap(stats, bits) for bits in range(1, size_y)]
     ring = load(weights, before[0], before[1], ring, (stats,))
     x = normed_rows(source, gain, rows, every_stat, ring)
 

time: 63.5 us -> 63.6 us (level)
  waiting for transfers between devices: 3.18 us -> 5.36 us
  starting transfers between devices: 17.9 us -> 16.6 us
  other arithmetic: 0.74 us -> 0.08 us
    ppermute x7 -> x4, starting transfers between devices: 8.24 us -> 5.2 us  [shift_y(): lax.ppermute(value, 'gy', [(i, (i + by) % size_y) for i in range(size_y)])]
    ppermute x9 -> x12, waiting for transfers between devices: 2.7 us -> 5.31 us  [the longest x5 5.29 us: swap_x(): return lax.ppermute(value, 'gx', [(i, i ^ bits) for i in range(size_x)])]
    ppermute x9 -> x12, starting transfers between devices: 9.61 us -> 11.4 us  [the longest x5 8.58 us: swap_x(): return lax.ppermute(value, 'gx', [(i, i ^ bits) for i in range(size_x)])]
    xor x1, other arithmetic: 0.66 us -> 0.01 us  [on_device(): me_x ^ sum(((number >> place & 1) * bit for place, bit in enumerate(bits)))]
  transfers between devices with their start and end apart: 16 -> 16, of which waited for: 2 -> 3; matrix products, arithmetic and copies ran while one was open for 1% -> 0% of each run, Pallas kernels for 51% -> 50%
where the time goes in v7:
time: 63.6 us; the launch traced here: 63.5 us
  Pallas kernels  40.6 us (64%)
  starting transfers between devices  16.6 us (26%)
  waiting for transfers between devices  5.36 us (8%)
  between operations  0.83 us (1%)
    pallas_call x3, Pallas kernels, wide_sums(): pl.pallas_call(functools.partial(wide_kernel, first, tiles, held, followi...  20.2 us
    pallas_call x2, Pallas kernels, load(): pl.pallas_call(functools.partial(load_kernel, first, last), out_shape=rin...  8.77 us
    ppermute x5, starting transfers between devices, swap_x(): return lax.ppermute(value, 'gx', [(i, i ^ bits) for i in range(size_x)])  8.58 us
    pallas_call x1, Pallas kernels, first_sums(): pl.pallas_call(functools.partial(first_kernel, tiles, following), out_sha...  7.05 us
    ppermute x5, waiting for transfers between devices, swap_x(): return lax.ppermute(value, 'gx', [(i, i ^ bits) for i in range(size_x)])  5.29 us
    ppermute x4, starting transfers between devices, shift_y(): lax.ppermute(value, 'gy', [(i, (i + by) % size_y) for i in range(size_y)])  5.2 us
    ppermute x7, starting transfers between devices, swap(): return lax.ppermute(value, 'gy', [(i, i ^ bits) for i in range(size_y)])  2.77 us
    pallas_call x1, Pallas kernels, attend(): pl.pallas_call(functools.partial(attend_kernel, count, steps, query_cols)...  2.48 us
  transfers between devices with their start and end apart: 16, of which 3 were waited for; matrix products, arithmetic and copies ran while one was open for 0% of the time, Pallas kernels for 50%

profile of v7, /device:TPU:0, one launch (start us, length us, event | category | flops | bytes accessed | tf_op | source)
XLA Modules:
  0.0 63.5 jit_solution(9897235811114428556)
XLA Ops:
  0.6 3.1 %collective-permute-start = (bf16[8,1,2,2304]{3,2,1,0:T(2,128)(2,1)}, bf16[8,1,2,2304]{3,2,1,0:T(2,128)(2,1)S(1)}, u32[]{:S(2)}, u32[]{:S(2)}) collective-permute-start(bf16[8,1,2,2304]{3,2,1,0:T(2,128)(2,1)} %refs_0_.1), channel_id=1, source_target_pairs={{0,4},{4,0},{8,12},{12,8},{1,5},{5,1},{9,13},{13,9},{2,6},{6,2},{1... | collective-permute-start | bytes 221192 | tf_op jit(solution)/shard_map/ppermute | solution.py:491
  3.7 2.6 %collective-permute-start.1 = (bf16[8,1,2,2304]{3,2,1,0:T(2,128)(2,1)}, bf16[8,1,2,2304]{3,2,1,0:T(2,128)(2,1)S(1)}, u32[]{:S(2)}, u32[]{:S(2)}) collective-permute-start(bf16[8,1,2,2304]{3,2,1,0:T(2,128)(2,1)} %refs_0_.1), channel_id=1, source_target_pairs={{0,8},{4,12},{8,0},{12,4},{1,9},{5,13},{9,1},{13,5},{2,10},{6,14},... | collective-permute-start | bytes 221192 | tf_op jit(solution)/shard_map/ppermute | solution.py:491
  6.3 0.0 collective-permute-start.2
  6.3 0.1 fusion.17.refs_0_.source_ref
  6.4 0.0 copy-start.3
  6.4 0.0 copy-start.1
  6.4 4.0 %shard_map.95.refs_4_.refs_0_ = bf16[10,2304,512]{2,1,0:T(8,128)(2,1)S(1)} custom-call(bf16[2304,9216]{1,0:T(8,128)(2,1)} %wg_ref.11, bf16[2304,9216]{1,0:T(8,128)(2,1)} %wu_ref.11, s32[64,1]{1,0:T(8,128)S(1)} %fusion.17.refs_0_.source_ref, s32[16,1]{1,0:T(8,128)S(1)} %fusion.38.refs_1_.source_ref, s32[4]{0:T(128)S(1)} %fusion.47.refs_2_.slot_ref), custom_call_target="tpu_custom_call" | custom-call | bytes 9437184 | tf_op jit(solution)/shard_map/pallas_call | solution.py:244
  10.5 0.0 copy-done.3
  10.5 0.0 collective-permute-done.refs_1_
  10.5 1.2 %collective-permute-done.1.refs_2_ = bf16[8,1,2,2304]{3,2,1,0:T(2,128)(2,1)S(1)} collective-permute-done((bf16[8,1,2,2304]{3,2,1,0:T(2,128)(2,1)}, bf16[8,1,2,2304]{3,2,1,0:T(2,128)(2,1)S(1)}, u32[]{:S(2)}, u32[]{:S(2)}) %collective-permute-start.1) | collective-permute-done | bytes 73760 | tf_op jit(solution)/shard_map/ppermute | solution.py:491
  11.7 1.0 %collective-permute-done.2.refs_3_ = bf16[8,1,2,2304]{3,2,1,0:T(2,128)(2,1)S(1)} collective-permute-done((bf16[8,1,2,2304]{3,2,1,0:T(2,128)(2,1)}, bf16[8,1,2,2304]{3,2,1,0:T(2,128)(2,1)S(1)}, u32[]{:S(2)}, u32[]{:S(2)}) %collective-permute-start.2) | collective-permute-done | bytes 73760 | tf_op jit(solution)/shard_map/ppermute | solution.py:491
  12.8 0.0 copy-done.1
  12.8 0.3 shard_map.96
  13.1 0.0 copy-start.2
  13.1 0.1 collective-permute-start.3
  13.2 1.6 %collective-permute-start.4 = (f32[64,128]{1,0:T(8,128)S(1)}, f32[64,128]{1,0:T(8,128)S(1)}, u32[]{:S(2)}, u32[]{:S(2)}) collective-permute-start(f32[64,128]{1,0:T(8,128)S(1)} %get-tuple-element.31.refs_1_.refs_0_), channel_id=1, source_target_pairs={{0,2},{1,3},{2,0},{3,1},{4,6},{5,7},{6,4},{7,5},{8,10},{9,11},{10,... | collective-permute-start | bytes 98312 | tf_op jit(solution)/shard_map/ppermute | solution.py:494
  14.8 0.3 collective-permute-start.5
  15.0 4.7 %shard_map.97.refs_4_._ = bf16[10,2304,512]{2,1,0:T(8,128)(2,1)S(1)} custom-call(bf16[2304,9216]{1,0:T(8,128)(2,1)} %wg_ref.11, bf16[2304,9216]{1,0:T(8,128)(2,1)} %wu_ref.11, bf16[10,2304,512]{2,1,0:T(8,128)(2,1)S(1)} %shard_map.95.refs_4_.refs_0_, f32[64,128]{1,0:T(8,128)S(1)} %get-tuple-element.31.refs_1_.refs_0_), custom_call_target="tpu_custom_call", output_to_operand_aliasing={{}: (2, {})} | custom-call | bytes 11796480 | tf_op jit(solution)/shard_map/pallas_call | solution.py:244
  19.8 0.0 collective-permute-done.3.refs_1_
  19.8 0.0 collective-permute-done.4.refs_2_
  19.8 0.0 collective-permute-done.5.refs_3_
  19.8 0.0 copy-done.2
  19.8 0.4 shard_map.98.x_ref
  20.2 7.1 %shard_map.99 = (bf16[2,32,3968]{2,1,0:T(8,128)(2,1)S(1)}, f32[2,32,2304]{2,1,0:T(8,128)S(1)}, f32[32,1664]{1,0:T(8,128)S(1)}, bf16[10,2304,512]{2,1,0:T(8,128)(2,1)S(1)}) custom-call(bf16[64,2304]{1,0:T(8,128)(2,1)S(1)} %shard_map.98.x_ref, bf16[2304,9216]{1,0:T(8,128)(2,1)} %wg_ref.11, ...), custom_call_target="tpu_custom_call", output_to_operand_aliasing={{3}: (5, {})} | custom-call | flops 1849688064 | bytes 21233664 | tf_op jit(solution)/shard_map/pallas_call | solution.py:334
  27.3 0.4 collective-permute-start.6
  27.7 8.4 %shard_map.103 = (bf16[2,32,2816]{2,1,0:T(8,128)(2,1)S(1)}, f32[2,32,2816]{2,1,0:T(8,128)S(1)}, bf16[10,2304,512]{2,1,0:T(8,128)(2,1)S(1)}) custom-call(bf16[64,2304]{1,0:T(8,128)(2,1)S(1)} %shard_map.98.x_ref, bf16[2304,9216]{1,0:T(8,128)(2,1)} %wg_ref.11, bf16[2304,9216]{1,0:T(8,128)(2,1)} %wu_ref.11, ...), custom_call_target="tpu_custom_call", output_to_operand_aliasing={{2}: (3, {})} | custom-call | flops 1660944384 | bytes 23592960 | tf_op jit(solution)/shard_map/pallas_call | solution.py:370
  36.1 0.2 collective-permute-start.11
  36.4 0.0 collective-permute-done.6.refs_0_
  36.4 0.1 shard_map.100
  36.5 1.6 %collective-permute-start.7 = (bf16[2,16,3968]{2,1,0:T(8,128)(2,1)S(1)}, bf16[2,16,3968]{2,1,0:T(8,128)(2,1)S(1)}, u32[]{:S(2)}, u32[]{:S(2)}) collective-permute-start(bf16[2,16,3968]{2,1,0:T(8,128)(2,1)S(1)} %get-tuple-element.36.refs_0_), channel_id=1, source_target_pairs={{0,2},{1,3},{2,0},{3,1},{4,6},{5,7},{6,4},{7,5},{8,10},{9,11},{10,... | collective-permute-start | bytes 761864 | tf_op jit(solution)/shard_map/ppermute | solution.py:488
  38.0 7.7 %shard_map.104 = (bf16[2,32,2304]{2,1,0:T(8,128)(2,1)S(1)}, f32[2,32,2304]{2,1,0:T(8,128)S(1)}, bf16[10,2304,512]{2,1,0:T(8,128)(2,1)S(1)}) custom-call(bf16[64,2304]{1,0:T(8,128)(2,1)S(1)} %shard_map.98.x_ref, bf16[2304,9216]{1,0:T(8,128)(2,1)} %wg_ref.11, bf16[2304,9216]{1,0:T(8,128)(2,1)} %wu_ref.11, ...), custom_call_target="tpu_custom_call", output_to_operand_aliasing={{2}: (3, {})} | custom-call | flops 1358954496 | bytes 21233664 | tf_op jit(solution)/shard_map/pallas_call | solution.py:370
  45.8 0.1 collective-permute-start.10
  45.9 0.0 collective-permute-done.11.refs_0_
  45.9 0.1 shard_map.105
  46.0 0.6 collective-permute-start.12
  46.6 0.0 collective-permute-done.7.refs_1_
  46.6 0.2 shard_map.101
  46.8 2.2 %collective-permute-start.8 = (bf16[1,8,1664]{2,1,0:T(8,128)(2,1)S(1)}, bf16[1,8,1664]{2,1,0:T(8,128)(2,1)S(1)}, u32[]{:S(2)}, u32[]{:S(2)}) collective-permute-start(bf16[1,8,1664]{2,1,0:T(8,128)(2,1)S(1)} %get-tuple-element.38), channel_id=1, source_target_pairs={{0,8},{4,12},{8,0},{12,4},{1,9},{5,13},{9,1},{13,5},{2,10},{6,14},... | collective-permute-start | bytes 79880 | tf_op jit(solution)/shard_map/ppermute | solution.py:491
  48.9 0.0 copy-start
  49.0 0.0 copy-start.4
  49.0 0.0 copy-start.5
  49.0 4.0 %shard_map.106 = (bf16[2,32,1792]{2,1,0:T(8,128)(2,1)S(1)}, f32[2,32,1792]{2,1,0:T(8,128)S(1)}, bf16[10,2304,512]{2,1,0:T(8,128)(2,1)S(1)}) custom-call(bf16[64,2304]{1,0:T(8,128)(2,1)S(1)} %shard_map.98.x_ref, bf16[2304,9216]{1,0:T(8,128)(2,1)} %wg_ref.11, bf16[2304,9216]{1,0:T(8,128)(2,1)} %wu_ref.11, ...), custom_call_target="tpu_custom_call", output_to_operand_aliasing={{2}: (3, {})} | custom-call | flops 1056964608 | bytes 7077888 | tf_op jit(solution)/shard_map/pallas_call | solution.py:370
  52.9 0.0 collective-permute-done.12.refs_3_
  53.0 0.0 collective-permute-done.8.came_ref.refs_2_
  53.0 0.0 collective-permute-done.10.refs_0_
  53.0 0.1 collective-permute-start.13
  53.1 1.6 %collective-permute-start.14 = (bf16[2,16,2304]{2,1,0:T(8,128)(2,1)S(1)}, bf16[2,16,2304]{2,1,0:T(8,128)(2,1)S(1)}, u32[]{:S(2)}, u32[]{:S(2)}) collective-permute-start(bf16[2,16,2304]{2,1,0:T(8,128)(2,1)S(1)} %get-tuple-element.56), channel_id=1, source_target_pairs={{0,2},{1,3},{2,0},{3,1},{4,6},{5,7},{6,4},{7,5},{8,10},{9,11},{10,... | collective-permute-start | bytes 442376 | tf_op jit(solution)/shard_map/ppermute | solution.py:488
  54.7 0.0 collective-permute-done.13.refs_0_
  54.7 1.5 %collective-permute-start.15 = (bf16[2,16,1792]{2,1,0:T(8,128)(2,1)S(1)}, bf16[2,16,1792]{2,1,0:T(8,128)(2,1)S(1)}, u32[]{:S(2)}, u32[]{:S(2)}) collective-permute-start(bf16[2,16,1792]{2,1,0:T(8,128)(2,1)S(1)} %get-tuple-element.52.refs_2_.refs_4_), channel_id=1, source_target_pairs={{0,2},{1,3},{2,0},{3,1},{4,6},{5,7},{6,4},{7,5},{8,10},{9,11},{10,... | collective-permute-start | bytes 344072 | tf_op jit(solution)/shard_map/ppermute | solution.py:488
  56.2 0.7 %collective-permute-start.9 = (bf16[2,4,1664]{2,1,0:T(4,128)(2,1)S(1)}, bf16[2,4,1664]{2,1,0:T(4,128)(2,1)S(1)}, u32[]{:S(2)}, u32[]{:S(2)}) collective-permute-start(bf16[2,4,1664]{2,1,0:T(4,128)(2,1)S(1)} %get-tuple-element.40), channel_id=1, source_target_pairs={{0,4},{4,0},{8,12},{12,8},{1,5},{5,1},{9,13},{13,9},{2,6},{6,2},{1... | collective-permute-start | bytes 79880 | tf_op jit(solution)/shard_map/ppermute | solution.py:491
  57.0 0.2 shard_map.110.refs_0_
  57.1 3.0 %collective-permute-done.9.refs_1_ = bf16[2,4,1664]{2,1,0:T(4,128)(2,1)S(1)} collective-permute-done((bf16[2,4,1664]{2,1,0:T(4,128)(2,1)S(1)}, bf16[2,4,1664]{2,1,0:T(4,128)(2,1)S(1)}, u32[]{:S(2)}, u32[]{:S(2)}) %collective-permute-start.9) | collective-permute-done | bytes 26656 | tf_op jit(solution)/shard_map/ppermute | solution.py:491
  60.1 0.0 copy-done
  60.1 0.0 copy-done.4
  60.1 0.0 copy-done.5
  60.2 2.5 %shard_map.109 = bf16[2,1,2,6144]{3,2,1,0:T(2,128)(2,1)} custom-call(s32[4]{0:T(128)S(1)} %copy-done.4, s32[2]{0:T(128)S(1)} %bitcast.3, bf16[2,1024,512]{2,1,0:T(8,128)(2,1)S(1)} %bitcast.2, bf16[2,4,1664]{2,1,0:T(4,128)(2,1)S(1)} %get-tuple-element.39.refs_0_, bf16[2,4,1664]{2,1,0:T(4,128)(2,1)S(1)} %collective-permute-done.9.refs_1_, ...), custom_call_target="tpu_custom_call" | custom-call | flops 100663296 | bytes 2097152 | tf_op jit(solution)/shard_map/pallas_call | solution.py:461
  62.6 0.0 collective-permute-done.14.refs_2_
  62.6 0.0 collective-permute-done.15.refs_4_
  62.6 0.9 %shard_map.111 = bf16[2,4,2,9216]{3,2,1,0:T(2,128)(2,1)} custom-call(bf16[2,4,2,5120]{3,2,1,0:T(2,128)(2,1)S(1)} %shard_map.110.refs_0_, f32[2,16,2304]{2,1,0:T(8,128)S(1)} %get-tuple-element.55.refs_1_, bf16[2,16,2304]{2,1,0:T(8,128)(2,1)S(1)} %collective-permute-done.14.refs_2_, f32[2,16,1792]{2,1,0:T(8,128)S(1)} %get-tuple-element.57.refs_3_, ...), custom_call_target="tpu_custom_call" | custom-call | flops 344064 | bytes 21504 | tf_op jit(solution)/shard_map/pallas_call | solution.py:185
  (5 shorter events, 0.1 us)
Async XLA Ops:
  0.6 9.9 %collective-permute-start = (bf16[8,1,2,2304]{3,2,1,0:T(2,128)(2,1)}, bf16[8,1,2,2304]{3,2,1,0:T(2,128)(2,1)S(1)}, u32[]{:S(2)}, u32[]{:S(2)}) collective-permute-start(bf16[8,1,2,2304]{3,2,1,0:T(2,128)(2,1)} %refs_0_.1), channel_id=1, source_target_pairs={{0,4},{4,0},{8,12},{12,8},{1,5},{5,1},{9,13},{13,9},{2,6},{6,2},{1... | collective-permute-start | bytes 221192 | tf_op jit(solution)/shard_map/ppermute | solution.py:491
  3.7 8.0 %collective-permute-start.1 = (bf16[8,1,2,2304]{3,2,1,0:T(2,128)(2,1)}, bf16[8,1,2,2304]{3,2,1,0:T(2,128)(2,1)S(1)}, u32[]{:S(2)}, u32[]{:S(2)}) collective-permute-start(bf16[8,1,2,2304]{3,2,1,0:T(2,128)(2,1)} %refs_0_.1), channel_id=1, source_target_pairs={{0,8},{4,12},{8,0},{12,4},{1,9},{5,13},{9,1},{13,5},{2,10},{6,14},... | collective-permute-start | bytes 221192 | tf_op jit(solution)/shard_map/ppermute | solution.py:491
  6.3 6.5 %collective-permute-start.2 = (bf16[8,1,2,2304]{3,2,1,0:T(2,128)(2,1)}, bf16[8,1,2,2304]{3,2,1,0:T(2,128)(2,1)S(1)}, u32[]{:S(2)}, u32[]{:S(2)}) collective-permute-start(bf16[8,1,2,2304]{3,2,1,0:T(2,128)(2,1)} %refs_0_.1), channel_id=1, source_target_pairs={{0,12},{4,8},{8,4},{12,0},{1,13},{5,9},{9,5},{13,1},{2,14},{6,10},... | collective-permute-start | bytes 221192 | tf_op jit(solution)/shard_map/ppermute | solution.py:491
  6.4 4.1 %copy-start.3 = (s32[4]{0:T(128)}, s32[4]{0:T(128)S(1)}, u32[]{:S(2)}) copy-start(s32[4]{0:T(128)S(1)} %fusion.47.refs_2_.slot_ref) | copy-start | bytes 52
  6.4 6.4 %copy-start.1 = (bf16[8,1,2,2304]{3,2,1,0:T(2,128)(2,1)S(1)}, bf16[8,1,2,2304]{3,2,1,0:T(2,128)(2,1)}, u32[]{:S(2)}) copy-start(bf16[8,1,2,2304]{3,2,1,0:T(2,128)(2,1)} %refs_0_.1) | copy-start | bytes 221188
  13.1 6.7 %copy-start.2 = (f32[2304]{0:T(1024)S(1)}, f32[2304]{0:T(1024)}, u32[]{:S(2)}) copy-start(f32[2304]{0:T(1024)} %gain_ref.1) | copy-start | bytes 27652
  13.1 6.7 %collective-permute-start.3 = (f32[64,128]{1,0:T(8,128)S(1)}, f32[64,128]{1,0:T(8,128)S(1)}, u32[]{:S(2)}, u32[]{:S(2)}) collective-permute-start(f32[64,128]{1,0:T(8,128)S(1)} %get-tuple-element.31.refs_1_.refs_0_), channel_id=1, source_target_pairs={{0,1},{1,0},{2,3},{3,2},{4,5},{5,4},{6,7},{7,6},{8,9},{9,8},{10,11... | collective-permute-start | bytes 98312 | tf_op jit(solution)/shard_map/ppermute | solution.py:494
  13.2 6.6 %collective-permute-start.4 = (f32[64,128]{1,0:T(8,128)S(1)}, f32[64,128]{1,0:T(8,128)S(1)}, u32[]{:S(2)}, u32[]{:S(2)}) collective-permute-start(f32[64,128]{1,0:T(8,128)S(1)} %get-tuple-element.31.refs_1_.refs_0_), channel_id=1, source_target_pairs={{0,2},{1,3},{2,0},{3,1},{4,6},{5,7},{6,4},{7,5},{8,10},{9,11},{10,... | collective-permute-start | bytes 98312 | tf_op jit(solution)/shard_map/ppermute | solution.py:494
  14.8 5.0 %collective-permute-start.5 = (f32[64,128]{1,0:T(8,128)S(1)}, f32[64,128]{1,0:T(8,128)S(1)}, u32[]{:S(2)}, u32[]{:S(2)}) collective-permute-start(f32[64,128]{1,0:T(8,128)S(1)} %get-tuple-element.31.refs_1_.refs_0_), channel_id=1, source_target_pairs={{0,3},{1,2},{2,1},{3,0},{4,7},{5,6},{6,5},{7,4},{8,11},{9,10},{10,... | collective-permute-start | bytes 98312 | tf_op jit(solution)/shard_map/ppermute | solution.py:494
  27.3 9.1 %collective-permute-start.6 = (bf16[2,32,3968]{2,1,0:T(8,128)(2,1)S(1)}, bf16[2,32,3968]{2,1,0:T(8,128)(2,1)S(1)}, u32[]{:S(2)}, u32[]{:S(2)}) collective-permute-start(bf16[2,32,3968]{2,1,0:T(8,128)(2,1)S(1)} %get-tuple-element.32.refs_0_), channel_id=1, source_target_pairs={{0,1},{1,0},{2,3},{3,2},{4,5},{5,4},{6,7},{7,6},{8,9},{9,8},{10,11... | collective-permute-start | bytes 1523720 | tf_op jit(solution)/shard_map/ppermute | solution.py:494
  36.1 9.8 %collective-permute-start.11 = (bf16[2,32,2816]{2,1,0:T(8,128)(2,1)S(1)}, bf16[2,32,2816]{2,1,0:T(8,128)(2,1)S(1)}, u32[]{:S(2)}, u32[]{:S(2)}) collective-permute-start(bf16[2,32,2816]{2,1,0:T(8,128)(2,1)S(1)} %get-tuple-element.43.refs_1_), channel_id=1, source_target_pairs={{0,1},{1,0},{2,3},{3,2},{4,5},{5,4},{6,7},{7,6},{8,9},{9,8},{10,11... | collective-permute-start | bytes 1081352 | tf_op jit(solution)/shard_map/ppermute | solution.py:494
  36.5 10.1 %collective-permute-start.7 = (bf16[2,16,3968]{2,1,0:T(8,128)(2,1)S(1)}, bf16[2,16,3968]{2,1,0:T(8,128)(2,1)S(1)}, u32[]{:S(2)}, u32[]{:S(2)}) collective-permute-start(bf16[2,16,3968]{2,1,0:T(8,128)(2,1)S(1)} %get-tuple-element.36.refs_0_), channel_id=1, source_target_pairs={{0,2},{1,3},{2,0},{3,1},{4,6},{5,7},{6,4},{7,5},{8,10},{9,11},{10,... | collective-permute-start | bytes 761864 | tf_op jit(solution)/shard_map/ppermute | solution.py:488
  45.8 7.2 %collective-permute-start.10 = (bf16[2,32,2304]{2,1,0:T(8,128)(2,1)S(1)}, bf16[2,32,2304]{2,1,0:T(8,128)(2,1)S(1)}, u32[]{:S(2)}, u32[]{:S(2)}) collective-permute-start(bf16[2,32,2304]{2,1,0:T(8,128)(2,1)S(1)} %get-tuple-element.44.refs_2_), channel_id=1, source_target_pairs={{0,1},{1,0},{2,3},{3,2},{4,5},{5,4},{6,7},{7,6},{8,9},{9,8},{10,11... | collective-permute-start | bytes 884744 | tf_op jit(solution)/shard_map/ppermute | solution.py:494
  46.0 7.0 %collective-permute-start.12 = (bf16[2,16,2816]{2,1,0:T(8,128)(2,1)S(1)}, bf16[2,16,2816]{2,1,0:T(8,128)(2,1)S(1)}, u32[]{:S(2)}, u32[]{:S(2)}) collective-permute-start(bf16[2,16,2816]{2,1,0:T(8,128)(2,1)S(1)} %get-tuple-element.47.refs_0_), channel_id=1, source_target_pairs={{0,2},{1,3},{2,0},{3,1},{4,6},{5,7},{6,4},{7,5},{8,10},{9,11},{10,... | collective-permute-start | bytes 540680 | tf_op jit(solution)/shard_map/ppermute | solution.py:488
  46.8 6.2 %collective-permute-start.8 = (bf16[1,8,1664]{2,1,0:T(8,128)(2,1)S(1)}, bf16[1,8,1664]{2,1,0:T(8,128)(2,1)S(1)}, u32[]{:S(2)}, u32[]{:S(2)}) collective-permute-start(bf16[1,8,1664]{2,1,0:T(8,128)(2,1)S(1)} %get-tuple-element.38), channel_id=1, source_target_pairs={{0,8},{4,12},{8,0},{12,4},{1,9},{5,13},{9,1},{13,5},{2,10},{6,14},... | collective-permute-start | bytes 79880 | tf_op jit(solution)/shard_map/ppermute | solution.py:491
  48.9 11.2 %copy-start = (bf16[2,1,1024,512]{3,2,1,0:T(8,128)(2,1)S(1)}, bf16[2,1,1024,512]{3,2,1,0:T(8,128)(2,1)}, u32[]{:S(2)}) copy-start(bf16[2,1,1024,512]{3,2,1,0:T(8,128)(2,1)} %param.14) | copy-start | bytes 6291460
  49.0 11.2 %copy-start.4 = (s32[4]{0:T(128)S(1)}, s32[4]{0:T(128)}, u32[]{:S(2)}) copy-start(s32[4]{0:T(128)} %copy-done.3) | copy-start | bytes 52
  49.0 11.2 %copy-start.5 = (s32[2,1]{0,1:T(1,128)S(1)}, s32[2,1]{0,1:T(1,128)}, u32[]{:S(2)}) copy-start(s32[2,1]{0,1:T(1,128)} %param.15) | copy-start | bytes 28
  53.0 1.7 %collective-permute-start.13 = (bf16[2,32,1792]{2,1,0:T(8,128)(2,1)S(1)}, bf16[2,32,1792]{2,1,0:T(8,128)(2,1)S(1)}, u32[]{:S(2)}, u32[]{:S(2)}) collective-permute-start(bf16[2,32,1792]{2,1,0:T(8,128)(2,1)S(1)} %get-tuple-element.50), channel_id=1, source_target_pairs={{0,1},{1,0},{2,3},{3,2},{4,5},{5,4},{6,7},{7,6},{8,9},{9,8},{10,11... | collective-permute-start | bytes 688136 | tf_op jit(solution)/shard_map/ppermute | solution.py:494
  53.1 9.5 %collective-permute-start.14 = (bf16[2,16,2304]{2,1,0:T(8,128)(2,1)S(1)}, bf16[2,16,2304]{2,1,0:T(8,128)(2,1)S(1)}, u32[]{:S(2)}, u32[]{:S(2)}) collective-permute-start(bf16[2,16,2304]{2,1,0:T(8,128)(2,1)S(1)} %get-tuple-element.56), channel_id=1, source_target_pairs={{0,2},{1,3},{2,0},{3,1},{4,6},{5,7},{6,4},{7,5},{8,10},{9,11},{10,... | collective-permute-start | bytes 442376 | tf_op jit(solution)/shard_map/ppermute | solution.py:488
  54.7 7.9 %collective-permute-start.15 = (bf16[2,16,1792]{2,1,0:T(8,128)(2,1)S(1)}, bf16[2,16,1792]{2,1,0:T(8,128)(2,1)S(1)}, u32[]{:S(2)}, u32[]{:S(2)}) collective-permute-start(bf16[2,16,1792]{2,1,0:T(8,128)(2,1)S(1)} %get-tuple-element.52.refs_2_.refs_4_), channel_id=1, source_target_pairs={{0,2},{1,3},{2,0},{3,1},{4,6},{5,7},{6,4},{7,5},{8,10},{9,11},{10,... | collective-permute-start | bytes 344072 | tf_op jit(solution)/shard_map/ppermute | solution.py:488
  56.2 3.9 %collective-permute-start.9 = (bf16[2,4,1664]{2,1,0:T(4,128)(2,1)S(1)}, bf16[2,4,1664]{2,1,0:T(4,128)(2,1)S(1)}, u32[]{:S(2)}, u32[]{:S(2)}) collective-permute-start(bf16[2,4,1664]{2,1,0:T(4,128)(2,1)S(1)} %get-tuple-element.40), channel_id=1, source_target_pairs={{0,4},{4,0},{8,12},{12,8},{1,5},{5,1},{9,13},{13,9},{2,6},{6,2},{1... | collective-permute-start | bytes 79880 | tf_op jit(solution)/shard_map/ppermute | solution.py:491

commit v8 on v7

--- a/solution.py
+++ b/solution.py
@@ -144,14 +144,14 @@
     )
     each = rows // count
     for index, ref in enumerate(out_refs):
-        ref[0] = turned[index * each : (index + 1) * each].astype(BF16)
+        ref[...] = turned[index * each : (index + 1) * each].astype(BF16)
 
 
 def query_rows(source, terms, count):
     rows, cols = terms[0].shape
     return pl.pallas_call(
         functools.partial(query_rows_kernel, count),
-        out_shape=[pltpu.VMEM((1, rows // count, cols), BF16)] * count,
+        out_shape=[pltpu.VMEM((rows // count, cols), BF16)] * count,
         in_specs=[whole()] * (1 + len(terms)),
         out_specs=[whole()] * count,
         compiler_params=params(),
@@ -388,35 +388,10 @@
     )(x, *in_hbm(weights), *in_vmem((ring,)), *after)
 
 
-def merge_kernel(kept_ref, came_ref, keep_ref, send_ref):
-    half = keep_ref.shape[1]
-    count = kept_ref.shape[0]
-    for index in range(2 * count):
-        both = (kept_ref[index] if index < count else came_ref[index - count]).astype(F32)
-        keep_ref[index] = both[:half].astype(BF16)
-        send_ref[index] = both[half:].astype(BF16)
-
-
-def merge(kept, came):
-    count, rows, cols = kept.shape
-    out = pltpu.VMEM((2 * count, rows // 2, cols), BF16)
-    return pl.pallas_call(
-        merge_kernel,
-        out_shape=(out, out),
-        in_specs=[whole()] * 2,
-        out_specs=(whole(), whole()),
-        compiler_params=params(),
-        cost_estimate=cost_of(kept, came),
-    )(kept, came)
-
-
 def attend_kernel(count, steps, query_cols, slot_ref, lengths_ref, cache_ref, *refs):
     part_refs, (out_ref, held, fresh) = refs[:count], refs[-3:]
-    each = part_refs[0].shape[0]
     for index, ref in enumerate(part_refs):
-        for source in range(each):
-            held[slot_ref[index * each + source]] = ref[source].astype(F32)
-    count = count * each
+        held[slot_ref[index]] = ref[...].astype(F32)
     pair_cols = held.shape[2] - query_cols
     heads = query_cols // HD
     scale = HD ** (-0.5)
@@ -457,14 +432,14 @@
 def attend(slots, lengths, cache, parts, steps, query_cols, after):
     batch = cache.shape[0]
     count = len(parts)
-    sources, rows, cols = parts[0].shape
+    rows, cols = parts[0].shape
     return pl.pallas_call(
         functools.partial(attend_kernel, count, steps, query_cols),
         out_shape=jax.ShapeDtypeStruct((batch, 1, steps, HEADS * HD), BF16),
         in_specs=[whole(pltpu.SMEM), whole(pltpu.SMEM)] + [whole()] * (1 + count) + [whole(pl.ANY)] * len(after),
         out_specs=whole(),
         scratch_shapes=[
-            pltpu.VMEM((count * sources, rows, cols), F32),
+            pltpu.VMEM((count, rows, cols), F32),
             pltpu.VMEM((batch, 8, 2 * HD), F32),
         ],
         compiler_params=params(),
@@ -504,16 +479,11 @@
     to = me_x ^ (row // (local * steps))
     order = row // steps % local * (size_x * steps) + to * steps + row % steps
     order = order[:, None]
-    bits, offsets = [], [0]
-    while len(offsets) < size_x:
-        bits.append(size_x // (2 * len(offsets)))
-        offsets = offsets + [offset ^ bits[-1] for offset in offsets]
-    number = jnp.arange(size_x, dtype=jnp.int32)
-    slots = me_x ^ sum((number >> place & 1) * bit for place, bit in enumerate(bits))
+    slots = me_x ^ jnp.arange(size_x, dtype=jnp.int32)
 
     weights = (w_gate, w_up)
     tiles = w_gate.shape[1] // TILE
-    before = [tiles * share // 36 for share in (4, 9)]
+    before = [tiles * share // 36 for share in (7, 9)]
     bounds = [0, before[1]] + [tiles * share // 36 for share in (20, 29, 36)]
     ahead = [before[1]] + [max(1, tiles * share // 36) for share in (5, 4, 4)] + [0]
     gathered = [tokens] + [swap_x(tokens, bits) for bits in range(1, size_x)]
@@ -540,15 +510,12 @@
     send_2, keep_2, ring = chunk_sums(2, ring, (parts_0[0], send_1))
     parts_1 = combine(chips, swap(send_1), keep_1)
     from_1 = to_chips(parts_1)
-    kept, leaving = query_rows(order, [parts_0[-1]] + from_0, 2)
-    came = swap_x(leaving, bits[0])
-
-    send_3, keep_3, _ = chunk_sums(3, ring, (parts_1[0], kept, send_2))
-    *parts_2, send_3 = combine(chips, swap(send_2), keep_2, None, send_3, (came, from_1[0]))
+    turned = query_rows(order, [parts_0[-1]] + from_0, size_x)
+    new = [turned[0]] + [swap_x(turned[bits], bits) for bits in range(1, size_x)]
+
+    send_3, keep_3, _ = chunk_sums(3, ring, (parts_1[0], turned[0], send_2))
+    *parts_2, send_3 = combine(chips, swap(send_2), keep_2, None, send_3, (*new[1:], from_1[0]))
     from_2 = to_chips(parts_2)
-    for bit in bits[1:]:
-        kept, leaving = merge(kept, came)
-        came = swap_x(leaving, bit)
     parts_3 = combine(chips, swap(send_3), keep_3)
     from_3 = to_chips(parts_3)
     half_done = gated(
@@ -561,7 +528,7 @@
         slots,
         lengths.reshape(local),
         cache.reshape(local, cache.shape[2], cache.shape[3]),
-        (kept, came),
+        new,
         steps,
         w_query.shape[1],
         (parts_3[0],),

time: 63.6 us -> 63.5 us (level)
  waiting for transfers between devices: 5.36 us -> 4.42 us
  starting transfers between devices: 16.6 us -> 17.4 us
    ppermute x5 -> x6, waiting for transfers between devices: 5.29 us -> 0.16 us  [swap_x(): return lax.ppermute(value, 'gx', [(i, i ^ bits) for i in range(size_x)])]
    ppermute x4, waiting for transfers between devices: 0.05 us -> 3.37 us  [shift_y(): lax.ppermute(value, 'gy', [(i, (i + by) % size_y) for i in range(size_y)])]
    ppermute x5 -> x6, starting transfers between devices: 8.58 us -> 10.1 us  [swap_x(): return lax.ppermute(value, 'gx', [(i, i ^ bits) for i in range(size_x)])]
    ppermute x7, waiting for transfers between devices: 0.02 us -> 0.88 us  [swap(): return lax.ppermute(value, 'gy', [(i, i ^ bits) for i in range(size_y)])]
    ppermute x4, starting transfers between devices: 5.2 us -> 4.46 us  [shift_y(): lax.ppermute(value, 'gy', [(i, (i + by) % size_y) for i in range(size_y)])]
  transfers between devices with their start and end apart: 16 -> 17, of which waited for: 3 -> 5; matrix products, arithmetic and copies ran while one was open for 0% -> 0% of each run, Pallas kernels for 50% -> 50%
where the time goes in v8:
time: 63.5 us; the launch traced here: 63.3 us
  Pallas kernels  40.6 us (64%)
  starting transfers between devices  17.4 us (27%)
  waiting for transfers between devices  4.42 us (7%)
  between operations  0.88 us (1%)
    pallas_call x3, Pallas kernels, wide_sums(): pl.pallas_call(functools.partial(wide_kernel, first, tiles, held, followi...  20.2 us
    ppermute x6, starting transfers between devices, swap_x(): return lax.ppermute(value, 'gx', [(i, i ^ bits) for i in range(size_x)])  10.1 us
    pallas_call x2, Pallas kernels, load(): pl.pallas_call(functools.partial(load_kernel, first, last), out_shape=rin...  8.73 us
    pallas_call x1, Pallas kernels, first_sums(): pl.pallas_call(functools.partial(first_kernel, tiles, following), out_sha...  7.05 us
    ppermute x4, starting transfers between devices, shift_y(): lax.ppermute(value, 'gy', [(i, (i + by) % size_y) for i in range(size_y)])  4.46 us
    ppermute x4, waiting for transfers between devices, shift_y(): lax.ppermute(value, 'gy', [(i, (i + by) % size_y) for i in range(size_y)])  3.37 us
    ppermute x7, starting transfers between devices, swap(): return lax.ppermute(value, 'gy', [(i, i ^ bits) for i in range(size_y)])  2.77 us
    pallas_call x1, Pallas kernels, attend(): pl.pallas_call(functools.partial(attend_kernel, count, steps, query_cols)...  2.48 us
  transfers between devices with their start and end apart: 17, of which 5 were waited for; matrix products, arithmetic and copies ran while one was open for 0% of the time, Pallas kernels for 50%

profile of v8, /device:TPU:0, one launch (start us, length us, event | category | flops | bytes accessed | tf_op | source)
XLA Modules:
  0.0 63.3 jit_solution(16850883506923494230)
XLA Ops:
  0.6 3.1 %collective-permute-start = (bf16[8,1,2,2304]{3,2,1,0:T(2,128)(2,1)}, bf16[8,1,2,2304]{3,2,1,0:T(2,128)(2,1)S(1)}, u32[]{:S(2)}, u32[]{:S(2)}) collective-permute-start(bf16[8,1,2,2304]{3,2,1,0:T(2,128)(2,1)} %refs_0_.1), channel_id=1, source_target_pairs={{0,4},{4,0},{8,12},{12,8},{1,5},{5,1},{9,13},{13,9},{2,6},{6,2},{1... | collective-permute-start | bytes 221192 | tf_op jit(solution)/shard_map/ppermute | solution.py:466
  3.7 2.6 %collective-permute-start.1 = (bf16[8,1,2,2304]{3,2,1,0:T(2,128)(2,1)}, bf16[8,1,2,2304]{3,2,1,0:T(2,128)(2,1)S(1)}, u32[]{:S(2)}, u32[]{:S(2)}) collective-permute-start(bf16[8,1,2,2304]{3,2,1,0:T(2,128)(2,1)} %refs_0_.1), channel_id=1, source_target_pairs={{0,8},{4,12},{8,0},{12,4},{1,9},{5,13},{9,1},{13,5},{2,10},{6,14},... | collective-permute-start | bytes 221192 | tf_op jit(solution)/shard_map/ppermute | solution.py:466
  6.3 0.0 collective-permute-start.2
  6.3 0.1 fusion.17.refs_0_.source_ref
  6.4 0.0 copy-start.3
  6.4 0.0 copy-start.1
  6.4 6.2 %shard_map.95.refs_4_.refs_0_ = bf16[10,2304,512]{2,1,0:T(8,128)(2,1)S(1)} custom-call(bf16[2304,9216]{1,0:T(8,128)(2,1)} %wg_ref.11, bf16[2304,9216]{1,0:T(8,128)(2,1)} %wu_ref.11, s32[64,1]{1,0:T(8,128)S(1)} %fusion.17.refs_0_.source_ref, s32[16,1]{1,0:T(8,128)S(1)} %fusion.38.refs_1_.source_ref, s32[4]{0:T(128)S(1)} %iota_xor_fusion.refs_2_.slot_ref), custom_call_target="tpu_custom_call" | custom-call | bytes 16515072 | tf_op jit(solution)/shard_map/pallas_call | solution.py:244
  12.6 0.0 copy-done.3
  12.6 0.0 collective-permute-done.refs_1_
  12.6 0.0 collective-permute-done.1.refs_2_
  12.6 0.1 collective-permute-done.2.refs_3_
  12.8 0.0 copy-done.1
  12.8 0.3 shard_map.96
  13.1 0.0 copy-start.2
  13.1 0.1 collective-permute-start.3
  13.2 1.7 %collective-permute-start.4 = (f32[64,128]{1,0:T(8,128)S(1)}, f32[64,128]{1,0:T(8,128)S(1)}, u32[]{:S(2)}, u32[]{:S(2)}) collective-permute-start(f32[64,128]{1,0:T(8,128)S(1)} %get-tuple-element.31.refs_1_.refs_0_), channel_id=1, source_target_pairs={{0,2},{1,3},{2,0},{3,1},{4,6},{5,7},{6,4},{7,5},{8,10},{9,11},{10,... | collective-permute-start | bytes 98312 | tf_op jit(solution)/shard_map/ppermute | solution.py:469
  14.8 0.2 collective-permute-start.5
  15.0 2.6 %shard_map.97.refs_4_._ = bf16[10,2304,512]{2,1,0:T(8,128)(2,1)S(1)} custom-call(bf16[2304,9216]{1,0:T(8,128)(2,1)} %wg_ref.11, bf16[2304,9216]{1,0:T(8,128)(2,1)} %wu_ref.11, bf16[10,2304,512]{2,1,0:T(8,128)(2,1)S(1)} %shard_map.95.refs_4_.refs_0_, f32[64,128]{1,0:T(8,128)S(1)} %get-tuple-element.31.refs_1_.refs_0_), custom_call_target="tpu_custom_call", output_to_operand_aliasing={{}: (2, {})} | custom-call | bytes 4718592 | tf_op jit(solution)/shard_map/pallas_call | solution.py:244
  17.6 0.0 collective-permute-done.3.refs_1_
  17.6 0.0 collective-permute-done.4.refs_2_
  17.6 0.6 collective-permute-done.5.refs_3_
  18.2 0.0 copy-done.2
  18.2 0.4 shard_map.98.x_ref
  18.6 7.1 %shard_map.99 = (bf16[2,32,3968]{2,1,0:T(8,128)(2,1)S(1)}, f32[2,32,2304]{2,1,0:T(8,128)S(1)}, f32[32,1664]{1,0:T(8,128)S(1)}, bf16[10,2304,512]{2,1,0:T(8,128)(2,1)S(1)}) custom-call(bf16[64,2304]{1,0:T(8,128)(2,1)S(1)} %shard_map.98.x_ref, bf16[2304,9216]{1,0:T(8,128)(2,1)} %wg_ref.11, ...), custom_call_target="tpu_custom_call", output_to_operand_aliasing={{3}: (5, {})} | custom-call | flops 1849688064 | bytes 21233664 | tf_op jit(solution)/shard_map/pallas_call | solution.py:334
  25.7 0.2 collective-permute-start.6
  25.9 8.4 %shard_map.102 = (bf16[2,32,2816]{2,1,0:T(8,128)(2,1)S(1)}, f32[2,32,2816]{2,1,0:T(8,128)S(1)}, bf16[10,2304,512]{2,1,0:T(8,128)(2,1)S(1)}) custom-call(bf16[64,2304]{1,0:T(8,128)(2,1)S(1)} %shard_map.98.x_ref, bf16[2304,9216]{1,0:T(8,128)(2,1)} %wg_ref.11, bf16[2304,9216]{1,0:T(8,128)(2,1)} %wu_ref.11, ...), custom_call_target="tpu_custom_call", output_to_operand_aliasing={{2}: (3, {})} | custom-call | flops 1660944384 | bytes 23592960 | tf_op jit(solution)/shard_map/pallas_call | solution.py:370
  34.3 0.4 collective-permute-start.12
  34.7 0.0 collective-permute-done.6.refs_0_
  34.8 0.1 shard_map.100
  34.8 1.1 %collective-permute-start.7 = (bf16[2,16,3968]{2,1,0:T(8,128)(2,1)S(1)}, bf16[2,16,3968]{2,1,0:T(8,128)(2,1)S(1)}, u32[]{:S(2)}, u32[]{:S(2)}) collective-permute-start(bf16[2,16,3968]{2,1,0:T(8,128)(2,1)S(1)} %get-tuple-element.36.refs_0_), channel_id=1, source_target_pairs={{0,2},{1,3},{2,0},{3,1},{4,6},{5,7},{6,4},{7,5},{8,10},{9,11},{10,... | collective-permute-start | bytes 761864 | tf_op jit(solution)/shard_map/ppermute | solution.py:463
  36.0 7.7 %shard_map.103 = (bf16[2,32,2304]{2,1,0:T(8,128)(2,1)S(1)}, f32[2,32,2304]{2,1,0:T(8,128)S(1)}, bf16[10,2304,512]{2,1,0:T(8,128)(2,1)S(1)}) custom-call(bf16[64,2304]{1,0:T(8,128)(2,1)S(1)} %shard_map.98.x_ref, bf16[2304,9216]{1,0:T(8,128)(2,1)} %wg_ref.11, bf16[2304,9216]{1,0:T(8,128)(2,1)} %wu_ref.11, ...), custom_call_target="tpu_custom_call", output_to_operand_aliasing={{2}: (3, {})} | custom-call | flops 1358954496 | bytes 21233664 | tf_op jit(solution)/shard_map/pallas_call | solution.py:370
  43.7 0.1 collective-permute-start.11
  43.8 0.0 collective-permute-done.12.refs_0_
  43.9 0.1 shard_map.104
  43.9 1.0 %collective-permute-start.13 = (bf16[2,16,2816]{2,1,0:T(8,128)(2,1)S(1)}, bf16[2,16,2816]{2,1,0:T(8,128)(2,1)S(1)}, u32[]{:S(2)}, u32[]{:S(2)}) collective-permute-start(bf16[2,16,2816]{2,1,0:T(8,128)(2,1)S(1)} %get-tuple-element.47.refs_0_), channel_id=1, source_target_pairs={{0,2},{1,3},{2,0},{3,1},{4,6},{5,7},{6,4},{7,5},{8,10},{9,11},{10,... | collective-permute-start | bytes 540680 | tf_op jit(solution)/shard_map/ppermute | solution.py:463
  44.9 0.0 collective-permute-done.7.refs_1_
  44.9 0.2 shard_map.101
  45.1 3.7 %collective-permute-start.10 = (bf16[4,1664]{1,0:T(4,128)(2,1)S(1)}, bf16[4,1664]{1,0:T(4,128)(2,1)S(1)}, u32[]{:S(2)}, u32[]{:S(2)}) collective-permute-start(bf16[4,1664]{1,0:T(4,128)(2,1)S(1)} %get-tuple-element.40), channel_id=1, source_target_pairs={{0,12},{4,8},{8,4},{12,0},{1,13},{5,9},{9,5},{13,1},{2,14},{6,10},... | collective-permute-start | bytes 39944 | tf_op jit(solution)/shard_map/ppermute | solution.py:466
  48.8 0.0 collective-permute-start.8
  48.8 0.8 %collective-permute-start.9 = (bf16[4,1664]{1,0:T(4,128)(2,1)S(1)}, bf16[4,1664]{1,0:T(4,128)(2,1)S(1)}, u32[]{:S(2)}, u32[]{:S(2)}) collective-permute-start(bf16[4,1664]{1,0:T(4,128)(2,1)S(1)} %get-tuple-element.39), channel_id=1, source_target_pairs={{0,8},{4,12},{8,0},{12,4},{1,9},{5,13},{9,1},{13,5},{2,10},{6,14},... | collective-permute-start | bytes 39944 | tf_op jit(solution)/shard_map/ppermute | solution.py:466
  49.6 0.0 copy-start
  49.6 0.0 copy-start.4
  49.6 0.0 copy-start.5
  49.6 4.0 %shard_map.105 = (bf16[2,32,1792]{2,1,0:T(8,128)(2,1)S(1)}, f32[2,32,1792]{2,1,0:T(8,128)S(1)}, bf16[10,2304,512]{2,1,0:T(8,128)(2,1)S(1)}) custom-call(bf16[64,2304]{1,0:T(8,128)(2,1)S(1)} %shard_map.98.x_ref, bf16[2304,9216]{1,0:T(8,128)(2,1)} %wg_ref.11, bf16[2304,9216]{1,0:T(8,128)(2,1)} %wu_ref.11, ...), custom_call_target="tpu_custom_call", output_to_operand_aliasing={{2}: (3, {})} | custom-call | flops 1056964608 | bytes 7077888 | tf_op jit(solution)/shard_map/pallas_call | solution.py:370
  53.6 0.0 collective-permute-done.13.refs_5_.refs_3_
  53.6 0.0 collective-permute-done.10.refs_4_.refs_3_
  53.6 0.0 collective-permute-done.8.refs_2_.refs_1_
  53.6 0.0 collective-permute-done.9.refs_3_.refs_2_
  53.6 0.0 collective-permute-done.11.refs_0_
  53.6 0.1 shard_map.106
  53.7 0.1 collective-permute-start.14
  53.8 1.2 %collective-permute-start.15 = (bf16[2,16,2304]{2,1,0:T(8,128)(2,1)S(1)}, bf16[2,16,2304]{2,1,0:T(8,128)(2,1)S(1)}, u32[]{:S(2)}, u32[]{:S(2)}) collective-permute-start(bf16[2,16,2304]{2,1,0:T(8,128)(2,1)S(1)} %get-tuple-element.56), channel_id=1, source_target_pairs={{0,2},{1,3},{2,0},{3,1},{4,6},{5,7},{6,4},{7,5},{8,10},{9,11},{10,... | collective-permute-start | bytes 442376 | tf_op jit(solution)/shard_map/ppermute | solution.py:463
  54.9 0.3 collective-permute-done.14.refs_0_
  55.3 1.2 %collective-permute-start.16 = (bf16[2,16,1792]{2,1,0:T(8,128)(2,1)S(1)}, bf16[2,16,1792]{2,1,0:T(8,128)(2,1)S(1)}, u32[]{:S(2)}, u32[]{:S(2)}) collective-permute-start(bf16[2,16,1792]{2,1,0:T(8,128)(2,1)S(1)} %get-tuple-element.52.refs_4_), channel_id=1, source_target_pairs={{0,2},{1,3},{2,0},{3,1},{4,6},{5,7},{6,4},{7,5},{8,10},{9,11},{10,... | collective-permute-start | bytes 344072 | tf_op jit(solution)/shard_map/ppermute | solution.py:463
  56.4 0.2 shard_map.109.refs_0_
  56.6 0.0 copy-done
  56.6 0.0 copy-done.4
  56.6 0.0 copy-done.5
  56.6 2.5 %shard_map.108 = bf16[2,1,2,6144]{3,2,1,0:T(2,128)(2,1)} custom-call(s32[4]{0:T(128)S(1)} %copy-done.4, s32[2]{0:T(128)S(1)} %bitcast.3, bf16[2,1024,512]{2,1,0:T(8,128)(2,1)S(1)} %bitcast.2, bf16[4,1664]{1,0:T(4,128)(2,1)S(1)} %get-tuple-element.37.refs_1_.refs_0_, bf16[4,1664]{1,0:T(4,128)(2,1)S(1)} %collective-permute-done.8.refs_2_.refs_1_, ...), custom_call_target="tpu_custom_call" | custom-call | flops 100663296 | bytes 2097152 | tf_op jit(solution)/shard_map/pallas_call | solution.py:436
  59.1 1.4 %collective-permute-done.15.refs_2_ = bf16[2,16,2304]{2,1,0:T(8,128)(2,1)S(1)} collective-permute-done((bf16[2,16,2304]{2,1,0:T(8,128)(2,1)S(1)}, bf16[2,16,2304]{2,1,0:T(8,128)(2,1)S(1)}, u32[]{:S(2)}, u32[]{:S(2)}) %collective-permute-start.15) | collective-permute-done | bytes 147488 | tf_op jit(solution)/shard_map/ppermute | solution.py:463
  60.5 2.0 %collective-permute-done.16.refs_4_ = bf16[2,16,1792]{2,1,0:T(8,128)(2,1)S(1)} collective-permute-done((bf16[2,16,1792]{2,1,0:T(8,128)(2,1)S(1)}, bf16[2,16,1792]{2,1,0:T(8,128)(2,1)S(1)}, u32[]{:S(2)}, u32[]{:S(2)}) %collective-permute-start.16) | collective-permute-done | bytes 114720 | tf_op jit(solution)/shard_map/ppermute | solution.py:463
  62.5 0.9 %shard_map.110 = bf16[2,4,2,9216]{3,2,1,0:T(2,128)(2,1)} custom-call(bf16[2,4,2,5120]{3,2,1,0:T(2,128)(2,1)S(1)} %shard_map.109.refs_0_, f32[2,16,2304]{2,1,0:T(8,128)S(1)} %get-tuple-element.55.refs_1_, bf16[2,16,2304]{2,1,0:T(8,128)(2,1)S(1)} %collective-permute-done.15.refs_2_, f32[2,16,1792]{2,1,0:T(8,128)S(1)} %get-tuple-element.57.refs_3_, ...), custom_call_target="tpu_custom_call" | custom-call | flops 344064 | bytes 21504 | tf_op jit(solution)/shard_map/pallas_call | solution.py:185
  (3 shorter events, 0.1 us)
Async XLA Ops:
  0.6 12.0 %collective-permute-start = (bf16[8,1,2,2304]{3,2,1,0:T(2,128)(2,1)}, bf16[8,1,2,2304]{3,2,1,0:T(2,128)(2,1)S(1)}, u32[]{:S(2)}, u32[]{:S(2)}) collective-permute-start(bf16[8,1,2,2304]{3,2,1,0:T(2,128)(2,1)} %refs_0_.1), channel_id=1, source_target_pairs={{0,4},{4,0},{8,12},{12,8},{1,5},{5,1},{9,13},{13,9},{2,6},{6,2},{1... | collective-permute-start | bytes 221192 | tf_op jit(solution)/shard_map/ppermute | solution.py:466
  3.7 8.9 %collective-permute-start.1 = (bf16[8,1,2,2304]{3,2,1,0:T(2,128)(2,1)}, bf16[8,1,2,2304]{3,2,1,0:T(2,128)(2,1)S(1)}, u32[]{:S(2)}, u32[]{:S(2)}) collective-permute-start(bf16[8,1,2,2304]{3,2,1,0:T(2,128)(2,1)} %refs_0_.1), channel_id=1, source_target_pairs={{0,8},{4,12},{8,0},{12,4},{1,9},{5,13},{9,1},{13,5},{2,10},{6,14},... | collective-permute-start | bytes 221192 | tf_op jit(solution)/shard_map/ppermute | solution.py:466
  6.3 6.5 %collective-permute-start.2 = (bf16[8,1,2,2304]{3,2,1,0:T(2,128)(2,1)}, bf16[8,1,2,2304]{3,2,1,0:T(2,128)(2,1)S(1)}, u32[]{:S(2)}, u32[]{:S(2)}) collective-permute-start(bf16[8,1,2,2304]{3,2,1,0:T(2,128)(2,1)} %refs_0_.1), channel_id=1, source_target_pairs={{0,12},{4,8},{8,4},{12,0},{1,13},{5,9},{9,5},{13,1},{2,14},{6,10},... | collective-permute-start | bytes 221192 | tf_op jit(solution)/shard_map/ppermute | solution.py:466
  6.4 6.2 %copy-start.3 = (s32[4]{0:T(128)}, s32[4]{0:T(128)S(1)}, u32[]{:S(2)}) copy-start(s32[4]{0:T(128)S(1)} %iota_xor_fusion.refs_2_.slot_ref) | copy-start | bytes 52
  6.4 6.4 %copy-start.1 = (bf16[8,1,2,2304]{3,2,1,0:T(2,128)(2,1)S(1)}, bf16[8,1,2,2304]{3,2,1,0:T(2,128)(2,1)}, u32[]{:S(2)}) copy-start(bf16[8,1,2,2304]{3,2,1,0:T(2,128)(2,1)} %refs_0_.1) | copy-start | bytes 221188
  13.1 5.1 %copy-start.2 = (f32[2304]{0:T(1024)S(1)}, f32[2304]{0:T(1024)}, u32[]{:S(2)}) copy-start(f32[2304]{0:T(1024)} %gain_ref.1) | copy-start | bytes 27652
  13.1 4.5 %collective-permute-start.3 = (f32[64,128]{1,0:T(8,128)S(1)}, f32[64,128]{1,0:T(8,128)S(1)}, u32[]{:S(2)}, u32[]{:S(2)}) collective-permute-start(f32[64,128]{1,0:T(8,128)S(1)} %get-tuple-element.31.refs_1_.refs_0_), channel_id=1, source_target_pairs={{0,1},{1,0},{2,3},{3,2},{4,5},{5,4},{6,7},{7,6},{8,9},{9,8},{10,11... | collective-permute-start | bytes 98312 | tf_op jit(solution)/shard_map/ppermute | solution.py:469
  13.2 4.4 %collective-permute-start.4 = (f32[64,128]{1,0:T(8,128)S(1)}, f32[64,128]{1,0:T(8,128)S(1)}, u32[]{:S(2)}, u32[]{:S(2)}) collective-permute-start(f32[64,128]{1,0:T(8,128)S(1)} %get-tuple-element.31.refs_1_.refs_0_), channel_id=1, source_target_pairs={{0,2},{1,3},{2,0},{3,1},{4,6},{5,7},{6,4},{7,5},{8,10},{9,11},{10,... | collective-permute-start | bytes 98312 | tf_op jit(solution)/shard_map/ppermute | solution.py:469
  14.8 3.3 %collective-permute-start.5 = (f32[64,128]{1,0:T(8,128)S(1)}, f32[64,128]{1,0:T(8,128)S(1)}, u32[]{:S(2)}, u32[]{:S(2)}) collective-permute-start(f32[64,128]{1,0:T(8,128)S(1)} %get-tuple-element.31.refs_1_.refs_0_), channel_id=1, source_target_pairs={{0,3},{1,2},{2,1},{3,0},{4,7},{5,6},{6,5},{7,4},{8,11},{9,10},{10,... | collective-permute-start | bytes 98312 | tf_op jit(solution)/shard_map/ppermute | solution.py:469
  25.7 9.1 %collective-permute-start.6 = (bf16[2,32,3968]{2,1,0:T(8,128)(2,1)S(1)}, bf16[2,32,3968]{2,1,0:T(8,128)(2,1)S(1)}, u32[]{:S(2)}, u32[]{:S(2)}) collective-permute-start(bf16[2,32,3968]{2,1,0:T(8,128)(2,1)S(1)} %get-tuple-element.32.refs_0_), channel_id=1, source_target_pairs={{0,1},{1,0},{2,3},{3,2},{4,5},{5,4},{6,7},{7,6},{8,9},{9,8},{10,11... | collective-permute-start | bytes 1523720 | tf_op jit(solution)/shard_map/ppermute | solution.py:469
  34.3 9.5 %collective-permute-start.12 = (bf16[2,32,2816]{2,1,0:T(8,128)(2,1)S(1)}, bf16[2,32,2816]{2,1,0:T(8,128)(2,1)S(1)}, u32[]{:S(2)}, u32[]{:S(2)}) collective-permute-start(bf16[2,32,2816]{2,1,0:T(8,128)(2,1)S(1)} %get-tuple-element.43.refs_1_), channel_id=1, source_target_pairs={{0,1},{1,0},{2,3},{3,2},{4,5},{5,4},{6,7},{7,6},{8,9},{9,8},{10,11... | collective-permute-start | bytes 1081352 | tf_op jit(solution)/shard_map/ppermute | solution.py:469
  34.8 10.1 %collective-permute-start.7 = (bf16[2,16,3968]{2,1,0:T(8,128)(2,1)S(1)}, bf16[2,16,3968]{2,1,0:T(8,128)(2,1)S(1)}, u32[]{:S(2)}, u32[]{:S(2)}) collective-permute-start(bf16[2,16,3968]{2,1,0:T(8,128)(2,1)S(1)} %get-tuple-element.36.refs_0_), channel_id=1, source_target_pairs={{0,2},{1,3},{2,0},{3,1},{4,6},{5,7},{6,4},{7,5},{8,10},{9,11},{10,... | collective-permute-start | bytes 761864 | tf_op jit(solution)/shard_map/ppermute | solution.py:463
  43.7 9.9 %collective-permute-start.11 = (bf16[2,32,2304]{2,1,0:T(8,128)(2,1)S(1)}, bf16[2,32,2304]{2,1,0:T(8,128)(2,1)S(1)}, u32[]{:S(2)}, u32[]{:S(2)}) collective-permute-start(bf16[2,32,2304]{2,1,0:T(8,128)(2,1)S(1)} %get-tuple-element.44.refs_2_), channel_id=1, source_target_pairs={{0,1},{1,0},{2,3},{3,2},{4,5},{5,4},{6,7},{7,6},{8,9},{9,8},{10,11... | collective-permute-start | bytes 884744 | tf_op jit(solution)/shard_map/ppermute | solution.py:469
  43.9 9.6 %collective-permute-start.13 = (bf16[2,16,2816]{2,1,0:T(8,128)(2,1)S(1)}, bf16[2,16,2816]{2,1,0:T(8,128)(2,1)S(1)}, u32[]{:S(2)}, u32[]{:S(2)}) collective-permute-start(bf16[2,16,2816]{2,1,0:T(8,128)(2,1)S(1)} %get-tuple-element.47.refs_0_), channel_id=1, source_target_pairs={{0,2},{1,3},{2,0},{3,1},{4,6},{5,7},{6,4},{7,5},{8,10},{9,11},{10,... | collective-permute-start | bytes 540680 | tf_op jit(solution)/shard_map/ppermute | solution.py:463
  45.1 8.4 %collective-permute-start.10 = (bf16[4,1664]{1,0:T(4,128)(2,1)S(1)}, bf16[4,1664]{1,0:T(4,128)(2,1)S(1)}, u32[]{:S(2)}, u32[]{:S(2)}) collective-permute-start(bf16[4,1664]{1,0:T(4,128)(2,1)S(1)} %get-tuple-element.40), channel_id=1, source_target_pairs={{0,12},{4,8},{8,4},{12,0},{1,13},{5,9},{9,5},{13,1},{2,14},{6,10},... | collective-permute-start | bytes 39944 | tf_op jit(solution)/shard_map/ppermute | solution.py:466
  48.8 4.8 %collective-permute-start.8 = (bf16[4,1664]{1,0:T(4,128)(2,1)S(1)}, bf16[4,1664]{1,0:T(4,128)(2,1)S(1)}, u32[]{:S(2)}, u32[]{:S(2)}) collective-permute-start(bf16[4,1664]{1,0:T(4,128)(2,1)S(1)} %get-tuple-element.38), channel_id=1, source_target_pairs={{0,4},{4,0},{8,12},{12,8},{1,5},{5,1},{9,13},{13,9},{2,6},{6,2},{1... | collective-permute-start | bytes 39944 | tf_op jit(solution)/shard_map/ppermute | solution.py:466
  48.8 4.8 %collective-permute-start.9 = (bf16[4,1664]{1,0:T(4,128)(2,1)S(1)}, bf16[4,1664]{1,0:T(4,128)(2,1)S(1)}, u32[]{:S(2)}, u32[]{:S(2)}) collective-permute-start(bf16[4,1664]{1,0:T(4,128)(2,1)S(1)} %get-tuple-element.39), channel_id=1, source_target_pairs={{0,8},{4,12},{8,0},{12,4},{1,9},{5,13},{9,1},{13,5},{2,10},{6,14},... | collective-permute-start | bytes 39944 | tf_op jit(solution)/shard_map/ppermute | solution.py:466
  49.6 7.0 %copy-start = (bf16[2,1,1024,512]{3,2,1,0:T(8,128)(2,1)S(1)}, bf16[2,1,1024,512]{3,2,1,0:T(8,128)(2,1)}, u32[]{:S(2)}) copy-start(bf16[2,1,1024,512]{3,2,1,0:T(8,128)(2,1)} %param.14) | copy-start | bytes 6291460
  49.6 7.0 %copy-start.4 = (s32[4]{0:T(128)S(1)}, s32[4]{0:T(128)}, u32[]{:S(2)}) copy-start(s32[4]{0:T(128)} %copy-done.3) | copy-start | bytes 52
  49.6 7.0 %copy-start.5 = (s32[2,1]{0,1:T(1,128)S(1)}, s32[2,1]{0,1:T(1,128)}, u32[]{:S(2)}) copy-start(s32[2,1]{0,1:T(1,128)} %param.15) | copy-start | bytes 28
  53.7 1.6 %collective-permute-start.14 = (bf16[2,32,1792]{2,1,0:T(8,128)(2,1)S(1)}, bf16[2,32,1792]{2,1,0:T(8,128)(2,1)S(1)}, u32[]{:S(2)}, u32[]{:S(2)}) collective-permute-start(bf16[2,32,1792]{2,1,0:T(8,128)(2,1)S(1)} %get-tuple-element.50), channel_id=1, source_target_pairs={{0,1},{1,0},{2,3},{3,2},{4,5},{5,4},{6,7},{7,6},{8,9},{9,8},{10,11... | collective-permute-start | bytes 688136 | tf_op jit(solution)/shard_map/ppermute | solution.py:469
  53.8 6.7 %collective-permute-start.15 = (bf16[2,16,2304]{2,1,0:T(8,128)(2,1)S(1)}, bf16[2,16,2304]{2,1,0:T(8,128)(2,1)S(1)}, u32[]{:S(2)}, u32[]{:S(2)}) collective-permute-start(bf16[2,16,2304]{2,1,0:T(8,128)(2,1)S(1)} %get-tuple-element.56), channel_id=1, source_target_pairs={{0,2},{1,3},{2,0},{3,1},{4,6},{5,7},{6,4},{7,5},{8,10},{9,11},{10,... | collective-permute-start | bytes 442376 | tf_op jit(solution)/shard_map/ppermute | solution.py:463
  55.3 7.2 %collective-permute-start.16 = (bf16[2,16,1792]{2,1,0:T(8,128)(2,1)S(1)}, bf16[2,16,1792]{2,1,0:T(8,128)(2,1)S(1)}, u32[]{:S(2)}, u32[]{:S(2)}) collective-permute-start(bf16[2,16,1792]{2,1,0:T(8,128)(2,1)S(1)} %get-tuple-element.52.refs_4_), channel_id=1, source_target_pairs={{0,2},{1,3},{2,0},{3,1},{4,6},{5,7},{6,4},{7,5},{8,10},{9,11},{10,... | collective-permute-start | bytes 344072 | tf_op jit(solution)/shard_map/ppermute | solution.py:463

commit v9 on v8

--- a/solution.py
+++ b/solution.py
@@ -484,7 +484,7 @@
     weights = (w_gate, w_up)
     tiles = w_gate.shape[1] // TILE
     before = [tiles * share // 36 for share in (7, 9)]
-    bounds = [0, before[1]] + [tiles * share // 36 for share in (20, 29, 36)]
+    bounds = [0, before[1]] + [tiles * share // 36 for share in (23, 31, 36)]
     ahead = [before[1]] + [max(1, tiles * share // 36) for share in (5, 4, 4)] + [0]
     gathered = [tokens] + [swap_x(tokens, bits) for bits in range(1, size_x)]
     ring = load(weights, 0, before[0], None, (source, order, slots))

time: 63.5 us -> 63.6 us (level)
    ppermute x4, waiting for transfers between devices: 3.37 us -> 2.41 us  [shift_y(): lax.ppermute(value, 'gy', [(i, (i + by) % size_y) for i in range(size_y)])]
    ppermute x6, waiting for transfers between devices: 0.16 us -> 1.11 us  [swap_x(): return lax.ppermute(value, 'gx', [(i, i ^ bits) for i in range(size_x)])]
  transfers between devices with their start and end apart: 17 -> 17, of which waited for: 5 -> 6; matrix products, arithmetic and copies ran while one was open for 0% -> 0% of each run, Pallas kernels for 50% -> 51%
where the time goes in v9:
time: 63.6 us; the launch traced here: 63.4 us
  Pallas kernels  40.8 us (64%)
  starting transfers between devices  17.4 us (27%)
  waiting for transfers between devices  4.31 us (7%)
  between operations  0.87 us (1%)
    pallas_call x3, Pallas kernels, wide_sums(): pl.pallas_call(functools.partial(wide_kernel, first, tiles, held, followi...  20.4 us
    ppermute x6, starting transfers between devices, swap_x(): return lax.ppermute(value, 'gx', [(i, i ^ bits) for i in range(size_x)])  10.1 us
    pallas_call x2, Pallas kernels, load(): pl.pallas_call(functools.partial(load_kernel, first, last), out_shape=rin...  8.73 us
    pallas_call x1, Pallas kernels, first_sums(): pl.pallas_call(functools.partial(first_kernel, tiles, following), out_sha...  7.05 us
    ppermute x4, starting transfers between devices, shift_y(): lax.ppermute(value, 'gy', [(i, (i + by) % size_y) for i in range(size_y)])  4.46 us
    ppermute x7, starting transfers between devices, swap(): return lax.ppermute(value, 'gy', [(i, i ^ bits) for i in range(size_y)])  2.77 us
    pallas_call x1, Pallas kernels, attend(): pl.pallas_call(functools.partial(attend_kernel, count, steps, query_cols)...  2.47 us
    ppermute x4, waiting for transfers between devices, shift_y(): lax.ppermute(value, 'gy', [(i, (i + by) % size_y) for i in range(size_y)])  2.41 us
  transfers between devices with their start and end apart: 17, of which 6 were waited for; matrix products, arithmetic and copies ran while one was open for 0% of the time, Pallas kernels for 51%

profile of v9, /device:TPU:0, one launch (start us, length us, event | category | flops | bytes accessed | tf_op | source)
XLA Modules:
  0.0 63.4 jit_solution(16677282999416529496)
XLA Ops:
  0.6 3.1 %collective-permute-start = (bf16[8,1,2,2304]{3,2,1,0:T(2,128)(2,1)}, bf16[8,1,2,2304]{3,2,1,0:T(2,128)(2,1)S(1)}, u32[]{:S(2)}, u32[]{:S(2)}) collective-permute-start(bf16[8,1,2,2304]{3,2,1,0:T(2,128)(2,1)} %refs_0_.1), channel_id=1, source_target_pairs={{0,4},{4,0},{8,12},{12,8},{1,5},{5,1},{9,13},{13,9},{2,6},{6,2},{1... | collective-permute-start | bytes 221192 | tf_op jit(solution)/shard_map/ppermute | solution.py:466
  3.7 2.6 %collective-permute-start.1 = (bf16[8,1,2,2304]{3,2,1,0:T(2,128)(2,1)}, bf16[8,1,2,2304]{3,2,1,0:T(2,128)(2,1)S(1)}, u32[]{:S(2)}, u32[]{:S(2)}) collective-permute-start(bf16[8,1,2,2304]{3,2,1,0:T(2,128)(2,1)} %refs_0_.1), channel_id=1, source_target_pairs={{0,8},{4,12},{8,0},{12,4},{1,9},{5,13},{9,1},{13,5},{2,10},{6,14},... | collective-permute-start | bytes 221192 | tf_op jit(solution)/shard_map/ppermute | solution.py:466
  6.3 0.0 collective-permute-start.2
  6.3 0.1 fusion.17.refs_0_.source_ref
  6.4 0.0 copy-start.3
  6.4 0.0 copy-start.1
  6.4 6.2 %shard_map.95.refs_4_.refs_0_ = bf16[10,2304,512]{2,1,0:T(8,128)(2,1)S(1)} custom-call(bf16[2304,9216]{1,0:T(8,128)(2,1)} %wg_ref.11, bf16[2304,9216]{1,0:T(8,128)(2,1)} %wu_ref.11, s32[64,1]{1,0:T(8,128)S(1)} %fusion.17.refs_0_.source_ref, s32[16,1]{1,0:T(8,128)S(1)} %fusion.38.refs_1_.source_ref, s32[4]{0:T(128)S(1)} %iota_xor_fusion.refs_2_.slot_ref), custom_call_target="tpu_custom_call" | custom-call | bytes 16515072 | tf_op jit(solution)/shard_map/pallas_call | solution.py:244
  12.6 0.0 copy-done.3
  12.6 0.0 collective-permute-done.refs_1_
  12.6 0.0 collective-permute-done.1.refs_2_
  12.6 0.1 collective-permute-done.2.refs_3_
  12.8 0.0 copy-done.1
  12.8 0.3 shard_map.96
  13.1 0.0 copy-start.2
  13.1 0.1 collective-permute-start.3
  13.2 1.7 %collective-permute-start.4 = (f32[64,128]{1,0:T(8,128)S(1)}, f32[64,128]{1,0:T(8,128)S(1)}, u32[]{:S(2)}, u32[]{:S(2)}) collective-permute-start(f32[64,128]{1,0:T(8,128)S(1)} %get-tuple-element.31.refs_1_.refs_0_), channel_id=1, source_target_pairs={{0,2},{1,3},{2,0},{3,1},{4,6},{5,7},{6,4},{7,5},{8,10},{9,11},{10,... | collective-permute-start | bytes 98312 | tf_op jit(solution)/shard_map/ppermute | solution.py:469
  14.8 0.2 collective-permute-start.5
  15.0 2.6 %shard_map.97.refs_4_._ = bf16[10,2304,512]{2,1,0:T(8,128)(2,1)S(1)} custom-call(bf16[2304,9216]{1,0:T(8,128)(2,1)} %wg_ref.11, bf16[2304,9216]{1,0:T(8,128)(2,1)} %wu_ref.11, bf16[10,2304,512]{2,1,0:T(8,128)(2,1)S(1)} %shard_map.95.refs_4_.refs_0_, f32[64,128]{1,0:T(8,128)S(1)} %get-tuple-element.31.refs_1_.refs_0_), custom_call_target="tpu_custom_call", output_to_operand_aliasing={{}: (2, {})} | custom-call | bytes 4718592 | tf_op jit(solution)/shard_map/pallas_call | solution.py:244
  17.6 0.0 collective-permute-done.3.refs_1_
  17.6 0.0 collective-permute-done.4.refs_2_
  17.6 0.6 collective-permute-done.5.refs_3_
  18.2 0.0 copy-done.2
  18.2 0.4 shard_map.98.x_ref
  18.6 7.1 %shard_map.99 = (bf16[2,32,3968]{2,1,0:T(8,128)(2,1)S(1)}, f32[2,32,2304]{2,1,0:T(8,128)S(1)}, f32[32,1664]{1,0:T(8,128)S(1)}, bf16[10,2304,512]{2,1,0:T(8,128)(2,1)S(1)}) custom-call(bf16[64,2304]{1,0:T(8,128)(2,1)S(1)} %shard_map.98.x_ref, bf16[2304,9216]{1,0:T(8,128)(2,1)} %wg_ref.11, ...), custom_call_target="tpu_custom_call", output_to_operand_aliasing={{3}: (5, {})} | custom-call | flops 1849688064 | bytes 21233664 | tf_op jit(solution)/shard_map/pallas_call | solution.py:334
  25.7 0.2 collective-permute-start.6
  25.9 10.5 %shard_map.102 = (bf16[2,32,3584]{2,1,0:T(8,128)(2,1)S(1)}, f32[2,32,3584]{2,1,0:T(8,128)S(1)}, bf16[10,2304,512]{2,1,0:T(8,128)(2,1)S(1)}) custom-call(bf16[64,2304]{1,0:T(8,128)(2,1)S(1)} %shard_map.98.x_ref, bf16[2304,9216]{1,0:T(8,128)(2,1)} %wg_ref.11, bf16[2304,9216]{1,0:T(8,128)(2,1)} %wu_ref.11, ...), custom_call_target="tpu_custom_call", output_to_operand_aliasing={{2}: (3, {})} | custom-call | flops 2113929216 | bytes 30670848 | tf_op jit(solution)/shard_map/pallas_call | solution.py:370
  36.4 0.4 collective-permute-start.12
  36.8 0.0 collective-permute-done.6.refs_0_
  36.8 0.1 shard_map.100
  36.9 1.1 %collective-permute-start.7 = (bf16[2,16,3968]{2,1,0:T(8,128)(2,1)S(1)}, bf16[2,16,3968]{2,1,0:T(8,128)(2,1)S(1)}, u32[]{:S(2)}, u32[]{:S(2)}) collective-permute-start(bf16[2,16,3968]{2,1,0:T(8,128)(2,1)S(1)} %get-tuple-element.36.refs_0_), channel_id=1, source_target_pairs={{0,2},{1,3},{2,0},{3,1},{4,6},{5,7},{6,4},{7,5},{8,10},{9,11},{10,... | collective-permute-start | bytes 761864 | tf_op jit(solution)/shard_map/ppermute | solution.py:463
  38.1 7.0 %shard_map.103 = (bf16[2,32,2048]{2,1,0:T(8,128)(2,1)S(1)}, f32[2,32,2048]{2,1,0:T(8,128)S(1)}, bf16[10,2304,512]{2,1,0:T(8,128)(2,1)S(1)}) custom-call(bf16[64,2304]{1,0:T(8,128)(2,1)S(1)} %shard_map.98.x_ref, bf16[2304,9216]{1,0:T(8,128)(2,1)} %wg_ref.11, bf16[2304,9216]{1,0:T(8,128)(2,1)} %wu_ref.11, ...), custom_call_target="tpu_custom_call", output_to_operand_aliasing={{2}: (3, {})} | custom-call | flops 1207959552 | bytes 18874368 | tf_op jit(solution)/shard_map/pallas_call | solution.py:370
  45.1 0.1 collective-permute-start.11
  45.2 0.0 collective-permute-done.12.refs_0_
  45.2 0.1 shard_map.104
  45.3 1.0 %collective-permute-start.13 = (bf16[2,16,3584]{2,1,0:T(8,128)(2,1)S(1)}, bf16[2,16,3584]{2,1,0:T(8,128)(2,1)S(1)}, u32[]{:S(2)}, u32[]{:S(2)}) collective-permute-start(bf16[2,16,3584]{2,1,0:T(8,128)(2,1)S(1)} %get-tuple-element.47.refs_0_), channel_id=1, source_target_pairs={{0,2},{1,3},{2,0},{3,1},{4,6},{5,7},{6,4},{7,5},{8,10},{9,11},{10,... | collective-permute-start | bytes 688136 | tf_op jit(solution)/shard_map/ppermute | solution.py:463
  46.3 0.0 collective-permute-done.7.refs_1_
  46.3 0.2 shard_map.101
  46.5 3.7 %collective-permute-start.10 = (bf16[4,1664]{1,0:T(4,128)(2,1)S(1)}, bf16[4,1664]{1,0:T(4,128)(2,1)S(1)}, u32[]{:S(2)}, u32[]{:S(2)}) collective-permute-start(bf16[4,1664]{1,0:T(4,128)(2,1)S(1)} %get-tuple-element.40), channel_id=1, source_target_pairs={{0,12},{4,8},{8,4},{12,0},{1,13},{5,9},{9,5},{13,1},{2,14},{6,10},... | collective-permute-start | bytes 39944 | tf_op jit(solution)/shard_map/ppermute | solution.py:466
  50.2 0.0 collective-permute-start.8
  50.2 0.8 %collective-permute-start.9 = (bf16[4,1664]{1,0:T(4,128)(2,1)S(1)}, bf16[4,1664]{1,0:T(4,128)(2,1)S(1)}, u32[]{:S(2)}, u32[]{:S(2)}) collective-permute-start(bf16[4,1664]{1,0:T(4,128)(2,1)S(1)} %get-tuple-element.39), channel_id=1, source_target_pairs={{0,8},{4,12},{8,0},{12,4},{1,9},{5,13},{9,1},{13,5},{2,10},{6,14},... | collective-permute-start | bytes 39944 | tf_op jit(solution)/shard_map/ppermute | solution.py:466
  51.0 0.0 copy-start
  51.0 0.0 copy-start.4
  51.0 0.0 copy-start.5
  51.0 2.8 %shard_map.105 = (bf16[2,32,1280]{2,1,0:T(8,128)(2,1)S(1)}, f32[2,32,1280]{2,1,0:T(8,128)S(1)}, bf16[10,2304,512]{2,1,0:T(8,128)(2,1)S(1)}) custom-call(bf16[64,2304]{1,0:T(8,128)(2,1)S(1)} %shard_map.98.x_ref, bf16[2304,9216]{1,0:T(8,128)(2,1)} %wg_ref.11, bf16[2304,9216]{1,0:T(8,128)(2,1)} %wu_ref.11, ...), custom_call_target="tpu_custom_call", output_to_operand_aliasing={{2}: (3, {})} | custom-call | flops 754974720 | bytes 2359296 | tf_op jit(solution)/shard_map/pallas_call | solution.py:370
  53.8 0.0 collective-permute-done.13.refs_5_.refs_3_
  53.8 0.0 collective-permute-done.11.refs_0_
  53.8 0.0 collective-permute-done.10.refs_4_.refs_3_
  53.8 0.0 collective-permute-done.8.refs_2_.refs_1_
  53.9 0.9 %collective-permute-done.9.refs_3_.refs_2_ = bf16[4,1664]{1,0:T(4,128)(2,1)S(1)} collective-permute-done((bf16[4,1664]{1,0:T(4,128)(2,1)S(1)}, bf16[4,1664]{1,0:T(4,128)(2,1)S(1)}, u32[]{:S(2)}, u32[]{:S(2)}) %collective-permute-start.9) | collective-permute-done | bytes 13344 | tf_op jit(solution)/shard_map/ppermute | solution.py:466
  54.8 0.1 collective-permute-start.14
  54.9 1.2 %collective-permute-start.15 = (bf16[2,16,2048]{2,1,0:T(8,128)(2,1)S(1)}, bf16[2,16,2048]{2,1,0:T(8,128)(2,1)S(1)}, u32[]{:S(2)}, u32[]{:S(2)}) collective-permute-start(bf16[2,16,2048]{2,1,0:T(8,128)(2,1)S(1)} %get-tuple-element.56), channel_id=1, source_target_pairs={{0,2},{1,3},{2,0},{3,1},{4,6},{5,7},{6,4},{7,5},{8,10},{9,11},{10,... | collective-permute-start | bytes 393224 | tf_op jit(solution)/shard_map/ppermute | solution.py:463
  56.1 0.2 collective-permute-done.14.refs_0_
  56.3 1.2 %collective-permute-start.16 = (bf16[2,16,1280]{2,1,0:T(8,128)(2,1)S(1)}, bf16[2,16,1280]{2,1,0:T(8,128)(2,1)S(1)}, u32[]{:S(2)}, u32[]{:S(2)}) collective-permute-start(bf16[2,16,1280]{2,1,0:T(8,128)(2,1)S(1)} %get-tuple-element.52.refs_4_), channel_id=1, source_target_pairs={{0,2},{1,3},{2,0},{3,1},{4,6},{5,7},{6,4},{7,5},{8,10},{9,11},{10,... | collective-permute-start | bytes 245768 | tf_op jit(solution)/shard_map/ppermute | solution.py:463
  57.5 0.2 shard_map.109.refs_0_
  57.7 0.0 copy-done
  57.7 0.0 copy-done.4
  57.7 0.0 copy-done.5
  57.7 2.5 %shard_map.108 = bf16[2,1,2,6144]{3,2,1,0:T(2,128)(2,1)} custom-call(s32[4]{0:T(128)S(1)} %copy-done.4, s32[2]{0:T(128)S(1)} %bitcast.3, bf16[2,1024,512]{2,1,0:T(8,128)(2,1)S(1)} %bitcast.2, bf16[4,1664]{1,0:T(4,128)(2,1)S(1)} %get-tuple-element.37.refs_1_.refs_0_, bf16[4,1664]{1,0:T(4,128)(2,1)S(1)} %collective-permute-done.8.refs_2_.refs_1_, ...), custom_call_target="tpu_custom_call" | custom-call | flops 100663296 | bytes 2097152 | tf_op jit(solution)/shard_map/pallas_call | solution.py:436
  60.2 1.1 %collective-permute-done.15.refs_2_ = bf16[2,16,2048]{2,1,0:T(8,128)(2,1)S(1)} collective-permute-done((bf16[2,16,2048]{2,1,0:T(8,128)(2,1)S(1)}, bf16[2,16,2048]{2,1,0:T(8,128)(2,1)S(1)}, u32[]{:S(2)}, u32[]{:S(2)}) %collective-permute-start.15) | collective-permute-done | bytes 131104 | tf_op jit(solution)/shard_map/ppermute | solution.py:463
  61.3 1.3 %collective-permute-done.16.refs_4_ = bf16[2,16,1280]{2,1,0:T(8,128)(2,1)S(1)} collective-permute-done((bf16[2,16,1280]{2,1,0:T(8,128)(2,1)S(1)}, bf16[2,16,1280]{2,1,0:T(8,128)(2,1)S(1)}, u32[]{:S(2)}, u32[]{:S(2)}) %collective-permute-start.16) | collective-permute-done | bytes 81952 | tf_op jit(solution)/shard_map/ppermute | solution.py:463
  62.6 0.8 %shard_map.110 = bf16[2,4,2,9216]{3,2,1,0:T(2,128)(2,1)} custom-call(bf16[2,4,2,5888]{3,2,1,0:T(2,128)(2,1)S(1)} %shard_map.109.refs_0_, f32[2,16,2048]{2,1,0:T(8,128)S(1)} %get-tuple-element.55.refs_1_, bf16[2,16,2048]{2,1,0:T(8,128)(2,1)S(1)} %collective-permute-done.15.refs_2_, f32[2,16,1280]{2,1,0:T(8,128)S(1)} %get-tuple-element.57.refs_3_, ...), custom_call_target="tpu_custom_call" | custom-call | flops 307200 | bytes 19200 | tf_op jit(solution)/shard_map/pallas_call | solution.py:185
  (4 shorter events, 0.1 us)
Async XLA Ops:
  0.6 12.0 %collective-permute-start = (bf16[8,1,2,2304]{3,2,1,0:T(2,128)(2,1)}, bf16[8,1,2,2304]{3,2,1,0:T(2,128)(2,1)S(1)}, u32[]{:S(2)}, u32[]{:S(2)}) collective-permute-start(bf16[8,1,2,2304]{3,2,1,0:T(2,128)(2,1)} %refs_0_.1), channel_id=1, source_target_pairs={{0,4},{4,0},{8,12},{12,8},{1,5},{5,1},{9,13},{13,9},{2,6},{6,2},{1... | collective-permute-start | bytes 221192 | tf_op jit(solution)/shard_map/ppermute | solution.py:466
  3.7 8.9 %collective-permute-start.1 = (bf16[8,1,2,2304]{3,2,1,0:T(2,128)(2,1)}, bf16[8,1,2,2304]{3,2,1,0:T(2,128)(2,1)S(1)}, u32[]{:S(2)}, u32[]{:S(2)}) collective-permute-start(bf16[8,1,2,2304]{3,2,1,0:T(2,128)(2,1)} %refs_0_.1), channel_id=1, source_target_pairs={{0,8},{4,12},{8,0},{12,4},{1,9},{5,13},{9,1},{13,5},{2,10},{6,14},... | collective-permute-start | bytes 221192 | tf_op jit(solution)/shard_map/ppermute | solution.py:466
  6.3 6.5 %collective-permute-start.2 = (bf16[8,1,2,2304]{3,2,1,0:T(2,128)(2,1)}, bf16[8,1,2,2304]{3,2,1,0:T(2,128)(2,1)S(1)}, u32[]{:S(2)}, u32[]{:S(2)}) collective-permute-start(bf16[8,1,2,2304]{3,2,1,0:T(2,128)(2,1)} %refs_0_.1), channel_id=1, source_target_pairs={{0,12},{4,8},{8,4},{12,0},{1,13},{5,9},{9,5},{13,1},{2,14},{6,10},... | collective-permute-start | bytes 221192 | tf_op jit(solution)/shard_map/ppermute | solution.py:466
  6.4 6.2 %copy-start.3 = (s32[4]{0:T(128)}, s32[4]{0:T(128)S(1)}, u32[]{:S(2)}) copy-start(s32[4]{0:T(128)S(1)} %iota_xor_fusion.refs_2_.slot_ref) | copy-start | bytes 52
  6.4 6.4 %copy-start.1 = (bf16[8,1,2,2304]{3,2,1,0:T(2,128)(2,1)S(1)}, bf16[8,1,2,2304]{3,2,1,0:T(2,128)(2,1)}, u32[]{:S(2)}) copy-start(bf16[8,1,2,2304]{3,2,1,0:T(2,128)(2,1)} %refs_0_.1) | copy-start | bytes 221188
  13.1 5.1 %copy-start.2 = (f32[2304]{0:T(1024)S(1)}, f32[2304]{0:T(1024)}, u32[]{:S(2)}) copy-start(f32[2304]{0:T(1024)} %gain_ref.1) | copy-start | bytes 27652
  13.1 4.5 %collective-permute-start.3 = (f32[64,128]{1,0:T(8,128)S(1)}, f32[64,128]{1,0:T(8,128)S(1)}, u32[]{:S(2)}, u32[]{:S(2)}) collective-permute-start(f32[64,128]{1,0:T(8,128)S(1)} %get-tuple-element.31.refs_1_.refs_0_), channel_id=1, source_target_pairs={{0,1},{1,0},{2,3},{3,2},{4,5},{5,4},{6,7},{7,6},{8,9},{9,8},{10,11... | collective-permute-start | bytes 98312 | tf_op jit(solution)/shard_map/ppermute | solution.py:469
  13.2 4.4 %collective-permute-start.4 = (f32[64,128]{1,0:T(8,128)S(1)}, f32[64,128]{1,0:T(8,128)S(1)}, u32[]{:S(2)}, u32[]{:S(2)}) collective-permute-start(f32[64,128]{1,0:T(8,128)S(1)} %get-tuple-element.31.refs_1_.refs_0_), channel_id=1, source_target_pairs={{0,2},{1,3},{2,0},{3,1},{4,6},{5,7},{6,4},{7,5},{8,10},{9,11},{10,... | collective-permute-start | bytes 98312 | tf_op jit(solution)/shard_map/ppermute | solution.py:469
  14.8 3.3 %collective-permute-start.5 = (f32[64,128]{1,0:T(8,128)S(1)}, f32[64,128]{1,0:T(8,128)S(1)}, u32[]{:S(2)}, u32[]{:S(2)}) collective-permute-start(f32[64,128]{1,0:T(8,128)S(1)} %get-tuple-element.31.refs_1_.refs_0_), channel_id=1, source_target_pairs={{0,3},{1,2},{2,1},{3,0},{4,7},{5,6},{6,5},{7,4},{8,11},{9,10},{10,... | collective-permute-start | bytes 98312 | tf_op jit(solution)/shard_map/ppermute | solution.py:469
  25.7 11.2 %collective-permute-start.6 = (bf16[2,32,3968]{2,1,0:T(8,128)(2,1)S(1)}, bf16[2,32,3968]{2,1,0:T(8,128)(2,1)S(1)}, u32[]{:S(2)}, u32[]{:S(2)}) collective-permute-start(bf16[2,32,3968]{2,1,0:T(8,128)(2,1)S(1)} %get-tuple-element.32.refs_0_), channel_id=1, source_target_pairs={{0,1},{1,0},{2,3},{3,2},{4,5},{5,4},{6,7},{7,6},{8,9},{9,8},{10,11... | collective-permute-start | bytes 1523720 | tf_op jit(solution)/shard_map/ppermute | solution.py:469
  36.4 8.8 %collective-permute-start.12 = (bf16[2,32,3584]{2,1,0:T(8,128)(2,1)S(1)}, bf16[2,32,3584]{2,1,0:T(8,128)(2,1)S(1)}, u32[]{:S(2)}, u32[]{:S(2)}) collective-permute-start(bf16[2,32,3584]{2,1,0:T(8,128)(2,1)S(1)} %get-tuple-element.43.refs_1_), channel_id=1, source_target_pairs={{0,1},{1,0},{2,3},{3,2},{4,5},{5,4},{6,7},{7,6},{8,9},{9,8},{10,11... | collective-permute-start | bytes 1376264 | tf_op jit(solution)/shard_map/ppermute | solution.py:469
  36.9 9.4 %collective-permute-start.7 = (bf16[2,16,3968]{2,1,0:T(8,128)(2,1)S(1)}, bf16[2,16,3968]{2,1,0:T(8,128)(2,1)S(1)}, u32[]{:S(2)}, u32[]{:S(2)}) collective-permute-start(bf16[2,16,3968]{2,1,0:T(8,128)(2,1)S(1)} %get-tuple-element.36.refs_0_), channel_id=1, source_target_pairs={{0,2},{1,3},{2,0},{3,1},{4,6},{5,7},{6,4},{7,5},{8,10},{9,11},{10,... | collective-permute-start | bytes 761864 | tf_op jit(solution)/shard_map/ppermute | solution.py:463
  45.1 8.7 %collective-permute-start.11 = (bf16[2,32,2048]{2,1,0:T(8,128)(2,1)S(1)}, bf16[2,32,2048]{2,1,0:T(8,128)(2,1)S(1)}, u32[]{:S(2)}, u32[]{:S(2)}) collective-permute-start(bf16[2,32,2048]{2,1,0:T(8,128)(2,1)S(1)} %get-tuple-element.44.refs_2_), channel_id=1, source_target_pairs={{0,1},{1,0},{2,3},{3,2},{4,5},{5,4},{6,7},{7,6},{8,9},{9,8},{10,11... | collective-permute-start | bytes 786440 | tf_op jit(solution)/shard_map/ppermute | solution.py:469
  45.3 8.5 %collective-permute-start.13 = (bf16[2,16,3584]{2,1,0:T(8,128)(2,1)S(1)}, bf16[2,16,3584]{2,1,0:T(8,128)(2,1)S(1)}, u32[]{:S(2)}, u32[]{:S(2)}) collective-permute-start(bf16[2,16,3584]{2,1,0:T(8,128)(2,1)S(1)} %get-tuple-element.47.refs_0_), channel_id=1, source_target_pairs={{0,2},{1,3},{2,0},{3,1},{4,6},{5,7},{6,4},{7,5},{8,10},{9,11},{10,... | collective-permute-start | bytes 688136 | tf_op jit(solution)/shard_map/ppermute | solution.py:463
  46.5 7.3 %collective-permute-start.10 = (bf16[4,1664]{1,0:T(4,128)(2,1)S(1)}, bf16[4,1664]{1,0:T(4,128)(2,1)S(1)}, u32[]{:S(2)}, u32[]{:S(2)}) collective-permute-start(bf16[4,1664]{1,0:T(4,128)(2,1)S(1)} %get-tuple-element.40), channel_id=1, source_target_pairs={{0,12},{4,8},{8,4},{12,0},{1,13},{5,9},{9,5},{13,1},{2,14},{6,10},... | collective-permute-start | bytes 39944 | tf_op jit(solution)/shard_map/ppermute | solution.py:466
  50.2 3.7 %collective-permute-start.8 = (bf16[4,1664]{1,0:T(4,128)(2,1)S(1)}, bf16[4,1664]{1,0:T(4,128)(2,1)S(1)}, u32[]{:S(2)}, u32[]{:S(2)}) collective-permute-start(bf16[4,1664]{1,0:T(4,128)(2,1)S(1)} %get-tuple-element.38), channel_id=1, source_target_pairs={{0,4},{4,0},{8,12},{12,8},{1,5},{5,1},{9,13},{13,9},{2,6},{6,2},{1... | collective-permute-start | bytes 39944 | tf_op jit(solution)/shard_map/ppermute | solution.py:466
  50.2 4.6 %collective-permute-start.9 = (bf16[4,1664]{1,0:T(4,128)(2,1)S(1)}, bf16[4,1664]{1,0:T(4,128)(2,1)S(1)}, u32[]{:S(2)}, u32[]{:S(2)}) collective-permute-start(bf16[4,1664]{1,0:T(4,128)(2,1)S(1)} %get-tuple-element.39), channel_id=1, source_target_pairs={{0,8},{4,12},{8,0},{12,4},{1,9},{5,13},{9,1},{13,5},{2,10},{6,14},... | collective-permute-start | bytes 39944 | tf_op jit(solution)/shard_map/ppermute | solution.py:466
  51.0 6.7 %copy-start = (bf16[2,1,1024,512]{3,2,1,0:T(8,128)(2,1)S(1)}, bf16[2,1,1024,512]{3,2,1,0:T(8,128)(2,1)}, u32[]{:S(2)}) copy-start(bf16[2,1,1024,512]{3,2,1,0:T(8,128)(2,1)} %param.14) | copy-start | bytes 6291460
  51.0 6.7 %copy-start.4 = (s32[4]{0:T(128)S(1)}, s32[4]{0:T(128)}, u32[]{:S(2)}) copy-start(s32[4]{0:T(128)} %copy-done.3) | copy-start | bytes 52
  51.0 6.7 %copy-start.5 = (s32[2,1]{0,1:T(1,128)S(1)}, s32[2,1]{0,1:T(1,128)}, u32[]{:S(2)}) copy-start(s32[2,1]{0,1:T(1,128)} %param.15) | copy-start | bytes 28
  54.8 1.5 %collective-permute-start.14 = (bf16[2,32,1280]{2,1,0:T(8,128)(2,1)S(1)}, bf16[2,32,1280]{2,1,0:T(8,128)(2,1)S(1)}, u32[]{:S(2)}, u32[]{:S(2)}) collective-permute-start(bf16[2,32,1280]{2,1,0:T(8,128)(2,1)S(1)} %get-tuple-element.50), channel_id=1, source_target_pairs={{0,1},{1,0},{2,3},{3,2},{4,5},{5,4},{6,7},{7,6},{8,9},{9,8},{10,11... | collective-permute-start | bytes 491528 | tf_op jit(solution)/shard_map/ppermute | solution.py:469
  54.9 6.4 %collective-permute-start.15 = (bf16[2,16,2048]{2,1,0:T(8,128)(2,1)S(1)}, bf16[2,16,2048]{2,1,0:T(8,128)(2,1)S(1)}, u32[]{:S(2)}, u32[]{:S(2)}) collective-permute-start(bf16[2,16,2048]{2,1,0:T(8,128)(2,1)S(1)} %get-tuple-element.56), channel_id=1, source_target_pairs={{0,2},{1,3},{2,0},{3,1},{4,6},{5,7},{6,4},{7,5},{8,10},{9,11},{10,... | collective-permute-start | bytes 393224 | tf_op jit(solution)/shard_map/ppermute | solution.py:463
  56.3 6.3 %collective-permute-start.16 = (bf16[2,16,1280]{2,1,0:T(8,128)(2,1)S(1)}, bf16[2,16,1280]{2,1,0:T(8,128)(2,1)S(1)}, u32[]{:S(2)}, u32[]{:S(2)}) collective-permute-start(bf16[2,16,1280]{2,1,0:T(8,128)(2,1)S(1)} %get-tuple-element.52.refs_4_), channel_id=1, source_target_pairs={{0,2},{1,3},{2,0},{3,1},{4,6},{5,7},{6,4},{7,5},{8,10},{9,11},{10,... | collective-permute-start | bytes 245768 | tf_op jit(solution)/shard_map/ppermute | solution.py:463

commit v10 on v7

--- a/solution.py
+++ b/solution.py
@@ -513,7 +513,7 @@
 
     weights = (w_gate, w_up)
     tiles = w_gate.shape[1] // TILE
-    before = [tiles * share // 36 for share in (4, 9)]
+    before = [tiles * share // 36 for share in (7, 9)]
     bounds = [0, before[1]] + [tiles * share // 36 for share in (20, 29, 36)]
     ahead = [before[1]] + [max(1, tiles * share // 36) for share in (5, 4, 4)] + [0]
     gathered = [tokens] + [swap_x(tokens, bits) for bits in range(1, size_x)]

time: 63.6 us -> 61.6 us (0.969)
  waiting for transfers between devices: 5.36 us -> 2.72 us
    ppermute x5, waiting for transfers between devices: 5.29 us -> 1.82 us  [swap_x(): return lax.ppermute(value, 'gx', [(i, i ^ bits) for i in range(size_x)])]
    ppermute x5, starting transfers between devices: 8.58 us -> 9.97 us  [swap_x(): return lax.ppermute(value, 'gx', [(i, i ^ bits) for i in range(size_x)])]
    ppermute x7, waiting for transfers between devices: 0.02 us -> 0.89 us  [swap(): return lax.ppermute(value, 'gy', [(i, i ^ bits) for i in range(size_y)])]
    ppermute x4, starting transfers between devices: 5.2 us -> 4.46 us  [shift_y(): lax.ppermute(value, 'gy', [(i, (i + by) % size_y) for i in range(size_y)])]
  transfers between devices with their start and end apart: 16 -> 16, of which waited for: 3 -> 4; matrix products, arithmetic and copies ran while one was open for 0% -> 0% of each run, Pallas kernels for 50% -> 52%
where the time goes in v10:
time: 61.6 us; the launch traced here: 61.5 us
  Pallas kernels  40.6 us (66%)
  starting transfers between devices  17.2 us (28%)
  waiting for transfers between devices  2.72 us (4%)
  between operations  0.85 us (1%)
    pallas_call x3, Pallas kernels, wide_sums(): pl.pallas_call(functools.partial(wide_kernel, first, tiles, held, followi...  20.2 us
    ppermute x5, starting transfers between devices, swap_x(): return lax.ppermute(value, 'gx', [(i, i ^ bits) for i in range(size_x)])  9.97 us
    pallas_call x2, Pallas kernels, load(): pl.pallas_call(functools.partial(load_kernel, first, last), out_shape=rin...  8.73 us
    pallas_call x1, Pallas kernels, first_sums(): pl.pallas_call(functools.partial(first_kernel, tiles, following), out_sha...  7.05 us
    ppermute x4, starting transfers between devices, shift_y(): lax.ppermute(value, 'gy', [(i, (i + by) % size_y) for i in range(size_y)])  4.46 us
    ppermute x7, starting transfers between devices, swap(): return lax.ppermute(value, 'gy', [(i, i ^ bits) for i in range(size_y)])  2.77 us
    pallas_call x1, Pallas kernels, attend(): pl.pallas_call(functools.partial(attend_kernel, count, steps, query_cols)...  2.48 us
    ppermute x5, waiting for transfers between devices, swap_x(): return lax.ppermute(value, 'gx', [(i, i ^ bits) for i in range(size_x)])  1.82 us
  transfers between devices with their start and end apart: 16, of which 4 were waited for; matrix products, arithmetic and copies ran while one was open for 0% of the time, Pallas kernels for 52%

profile of v10, /device:TPU:0, one launch (start us, length us, event | category | flops | bytes accessed | tf_op | source)
XLA Modules:
  0.0 61.5 jit_solution(8242696473954870363)
XLA Ops:
  0.6 3.1 %collective-permute-start = (bf16[8,1,2,2304]{3,2,1,0:T(2,128)(2,1)}, bf16[8,1,2,2304]{3,2,1,0:T(2,128)(2,1)S(1)}, u32[]{:S(2)}, u32[]{:S(2)}) collective-permute-start(bf16[8,1,2,2304]{3,2,1,0:T(2,128)(2,1)} %refs_0_.1), channel_id=1, source_target_pairs={{0,4},{4,0},{8,12},{12,8},{1,5},{5,1},{9,13},{13,9},{2,6},{6,2},{1... | collective-permute-start | bytes 221192 | tf_op jit(solution)/shard_map/ppermute | solution.py:491
  3.7 2.6 %collective-permute-start.1 = (bf16[8,1,2,2304]{3,2,1,0:T(2,128)(2,1)}, bf16[8,1,2,2304]{3,2,1,0:T(2,128)(2,1)S(1)}, u32[]{:S(2)}, u32[]{:S(2)}) collective-permute-start(bf16[8,1,2,2304]{3,2,1,0:T(2,128)(2,1)} %refs_0_.1), channel_id=1, source_target_pairs={{0,8},{4,12},{8,0},{12,4},{1,9},{5,13},{9,1},{13,5},{2,10},{6,14},... | collective-permute-start | bytes 221192 | tf_op jit(solution)/shard_map/ppermute | solution.py:491
  6.3 0.0 collective-permute-start.2
  6.3 0.1 fusion.17.refs_0_.source_ref
  6.4 0.0 copy-start.3
  6.4 0.0 copy-start.1
  6.4 6.2 %shard_map.95.refs_4_.refs_0_ = bf16[10,2304,512]{2,1,0:T(8,128)(2,1)S(1)} custom-call(bf16[2304,9216]{1,0:T(8,128)(2,1)} %wg_ref.11, bf16[2304,9216]{1,0:T(8,128)(2,1)} %wu_ref.11, s32[64,1]{1,0:T(8,128)S(1)} %fusion.17.refs_0_.source_ref, s32[16,1]{1,0:T(8,128)S(1)} %fusion.38.refs_1_.source_ref, s32[4]{0:T(128)S(1)} %fusion.47.refs_2_.slot_ref), custom_call_target="tpu_custom_call" | custom-call | bytes 16515072 | tf_op jit(solution)/shard_map/pallas_call | solution.py:244
  12.6 0.0 copy-done.3
  12.6 0.0 collective-permute-done.refs_1_
  12.6 0.0 collective-permute-done.1.refs_2_
  12.6 0.1 collective-permute-done.2.refs_3_
  12.8 0.0 copy-done.1
  12.8 0.3 shard_map.96
  13.1 0.0 copy-start.2
  13.1 0.1 collective-permute-start.3
  13.2 1.7 %collective-permute-start.4 = (f32[64,128]{1,0:T(8,128)S(1)}, f32[64,128]{1,0:T(8,128)S(1)}, u32[]{:S(2)}, u32[]{:S(2)}) collective-permute-start(f32[64,128]{1,0:T(8,128)S(1)} %get-tuple-element.31.refs_1_.refs_0_), channel_id=1, source_target_pairs={{0,2},{1,3},{2,0},{3,1},{4,6},{5,7},{6,4},{7,5},{8,10},{9,11},{10,... | collective-permute-start | bytes 98312 | tf_op jit(solution)/shard_map/ppermute | solution.py:494
  14.9 0.2 collective-permute-start.5
  15.0 2.6 %shard_map.97.refs_4_._ = bf16[10,2304,512]{2,1,0:T(8,128)(2,1)S(1)} custom-call(bf16[2304,9216]{1,0:T(8,128)(2,1)} %wg_ref.11, bf16[2304,9216]{1,0:T(8,128)(2,1)} %wu_ref.11, bf16[10,2304,512]{2,1,0:T(8,128)(2,1)S(1)} %shard_map.95.refs_4_.refs_0_, f32[64,128]{1,0:T(8,128)S(1)} %get-tuple-element.31.refs_1_.refs_0_), custom_call_target="tpu_custom_call", output_to_operand_aliasing={{}: (2, {})} | custom-call | bytes 4718592 | tf_op jit(solution)/shard_map/pallas_call | solution.py:244
  17.6 0.0 collective-permute-done.3.refs_1_
  17.6 0.0 collective-permute-done.4.refs_2_
  17.6 0.6 collective-permute-done.5.refs_3_
  18.2 0.0 copy-done.2
  18.2 0.4 shard_map.98.x_ref
  18.6 7.1 %shard_map.99 = (bf16[2,32,3968]{2,1,0:T(8,128)(2,1)S(1)}, f32[2,32,2304]{2,1,0:T(8,128)S(1)}, f32[32,1664]{1,0:T(8,128)S(1)}, bf16[10,2304,512]{2,1,0:T(8,128)(2,1)S(1)}) custom-call(bf16[64,2304]{1,0:T(8,128)(2,1)S(1)} %shard_map.98.x_ref, bf16[2304,9216]{1,0:T(8,128)(2,1)} %wg_ref.11, ...), custom_call_target="tpu_custom_call", output_to_operand_aliasing={{3}: (5, {})} | custom-call | flops 1849688064 | bytes 21233664 | tf_op jit(solution)/shard_map/pallas_call | solution.py:334
  25.7 0.2 collective-permute-start.6
  25.9 8.4 %shard_map.103 = (bf16[2,32,2816]{2,1,0:T(8,128)(2,1)S(1)}, f32[2,32,2816]{2,1,0:T(8,128)S(1)}, bf16[10,2304,512]{2,1,0:T(8,128)(2,1)S(1)}) custom-call(bf16[64,2304]{1,0:T(8,128)(2,1)S(1)} %shard_map.98.x_ref, bf16[2304,9216]{1,0:T(8,128)(2,1)} %wg_ref.11, bf16[2304,9216]{1,0:T(8,128)(2,1)} %wu_ref.11, ...), custom_call_target="tpu_custom_call", output_to_operand_aliasing={{2}: (3, {})} | custom-call | flops 1660944384 | bytes 23592960 | tf_op jit(solution)/shard_map/pallas_call | solution.py:370
  34.3 0.4 collective-permute-start.11
  34.7 0.0 collective-permute-done.6.refs_0_
  34.8 0.1 shard_map.100
  34.8 1.1 %collective-permute-start.7 = (bf16[2,16,3968]{2,1,0:T(8,128)(2,1)S(1)}, bf16[2,16,3968]{2,1,0:T(8,128)(2,1)S(1)}, u32[]{:S(2)}, u32[]{:S(2)}) collective-permute-start(bf16[2,16,3968]{2,1,0:T(8,128)(2,1)S(1)} %get-tuple-element.36.refs_0_), channel_id=1, source_target_pairs={{0,2},{1,3},{2,0},{3,1},{4,6},{5,7},{6,4},{7,5},{8,10},{9,11},{10,... | collective-permute-start | bytes 761864 | tf_op jit(solution)/shard_map/ppermute | solution.py:488
  36.0 7.7 %shard_map.104 = (bf16[2,32,2304]{2,1,0:T(8,128)(2,1)S(1)}, f32[2,32,2304]{2,1,0:T(8,128)S(1)}, bf16[10,2304,512]{2,1,0:T(8,128)(2,1)S(1)}) custom-call(bf16[64,2304]{1,0:T(8,128)(2,1)S(1)} %shard_map.98.x_ref, bf16[2304,9216]{1,0:T(8,128)(2,1)} %wg_ref.11, bf16[2304,9216]{1,0:T(8,128)(2,1)} %wu_ref.11, ...), custom_call_target="tpu_custom_call", output_to_operand_aliasing={{2}: (3, {})} | custom-call | flops 1358954496 | bytes 21233664 | tf_op jit(solution)/shard_map/pallas_call | solution.py:370
  43.7 0.1 collective-permute-start.10
  43.9 0.0 collective-permute-done.11.refs_0_
  43.9 0.1 shard_map.105
  43.9 1.0 %collective-permute-start.12 = (bf16[2,16,2816]{2,1,0:T(8,128)(2,1)S(1)}, bf16[2,16,2816]{2,1,0:T(8,128)(2,1)S(1)}, u32[]{:S(2)}, u32[]{:S(2)}) collective-permute-start(bf16[2,16,2816]{2,1,0:T(8,128)(2,1)S(1)} %get-tuple-element.47.refs_0_), channel_id=1, source_target_pairs={{0,2},{1,3},{2,0},{3,1},{4,6},{5,7},{6,4},{7,5},{8,10},{9,11},{10,... | collective-permute-start | bytes 540680 | tf_op jit(solution)/shard_map/ppermute | solution.py:488
  44.9 0.0 collective-permute-done.7.refs_1_
  44.9 0.2 shard_map.101
  45.1 2.1 %collective-permute-start.8 = (bf16[1,8,1664]{2,1,0:T(8,128)(2,1)S(1)}, bf16[1,8,1664]{2,1,0:T(8,128)(2,1)S(1)}, u32[]{:S(2)}, u32[]{:S(2)}) collective-permute-start(bf16[1,8,1664]{2,1,0:T(8,128)(2,1)S(1)} %get-tuple-element.38), channel_id=1, source_target_pairs={{0,8},{4,12},{8,0},{12,4},{1,9},{5,13},{9,1},{13,5},{2,10},{6,14},... | collective-permute-start | bytes 79880 | tf_op jit(solution)/shard_map/ppermute | solution.py:491
  47.2 0.0 copy-start
  47.2 0.0 copy-start.4
  47.2 0.0 copy-start.5
  47.2 4.0 %shard_map.106 = (bf16[2,32,1792]{2,1,0:T(8,128)(2,1)S(1)}, f32[2,32,1792]{2,1,0:T(8,128)S(1)}, bf16[10,2304,512]{2,1,0:T(8,128)(2,1)S(1)}) custom-call(bf16[64,2304]{1,0:T(8,128)(2,1)S(1)} %shard_map.98.x_ref, bf16[2304,9216]{1,0:T(8,128)(2,1)} %wg_ref.11, bf16[2304,9216]{1,0:T(8,128)(2,1)} %wu_ref.11, ...), custom_call_target="tpu_custom_call", output_to_operand_aliasing={{2}: (3, {})} | custom-call | flops 1056964608 | bytes 7077888 | tf_op jit(solution)/shard_map/pallas_call | solution.py:370
  51.2 0.0 collective-permute-done.12.refs_3_
  51.2 0.0 collective-permute-done.8.came_ref.refs_2_
  51.2 0.0 collective-permute-done.10.refs_0_
  51.2 0.1 shard_map.107
  51.3 0.1 collective-permute-start.13
  51.4 1.2 %collective-permute-start.14 = (bf16[2,16,2304]{2,1,0:T(8,128)(2,1)S(1)}, bf16[2,16,2304]{2,1,0:T(8,128)(2,1)S(1)}, u32[]{:S(2)}, u32[]{:S(2)}) collective-permute-start(bf16[2,16,2304]{2,1,0:T(8,128)(2,1)S(1)} %get-tuple-element.56), channel_id=1, source_target_pairs={{0,2},{1,3},{2,0},{3,1},{4,6},{5,7},{6,4},{7,5},{8,10},{9,11},{10,... | collective-permute-start | bytes 442376 | tf_op jit(solution)/shard_map/ppermute | solution.py:488
  52.5 0.3 collective-permute-done.13.refs_0_
  52.9 1.2 %collective-permute-start.15 = (bf16[2,16,1792]{2,1,0:T(8,128)(2,1)S(1)}, bf16[2,16,1792]{2,1,0:T(8,128)(2,1)S(1)}, u32[]{:S(2)}, u32[]{:S(2)}) collective-permute-start(bf16[2,16,1792]{2,1,0:T(8,128)(2,1)S(1)} %get-tuple-element.52.refs_2_.refs_4_), channel_id=1, source_target_pairs={{0,2},{1,3},{2,0},{3,1},{4,6},{5,7},{6,4},{7,5},{8,10},{9,11},{10,... | collective-permute-start | bytes 344072 | tf_op jit(solution)/shard_map/ppermute | solution.py:488
  54.1 2.2 %collective-permute-start.9 = (bf16[2,4,1664]{2,1,0:T(4,128)(2,1)S(1)}, bf16[2,4,1664]{2,1,0:T(4,128)(2,1)S(1)}, u32[]{:S(2)}, u32[]{:S(2)}) collective-permute-start(bf16[2,4,1664]{2,1,0:T(4,128)(2,1)S(1)} %get-tuple-element.40), channel_id=1, source_target_pairs={{0,4},{4,0},{8,12},{12,8},{1,5},{5,1},{9,13},{13,9},{2,6},{6,2},{1... | collective-permute-start | bytes 79880 | tf_op jit(solution)/shard_map/ppermute | solution.py:491
  56.3 0.2 shard_map.110.refs_0_
  56.4 1.7 %collective-permute-done.9.refs_1_ = bf16[2,4,1664]{2,1,0:T(4,128)(2,1)S(1)} collective-permute-done((bf16[2,4,1664]{2,1,0:T(4,128)(2,1)S(1)}, bf16[2,4,1664]{2,1,0:T(4,128)(2,1)S(1)}, u32[]{:S(2)}, u32[]{:S(2)}) %collective-permute-start.9) | collective-permute-done | bytes 26656 | tf_op jit(solution)/shard_map/ppermute | solution.py:491
  58.1 0.0 copy-done
  58.1 0.0 copy-done.4
  58.1 0.0 copy-done.5
  58.1 2.5 %shard_map.109 = bf16[2,1,2,6144]{3,2,1,0:T(2,128)(2,1)} custom-call(s32[4]{0:T(128)S(1)} %copy-done.4, s32[2]{0:T(128)S(1)} %bitcast.3, bf16[2,1024,512]{2,1,0:T(8,128)(2,1)S(1)} %bitcast.2, bf16[2,4,1664]{2,1,0:T(4,128)(2,1)S(1)} %get-tuple-element.39.refs_0_, bf16[2,4,1664]{2,1,0:T(4,128)(2,1)S(1)} %collective-permute-done.9.refs_1_, ...), custom_call_target="tpu_custom_call" | custom-call | flops 100663296 | bytes 2097152 | tf_op jit(solution)/shard_map/pallas_call | solution.py:461
  60.6 0.0 collective-permute-done.14.refs_2_
  60.6 0.0 collective-permute-done.15.refs_4_
  60.6 0.9 %shard_map.111 = bf16[2,4,2,9216]{3,2,1,0:T(2,128)(2,1)} custom-call(bf16[2,4,2,5120]{3,2,1,0:T(2,128)(2,1)S(1)} %shard_map.110.refs_0_, f32[2,16,2304]{2,1,0:T(8,128)S(1)} %get-tuple-element.55.refs_1_, bf16[2,16,2304]{2,1,0:T(8,128)(2,1)S(1)} %collective-permute-done.14.refs_2_, f32[2,16,1792]{2,1,0:T(8,128)S(1)} %get-tuple-element.57.refs_3_, ...), custom_call_target="tpu_custom_call" | custom-call | flops 344064 | bytes 21504 | tf_op jit(solution)/shard_map/pallas_call | solution.py:185
  (4 shorter events, 0.1 us)
Async XLA Ops:
  0.6 12.0 %collective-permute-start = (bf16[8,1,2,2304]{3,2,1,0:T(2,128)(2,1)}, bf16[8,1,2,2304]{3,2,1,0:T(2,128)(2,1)S(1)}, u32[]{:S(2)}, u32[]{:S(2)}) collective-permute-start(bf16[8,1,2,2304]{3,2,1,0:T(2,128)(2,1)} %refs_0_.1), channel_id=1, source_target_pairs={{0,4},{4,0},{8,12},{12,8},{1,5},{5,1},{9,13},{13,9},{2,6},{6,2},{1... | collective-permute-start | bytes 221192 | tf_op jit(solution)/shard_map/ppermute | solution.py:491
  3.7 8.9 %collective-permute-start.1 = (bf16[8,1,2,2304]{3,2,1,0:T(2,128)(2,1)}, bf16[8,1,2,2304]{3,2,1,0:T(2,128)(2,1)S(1)}, u32[]{:S(2)}, u32[]{:S(2)}) collective-permute-start(bf16[8,1,2,2304]{3,2,1,0:T(2,128)(2,1)} %refs_0_.1), channel_id=1, source_target_pairs={{0,8},{4,12},{8,0},{12,4},{1,9},{5,13},{9,1},{13,5},{2,10},{6,14},... | collective-permute-start | bytes 221192 | tf_op jit(solution)/shard_map/ppermute | solution.py:491
  6.3 6.5 %collective-permute-start.2 = (bf16[8,1,2,2304]{3,2,1,0:T(2,128)(2,1)}, bf16[8,1,2,2304]{3,2,1,0:T(2,128)(2,1)S(1)}, u32[]{:S(2)}, u32[]{:S(2)}) collective-permute-start(bf16[8,1,2,2304]{3,2,1,0:T(2,128)(2,1)} %refs_0_.1), channel_id=1, source_target_pairs={{0,12},{4,8},{8,4},{12,0},{1,13},{5,9},{9,5},{13,1},{2,14},{6,10},... | collective-permute-start | bytes 221192 | tf_op jit(solution)/shard_map/ppermute | solution.py:491
  6.4 6.2 %copy-start.3 = (s32[4]{0:T(128)}, s32[4]{0:T(128)S(1)}, u32[]{:S(2)}) copy-start(s32[4]{0:T(128)S(1)} %fusion.47.refs_2_.slot_ref) | copy-start | bytes 52
  6.4 6.4 %copy-start.1 = (bf16[8,1,2,2304]{3,2,1,0:T(2,128)(2,1)S(1)}, bf16[8,1,2,2304]{3,2,1,0:T(2,128)(2,1)}, u32[]{:S(2)}) copy-start(bf16[8,1,2,2304]{3,2,1,0:T(2,128)(2,1)} %refs_0_.1) | copy-start | bytes 221188
  13.1 5.1 %copy-start.2 = (f32[2304]{0:T(1024)S(1)}, f32[2304]{0:T(1024)}, u32[]{:S(2)}) copy-start(f32[2304]{0:T(1024)} %gain_ref.1) | copy-start | bytes 27652
  13.1 4.5 %collective-permute-start.3 = (f32[64,128]{1,0:T(8,128)S(1)}, f32[64,128]{1,0:T(8,128)S(1)}, u32[]{:S(2)}, u32[]{:S(2)}) collective-permute-start(f32[64,128]{1,0:T(8,128)S(1)} %get-tuple-element.31.refs_1_.refs_0_), channel_id=1, source_target_pairs={{0,1},{1,0},{2,3},{3,2},{4,5},{5,4},{6,7},{7,6},{8,9},{9,8},{10,11... | collective-permute-start | bytes 98312 | tf_op jit(solution)/shard_map/ppermute | solution.py:494
  13.2 4.4 %collective-permute-start.4 = (f32[64,128]{1,0:T(8,128)S(1)}, f32[64,128]{1,0:T(8,128)S(1)}, u32[]{:S(2)}, u32[]{:S(2)}) collective-permute-start(f32[64,128]{1,0:T(8,128)S(1)} %get-tuple-element.31.refs_1_.refs_0_), channel_id=1, source_target_pairs={{0,2},{1,3},{2,0},{3,1},{4,6},{5,7},{6,4},{7,5},{8,10},{9,11},{10,... | collective-permute-start | bytes 98312 | tf_op jit(solution)/shard_map/ppermute | solution.py:494
  14.9 3.3 %collective-permute-start.5 = (f32[64,128]{1,0:T(8,128)S(1)}, f32[64,128]{1,0:T(8,128)S(1)}, u32[]{:S(2)}, u32[]{:S(2)}) collective-permute-start(f32[64,128]{1,0:T(8,128)S(1)} %get-tuple-element.31.refs_1_.refs_0_), channel_id=1, source_target_pairs={{0,3},{1,2},{2,1},{3,0},{4,7},{5,6},{6,5},{7,4},{8,11},{9,10},{10,... | collective-permute-start | bytes 98312 | tf_op jit(solution)/shard_map/ppermute | solution.py:494
  25.7 9.1 %collective-permute-start.6 = (bf16[2,32,3968]{2,1,0:T(8,128)(2,1)S(1)}, bf16[2,32,3968]{2,1,0:T(8,128)(2,1)S(1)}, u32[]{:S(2)}, u32[]{:S(2)}) collective-permute-start(bf16[2,32,3968]{2,1,0:T(8,128)(2,1)S(1)} %get-tuple-element.32.refs_0_), channel_id=1, source_target_pairs={{0,1},{1,0},{2,3},{3,2},{4,5},{5,4},{6,7},{7,6},{8,9},{9,8},{10,11... | collective-permute-start | bytes 1523720 | tf_op jit(solution)/shard_map/ppermute | solution.py:494
  34.3 9.5 %collective-permute-start.11 = (bf16[2,32,2816]{2,1,0:T(8,128)(2,1)S(1)}, bf16[2,32,2816]{2,1,0:T(8,128)(2,1)S(1)}, u32[]{:S(2)}, u32[]{:S(2)}) collective-permute-start(bf16[2,32,2816]{2,1,0:T(8,128)(2,1)S(1)} %get-tuple-element.43.refs_1_), channel_id=1, source_target_pairs={{0,1},{1,0},{2,3},{3,2},{4,5},{5,4},{6,7},{7,6},{8,9},{9,8},{10,11... | collective-permute-start | bytes 1081352 | tf_op jit(solution)/shard_map/ppermute | solution.py:494
  34.8 10.1 %collective-permute-start.7 = (bf16[2,16,3968]{2,1,0:T(8,128)(2,1)S(1)}, bf16[2,16,3968]{2,1,0:T(8,128)(2,1)S(1)}, u32[]{:S(2)}, u32[]{:S(2)}) collective-permute-start(bf16[2,16,3968]{2,1,0:T(8,128)(2,1)S(1)} %get-tuple-element.36.refs_0_), channel_id=1, source_target_pairs={{0,2},{1,3},{2,0},{3,1},{4,6},{5,7},{6,4},{7,5},{8,10},{9,11},{10,... | collective-permute-start | bytes 761864 | tf_op jit(solution)/shard_map/ppermute | solution.py:488
  43.7 7.5 %collective-permute-start.10 = (bf16[2,32,2304]{2,1,0:T(8,128)(2,1)S(1)}, bf16[2,32,2304]{2,1,0:T(8,128)(2,1)S(1)}, u32[]{:S(2)}, u32[]{:S(2)}) collective-permute-start(bf16[2,32,2304]{2,1,0:T(8,128)(2,1)S(1)} %get-tuple-element.44.refs_2_), channel_id=1, source_target_pairs={{0,1},{1,0},{2,3},{3,2},{4,5},{5,4},{6,7},{7,6},{8,9},{9,8},{10,11... | collective-permute-start | bytes 884744 | tf_op jit(solution)/shard_map/ppermute | solution.py:494
  43.9 7.2 %collective-permute-start.12 = (bf16[2,16,2816]{2,1,0:T(8,128)(2,1)S(1)}, bf16[2,16,2816]{2,1,0:T(8,128)(2,1)S(1)}, u32[]{:S(2)}, u32[]{:S(2)}) collective-permute-start(bf16[2,16,2816]{2,1,0:T(8,128)(2,1)S(1)} %get-tuple-element.47.refs_0_), channel_id=1, source_target_pairs={{0,2},{1,3},{2,0},{3,1},{4,6},{5,7},{6,4},{7,5},{8,10},{9,11},{10,... | collective-permute-start | bytes 540680 | tf_op jit(solution)/shard_map/ppermute | solution.py:488
  45.1 6.1 %collective-permute-start.8 = (bf16[1,8,1664]{2,1,0:T(8,128)(2,1)S(1)}, bf16[1,8,1664]{2,1,0:T(8,128)(2,1)S(1)}, u32[]{:S(2)}, u32[]{:S(2)}) collective-permute-start(bf16[1,8,1664]{2,1,0:T(8,128)(2,1)S(1)} %get-tuple-element.38), channel_id=1, source_target_pairs={{0,8},{4,12},{8,0},{12,4},{1,9},{5,13},{9,1},{13,5},{2,10},{6,14},... | collective-permute-start | bytes 79880 | tf_op jit(solution)/shard_map/ppermute | solution.py:491
  47.2 10.9 %copy-start = (bf16[2,1,1024,512]{3,2,1,0:T(8,128)(2,1)S(1)}, bf16[2,1,1024,512]{3,2,1,0:T(8,128)(2,1)}, u32[]{:S(2)}) copy-start(bf16[2,1,1024,512]{3,2,1,0:T(8,128)(2,1)} %param.14) | copy-start | bytes 6291460
  47.2 10.9 %copy-start.4 = (s32[4]{0:T(128)S(1)}, s32[4]{0:T(128)}, u32[]{:S(2)}) copy-start(s32[4]{0:T(128)} %copy-done.3) | copy-start | bytes 52
  47.2 10.9 %copy-start.5 = (s32[2,1]{0,1:T(1,128)S(1)}, s32[2,1]{0,1:T(1,128)}, u32[]{:S(2)}) copy-start(s32[2,1]{0,1:T(1,128)} %param.15) | copy-start | bytes 28
  51.3 1.6 %collective-permute-start.13 = (bf16[2,32,1792]{2,1,0:T(8,128)(2,1)S(1)}, bf16[2,32,1792]{2,1,0:T(8,128)(2,1)S(1)}, u32[]{:S(2)}, u32[]{:S(2)}) collective-permute-start(bf16[2,32,1792]{2,1,0:T(8,128)(2,1)S(1)} %get-tuple-element.50), channel_id=1, source_target_pairs={{0,1},{1,0},{2,3},{3,2},{4,5},{5,4},{6,7},{7,6},{8,9},{9,8},{10,11... | collective-permute-start | bytes 688136 | tf_op jit(solution)/shard_map/ppermute | solution.py:494
  51.4 9.3 %collective-permute-start.14 = (bf16[2,16,2304]{2,1,0:T(8,128)(2,1)S(1)}, bf16[2,16,2304]{2,1,0:T(8,128)(2,1)S(1)}, u32[]{:S(2)}, u32[]{:S(2)}) collective-permute-start(bf16[2,16,2304]{2,1,0:T(8,128)(2,1)S(1)} %get-tuple-element.56), channel_id=1, source_target_pairs={{0,2},{1,3},{2,0},{3,1},{4,6},{5,7},{6,4},{7,5},{8,10},{9,11},{10,... | collective-permute-start | bytes 442376 | tf_op jit(solution)/shard_map/ppermute | solution.py:488
  52.9 7.7 %collective-permute-start.15 = (bf16[2,16,1792]{2,1,0:T(8,128)(2,1)S(1)}, bf16[2,16,1792]{2,1,0:T(8,128)(2,1)S(1)}, u32[]{:S(2)}, u32[]{:S(2)}) collective-permute-start(bf16[2,16,1792]{2,1,0:T(8,128)(2,1)S(1)} %get-tuple-element.52.refs_2_.refs_4_), channel_id=1, source_target_pairs={{0,2},{1,3},{2,0},{3,1},{4,6},{5,7},{6,4},{7,5},{8,10},{9,11},{10,... | collective-permute-start | bytes 344072 | tf_op jit(solution)/shard_map/ppermute | solution.py:488
  54.1 4.1 %collective-permute-start.9 = (bf16[2,4,1664]{2,1,0:T(4,128)(2,1)S(1)}, bf16[2,4,1664]{2,1,0:T(4,128)(2,1)S(1)}, u32[]{:S(2)}, u32[]{:S(2)}) collective-permute-start(bf16[2,4,1664]{2,1,0:T(4,128)(2,1)S(1)} %get-tuple-element.40), channel_id=1, source_target_pairs={{0,4},{4,0},{8,12},{12,8},{1,5},{5,1},{9,13},{13,9},{2,6},{6,2},{1... | collective-permute-start | bytes 79880 | tf_op jit(solution)/shard_map/ppermute | solution.py:491

commit v11 on v10

--- a/solution.py
+++ b/solution.py
@@ -14,7 +14,7 @@
 MASKED = -1e30
 MIB = 1024 * 1024
 TILE = 256
-SLOTS = 10
+SLOTS = 11
 F32 = jnp.float32
 BF16 = jnp.bfloat16
 
@@ -513,8 +513,8 @@
 
     weights = (w_gate, w_up)
     tiles = w_gate.shape[1] // TILE
-    before = [tiles * share // 36 for share in (7, 9)]
-    bounds = [0, before[1]] + [tiles * share // 36 for share in (20, 29, 36)]
+    before = [tiles * share // 36 for share in (7, 10)]
+    bounds = [0, before[1]] + [tiles * share // 36 for share in (21, 29, 36)]
     ahead = [before[1]] + [max(1, tiles * share // 36) for share in (5, 4, 4)] + [0]
     gathered = [tokens] + [swap_x(tokens, bits) for bits in range(1, size_x)]
     ring = load(weights, 0, before[0], None, (source, order, slots))

time: 61.6 us -> 62.1 us (level)
  starting transfers between devices: 17.2 us -> 18 us
  waiting for transfers between devices: 2.72 us -> 1.96 us
    ppermute x7, waiting for transfers between devices: 0.89 us -> 0.02 us  [swap(): return lax.ppermute(value, 'gy', [(i, i ^ bits) for i in range(size_y)])]
    pallas_call x2, Pallas kernels: 8.73 us -> 9.5 us  [load(): pl.pallas_call(functools.partial(load_kernel, first, last), out_shape=rin...]
    pallas_call x3, Pallas kernels: 20.2 us -> 19.5 us  [wide_sums(): pl.pallas_call(functools.partial(wide_kernel, first, tiles, held, followi...]
    ppermute x4, starting transfers between devices: 4.46 us -> 5.1 us  [shift_y(): lax.ppermute(value, 'gy', [(i, (i + by) % size_y) for i in range(size_y)])]
  transfers between devices with their start and end apart: 16 -> 16, of which waited for: 4 -> 3; matrix products, arithmetic and copies ran while one was open for 0% -> 0% of each run, Pallas kernels for 52% -> 52%
where the time goes in v11:
time: 62.1 us; the launch traced here: 61.9 us
  Pallas kernels  41.1 us (66%)
  starting transfers between devices  18 us (29%)
  waiting for transfers between devices  1.96 us (3%)
  between operations  0.84 us (1%)
    pallas_call x3, Pallas kernels, wide_sums(): pl.pallas_call(functools.partial(wide_kernel, first, tiles, held, followi...  19.5 us
    ppermute x5, starting transfers between devices, swap_x(): return lax.ppermute(value, 'gx', [(i, i ^ bits) for i in range(size_x)])  10.1 us
    pallas_call x2, Pallas kernels, load(): pl.pallas_call(functools.partial(load_kernel, first, last), out_shape=rin...  9.5 us
    pallas_call x1, Pallas kernels, first_sums(): pl.pallas_call(functools.partial(first_kernel, tiles, following), out_sha...  7.43 us
    ppermute x4, starting transfers between devices, shift_y(): lax.ppermute(value, 'gy', [(i, (i + by) % size_y) for i in range(size_y)])  5.1 us
    ppermute x7, starting transfers between devices, swap(): return lax.ppermute(value, 'gy', [(i, i ^ bits) for i in range(size_y)])  2.78 us
    pallas_call x1, Pallas kernels, attend(): pl.pallas_call(functools.partial(attend_kernel, count, steps, query_cols)...  2.48 us
    ppermute x5, waiting for transfers between devices, swap_x(): return lax.ppermute(value, 'gx', [(i, i ^ bits) for i in range(size_x)])  1.8 us
  transfers between devices with their start and end apart: 16, of which 3 were waited for; matrix products, arithmetic and copies ran while one was open for 0% of the time, Pallas kernels for 52%

profile of v11, /device:TPU:0, one launch (start us, length us, event | category | flops | bytes accessed | tf_op | source)
XLA Modules:
  0.0 61.9 jit_solution(4042847072342300889)
XLA Ops:
  0.6 3.1 %collective-permute-start = (bf16[8,1,2,2304]{3,2,1,0:T(2,128)(2,1)}, bf16[8,1,2,2304]{3,2,1,0:T(2,128)(2,1)S(1)}, u32[]{:S(2)}, u32[]{:S(2)}) collective-permute-start(bf16[8,1,2,2304]{3,2,1,0:T(2,128)(2,1)} %refs_0_.1), channel_id=1, source_target_pairs={{0,4},{4,0},{8,12},{12,8},{1,5},{5,1},{9,13},{13,9},{2,6},{6,2},{1... | collective-permute-start | bytes 221192 | tf_op jit(solution)/shard_map/ppermute | solution.py:491
  3.7 2.6 %collective-permute-start.1 = (bf16[8,1,2,2304]{3,2,1,0:T(2,128)(2,1)}, bf16[8,1,2,2304]{3,2,1,0:T(2,128)(2,1)S(1)}, u32[]{:S(2)}, u32[]{:S(2)}) collective-permute-start(bf16[8,1,2,2304]{3,2,1,0:T(2,128)(2,1)} %refs_0_.1), channel_id=1, source_target_pairs={{0,8},{4,12},{8,0},{12,4},{1,9},{5,13},{9,1},{13,5},{2,10},{6,14},... | collective-permute-start | bytes 221192 | tf_op jit(solution)/shard_map/ppermute | solution.py:491
  6.3 0.0 collective-permute-start.2
  6.3 0.1 fusion.17.refs_0_.source_ref
  6.4 0.0 copy-start.3
  6.4 0.0 copy-start.1
  6.4 6.2 %shard_map.95.refs_4_.refs_0_ = bf16[11,2304,512]{2,1,0:T(8,128)(2,1)S(1)} custom-call(bf16[2304,9216]{1,0:T(8,128)(2,1)} %wg_ref.11, bf16[2304,9216]{1,0:T(8,128)(2,1)} %wu_ref.11, s32[64,1]{1,0:T(8,128)S(1)} %fusion.17.refs_0_.source_ref, s32[16,1]{1,0:T(8,128)S(1)} %fusion.38.refs_1_.source_ref, s32[4]{0:T(128)S(1)} %fusion.47.refs_2_.slot_ref), custom_call_target="tpu_custom_call" | custom-call | bytes 16515072 | tf_op jit(solution)/shard_map/pallas_call | solution.py:244
  12.6 0.0 copy-done.3
  12.6 0.0 collective-permute-done.refs_1_
  12.6 0.0 collective-permute-done.1.refs_2_
  12.6 0.1 collective-permute-done.2.refs_3_
  12.8 0.0 copy-done.1
  12.8 0.3 shard_map.96
  13.1 0.0 copy-start.2
  13.1 0.1 collective-permute-start.3
  13.2 1.7 %collective-permute-start.4 = (f32[64,128]{1,0:T(8,128)S(1)}, f32[64,128]{1,0:T(8,128)S(1)}, u32[]{:S(2)}, u32[]{:S(2)}) collective-permute-start(f32[64,128]{1,0:T(8,128)S(1)} %get-tuple-element.31.refs_1_.refs_0_), channel_id=1, source_target_pairs={{0,2},{1,3},{2,0},{3,1},{4,6},{5,7},{6,4},{7,5},{8,10},{9,11},{10,... | collective-permute-start | bytes 98312 | tf_op jit(solution)/shard_map/ppermute | solution.py:494
  14.9 0.2 collective-permute-start.5
  15.0 3.3 %shard_map.97.refs_4_._ = bf16[11,2304,512]{2,1,0:T(8,128)(2,1)S(1)} custom-call(bf16[2304,9216]{1,0:T(8,128)(2,1)} %wg_ref.11, bf16[2304,9216]{1,0:T(8,128)(2,1)} %wu_ref.11, bf16[11,2304,512]{2,1,0:T(8,128)(2,1)S(1)} %shard_map.95.refs_4_.refs_0_, f32[64,128]{1,0:T(8,128)S(1)} %get-tuple-element.31.refs_1_.refs_0_), custom_call_target="tpu_custom_call", output_to_operand_aliasing={{}: (2, {})} | custom-call | bytes 7077888 | tf_op jit(solution)/shard_map/pallas_call | solution.py:244
  18.4 0.0 collective-permute-done.3.refs_1_
  18.4 0.0 collective-permute-done.4.refs_2_
  18.4 0.0 collective-permute-done.5.refs_3_
  18.4 0.0 copy-done.2
  18.4 0.4 shard_map.98.x_ref
  18.8 7.4 %shard_map.99 = (bf16[2,32,4224]{2,1,0:T(8,128)(2,1)S(1)}, f32[2,32,2560]{2,1,0:T(8,128)S(1)}, f32[32,1664]{1,0:T(8,128)S(1)}, bf16[11,2304,512]{2,1,0:T(8,128)(2,1)S(1)}) custom-call(bf16[64,2304]{1,0:T(8,128)(2,1)S(1)} %shard_map.98.x_ref, bf16[2304,9216]{1,0:T(8,128)(2,1)} %wg_ref.11, ...), custom_call_target="tpu_custom_call", output_to_operand_aliasing={{3}: (5, {})} | custom-call | flops 2000683008 | bytes 23592960 | tf_op jit(solution)/shard_map/pallas_call | solution.py:334
  26.2 0.4 collective-permute-start.6
  26.6 8.5 %shard_map.103 = (bf16[2,32,2816]{2,1,0:T(8,128)(2,1)S(1)}, f32[2,32,2816]{2,1,0:T(8,128)S(1)}, bf16[11,2304,512]{2,1,0:T(8,128)(2,1)S(1)}) custom-call(bf16[64,2304]{1,0:T(8,128)(2,1)S(1)} %shard_map.98.x_ref, bf16[2304,9216]{1,0:T(8,128)(2,1)} %wg_ref.11, bf16[2304,9216]{1,0:T(8,128)(2,1)} %wu_ref.11, ...), custom_call_target="tpu_custom_call", output_to_operand_aliasing={{2}: (3, {})} | custom-call | flops 1660944384 | bytes 23592960 | tf_op jit(solution)/shard_map/pallas_call | solution.py:370
  35.1 0.2 collective-permute-start.11
  35.3 0.0 collective-permute-done.6.refs_0_
  35.3 0.1 shard_map.100
  35.4 1.7 %collective-permute-start.7 = (bf16[2,16,4224]{2,1,0:T(8,128)(2,1)S(1)}, bf16[2,16,4224]{2,1,0:T(8,128)(2,1)S(1)}, u32[]{:S(2)}, u32[]{:S(2)}) collective-permute-start(bf16[2,16,4224]{2,1,0:T(8,128)(2,1)S(1)} %get-tuple-element.36.refs_0_), channel_id=1, source_target_pairs={{0,2},{1,3},{2,0},{3,1},{4,6},{5,7},{6,4},{7,5},{8,10},{9,11},{10,... | collective-permute-start | bytes 811016 | tf_op jit(solution)/shard_map/ppermute | solution.py:488
  37.1 7.0 %shard_map.104 = (bf16[2,32,2048]{2,1,0:T(8,128)(2,1)S(1)}, f32[2,32,2048]{2,1,0:T(8,128)S(1)}, bf16[11,2304,512]{2,1,0:T(8,128)(2,1)S(1)}) custom-call(bf16[64,2304]{1,0:T(8,128)(2,1)S(1)} %shard_map.98.x_ref, bf16[2304,9216]{1,0:T(8,128)(2,1)} %wg_ref.11, bf16[2304,9216]{1,0:T(8,128)(2,1)} %wu_ref.11, ...), custom_call_target="tpu_custom_call", output_to_operand_aliasing={{2}: (3, {})} | custom-call | flops 1207959552 | bytes 18874368 | tf_op jit(solution)/shard_map/pallas_call | solution.py:370
  44.2 0.1 collective-permute-start.10
  44.3 0.0 collective-permute-done.11.refs_0_
  44.3 0.1 shard_map.105
  44.4 0.5 collective-permute-start.12
  44.9 0.0 collective-permute-done.7.refs_1_
  44.9 0.2 shard_map.101
  45.1 2.2 %collective-permute-start.8 = (bf16[1,8,1664]{2,1,0:T(8,128)(2,1)S(1)}, bf16[1,8,1664]{2,1,0:T(8,128)(2,1)S(1)}, u32[]{:S(2)}, u32[]{:S(2)}) collective-permute-start(bf16[1,8,1664]{2,1,0:T(8,128)(2,1)S(1)} %get-tuple-element.38), channel_id=1, source_target_pairs={{0,8},{4,12},{8,0},{12,4},{1,9},{5,13},{9,1},{13,5},{2,10},{6,14},... | collective-permute-start | bytes 79880 | tf_op jit(solution)/shard_map/ppermute | solution.py:491
  47.2 0.0 copy-start
  47.2 0.0 copy-start.4
  47.2 0.0 copy-start.5
  47.2 4.0 %shard_map.106 = (bf16[2,32,1792]{2,1,0:T(8,128)(2,1)S(1)}, f32[2,32,1792]{2,1,0:T(8,128)S(1)}, bf16[11,2304,512]{2,1,0:T(8,128)(2,1)S(1)}) custom-call(bf16[64,2304]{1,0:T(8,128)(2,1)S(1)} %shard_map.98.x_ref, bf16[2304,9216]{1,0:T(8,128)(2,1)} %wg_ref.11, bf16[2304,9216]{1,0:T(8,128)(2,1)} %wu_ref.11, ...), custom_call_target="tpu_custom_call", output_to_operand_aliasing={{2}: (3, {})} | custom-call | flops 1056964608 | bytes 7077888 | tf_op jit(solution)/shard_map/pallas_call | solution.py:370
  51.2 0.1 collective-permute-done.12.refs_3_
  51.4 0.0 collective-permute-done.10.refs_0_
  51.4 0.0 collective-permute-done.8.came_ref.refs_2_
  51.4 0.1 collective-permute-start.13
  51.5 1.5 %collective-permute-start.14 = (bf16[2,16,2048]{2,1,0:T(8,128)(2,1)S(1)}, bf16[2,16,2048]{2,1,0:T(8,128)(2,1)S(1)}, u32[]{:S(2)}, u32[]{:S(2)}) collective-permute-start(bf16[2,16,2048]{2,1,0:T(8,128)(2,1)S(1)} %get-tuple-element.56), channel_id=1, source_target_pairs={{0,2},{1,3},{2,0},{3,1},{4,6},{5,7},{6,4},{7,5},{8,10},{9,11},{10,... | collective-permute-start | bytes 393224 | tf_op jit(solution)/shard_map/ppermute | solution.py:488
  53.0 0.0 collective-permute-done.13.refs_0_
  53.0 1.5 %collective-permute-start.15 = (bf16[2,16,1792]{2,1,0:T(8,128)(2,1)S(1)}, bf16[2,16,1792]{2,1,0:T(8,128)(2,1)S(1)}, u32[]{:S(2)}, u32[]{:S(2)}) collective-permute-start(bf16[2,16,1792]{2,1,0:T(8,128)(2,1)S(1)} %get-tuple-element.52.refs_2_.refs_4_), channel_id=1, source_target_pairs={{0,2},{1,3},{2,0},{3,1},{4,6},{5,7},{6,4},{7,5},{8,10},{9,11},{10,... | collective-permute-start | bytes 344072 | tf_op jit(solution)/shard_map/ppermute | solution.py:488
  54.5 2.2 %collective-permute-start.9 = (bf16[2,4,1664]{2,1,0:T(4,128)(2,1)S(1)}, bf16[2,4,1664]{2,1,0:T(4,128)(2,1)S(1)}, u32[]{:S(2)}, u32[]{:S(2)}) collective-permute-start(bf16[2,4,1664]{2,1,0:T(4,128)(2,1)S(1)} %get-tuple-element.40), channel_id=1, source_target_pairs={{0,4},{4,0},{8,12},{12,8},{1,5},{5,1},{9,13},{13,9},{2,6},{6,2},{1... | collective-permute-start | bytes 79880 | tf_op jit(solution)/shard_map/ppermute | solution.py:491
  56.8 0.2 shard_map.110.refs_0_
  56.9 1.7 %collective-permute-done.9.refs_1_ = bf16[2,4,1664]{2,1,0:T(4,128)(2,1)S(1)} collective-permute-done((bf16[2,4,1664]{2,1,0:T(4,128)(2,1)S(1)}, bf16[2,4,1664]{2,1,0:T(4,128)(2,1)S(1)}, u32[]{:S(2)}, u32[]{:S(2)}) %collective-permute-start.9) | collective-permute-done | bytes 26656 | tf_op jit(solution)/shard_map/ppermute | solution.py:491
  58.6 0.0 copy-done
  58.6 0.0 copy-done.4
  58.6 0.0 copy-done.5
  58.6 2.5 %shard_map.109 = bf16[2,1,2,6144]{3,2,1,0:T(2,128)(2,1)} custom-call(s32[4]{0:T(128)S(1)} %copy-done.4, s32[2]{0:T(128)S(1)} %bitcast.3, bf16[2,1024,512]{2,1,0:T(8,128)(2,1)S(1)} %bitcast.2, bf16[2,4,1664]{2,1,0:T(4,128)(2,1)S(1)} %get-tuple-element.39.refs_0_, bf16[2,4,1664]{2,1,0:T(4,128)(2,1)S(1)} %collective-permute-done.9.refs_1_, ...), custom_call_target="tpu_custom_call" | custom-call | flops 100663296 | bytes 2097152 | tf_op jit(solution)/shard_map/pallas_call | solution.py:461
  61.1 0.0 collective-permute-done.14.refs_2_
  61.1 0.0 collective-permute-done.15.refs_4_
  61.1 0.8 %shard_map.111 = bf16[2,4,2,9216]{3,2,1,0:T(2,128)(2,1)} custom-call(bf16[2,4,2,5376]{3,2,1,0:T(2,128)(2,1)S(1)} %shard_map.110.refs_0_, f32[2,16,2048]{2,1,0:T(8,128)S(1)} %get-tuple-element.55.refs_1_, bf16[2,16,2048]{2,1,0:T(8,128)(2,1)S(1)} %collective-permute-done.14.refs_2_, f32[2,16,1792]{2,1,0:T(8,128)S(1)} %get-tuple-element.57.refs_3_, ...), custom_call_target="tpu_custom_call" | custom-call | flops 331776 | bytes 20736 | tf_op jit(solution)/shard_map/pallas_call | solution.py:185
  (5 shorter events, 0.1 us)
Async XLA Ops:
  0.6 12.0 %collective-permute-start = (bf16[8,1,2,2304]{3,2,1,0:T(2,128)(2,1)}, bf16[8,1,2,2304]{3,2,1,0:T(2,128)(2,1)S(1)}, u32[]{:S(2)}, u32[]{:S(2)}) collective-permute-start(bf16[8,1,2,2304]{3,2,1,0:T(2,128)(2,1)} %refs_0_.1), channel_id=1, source_target_pairs={{0,4},{4,0},{8,12},{12,8},{1,5},{5,1},{9,13},{13,9},{2,6},{6,2},{1... | collective-permute-start | bytes 221192 | tf_op jit(solution)/shard_map/ppermute | solution.py:491
  3.7 8.9 %collective-permute-start.1 = (bf16[8,1,2,2304]{3,2,1,0:T(2,128)(2,1)}, bf16[8,1,2,2304]{3,2,1,0:T(2,128)(2,1)S(1)}, u32[]{:S(2)}, u32[]{:S(2)}) collective-permute-start(bf16[8,1,2,2304]{3,2,1,0:T(2,128)(2,1)} %refs_0_.1), channel_id=1, source_target_pairs={{0,8},{4,12},{8,0},{12,4},{1,9},{5,13},{9,1},{13,5},{2,10},{6,14},... | collective-permute-start | bytes 221192 | tf_op jit(solution)/shard_map/ppermute | solution.py:491
  6.3 6.5 %collective-permute-start.2 = (bf16[8,1,2,2304]{3,2,1,0:T(2,128)(2,1)}, bf16[8,1,2,2304]{3,2,1,0:T(2,128)(2,1)S(1)}, u32[]{:S(2)}, u32[]{:S(2)}) collective-permute-start(bf16[8,1,2,2304]{3,2,1,0:T(2,128)(2,1)} %refs_0_.1), channel_id=1, source_target_pairs={{0,12},{4,8},{8,4},{12,0},{1,13},{5,9},{9,5},{13,1},{2,14},{6,10},... | collective-permute-start | bytes 221192 | tf_op jit(solution)/shard_map/ppermute | solution.py:491
  6.4 6.2 %copy-start.3 = (s32[4]{0:T(128)}, s32[4]{0:T(128)S(1)}, u32[]{:S(2)}) copy-start(s32[4]{0:T(128)S(1)} %fusion.47.refs_2_.slot_ref) | copy-start | bytes 52
  6.4 6.4 %copy-start.1 = (bf16[8,1,2,2304]{3,2,1,0:T(2,128)(2,1)S(1)}, bf16[8,1,2,2304]{3,2,1,0:T(2,128)(2,1)}, u32[]{:S(2)}) copy-start(bf16[8,1,2,2304]{3,2,1,0:T(2,128)(2,1)} %refs_0_.1) | copy-start | bytes 221188
  13.1 5.3 %copy-start.2 = (f32[2304]{0:T(1024)S(1)}, f32[2304]{0:T(1024)}, u32[]{:S(2)}) copy-start(f32[2304]{0:T(1024)} %gain_ref.1) | copy-start | bytes 27652
  13.1 5.3 %collective-permute-start.3 = (f32[64,128]{1,0:T(8,128)S(1)}, f32[64,128]{1,0:T(8,128)S(1)}, u32[]{:S(2)}, u32[]{:S(2)}) collective-permute-start(f32[64,128]{1,0:T(8,128)S(1)} %get-tuple-element.31.refs_1_.refs_0_), channel_id=1, source_target_pairs={{0,1},{1,0},{2,3},{3,2},{4,5},{5,4},{6,7},{7,6},{8,9},{9,8},{10,11... | collective-permute-start | bytes 98312 | tf_op jit(solution)/shard_map/ppermute | solution.py:494
  13.2 5.2 %collective-permute-start.4 = (f32[64,128]{1,0:T(8,128)S(1)}, f32[64,128]{1,0:T(8,128)S(1)}, u32[]{:S(2)}, u32[]{:S(2)}) collective-permute-start(f32[64,128]{1,0:T(8,128)S(1)} %get-tuple-element.31.refs_1_.refs_0_), channel_id=1, source_target_pairs={{0,2},{1,3},{2,0},{3,1},{4,6},{5,7},{6,4},{7,5},{8,10},{9,11},{10,... | collective-permute-start | bytes 98312 | tf_op jit(solution)/shard_map/ppermute | solution.py:494
  14.9 3.5 %collective-permute-start.5 = (f32[64,128]{1,0:T(8,128)S(1)}, f32[64,128]{1,0:T(8,128)S(1)}, u32[]{:S(2)}, u32[]{:S(2)}) collective-permute-start(f32[64,128]{1,0:T(8,128)S(1)} %get-tuple-element.31.refs_1_.refs_0_), channel_id=1, source_target_pairs={{0,3},{1,2},{2,1},{3,0},{4,7},{5,6},{6,5},{7,4},{8,11},{9,10},{10,... | collective-permute-start | bytes 98312 | tf_op jit(solution)/shard_map/ppermute | solution.py:494
  26.2 9.1 %collective-permute-start.6 = (bf16[2,32,4224]{2,1,0:T(8,128)(2,1)S(1)}, bf16[2,32,4224]{2,1,0:T(8,128)(2,1)S(1)}, u32[]{:S(2)}, u32[]{:S(2)}) collective-permute-start(bf16[2,32,4224]{2,1,0:T(8,128)(2,1)S(1)} %get-tuple-element.32.refs_0_), channel_id=1, source_target_pairs={{0,1},{1,0},{2,3},{3,2},{4,5},{5,4},{6,7},{7,6},{8,9},{9,8},{10,11... | collective-permute-start | bytes 1622024 | tf_op jit(solution)/shard_map/ppermute | solution.py:494
  35.1 9.2 %collective-permute-start.11 = (bf16[2,32,2816]{2,1,0:T(8,128)(2,1)S(1)}, bf16[2,32,2816]{2,1,0:T(8,128)(2,1)S(1)}, u32[]{:S(2)}, u32[]{:S(2)}) collective-permute-start(bf16[2,32,2816]{2,1,0:T(8,128)(2,1)S(1)} %get-tuple-element.43.refs_1_), channel_id=1, source_target_pairs={{0,1},{1,0},{2,3},{3,2},{4,5},{5,4},{6,7},{7,6},{8,9},{9,8},{10,11... | collective-permute-start | bytes 1081352 | tf_op jit(solution)/shard_map/ppermute | solution.py:494
  35.4 9.4 %collective-permute-start.7 = (bf16[2,16,4224]{2,1,0:T(8,128)(2,1)S(1)}, bf16[2,16,4224]{2,1,0:T(8,128)(2,1)S(1)}, u32[]{:S(2)}, u32[]{:S(2)}) collective-permute-start(bf16[2,16,4224]{2,1,0:T(8,128)(2,1)S(1)} %get-tuple-element.36.refs_0_), channel_id=1, source_target_pairs={{0,2},{1,3},{2,0},{3,1},{4,6},{5,7},{6,4},{7,5},{8,10},{9,11},{10,... | collective-permute-start | bytes 811016 | tf_op jit(solution)/shard_map/ppermute | solution.py:488
  44.2 7.2 %collective-permute-start.10 = (bf16[2,32,2048]{2,1,0:T(8,128)(2,1)S(1)}, bf16[2,32,2048]{2,1,0:T(8,128)(2,1)S(1)}, u32[]{:S(2)}, u32[]{:S(2)}) collective-permute-start(bf16[2,32,2048]{2,1,0:T(8,128)(2,1)S(1)} %get-tuple-element.44.refs_2_), channel_id=1, source_target_pairs={{0,1},{1,0},{2,3},{3,2},{4,5},{5,4},{6,7},{7,6},{8,9},{9,8},{10,11... | collective-permute-start | bytes 786440 | tf_op jit(solution)/shard_map/ppermute | solution.py:494
  44.4 7.0 %collective-permute-start.12 = (bf16[2,16,2816]{2,1,0:T(8,128)(2,1)S(1)}, bf16[2,16,2816]{2,1,0:T(8,128)(2,1)S(1)}, u32[]{:S(2)}, u32[]{:S(2)}) collective-permute-start(bf16[2,16,2816]{2,1,0:T(8,128)(2,1)S(1)} %get-tuple-element.47.refs_0_), channel_id=1, source_target_pairs={{0,2},{1,3},{2,0},{3,1},{4,6},{5,7},{6,4},{7,5},{8,10},{9,11},{10,... | collective-permute-start | bytes 540680 | tf_op jit(solution)/shard_map/ppermute | solution.py:488
  45.1 6.3 %collective-permute-start.8 = (bf16[1,8,1664]{2,1,0:T(8,128)(2,1)S(1)}, bf16[1,8,1664]{2,1,0:T(8,128)(2,1)S(1)}, u32[]{:S(2)}, u32[]{:S(2)}) collective-permute-start(bf16[1,8,1664]{2,1,0:T(8,128)(2,1)S(1)} %get-tuple-element.38), channel_id=1, source_target_pairs={{0,8},{4,12},{8,0},{12,4},{1,9},{5,13},{9,1},{13,5},{2,10},{6,14},... | collective-permute-start | bytes 79880 | tf_op jit(solution)/shard_map/ppermute | solution.py:491
  47.2 11.4 %copy-start = (bf16[2,1,1024,512]{3,2,1,0:T(8,128)(2,1)S(1)}, bf16[2,1,1024,512]{3,2,1,0:T(8,128)(2,1)}, u32[]{:S(2)}) copy-start(bf16[2,1,1024,512]{3,2,1,0:T(8,128)(2,1)} %param.14) | copy-start | bytes 6291460
  47.2 11.4 %copy-start.4 = (s32[4]{0:T(128)S(1)}, s32[4]{0:T(128)}, u32[]{:S(2)}) copy-start(s32[4]{0:T(128)} %copy-done.3) | copy-start | bytes 52
  47.2 11.4 %copy-start.5 = (s32[2,1]{0,1:T(1,128)S(1)}, s32[2,1]{0,1:T(1,128)}, u32[]{:S(2)}) copy-start(s32[2,1]{0,1:T(1,128)} %param.15) | copy-start | bytes 28
  51.4 1.6 %collective-permute-start.13 = (bf16[2,32,1792]{2,1,0:T(8,128)(2,1)S(1)}, bf16[2,32,1792]{2,1,0:T(8,128)(2,1)S(1)}, u32[]{:S(2)}, u32[]{:S(2)}) collective-permute-start(bf16[2,32,1792]{2,1,0:T(8,128)(2,1)S(1)} %get-tuple-element.50), channel_id=1, source_target_pairs={{0,1},{1,0},{2,3},{3,2},{4,5},{5,4},{6,7},{7,6},{8,9},{9,8},{10,11... | collective-permute-start | bytes 688136 | tf_op jit(solution)/shard_map/ppermute | solution.py:494
  51.5 9.6 %collective-permute-start.14 = (bf16[2,16,2048]{2,1,0:T(8,128)(2,1)S(1)}, bf16[2,16,2048]{2,1,0:T(8,128)(2,1)S(1)}, u32[]{:S(2)}, u32[]{:S(2)}) collective-permute-start(bf16[2,16,2048]{2,1,0:T(8,128)(2,1)S(1)} %get-tuple-element.56), channel_id=1, source_target_pairs={{0,2},{1,3},{2,0},{3,1},{4,6},{5,7},{6,4},{7,5},{8,10},{9,11},{10,... | collective-permute-start | bytes 393224 | tf_op jit(solution)/shard_map/ppermute | solution.py:488
  53.0 8.0 %collective-permute-start.15 = (bf16[2,16,1792]{2,1,0:T(8,128)(2,1)S(1)}, bf16[2,16,1792]{2,1,0:T(8,128)(2,1)S(1)}, u32[]{:S(2)}, u32[]{:S(2)}) collective-permute-start(bf16[2,16,1792]{2,1,0:T(8,128)(2,1)S(1)} %get-tuple-element.52.refs_2_.refs_4_), channel_id=1, source_target_pairs={{0,2},{1,3},{2,0},{3,1},{4,6},{5,7},{6,4},{7,5},{8,10},{9,11},{10,... | collective-permute-start | bytes 344072 | tf_op jit(solution)/shard_map/ppermute | solution.py:488
  54.5 4.1 %collective-permute-start.9 = (bf16[2,4,1664]{2,1,0:T(4,128)(2,1)S(1)}, bf16[2,4,1664]{2,1,0:T(4,128)(2,1)S(1)}, u32[]{:S(2)}, u32[]{:S(2)}) collective-permute-start(bf16[2,4,1664]{2,1,0:T(4,128)(2,1)S(1)} %get-tuple-element.40), channel_id=1, source_target_pairs={{0,4},{4,0},{8,12},{12,8},{1,5},{5,1},{9,13},{13,9},{2,6},{6,2},{1... | collective-permute-start | bytes 79880 | tf_op jit(solution)/shard_map/ppermute | solution.py:491

commit v12 on v10

--- a/solution.py
+++ b/solution.py
@@ -514,7 +514,7 @@
     weights = (w_gate, w_up)
     tiles = w_gate.shape[1] // TILE
     before = [tiles * share // 36 for share in (7, 9)]
-    bounds = [0, before[1]] + [tiles * share // 36 for share in (20, 29, 36)]
+    bounds = [0, before[1]] + [tiles * share // 36 for share in (21, 30, 36)]
     ahead = [before[1]] + [max(1, tiles * share // 36) for share in (5, 4, 4)] + [0]
     gathered = [tokens] + [swap_x(tokens, bits) for bits in range(1, size_x)]
     ring = load(weights, 0, before[0], None, (source, order, slots))

time: 61.6 us -> 62 us (level)
  waiting for transfers between devices: 2.72 us -> 3.84 us
  starting transfers between devices: 17.2 us -> 16.4 us
    ppermute x4, waiting for transfers between devices: 0.01 us -> 0.68 us  [shift_y(): lax.ppermute(value, 'gy', [(i, (i + by) % size_y) for i in range(size_y)])]
  transfers between devices with their start and end apart: 16 -> 16, of which waited for: 4 -> 5; matrix products, arithmetic and copies ran while one was open for 0% -> 0% of each run, Pallas kernels for 52% -> 52%
where the time goes in v12:
time: 62 us; the launch traced here: 61.9 us
  Pallas kernels  40.7 us (66%)
  starting transfers between devices  16.4 us (26%)
  waiting for transfers between devices  3.84 us (6%)
  between operations  0.83 us (1%)
    pallas_call x3, Pallas kernels, wide_sums(): pl.pallas_call(functools.partial(wide_kernel, first, tiles, held, followi...  20.3 us
    ppermute x5, starting transfers between devices, swap_x(): return lax.ppermute(value, 'gx', [(i, i ^ bits) for i in range(size_x)])  9.48 us
    pallas_call x2, Pallas kernels, load(): pl.pallas_call(functools.partial(load_kernel, first, last), out_shape=rin...  8.73 us
    pallas_call x1, Pallas kernels, first_sums(): pl.pallas_call(functools.partial(first_kernel, tiles, following), out_sha...  7.05 us
    ppermute x4, starting transfers between devices, shift_y(): lax.ppermute(value, 'gy', [(i, (i + by) % size_y) for i in range(size_y)])  4.17 us
    ppermute x7, starting transfers between devices, swap(): return lax.ppermute(value, 'gy', [(i, i ^ bits) for i in range(size_y)])  2.77 us
    pallas_call x1, Pallas kernels, attend(): pl.pallas_call(functools.partial(attend_kernel, count, steps, query_cols)...  2.48 us
    ppermute x5, waiting for transfers between devices, swap_x(): return lax.ppermute(value, 'gx', [(i, i ^ bits) for i in range(size_x)])  2.17 us
  transfers between devices with their start and end apart: 16, of which 5 were waited for; matrix products, arithmetic and copies ran while one was open for 0% of the time, Pallas kernels for 52%

profile of v12, /device:TPU:0, one launch (start us, length us, event | category | flops | bytes accessed | tf_op | source)
XLA Modules:
  0.0 61.9 jit_solution(432180262839933412)
XLA Ops:
  0.6 3.1 %collective-permute-start = (bf16[8,1,2,2304]{3,2,1,0:T(2,128)(2,1)}, bf16[8,1,2,2304]{3,2,1,0:T(2,128)(2,1)S(1)}, u32[]{:S(2)}, u32[]{:S(2)}) collective-permute-start(bf16[8,1,2,2304]{3,2,1,0:T(2,128)(2,1)} %refs_0_.1), channel_id=1, source_target_pairs={{0,4},{4,0},{8,12},{12,8},{1,5},{5,1},{9,13},{13,9},{2,6},{6,2},{1... | collective-permute-start | bytes 221192 | tf_op jit(solution)/shard_map/ppermute | solution.py:491
  3.7 2.6 %collective-permute-start.1 = (bf16[8,1,2,2304]{3,2,1,0:T(2,128)(2,1)}, bf16[8,1,2,2304]{3,2,1,0:T(2,128)(2,1)S(1)}, u32[]{:S(2)}, u32[]{:S(2)}) collective-permute-start(bf16[8,1,2,2304]{3,2,1,0:T(2,128)(2,1)} %refs_0_.1), channel_id=1, source_target_pairs={{0,8},{4,12},{8,0},{12,4},{1,9},{5,13},{9,1},{13,5},{2,10},{6,14},... | collective-permute-start | bytes 221192 | tf_op jit(solution)/shard_map/ppermute | solution.py:491
  6.3 0.0 collective-permute-start.2
  6.3 0.1 fusion.17.refs_0_.source_ref
  6.4 0.0 copy-start.3
  6.4 0.0 copy-start.1
  6.4 6.2 %shard_map.95.refs_4_.refs_0_ = bf16[10,2304,512]{2,1,0:T(8,128)(2,1)S(1)} custom-call(bf16[2304,9216]{1,0:T(8,128)(2,1)} %wg_ref.11, bf16[2304,9216]{1,0:T(8,128)(2,1)} %wu_ref.11, s32[64,1]{1,0:T(8,128)S(1)} %fusion.17.refs_0_.source_ref, s32[16,1]{1,0:T(8,128)S(1)} %fusion.38.refs_1_.source_ref, s32[4]{0:T(128)S(1)} %fusion.47.refs_2_.slot_ref), custom_call_target="tpu_custom_call" | custom-call | bytes 16515072 | tf_op jit(solution)/shard_map/pallas_call | solution.py:244
  12.6 0.0 copy-done.3
  12.6 0.0 collective-permute-done.refs_1_
  12.6 0.0 collective-permute-done.1.refs_2_
  12.6 0.1 collective-permute-done.2.refs_3_
  12.8 0.0 copy-done.1
  12.8 0.3 shard_map.96
  13.1 0.0 copy-start.2
  13.1 0.1 collective-permute-start.3
  13.2 1.7 %collective-permute-start.4 = (f32[64,128]{1,0:T(8,128)S(1)}, f32[64,128]{1,0:T(8,128)S(1)}, u32[]{:S(2)}, u32[]{:S(2)}) collective-permute-start(f32[64,128]{1,0:T(8,128)S(1)} %get-tuple-element.31.refs_1_.refs_0_), channel_id=1, source_target_pairs={{0,2},{1,3},{2,0},{3,1},{4,6},{5,7},{6,4},{7,5},{8,10},{9,11},{10,... | collective-permute-start | bytes 98312 | tf_op jit(solution)/shard_map/ppermute | solution.py:494
  14.9 0.2 collective-permute-start.5
  15.0 2.6 %shard_map.97.refs_4_._ = bf16[10,2304,512]{2,1,0:T(8,128)(2,1)S(1)} custom-call(bf16[2304,9216]{1,0:T(8,128)(2,1)} %wg_ref.11, bf16[2304,9216]{1,0:T(8,128)(2,1)} %wu_ref.11, bf16[10,2304,512]{2,1,0:T(8,128)(2,1)S(1)} %shard_map.95.refs_4_.refs_0_, f32[64,128]{1,0:T(8,128)S(1)} %get-tuple-element.31.refs_1_.refs_0_), custom_call_target="tpu_custom_call", output_to_operand_aliasing={{}: (2, {})} | custom-call | bytes 4718592 | tf_op jit(solution)/shard_map/pallas_call | solution.py:244
  17.6 0.0 collective-permute-done.3.refs_1_
  17.6 0.0 collective-permute-done.4.refs_2_
  17.6 0.6 collective-permute-done.5.refs_3_
  18.2 0.0 copy-done.2
  18.2 0.4 shard_map.98.x_ref
  18.6 7.1 %shard_map.99 = (bf16[2,32,3968]{2,1,0:T(8,128)(2,1)S(1)}, f32[2,32,2304]{2,1,0:T(8,128)S(1)}, f32[32,1664]{1,0:T(8,128)S(1)}, bf16[10,2304,512]{2,1,0:T(8,128)(2,1)S(1)}) custom-call(bf16[64,2304]{1,0:T(8,128)(2,1)S(1)} %shard_map.98.x_ref, bf16[2304,9216]{1,0:T(8,128)(2,1)} %wg_ref.11, ...), custom_call_target="tpu_custom_call", output_to_operand_aliasing={{3}: (5, {})} | custom-call | flops 1849688064 | bytes 21233664 | tf_op jit(solution)/shard_map/pallas_call | solution.py:334
  25.7 0.2 collective-permute-start.6
  25.9 9.1 %shard_map.103 = (bf16[2,32,3072]{2,1,0:T(8,128)(2,1)S(1)}, f32[2,32,3072]{2,1,0:T(8,128)S(1)}, bf16[10,2304,512]{2,1,0:T(8,128)(2,1)S(1)}) custom-call(bf16[64,2304]{1,0:T(8,128)(2,1)S(1)} %shard_map.98.x_ref, bf16[2304,9216]{1,0:T(8,128)(2,1)} %wg_ref.11, bf16[2304,9216]{1,0:T(8,128)(2,1)} %wu_ref.11, ...), custom_call_target="tpu_custom_call", output_to_operand_aliasing={{2}: (3, {})} | custom-call | flops 1811939328 | bytes 25952256 | tf_op jit(solution)/shard_map/pallas_call | solution.py:370
  35.0 0.4 collective-permute-start.11
  35.5 0.0 collective-permute-done.6.refs_0_
  35.5 0.1 shard_map.100
  35.5 1.1 %collective-permute-start.7 = (bf16[2,16,3968]{2,1,0:T(8,128)(2,1)S(1)}, bf16[2,16,3968]{2,1,0:T(8,128)(2,1)S(1)}, u32[]{:S(2)}, u32[]{:S(2)}) collective-permute-start(bf16[2,16,3968]{2,1,0:T(8,128)(2,1)S(1)} %get-tuple-element.36.refs_0_), channel_id=1, source_target_pairs={{0,2},{1,3},{2,0},{3,1},{4,6},{5,7},{6,4},{7,5},{8,10},{9,11},{10,... | collective-permute-start | bytes 761864 | tf_op jit(solution)/shard_map/ppermute | solution.py:488
  36.7 7.7 %shard_map.104 = (bf16[2,32,2304]{2,1,0:T(8,128)(2,1)S(1)}, f32[2,32,2304]{2,1,0:T(8,128)S(1)}, bf16[10,2304,512]{2,1,0:T(8,128)(2,1)S(1)}) custom-call(bf16[64,2304]{1,0:T(8,128)(2,1)S(1)} %shard_map.98.x_ref, bf16[2304,9216]{1,0:T(8,128)(2,1)} %wg_ref.11, bf16[2304,9216]{1,0:T(8,128)(2,1)} %wu_ref.11, ...), custom_call_target="tpu_custom_call", output_to_operand_aliasing={{2}: (3, {})} | custom-call | flops 1358954496 | bytes 21233664 | tf_op jit(solution)/shard_map/pallas_call | solution.py:370
  44.4 0.1 collective-permute-start.10
  44.6 0.0 collective-permute-done.11.refs_0_
  44.6 0.1 shard_map.105
  44.6 1.0 %collective-permute-start.12 = (bf16[2,16,3072]{2,1,0:T(8,128)(2,1)S(1)}, bf16[2,16,3072]{2,1,0:T(8,128)(2,1)S(1)}, u32[]{:S(2)}, u32[]{:S(2)}) collective-permute-start(bf16[2,16,3072]{2,1,0:T(8,128)(2,1)S(1)} %get-tuple-element.47.refs_0_), channel_id=1, source_target_pairs={{0,2},{1,3},{2,0},{3,1},{4,6},{5,7},{6,4},{7,5},{8,10},{9,11},{10,... | collective-permute-start | bytes 589832 | tf_op jit(solution)/shard_map/ppermute | solution.py:488
  45.6 0.0 collective-permute-done.7.refs_1_
  45.6 0.2 shard_map.101
  45.8 2.1 %collective-permute-start.8 = (bf16[1,8,1664]{2,1,0:T(8,128)(2,1)S(1)}, bf16[1,8,1664]{2,1,0:T(8,128)(2,1)S(1)}, u32[]{:S(2)}, u32[]{:S(2)}) collective-permute-start(bf16[1,8,1664]{2,1,0:T(8,128)(2,1)S(1)} %get-tuple-element.38), channel_id=1, source_target_pairs={{0,8},{4,12},{8,0},{12,4},{1,9},{5,13},{9,1},{13,5},{2,10},{6,14},... | collective-permute-start | bytes 79880 | tf_op jit(solution)/shard_map/ppermute | solution.py:491
  47.9 0.0 copy-start
  47.9 0.0 copy-start.4
  47.9 0.0 copy-start.5
  47.9 3.4 %shard_map.106 = (bf16[2,32,1536]{2,1,0:T(8,128)(2,1)S(1)}, f32[2,32,1536]{2,1,0:T(8,128)S(1)}, bf16[10,2304,512]{2,1,0:T(8,128)(2,1)S(1)}) custom-call(bf16[64,2304]{1,0:T(8,128)(2,1)S(1)} %shard_map.98.x_ref, bf16[2304,9216]{1,0:T(8,128)(2,1)} %wg_ref.11, bf16[2304,9216]{1,0:T(8,128)(2,1)} %wu_ref.11, ...), custom_call_target="tpu_custom_call", output_to_operand_aliasing={{2}: (3, {})} | custom-call | flops 905969664 | bytes 4718592 | tf_op jit(solution)/shard_map/pallas_call | solution.py:370
  51.3 0.7 %collective-permute-done.12.refs_3_ = bf16[2,16,3072]{2,1,0:T(8,128)(2,1)S(1)} collective-permute-done((bf16[2,16,3072]{2,1,0:T(8,128)(2,1)S(1)}, bf16[2,16,3072]{2,1,0:T(8,128)(2,1)S(1)}, u32[]{:S(2)}, u32[]{:S(2)}) %collective-permute-start.12) | collective-permute-done | bytes 196640 | tf_op jit(solution)/shard_map/ppermute | solution.py:488
  52.0 0.0 collective-permute-done.8.came_ref.refs_2_
  52.0 0.0 collective-permute-done.10.refs_0_
  52.0 0.1 collective-permute-start.13
  52.1 1.0 %collective-permute-start.14 = (bf16[2,16,2304]{2,1,0:T(8,128)(2,1)S(1)}, bf16[2,16,2304]{2,1,0:T(8,128)(2,1)S(1)}, u32[]{:S(2)}, u32[]{:S(2)}) collective-permute-start(bf16[2,16,2304]{2,1,0:T(8,128)(2,1)S(1)} %get-tuple-element.56), channel_id=1, source_target_pairs={{0,2},{1,3},{2,0},{3,1},{4,6},{5,7},{6,4},{7,5},{8,10},{9,11},{10,... | collective-permute-start | bytes 442376 | tf_op jit(solution)/shard_map/ppermute | solution.py:488
  53.1 0.4 collective-permute-done.13.refs_0_
  53.6 1.0 %collective-permute-start.15 = (bf16[2,16,1536]{2,1,0:T(8,128)(2,1)S(1)}, bf16[2,16,1536]{2,1,0:T(8,128)(2,1)S(1)}, u32[]{:S(2)}, u32[]{:S(2)}) collective-permute-start(bf16[2,16,1536]{2,1,0:T(8,128)(2,1)S(1)} %get-tuple-element.52.refs_2_.refs_4_), channel_id=1, source_target_pairs={{0,2},{1,3},{2,0},{3,1},{4,6},{5,7},{6,4},{7,5},{8,10},{9,11},{10,... | collective-permute-start | bytes 294920 | tf_op jit(solution)/shard_map/ppermute | solution.py:488
  54.6 1.7 %collective-permute-start.9 = (bf16[2,4,1664]{2,1,0:T(4,128)(2,1)S(1)}, bf16[2,4,1664]{2,1,0:T(4,128)(2,1)S(1)}, u32[]{:S(2)}, u32[]{:S(2)}) collective-permute-start(bf16[2,4,1664]{2,1,0:T(4,128)(2,1)S(1)} %get-tuple-element.40), channel_id=1, source_target_pairs={{0,4},{4,0},{8,12},{12,8},{1,5},{5,1},{9,13},{13,9},{2,6},{6,2},{1... | collective-permute-start | bytes 79880 | tf_op jit(solution)/shard_map/ppermute | solution.py:491
  56.3 0.2 shard_map.110.refs_0_
  56.5 2.0 %collective-permute-done.9.refs_1_ = bf16[2,4,1664]{2,1,0:T(4,128)(2,1)S(1)} collective-permute-done((bf16[2,4,1664]{2,1,0:T(4,128)(2,1)S(1)}, bf16[2,4,1664]{2,1,0:T(4,128)(2,1)S(1)}, u32[]{:S(2)}, u32[]{:S(2)}) %collective-permute-start.9) | collective-permute-done | bytes 26656 | tf_op jit(solution)/shard_map/ppermute | solution.py:491
  58.5 0.0 copy-done
  58.5 0.0 copy-done.4
  58.5 0.0 copy-done.5
  58.5 2.5 %shard_map.109 = bf16[2,1,2,6144]{3,2,1,0:T(2,128)(2,1)} custom-call(s32[4]{0:T(128)S(1)} %copy-done.4, s32[2]{0:T(128)S(1)} %bitcast.3, bf16[2,1024,512]{2,1,0:T(8,128)(2,1)S(1)} %bitcast.2, bf16[2,4,1664]{2,1,0:T(4,128)(2,1)S(1)} %get-tuple-element.39.refs_0_, bf16[2,4,1664]{2,1,0:T(4,128)(2,1)S(1)} %collective-permute-done.9.refs_1_, ...), custom_call_target="tpu_custom_call" | custom-call | flops 100663296 | bytes 2097152 | tf_op jit(solution)/shard_map/pallas_call | solution.py:461
  61.0 0.0 collective-permute-done.14.refs_2_
  61.0 0.0 collective-permute-done.15.refs_4_
  61.0 0.8 %shard_map.111 = bf16[2,4,2,9216]{3,2,1,0:T(2,128)(2,1)} custom-call(bf16[2,4,2,5376]{3,2,1,0:T(2,128)(2,1)S(1)} %shard_map.110.refs_0_, f32[2,16,2304]{2,1,0:T(8,128)S(1)} %get-tuple-element.55.refs_1_, bf16[2,16,2304]{2,1,0:T(8,128)(2,1)S(1)} %collective-permute-done.14.refs_2_, f32[2,16,1536]{2,1,0:T(8,128)S(1)} %get-tuple-element.57.refs_3_, ...), custom_call_target="tpu_custom_call" | custom-call | flops 331776 | bytes 20736 | tf_op jit(solution)/shard_map/pallas_call | solution.py:185
  (5 shorter events, 0.1 us)
Async XLA Ops:
  0.6 12.0 %collective-permute-start = (bf16[8,1,2,2304]{3,2,1,0:T(2,128)(2,1)}, bf16[8,1,2,2304]{3,2,1,0:T(2,128)(2,1)S(1)}, u32[]{:S(2)}, u32[]{:S(2)}) collective-permute-start(bf16[8,1,2,2304]{3,2,1,0:T(2,128)(2,1)} %refs_0_.1), channel_id=1, source_target_pairs={{0,4},{4,0},{8,12},{12,8},{1,5},{5,1},{9,13},{13,9},{2,6},{6,2},{1... | collective-permute-start | bytes 221192 | tf_op jit(solution)/shard_map/ppermute | solution.py:491
  3.7 8.9 %collective-permute-start.1 = (bf16[8,1,2,2304]{3,2,1,0:T(2,128)(2,1)}, bf16[8,1,2,2304]{3,2,1,0:T(2,128)(2,1)S(1)}, u32[]{:S(2)}, u32[]{:S(2)}) collective-permute-start(bf16[8,1,2,2304]{3,2,1,0:T(2,128)(2,1)} %refs_0_.1), channel_id=1, source_target_pairs={{0,8},{4,12},{8,0},{12,4},{1,9},{5,13},{9,1},{13,5},{2,10},{6,14},... | collective-permute-start | bytes 221192 | tf_op jit(solution)/shard_map/ppermute | solution.py:491
  6.3 6.5 %collective-permute-start.2 = (bf16[8,1,2,2304]{3,2,1,0:T(2,128)(2,1)}, bf16[8,1,2,2304]{3,2,1,0:T(2,128)(2,1)S(1)}, u32[]{:S(2)}, u32[]{:S(2)}) collective-permute-start(bf16[8,1,2,2304]{3,2,1,0:T(2,128)(2,1)} %refs_0_.1), channel_id=1, source_target_pairs={{0,12},{4,8},{8,4},{12,0},{1,13},{5,9},{9,5},{13,1},{2,14},{6,10},... | collective-permute-start | bytes 221192 | tf_op jit(solution)/shard_map/ppermute | solution.py:491
  6.4 6.2 %copy-start.3 = (s32[4]{0:T(128)}, s32[4]{0:T(128)S(1)}, u32[]{:S(2)}) copy-start(s32[4]{0:T(128)S(1)} %fusion.47.refs_2_.slot_ref) | copy-start | bytes 52
  6.4 6.4 %copy-start.1 = (bf16[8,1,2,2304]{3,2,1,0:T(2,128)(2,1)S(1)}, bf16[8,1,2,2304]{3,2,1,0:T(2,128)(2,1)}, u32[]{:S(2)}) copy-start(bf16[8,1,2,2304]{3,2,1,0:T(2,128)(2,1)} %refs_0_.1) | copy-start | bytes 221188
  13.1 5.1 %copy-start.2 = (f32[2304]{0:T(1024)S(1)}, f32[2304]{0:T(1024)}, u32[]{:S(2)}) copy-start(f32[2304]{0:T(1024)} %gain_ref.1) | copy-start | bytes 27652
  13.1 4.5 %collective-permute-start.3 = (f32[64,128]{1,0:T(8,128)S(1)}, f32[64,128]{1,0:T(8,128)S(1)}, u32[]{:S(2)}, u32[]{:S(2)}) collective-permute-start(f32[64,128]{1,0:T(8,128)S(1)} %get-tuple-element.31.refs_1_.refs_0_), channel_id=1, source_target_pairs={{0,1},{1,0},{2,3},{3,2},{4,5},{5,4},{6,7},{7,6},{8,9},{9,8},{10,11... | collective-permute-start | bytes 98312 | tf_op jit(solution)/shard_map/ppermute | solution.py:494
  13.2 4.4 %collective-permute-start.4 = (f32[64,128]{1,0:T(8,128)S(1)}, f32[64,128]{1,0:T(8,128)S(1)}, u32[]{:S(2)}, u32[]{:S(2)}) collective-permute-start(f32[64,128]{1,0:T(8,128)S(1)} %get-tuple-element.31.refs_1_.refs_0_), channel_id=1, source_target_pairs={{0,2},{1,3},{2,0},{3,1},{4,6},{5,7},{6,4},{7,5},{8,10},{9,11},{10,... | collective-permute-start | bytes 98312 | tf_op jit(solution)/shard_map/ppermute | solution.py:494
  14.9 3.3 %collective-permute-start.5 = (f32[64,128]{1,0:T(8,128)S(1)}, f32[64,128]{1,0:T(8,128)S(1)}, u32[]{:S(2)}, u32[]{:S(2)}) collective-permute-start(f32[64,128]{1,0:T(8,128)S(1)} %get-tuple-element.31.refs_1_.refs_0_), channel_id=1, source_target_pairs={{0,3},{1,2},{2,1},{3,0},{4,7},{5,6},{6,5},{7,4},{8,11},{9,10},{10,... | collective-permute-start | bytes 98312 | tf_op jit(solution)/shard_map/ppermute | solution.py:494
  25.7 9.8 %collective-permute-start.6 = (bf16[2,32,3968]{2,1,0:T(8,128)(2,1)S(1)}, bf16[2,32,3968]{2,1,0:T(8,128)(2,1)S(1)}, u32[]{:S(2)}, u32[]{:S(2)}) collective-permute-start(bf16[2,32,3968]{2,1,0:T(8,128)(2,1)S(1)} %get-tuple-element.32.refs_0_), channel_id=1, source_target_pairs={{0,1},{1,0},{2,3},{3,2},{4,5},{5,4},{6,7},{7,6},{8,9},{9,8},{10,11... | collective-permute-start | bytes 1523720 | tf_op jit(solution)/shard_map/ppermute | solution.py:494
  35.0 9.5 %collective-permute-start.11 = (bf16[2,32,3072]{2,1,0:T(8,128)(2,1)S(1)}, bf16[2,32,3072]{2,1,0:T(8,128)(2,1)S(1)}, u32[]{:S(2)}, u32[]{:S(2)}) collective-permute-start(bf16[2,32,3072]{2,1,0:T(8,128)(2,1)S(1)} %get-tuple-element.43.refs_1_), channel_id=1, source_target_pairs={{0,1},{1,0},{2,3},{3,2},{4,5},{5,4},{6,7},{7,6},{8,9},{9,8},{10,11... | collective-permute-start | bytes 1179656 | tf_op jit(solution)/shard_map/ppermute | solution.py:494
  35.5 10.1 %collective-permute-start.7 = (bf16[2,16,3968]{2,1,0:T(8,128)(2,1)S(1)}, bf16[2,16,3968]{2,1,0:T(8,128)(2,1)S(1)}, u32[]{:S(2)}, u32[]{:S(2)}) collective-permute-start(bf16[2,16,3968]{2,1,0:T(8,128)(2,1)S(1)} %get-tuple-element.36.refs_0_), channel_id=1, source_target_pairs={{0,2},{1,3},{2,0},{3,1},{4,6},{5,7},{6,4},{7,5},{8,10},{9,11},{10,... | collective-permute-start | bytes 761864 | tf_op jit(solution)/shard_map/ppermute | solution.py:488
  44.4 7.5 %collective-permute-start.10 = (bf16[2,32,2304]{2,1,0:T(8,128)(2,1)S(1)}, bf16[2,32,2304]{2,1,0:T(8,128)(2,1)S(1)}, u32[]{:S(2)}, u32[]{:S(2)}) collective-permute-start(bf16[2,32,2304]{2,1,0:T(8,128)(2,1)S(1)} %get-tuple-element.44.refs_2_), channel_id=1, source_target_pairs={{0,1},{1,0},{2,3},{3,2},{4,5},{5,4},{6,7},{7,6},{8,9},{9,8},{10,11... | collective-permute-start | bytes 884744 | tf_op jit(solution)/shard_map/ppermute | solution.py:494
  44.6 7.3 %collective-permute-start.12 = (bf16[2,16,3072]{2,1,0:T(8,128)(2,1)S(1)}, bf16[2,16,3072]{2,1,0:T(8,128)(2,1)S(1)}, u32[]{:S(2)}, u32[]{:S(2)}) collective-permute-start(bf16[2,16,3072]{2,1,0:T(8,128)(2,1)S(1)} %get-tuple-element.47.refs_0_), channel_id=1, source_target_pairs={{0,2},{1,3},{2,0},{3,1},{4,6},{5,7},{6,4},{7,5},{8,10},{9,11},{10,... | collective-permute-start | bytes 589832 | tf_op jit(solution)/shard_map/ppermute | solution.py:488
  45.8 6.1 %collective-permute-start.8 = (bf16[1,8,1664]{2,1,0:T(8,128)(2,1)S(1)}, bf16[1,8,1664]{2,1,0:T(8,128)(2,1)S(1)}, u32[]{:S(2)}, u32[]{:S(2)}) collective-permute-start(bf16[1,8,1664]{2,1,0:T(8,128)(2,1)S(1)} %get-tuple-element.38), channel_id=1, source_target_pairs={{0,8},{4,12},{8,0},{12,4},{1,9},{5,13},{9,1},{13,5},{2,10},{6,14},... | collective-permute-start | bytes 79880 | tf_op jit(solution)/shard_map/ppermute | solution.py:491
  47.9 10.6 %copy-start = (bf16[2,1,1024,512]{3,2,1,0:T(8,128)(2,1)S(1)}, bf16[2,1,1024,512]{3,2,1,0:T(8,128)(2,1)}, u32[]{:S(2)}) copy-start(bf16[2,1,1024,512]{3,2,1,0:T(8,128)(2,1)} %param.14) | copy-start | bytes 6291460
  47.9 10.6 %copy-start.4 = (s32[4]{0:T(128)S(1)}, s32[4]{0:T(128)}, u32[]{:S(2)}) copy-start(s32[4]{0:T(128)} %copy-done.3) | copy-start | bytes 52
  47.9 10.6 %copy-start.5 = (s32[2,1]{0,1:T(1,128)S(1)}, s32[2,1]{0,1:T(1,128)}, u32[]{:S(2)}) copy-start(s32[2,1]{0,1:T(1,128)} %param.15) | copy-start | bytes 28
  52.0 1.5 %collective-permute-start.13 = (bf16[2,32,1536]{2,1,0:T(8,128)(2,1)S(1)}, bf16[2,32,1536]{2,1,0:T(8,128)(2,1)S(1)}, u32[]{:S(2)}, u32[]{:S(2)}) collective-permute-start(bf16[2,32,1536]{2,1,0:T(8,128)(2,1)S(1)} %get-tuple-element.50), channel_id=1, source_target_pairs={{0,1},{1,0},{2,3},{3,2},{4,5},{5,4},{6,7},{7,6},{8,9},{9,8},{10,11... | collective-permute-start | bytes 589832 | tf_op jit(solution)/shard_map/ppermute | solution.py:494
  52.1 8.9 %collective-permute-start.14 = (bf16[2,16,2304]{2,1,0:T(8,128)(2,1)S(1)}, bf16[2,16,2304]{2,1,0:T(8,128)(2,1)S(1)}, u32[]{:S(2)}, u32[]{:S(2)}) collective-permute-start(bf16[2,16,2304]{2,1,0:T(8,128)(2,1)S(1)} %get-tuple-element.56), channel_id=1, source_target_pairs={{0,2},{1,3},{2,0},{3,1},{4,6},{5,7},{6,4},{7,5},{8,10},{9,11},{10,... | collective-permute-start | bytes 442376 | tf_op jit(solution)/shard_map/ppermute | solution.py:488
  53.6 7.5 %collective-permute-start.15 = (bf16[2,16,1536]{2,1,0:T(8,128)(2,1)S(1)}, bf16[2,16,1536]{2,1,0:T(8,128)(2,1)S(1)}, u32[]{:S(2)}, u32[]{:S(2)}) collective-permute-start(bf16[2,16,1536]{2,1,0:T(8,128)(2,1)S(1)} %get-tuple-element.52.refs_2_.refs_4_), channel_id=1, source_target_pairs={{0,2},{1,3},{2,0},{3,1},{4,6},{5,7},{6,4},{7,5},{8,10},{9,11},{10,... | collective-permute-start | bytes 294920 | tf_op jit(solution)/shard_map/ppermute | solution.py:488
  54.6 3.9 %collective-permute-start.9 = (bf16[2,4,1664]{2,1,0:T(4,128)(2,1)S(1)}, bf16[2,4,1664]{2,1,0:T(4,128)(2,1)S(1)}, u32[]{:S(2)}, u32[]{:S(2)}) collective-permute-start(bf16[2,4,1664]{2,1,0:T(4,128)(2,1)S(1)} %get-tuple-element.40), channel_id=1, source_target_pairs={{0,4},{4,0},{8,12},{12,8},{1,5},{5,1},{9,13},{13,9},{2,6},{6,2},{1... | collective-permute-start | bytes 79880 | tf_op jit(solution)/shard_map/ppermute | solution.py:491
